TPU v7x, 512 devices: a whole 4x4x16 slice. The times are simulated.
512 devices in a mesh: dp: 4 (over z_hi, core), ep: 32 (over z_lo, y), tp: 4 (over x).
Axes of the slice: x: 4, y: 4, z: 16 (z_hi: 2, z_lo: 8; z = z_hi * 8 + z_lo), core: 2. Of those that a mesh axis runs over, the one named last changes fastest.
Arguments:
- tokens: bfloat16 [2, 8192, 4096], P(None, ('dp', 'ep')), may hold values from -6 to 6
- expert_ids: int32 [2, 8192, 8], P(None, ('dp', 'ep')), may hold values from 0 to 31, as said below
- slot_index: int32 [2, 8192, 8], P(None, ('dp', 'ep')), may hold values from -1 to 17, as said below
- gate_weights: float32 [2, 8192, 8], P(None, ('dp', 'ep')), may hold values from 0.02 to 0.3
- up_gradient: bfloat16 [4, 2, 32, 576, 1536], P('dp', None, 'ep', None, 'tp'), may hold values from -6 to 6
- up_weight: bfloat16 [32, 4096, 1536], P('ep', 'tp', 'dp'), may hold values from -0.09375 to 0.09375
- attention_partial: bfloat16 [4, 2, 8192, 4096], P('tp', None, ('dp', 'ep')), may hold values from -6 to 6
- residual_gradient: bfloat16 [2, 8192, 4096], P(None, ('dp', 'ep'), 'tp'), may hold values from -6 to 6
Outputs:
- token_gradient: bfloat16 [2, 8192, 4096], P(None, ('dp', 'ep'), 'tp')
- weight_gradient: bfloat16 [32, 4096, 1536], P('ep', 'tp', 'dp')
Inputs may be any that keep to these rules, and one draw needn't show every extreme that they name: `expert_ids`: each token names 8 different experts. `slot_index`: within the rows of one device and one micro-batch no two routes share an expert and a slot, and the kept routes of an expert take slots 0, 1, 2 and so on; -1 marks a dropped route. In every micro-batch some expert fills all 18 slots of every device.
All inputs are finite; a program needn't handle non-finite values.
Results may differ from a plain program's by a relative error of at most 0.013.
Values may be sent and summed in bfloat16 or wider, within the bound.
No kernel may reach another device: no remote copies, remote signals or barrier semaphores. Data moves between devices by JAX's collectives and lax.ppermute only.
A program may use at most 64 MiB of HBM per device.

v0:
```python
import jax
import jax.numpy as jnp
from jax import lax
from jax.sharding import PartitionSpec as P


def route_tables(expert_row, slot_row, gate_row, capacity, place_iota):
    position = jnp.where(slot_row >= 0, expert_row * capacity + slot_row, -1)
    matches = position[:, :, None] == place_iota
    picks = jnp.any(matches, axis=1).astype(jnp.bfloat16)
    slot_gate = jnp.sum(jnp.where(matches, gate_row[:, :, None], 0.0), axis=(0, 1))
    route_gate = jnp.where(slot_row >= 0, gate_row, 0.0)
    return (jnp.maximum(position, 0), picks, slot_gate, route_gate)


def make_adder(hidden, piece):
    return jnp.einsum("...erf,edf->...erd", hidden, piece, preferred_element_type=jnp.float32)


def on_device(
    tokens,
    expert_ids,
    slot_index,
    gate_weights,
    up_gradient,
    up_weight,
    attention_partial,
    residual_gradient,
):
    batches = tokens.shape[0]
    exp_local, quarter, ff_part = up_weight.shape
    buffer_rows = up_gradient.shape[3]
    ep_count = lax.axis_size("ep")
    capacity = buffer_rows // ep_count
    experts_all = exp_local * ep_count
    lane_index = lax.axis_index("tp")
    place_iota = jnp.arange(experts_all * capacity, dtype=jnp.int32)
    hidden_full = lax.all_gather(up_gradient[0], "tp", axis=3, tiled=True)
    positions = []
    route_gates = []
    inbound = []
    for batch_index in range(batches):
        position, picks, slot_gate, route_gate = route_tables(
            expert_ids[batch_index],
            slot_index[batch_index],
            gate_weights[batch_index],
            capacity,
            place_iota,
        )
        own_part = lax.dynamic_slice_in_dim(tokens[batch_index], lane_index * quarter, quarter, 1)
        gathered_rows = jnp.dot(picks.T, own_part, preferred_element_type=jnp.float32)
        outgoing = (
            (gathered_rows * slot_gate[:, None])
            .astype(jnp.bfloat16)
            .reshape(ep_count, exp_local, capacity, quarter)
        )
        arrived = lax.all_to_all(outgoing, "ep", split_axis=0, concat_axis=2, tiled=True)
        positions.append(position)
        route_gates.append(route_gate)
        inbound.append(arrived.reshape(exp_local, buffer_rows, quarter))
    input_parts = []
    for batch_index in range(batches):
        input_parts.append(
            make_adder(
                hidden_full[batch_index], lax.all_gather(up_weight, "dp", axis=2, tiled=True)
            )
        )
    expert_parts = []
    for batch_index in range(batches):
        outgoing = (
            input_parts[batch_index]
            .astype(jnp.bfloat16)
            .reshape(exp_local, ep_count, capacity, quarter)
        )
        returned = lax.all_to_all(outgoing, "ep", split_axis=1, concat_axis=0, tiled=True).reshape(
            experts_all * capacity, quarter
        )
        picked_rows = jnp.take(returned, positions[batch_index], axis=0)
        expert_parts.append(
            jnp.sum(picked_rows.astype(jnp.float32) * route_gates[batch_index][:, :, None], axis=1)
        )
    attention_total = lax.psum_scatter(
        attention_partial[0].astype(jnp.float32).astype(jnp.bfloat16),
        "tp",
        scatter_dimension=2,
        tiled=True,
    ).astype(jnp.float32)
    token_gradient = (
        residual_gradient.astype(jnp.float32) + attention_total + jnp.stack(expert_parts)
    ).astype(jnp.bfloat16)
    partial_sum = jnp.zeros((exp_local, quarter, hidden_full.shape[3]), jnp.float32)
    for batch_index in range(batches):
        partial_sum = partial_sum + jnp.einsum(
            "erd,erf->edf",
            inbound[batch_index],
            hidden_full[batch_index],
            preferred_element_type=jnp.float32,
        )
    summed = lax.psum_scatter(
        partial_sum.astype(jnp.bfloat16), "dp", scatter_dimension=2, tiled=True
    ).astype(jnp.float32)
    weight_gradient = (summed * (1.0 / lax.axis_size("dp"))).astype(jnp.bfloat16)
    return (token_gradient, weight_gradient)


def solution(mesh):
    return jax.shard_map(
        on_device,
        mesh=mesh,
        in_specs=(
            P(None, ("dp", "ep"), None),
            P(None, ("dp", "ep"), None),
            P(None, ("dp", "ep"), None),
            P(None, ("dp", "ep"), None),
            P("dp", None, "ep", None, "tp"),
            P("ep", "tp", "dp"),
            P("tp", None, ("dp", "ep"), None),
            P(None, ("dp", "ep"), "tp"),
        ),
        out_specs=(P(None, ("dp", "ep"), "tp"), P("ep", "tp", "dp")),
        check_vma=False,
    )
```

profile of v0, /device:TPU:1, one launch (start us, length us, event | category | flops | bytes accessed | tf_op | source)
XLA Modules:
  0.0 494.6 jit_solution(8500235374546426128)
XLA Ops:
  10.2 0.9 fusion.21
  11.6 1.3 reshape.148
  13.0 16.1 %all-to-all-start.2 = ((bf16[32,1,18,1024]{3,2,1,0:T(8,128)(2,1)}), bf16[32,1,18,1024]{3,2,1,0:T(8,128)(2,1)S(1)}, u32[]{:S(2)}, u32[]{:S(2)}) async-start(bf16[32,1,18,1024]{3,2,1,0:T(8,128)(2,1)} %bitcast.17), calls=%async_computation.3 | async-start | bytes 3145728 | tf_op jit(solution)/shard_map/all_to_all | solution.py:57
  30.7 1.4 multiply_convert_fusion
  32.1 1.3 reshape.150
  33.5 135.1 %all-to-all-done.2 = bf16[32,1,18,1024]{3,2,1,0:T(8,128)(2,1)S(1)} async-done(((bf16[32,1,18,1024]{3,2,1,0:T(8,128)(2,1)}), bf16[32,1,18,1024]{3,2,1,0:T(8,128)(2,1)S(1)}, u32[]{:S(2)}, u32[]{:S(2)}) %all-to-all-start.2) | async-done | bytes 1179680 | tf_op jit(solution)/shard_map/all_to_all | solution.py:57
  168.6 7.9 %all-to-all-start.3 = ((bf16[32,1,18,1024]{3,2,1,0:T(8,128)(2,1)}), bf16[32,1,18,1024]{3,2,1,0:T(8,128)(2,1)S(1)}, u32[]{:S(2)}, u32[]{:S(2)}) async-start(bf16[32,1,18,1024]{3,2,1,0:T(8,128)(2,1)} %bitcast.83), calls=%async_computation.4 | async-start | bytes 3145728 | tf_op jit(solution)/shard_map/all_to_all | solution.py:57
  176.6 39.1 %all-gather.6.cloned.1.call-done = bf16[1,2,1,576,1536]{4,3,2,1,0:T(8,128)(2,1)} async-done(((bf16[1,2,1,576,384]{4,3,2,1,0:T(8,128)(2,1)}), bf16[1,2,1,576,1536]{4,3,2,1,0:T(8,128)(2,1)}) %all-gather.6.cloned.1.call-update) | async-done | bytes 3538960 | tf_op jit(solution)/shard_map/all_gather | solution.py:38
  215.7 5.5 %fusion.6 = bf16[576,1024]{1,0:T(8,128)(2,1)} fusion(bf16[1,1024,1536]{2,1,0:T(8,128)(2,1)} %all-gather.4.cloned.1.call-done, bf16[1,2,1,576,1536]{4,3,2,1,0:T(8,128)(2,1)} %all-gather.6.cloned.1.call-done), kind=kOutput, calls=%fused_computation.18 | convolution fusion | flops 1812529152 | bytes 6094848 | tf_op jit(solution)/shard_map/...erf,edf->...erd/dot_general | solution.py:17
  221.1 2.4 reshape.143
  223.5 25.1 %all-to-all-done.3 = bf16[32,1,18,1024]{3,2,1,0:T(8,128)(2,1)S(1)} async-done(((bf16[32,1,18,1024]{3,2,1,0:T(8,128)(2,1)}), bf16[32,1,18,1024]{3,2,1,0:T(8,128)(2,1)S(1)}, u32[]{:S(2)}, u32[]{:S(2)}) %all-to-all-start.3) | async-done | bytes 1179680 | tf_op jit(solution)/shard_map/all_to_all | solution.py:57
  248.6 1.1 copy-done
  249.7 8.1 %all-to-all-start = ((bf16[1,32,18,1024]{3,2,0,1:T(8,128)(2,1)}), bf16[1,32,18,1024]{3,2,0,1:T(8,128)(2,1)S(1)}, u32[]{:S(2)}, u32[]{:S(2)}) async-start(bf16[1,32,18,1024]{3,2,0,1:T(8,128)(2,1)} %bitcast.82), calls=%async_computation.1 | async-start | bytes 3145728 | tf_op jit(solution)/shard_map/all_to_all | solution.py:75
  258.8 1.2 reshape.149
  260.0 2.5 reshape.151
  262.5 4.3 fusion.5
  266.8 4.3 fusion
  271.1 15.7 %copy.56 = bf16[1,1024,1536]{1,0,2:T(2,128)(2,1)} copy(bf16[1,1024,1536]{2,1,0:T(8,128)(2,1)} %fusion) | data formatting | bytes 6291456
  286.8 5.7 %copy.60 = bf16[1536,1,1024]{2,0,1:T(8,128)(2,1)} copy(bf16[1536,1,1024]{2,1,0:T(2,128)(2,1)} %bitcast.80) | data formatting | bytes 6291456
  292.6 4.4 fusion.9
  297.0 1.3 reshape.146
  298.4 31.5 %all-to-all-done = bf16[1,32,18,1024]{3,2,0,1:T(8,128)(2,1)S(1)} async-done(((bf16[1,32,18,1024]{3,2,0,1:T(8,128)(2,1)}), bf16[1,32,18,1024]{3,2,0,1:T(8,128)(2,1)S(1)}, u32[]{:S(2)}, u32[]{:S(2)}) %all-to-all-start) | async-done | bytes 1179680 | tf_op jit(solution)/shard_map/all_to_all | solution.py:75
  329.8 8.4 %all-to-all-start.1 = ((bf16[1,32,18,1024]{3,2,0,1:T(8,128)(2,1)}), bf16[1,32,18,1024]{3,2,0,1:T(8,128)(2,1)}, u32[]{:S(2)}, u32[]{:S(2)}) async-start(bf16[1,32,18,1024]{3,2,0,1:T(8,128)(2,1)} %bitcast.12), calls=%async_computation.2 | async-start | bytes 3145728 | tf_op jit(solution)/shard_map/all_to_all | solution.py:75
  339.5 2.8 gather_fusion
  342.3 134.5 %all-to-all-done.1 = bf16[1,32,18,1024]{3,2,0,1:T(8,128)(2,1)} async-done(((bf16[1,32,18,1024]{3,2,0,1:T(8,128)(2,1)}), bf16[1,32,18,1024]{3,2,0,1:T(8,128)(2,1)}, u32[]{:S(2)}, u32[]{:S(2)}) %all-to-all-start.1) | async-done | bytes 1179680 | tf_op jit(solution)/shard_map/all_to_all | solution.py:75
  476.7 1.6 reshape.147
  478.3 2.1 gather_fusion.1
  480.4 0.8 multiply_reduce_fusion.1
  482.0 1.7 fusion.14
  483.8 1.9 reshape_bitcast_fusion
  485.7 1.3 copy.57
  487.0 1.0 multiply_convert_fusion.2
  (53 shorter events, 8.1 us)
Async XLA Ops:
  7.2 3.1 copy-start.4
  7.2 169.4 %all-gather.4.cloned.1.call-start = ((), (), s32[]{:S(2)}) async-start(), calls=%async_computation.7 | async-start | bytes 3932160 | tf_op jit(solution)/shard_map/all_gather | solution.py:65
  13.0 155.6 %all-to-all-start.2 = ((bf16[32,1,18,1024]{3,2,1,0:T(8,128)(2,1)}), bf16[32,1,18,1024]{3,2,1,0:T(8,128)(2,1)S(1)}, u32[]{:S(2)}, u32[]{:S(2)}) async-start(bf16[32,1,18,1024]{3,2,1,0:T(8,128)(2,1)} %bitcast.17), calls=%async_computation.3 | async-start | bytes 3145728 | tf_op jit(solution)/shard_map/all_to_all | solution.py:57
  29.1 186.6 %all-gather.6.cloned.1.call-start = ((), (), s32[]{:S(2)}) async-start(), calls=%async_computation.8 | async-start | bytes 4423680 | tf_op jit(solution)/shard_map/all_gather | solution.py:38
  168.6 79.9 %all-to-all-start.3 = ((bf16[32,1,18,1024]{3,2,1,0:T(8,128)(2,1)}), bf16[32,1,18,1024]{3,2,1,0:T(8,128)(2,1)S(1)}, u32[]{:S(2)}, u32[]{:S(2)}) async-start(bf16[32,1,18,1024]{3,2,1,0:T(8,128)(2,1)} %bitcast.83), calls=%async_computation.4 | async-start | bytes 3145728 | tf_op jit(solution)/shard_map/all_to_all | solution.py:57
  248.6 1.1 copy-start
  249.7 80.1 %all-to-all-start = ((bf16[1,32,18,1024]{3,2,0,1:T(8,128)(2,1)}), bf16[1,32,18,1024]{3,2,0,1:T(8,128)(2,1)S(1)}, u32[]{:S(2)}, u32[]{:S(2)}) async-start(bf16[1,32,18,1024]{3,2,0,1:T(8,128)(2,1)} %bitcast.82), calls=%async_computation.1 | async-start | bytes 3145728 | tf_op jit(solution)/shard_map/all_to_all | solution.py:75
  257.8 224.2 %reduce-scatter.5.cloned.1.call-start = ((), (), s32[]{:S(2)}) async-start(), calls=%async_computation.6 | async-start | bytes 1310720 | tf_op jit(solution)/shard_map/reduce_scatter | solution.py:82
  258.6 225.2 %reduce-scatter.7.cloned.1.call-start = ((), (), s32[]{:S(2)}) async-start(), calls=%async_computation.9 | async-start | bytes 3932160
  260.0 2.5 copy-start.2
  262.5 4.3 copy-start.3
  262.5 4.3 copy-start.8
  298.4 40.2 %copy-start.6 = (s32[2,64,8]{1,2,0:T(8,128)S(1)}, s32[2,64,8]{1,2,0:T(8,128)}, u32[]{:S(2)}) copy-start(s32[2,64,8]{1,2,0:T(8,128)} %param.12) | copy-start | bytes 12292
  298.4 40.2 %copy-start.7 = (f32[2,64,8]{1,2,0:T(8,128)S(1)}, f32[2,64,8]{1,2,0:T(8,128)}, u32[]{:S(2)}) copy-start(f32[2,64,8]{1,2,0:T(8,128)} %param.13) | copy-start | bytes 12292
  329.8 146.9 %all-to-all-start.1 = ((bf16[1,32,18,1024]{3,2,0,1:T(8,128)(2,1)}), bf16[1,32,18,1024]{3,2,0,1:T(8,128)(2,1)}, u32[]{:S(2)}, u32[]{:S(2)}) async-start(bf16[1,32,18,1024]{3,2,0,1:T(8,128)(2,1)} %bitcast.12), calls=%async_computation.2 | async-start | bytes 3145728 | tf_op jit(solution)/shard_map/all_to_all | solution.py:75
  478.3 2.1 copy-start.1
  480.4 1.6 copy-start.5
Sparse Core Ops, SparseCore 0:
  10.1 93.2 all-gather.3
  105.5 110.0 all-gather.5
  261.5 29.6 reduce-scatter.4
  294.4 112.3 reduce-scatter.6
where the time goes:
time: 496 us; the launch traced here: 495 us
  waiting for transfers between devices  367 us (74%)
  local copies, waits for them, and re-layouts  45.4 us (9%)
  starting transfers between devices  40.9 us (8%)
  matrix products  20.4 us (4%)
  between operations  14 us (3%)
  other arithmetic  6.49 us (1%)
    all_to_all x2, waiting for transfers between devices, on_device(): lax.all_to_all(outgoing, 'ep', split_axis=1, concat_axis=0, tiled=True)  166 us
    all_to_all x2, waiting for transfers between devices, on_device(): lax.all_to_all(outgoing, 'ep', split_axis=0, concat_axis=2, tiled=True)  160 us
    all_gather x1, waiting for transfers between devices, on_device(): hidden_full = lax.all_gather(up_gradient[0], 'tp', axis=3, tiled=True)  39.1 us
    unnamed x22, local copies, waits for them, and re-layouts  25.8 us
    all_to_all x2, starting transfers between devices, on_device(): lax.all_to_all(outgoing, 'ep', split_axis=0, concat_axis=2, tiled=True)  24 us
    all_to_all x2, starting transfers between devices, on_device(): lax.all_to_all(outgoing, 'ep', split_axis=1, concat_axis=0, tiled=True)  16.5 us
  transfers between devices with their start and end apart: 8, of which 5 were waited for; matrix products, arithmetic and copies ran while one was open for 14% of the time, Pallas kernels for 0%

commit v1 on v0

v1 whole, which is shorter than its diff:
```python
import jax
import jax.numpy as jnp
from jax import lax
from jax.sharding import Mesh, PartitionSpec as P

AXES = ("zh", "co", "zl", "y", "x")
SIZES = (2, 2, 8, 4, 4)
SWAP = [(0, 1), (1, 0)]


def slot_tables(expert_ids, slot_index, gate_weights, capacity, places):
    rows = expert_ids.shape[1]
    position = jnp.where(slot_index >= 0, expert_ids * capacity + slot_index, -1)
    matches = position[..., None] == jnp.arange(places, dtype=jnp.int32)
    token = jnp.arange(1, rows + 1, dtype=jnp.float32)[None, :, None, None]
    held = jnp.sum(jnp.where(matches, token, 0.0), axis=(1, 2)) - 1.0
    gate = jnp.sum(jnp.where(matches, gate_weights[..., None], 0.0), axis=(1, 2))
    return held, gate


def on_device(
    tokens,
    expert_ids,
    slot_index,
    gate_weights,
    up_gradient,
    up_weight,
    attention_partial,
    residual_gradient,
):
    nzl, ny, nx = (lax.axis_size(a) for a in ("zl", "y", "x"))
    zh, co, x = (lax.axis_index(a) for a in ("zh", "co", "x"))
    batches, held_tokens, width = tokens.shape
    quarter = width // nx
    buffer_rows, ff_part = up_gradient.shape[3:]
    capacity = buffer_rows // (nzl * ny)
    group = nzl * batches * capacity
    rows = ny * group
    bf16, f32 = jnp.bfloat16, jnp.float32

    own_part = lax.dynamic_slice_in_dim(tokens, x * quarter, quarter, 2)
    line = lax.all_gather(
        own_part.reshape(batches * held_tokens, quarter), "zl", axis=0, tiled=True
    )

    own = up_weight[0]
    across = lax.ppermute(own, "zh", SWAP)

    held, gate = slot_tables(
        expert_ids, slot_index, gate_weights, capacity, nzl * ny * capacity
    )
    table = jnp.stack([held, gate]).reshape(2, batches, nzl, ny * capacity)
    table = lax.all_to_all(
        table.transpose(2, 0, 1, 3), "zl", split_axis=0, concat_axis=0, tiled=True
    )
    table = table.reshape(nzl, 2, batches, ny, capacity).transpose(1, 3, 2, 0, 4)
    held = table[0].astype(jnp.int32)
    start = (
        jnp.arange(nzl, dtype=jnp.int32)[None, None, :, None] * (batches * held_tokens)
        + jnp.arange(batches, dtype=jnp.int32)[None, :, None, None] * held_tokens
    )
    column = jnp.where(held >= 0, held + start, -1).reshape(rows)
    slot_gate = table[1].reshape(rows)
    column_iota = jnp.arange(nzl * batches * held_tokens, dtype=jnp.int32)

    r = jnp.arange(rows, dtype=jnp.int32)
    r_slot = r % capacity
    r_zl = (r // capacity) % nzl
    r_batch = (r // (capacity * nzl)) % batches
    r_y = r // group
    source_row = ((r_batch * nzl + r_zl) * ny + r_y) * capacity + r_slot
    order = (source_row[:, None] == r[None, :]).astype(bf16)
    hidden = jnp.dot(
        order, up_gradient.reshape(rows, ff_part), preferred_element_type=f32
    ).astype(bf16)
    hidden = lax.all_to_all(
        jnp.broadcast_to(hidden, (nx, rows, ff_part)),
        "x",
        split_axis=0,
        concat_axis=0,
        tiled=True,
    )

    shares = attention_partial.reshape(batches * held_tokens, nx, quarter)
    shares = lax.all_to_all(
        shares.transpose(1, 0, 2), "x", split_axis=0, concat_axis=0, tiled=True
    )
    base = residual_gradient.reshape(batches * held_tokens, quarter).astype(f32) + jnp.sum(
        shares.astype(f32), axis=0
    )

    pick = (column[:, None] == column_iota[None, :]).astype(bf16)
    sent = jnp.dot(pick, line, preferred_element_type=f32) * slot_gate[:, None]
    inbound = lax.all_to_all(
        sent.astype(bf16).reshape(ny, group, quarter),
        "y",
        split_axis=0,
        concat_axis=0,
        tiled=True,
    ).reshape(rows, quarter)

    def part_of(a, b):
        return lax.dynamic_index_in_dim(hidden, 2 * a + b, 0, keepdims=False)

    beside = lax.ppermute(own, "co", SWAP)
    diagonal = lax.ppermute(across, "co", SWAP)
    back = jnp.zeros((rows, quarter), f32)
    for a, b, weight in (
        (zh, co, own),
        (zh, 1 - co, beside),
        (1 - zh, co, across),
        (1 - zh, 1 - co, diagonal),
    ):
        back = back + jnp.einsum("rf,df->rd", part_of(a, b), weight, preferred_element_type=f32)
    returned = lax.all_to_all(
        back.astype(bf16).reshape(ny, group, quarter),
        "y",
        split_axis=0,
        concat_axis=0,
        tiled=True,
    ).reshape(rows, quarter)

    def grad_of(a, b):
        return jnp.einsum("rd,rf->df", inbound, part_of(a, b), preferred_element_type=f32)

    other_far = lax.ppermute(grad_of(1 - zh, 1 - co).astype(bf16), "co", SWAP)
    other_near = lax.ppermute(grad_of(zh, 1 - co).astype(bf16), "co", SWAP)
    far = grad_of(1 - zh, co) + other_far.astype(f32)
    far = lax.ppermute(far.astype(bf16), "zh", SWAP)
    near = grad_of(zh, co) + other_near.astype(f32)
    weight_gradient = ((near + far.astype(f32)) * 0.25).astype(bf16)

    gate_high = lax.reduce_precision(slot_gate, 8, 7)
    gate_low = slot_gate - gate_high
    mine = column[None, :] == column_iota[:, None]
    spread = jnp.dot(
        jnp.where(mine, gate_high[None, :], 0.0).astype(bf16),
        returned,
        preferred_element_type=f32,
    ) + jnp.dot(
        jnp.where(mine, gate_low[None, :], 0.0).astype(bf16),
        returned,
        preferred_element_type=f32,
    )
    expert_part = lax.psum_scatter(spread.astype(bf16), "zl", scatter_dimension=0, tiled=True)
    token_gradient = (base + expert_part.astype(f32)).astype(bf16)
    return (
        token_gradient.reshape(batches, held_tokens, quarter),
        weight_gradient[None],
    )


def solution(mesh):
    split = Mesh(mesh.devices.reshape(SIZES), AXES)
    dp, ep, tp = ("zh", "co"), ("zl", "y"), "x"
    return jax.shard_map(
        on_device,
        mesh=split,
        in_specs=(
            P(None, dp + ep, None),
            P(None, dp + ep, None),
            P(None, dp + ep, None),
            P(None, dp + ep, None),
            P(dp, None, ep, None, tp),
            P(ep, tp, dp),
            P(tp, None, dp + ep, None),
            P(None, dp + ep, tp),
        ),
        out_specs=(P(None, dp + ep, tp), P(ep, tp, dp)),
        check_vma=False,
    )
```

time: 496 us -> 346 us (0.70)
  waiting for transfers between devices: 367 us -> 167 us
  starting transfers between devices: 40.9 us -> 101 us
  local copies, waits for them, and re-layouts: 45.4 us -> 9.07 us
  matrix products: 20.4 us -> 45.4 us
    all_to_all x4 -> x5, waiting for transfers between devices: 326 us -> 40.7 us  [the longest x1 22.1 us: on_device(): lax.all_to_all(back.astype(bf16).reshape(ny, group, quarter), 'y', split_...]
    ppermute x0 -> x6, waiting for transfers between devices: none -> 127 us  [the longest x1 71.2 us: on_device(): far = lax.ppermute(far.astype(bf16), 'zh', SWAP)]
    all_gather x2 -> x1, waiting for transfers between devices: 39.1 us -> 0.02 us  [on_device(): lax.all_gather(own_part.reshape(batches * held_tokens, quarter), 'zl', ax...]
    ppermute x0 -> x6, starting transfers between devices: none -> 37.3 us  [the longest x1 10.1 us: on_device(): across = lax.ppermute(own, 'zh', SWAP)]
    dot_general x6 -> x12, matrix products: 20.4 us -> 45.4 us  [the longest x4 15.8 us: grad_of(): jnp.einsum('rd,rf->df', inbound, part_of(a, b), preferred_element_type=f32)]
    unnamed x22 -> x21, local copies, waits for them, and re-layouts: 25.8 us -> 1.55 us
    all_to_all x4 -> x5, starting transfers between devices: 40.6 us -> 63.3 us  [the longest x1 46.5 us: on_device(): lax.all_to_all(table.transpose(2, 0, 1, 3), 'zl', split_axis=0, concat_ax...]
    reshape x6 -> x3, local copies, waits for them, and re-layouts: 8.37 us -> 1.98 us  [the longest x1 1.86 us: on_device(): shares = attention_partial.reshape(batches * held_tokens, nx, quarter)]
  transfers between devices with their start and end apart: 8 -> 13, of which waited for: 5 -> 4; matrix products, arithmetic and copies ran while one was open for 14% -> 15% of each run, Pallas kernels for 0% -> 0%
where the time goes in v1:
time: 346 us; the launch traced here: 342 us
  waiting for transfers between devices  167 us (48%)
  starting transfers between devices  101 us (29%)
  matrix products  45.4 us (13%)
  between operations  14.4 us (4%)
  local copies, waits for them, and re-layouts  9.07 us (3%)
  other arithmetic  5.15 us (1%)
    ppermute x1, waiting for transfers between devices, on_device(): far = lax.ppermute(far.astype(bf16), 'zh', SWAP)  71.2 us
    ppermute x1, waiting for transfers between devices, on_device(): across = lax.ppermute(own, 'zh', SWAP)  55.4 us
    all_to_all x1, starting transfers between devices, on_device(): lax.all_to_all(table.transpose(2, 0, 1, 3), 'zl', split_axis=0, concat_ax...  46.5 us
    all_to_all x1, waiting for transfers between devices, on_device(): lax.all_to_all(back.astype(bf16).reshape(ny, group, quarter), 'y', split_...  22.1 us
    all_to_all x1, waiting for transfers between devices, on_device(): lax.all_to_all(sent.astype(bf16).reshape(ny, group, quarter), 'y', split_...  18.7 us
    dot_general x4, matrix products, grad_of(): jnp.einsum('rd,rf->df', inbound, part_of(a, b), preferred_element_type=f32)  15.8 us
    dot_general x4, matrix products, on_device(): jnp.einsum('rf,df->rd', part_of(a, b), weight, preferred_element_type=f32)  12.1 us
    ppermute x1, starting transfers between devices, on_device(): across = lax.ppermute(own, 'zh', SWAP)  10.1 us
  transfers between devices with their start and end apart: 13, of which 4 were waited for; matrix products, arithmetic and copies ran while one was open for 15% of the time, Pallas kernels for 0%

profile of v1, /device:TPU:1, one launch (start us, length us, event | category | flops | bytes accessed | tf_op | source)
XLA Modules:
  0.0 342.1 jit_solution(4537042531638614658)
XLA Ops:
  7.2 2.9 fusion.3
  10.1 2.1 broadcast_in_dim.73
  12.2 5.0 %all-to-all-start.2 = ((bf16[4,1152,384]{2,1,0:T(8,128)(2,1)}), bf16[4,1152,384]{2,1,0:T(8,128)(2,1)}, u32[]{:S(2)}, u32[]{:S(2)}) async-start(bf16[4,1152,384]{2,1,0:T(8,128)(2,1)} %broadcast_in_dim.73), calls=%async_computation.2 | async-start | bytes 7077888 | tf_op jit(solution)/shard_map/all_to_all | solution.py:76
  17.2 8.7 %collective-permute-start = (bf16[1024,384]{1,0:T(8,128)(2,1)S(1)}, bf16[1024,384]{1,0:T(8,128)(2,1)S(1)}, u32[]{:S(2)}, u32[]{:S(2)}) collective-permute-start(bf16[1024,384]{1,0:T(8,128)(2,1)S(1)} %bitcast.71), channel_id=1, source_target_pairs={{0,128},{128,0},{1,129},{129,1},{2,130},{130,2},{3,131},{131,3},{4... | collective-permute-start | bytes 2359304 | tf_op jit(solution)/shard_map/ppermute | solution.py:105
  26.0 10.1 %collective-permute-start.1 = (bf16[1024,384]{1,0:T(8,128)(2,1)S(1)}, bf16[1024,384]{1,0:T(8,128)(2,1)S(1)}, u32[]{:S(2)}, u32[]{:S(2)}) collective-permute-start(bf16[1024,384]{1,0:T(8,128)(2,1)S(1)} %bitcast.72), channel_id=1, source_target_pairs={{0,256},{256,0},{1,257},{257,1},{2,258},{258,2},{3,259},{259,3},{4... | collective-permute-start | bytes 2359304 | tf_op jit(solution)/shard_map/ppermute | solution.py:47
  38.6 55.4 %collective-permute-done.1 = bf16[1024,384]{1,0:T(8,128)(2,1)S(1)} collective-permute-done((bf16[1024,384]{1,0:T(8,128)(2,1)S(1)}, bf16[1024,384]{1,0:T(8,128)(2,1)S(1)}, u32[]{:S(2)}, u32[]{:S(2)}) %collective-permute-start.1) | collective-permute-done | bytes 786464 | tf_op jit(solution)/shard_map/ppermute | solution.py:47
  93.9 2.8 collective-permute-start.2
  96.8 46.5 %all-to-all-start.1 = ((f32[8,2,2,72]{3,2,1,0:T(2,128)}), f32[8,2,2,72]{3,2,1,0:T(2,128)S(1)}, u32[]{:S(2)}, u32[]{:S(2)}) async-start(f32[8,2,2,72]{3,2,1,0:T(2,128)} %copy.40), calls=%async_computation.1 | async-start | bytes 32768 | tf_op jit(solution)/shard_map/all_to_all | solution.py:53
  143.3 2.6 fusion.25
  145.9 2.6 convolution_add_fusion.2
  148.5 2.6 convolution_add_fusion.1
  151.1 4.2 %fusion.1 = bf16[1152,1024]{1,0:T(8,128)(2,1)} fusion(f32[1152,1024]{1,0:T(8,128)S(1)} %convolution_add_fusion.1, bf16[1024,384]{1,0:T(8,128)(2,1)} %collective-permute-done.2, bf16[4,1152,384]{2,1,0:T(8,128)(2,1)} %all-to-all-done.2, s32[]{:T(128)S(6)} %select_n.115), kind=kOutput, calls=%fused_computation.11 | convolution fusion | flops 908328960 | bytes 8749060 | tf_op jit(solution)/shard_map/rf,df->rd/dot_general | solution.py:114
  155.4 3.6 %all-to-all-start.3 = ((bf16[4,288,1024]{2,1,0:T(8,128)(2,1)}), bf16[4,288,1024]{2,1,0:T(8,128)(2,1)S(1)}, u32[]{:S(2)}, u32[]{:S(2)}) async-start(bf16[4,288,1024]{2,1,0:T(8,128)(2,1)} %bitcast.10), calls=%async_computation.3 | async-start | bytes 4718592 | tf_op jit(solution)/shard_map/all_to_all | solution.py:115
  159.8 5.8 %fusion.2 = bf16[1152,1024]{1,0:T(8,128)(2,1)} fusion(bf16[1024,1024]{1,0:T(8,128)(2,1)} %all-gather.2.cloned.1.call-done, f32[1152]{0:T(1024)S(1)} %reshape_squeeze.3, s32[1152]{0:T(1024)S(1)} %add_select_fusion.5), kind=kOutput, calls=%fused_computation.12 | convolution fusion | flops 2419458048 | bytes 4465664 | tf_op jit(solution)/shard_map/dot_general | solution.py:93
  165.6 22.1 %all-to-all-done.3 = bf16[4,288,1024]{2,1,0:T(8,128)(2,1)S(1)} async-done(((bf16[4,288,1024]{2,1,0:T(8,128)(2,1)}), bf16[4,288,1024]{2,1,0:T(8,128)(2,1)S(1)}, u32[]{:S(2)}, u32[]{:S(2)}) %all-to-all-start.3) | async-done | bytes 2359328 | tf_op jit(solution)/shard_map/all_to_all | solution.py:115
  187.7 1.4 copy-done.3
  189.1 3.6 %all-to-all-start.4 = ((bf16[4,288,1024]{2,1,0:T(8,128)(2,1)}), bf16[4,288,1024]{2,1,0:T(8,128)(2,1)S(1)}, u32[]{:S(2)}, u32[]{:S(2)}) async-start(bf16[4,288,1024]{2,1,0:T(8,128)(2,1)} %bitcast.69), calls=%async_computation.5 | async-start | bytes 4718592 | tf_op jit(solution)/shard_map/all_to_all | solution.py:94
  193.0 4.7 %fusion.5 = f32[1024,1024]{1,0:T(8,128)S(1)} fusion(bf16[1152,1024]{1,0:T(8,128)(2,1)} %bitcast.67, bf16[1152]{0:T(1024)(128)(2,1)S(1)} %get-tuple-element.7, s32[1152]{0:T(1024)S(1)} %add_select_fusion.5), kind=kOutput, calls=%fused_computation.18 | convolution fusion | flops 2418278400 | bytes 6560512 | tf_op jit(solution)/shard_map/dot_general | solution.py:136
  197.7 4.1 %add_convert_fusion = bf16[1024,1024]{1,0:T(8,128)(2,1)} fusion(f32[1024,1024]{1,0:T(8,128)S(1)} %fusion.5, bf16[1152,1024]{1,0:T(8,128)(2,1)S(1)} %bitcast.68, bf16[1152]{0:T(1024)(128)(2,1)S(1)} %get-tuple-element.6, s32[1152]{0:T(1024)S(1)} %add_select_fusion.5), kind=kOutput, calls=%fused_computation.10 | convolution fusion | flops 2420375552 | bytes 8657664 | tf_op jit(solution)/shard_map/dot_general | solution.py:140
  201.7 18.7 %all-to-all-done.4 = bf16[4,288,1024]{2,1,0:T(8,128)(2,1)S(1)} async-done(((bf16[4,288,1024]{2,1,0:T(8,128)(2,1)}), bf16[4,288,1024]{2,1,0:T(8,128)(2,1)S(1)}, u32[]{:S(2)}, u32[]{:S(2)}) %all-to-all-start.4) | async-done | bytes 2359328 | tf_op jit(solution)/shard_map/all_to_all | solution.py:94
  220.4 4.2 %convolution_convert_fusion = bf16[1024,384]{1,0:T(8,128)(2,1)} fusion(bf16[1152,1024]{1,0:T(8,128)(2,1)S(1)} %bitcast.63, bf16[4,1152,384]{2,1,0:T(8,128)(2,1)} %all-to-all-done.2, s32[]{:T(128)S(6)} %select_n.115), kind=kOutput, calls=%fused_computation.30 | convolution fusion | flops 906362880 | bytes 4030468 | tf_op jit(solution)/shard_map/rd,rf->df/dot_general | solution.py:124
  224.6 4.3 %collective-permute-start.4 = (bf16[1024,384]{1,0:T(8,128)(2,1)}, bf16[1024,384]{1,0:T(8,128)(2,1)}, u32[]{:S(2)}, u32[]{:S(2)}) collective-permute-start(bf16[1024,384]{1,0:T(8,128)(2,1)} %convolution_convert_fusion), channel_id=1, source_target_pairs={{0,128},{128,0},{1,129},{129,1},{2,130},{130,2},{3,131},{131,3},{4... | collective-permute-start | bytes 2359304 | tf_op jit(solution)/shard_map/ppermute | solution.py:126
  228.9 1.9 reshape.206
  232.1 4.5 %all-to-all-start = ((bf16[4,128,1024]{2,1,0:T(8,128)(2,1)}), bf16[4,128,1024]{2,1,0:T(8,128)(2,1)S(1)}, u32[]{:S(2)}, u32[]{:S(2)}) async-start(bf16[4,128,1024]{2,1,0:T(8,128)(2,1)} %copy.37), calls=%async_computation | async-start | bytes 2097152 | tf_op jit(solution)/shard_map/all_to_all | solution.py:85
  236.7 4.4 %convolution_convert_fusion.1 = bf16[1024,384]{1,0:T(8,128)(2,1)} fusion(bf16[1152,1024]{1,0:T(8,128)(2,1)} %bitcast.64, bf16[4,1152,384]{2,1,0:T(8,128)(2,1)} %all-to-all-done.2, s32[]{:T(128)S(6)} %select_n.113), kind=kOutput, calls=%fused_computation.31 | convolution fusion | flops 906362880 | bytes 4030468 | tf_op jit(solution)/shard_map/rd,rf->df/dot_general | solution.py:124
  241.1 2.2 collective-permute-start.3
  243.3 3.8 %add_convert_fusion.1 = bf16[1024,384]{1,0:T(8,128)(2,1)} fusion(bf16[1024,384]{1,0:T(8,128)(2,1)} %collective-permute-done.4, bf16[1152,1024]{1,0:T(8,128)(2,1)S(1)} %bitcast.66, bf16[4,1152,384]{2,1,0:T(8,128)(2,1)} %all-to-all-done.2, s32[]{:T(128)S(6)} %select_n.114), kind=kOutput, calls=%fused_computation.29 | convolution fusion | flops 907149312 | bytes 4816900 | tf_op jit(solution)/shard_map/rd,rf->df/dot_general | solution.py:124
  247.1 9.2 %collective-permute-start.5 = (bf16[1024,384]{1,0:T(8,128)(2,1)}, bf16[1024,384]{1,0:T(8,128)(2,1)}, u32[]{:S(2)}, u32[]{:S(2)}) collective-permute-start(bf16[1024,384]{1,0:T(8,128)(2,1)} %add_convert_fusion.1), channel_id=1, source_target_pairs={{0,256},{256,0},{1,257},{257,1},{2,258},{258,2},{3,259},{259,3},{4... | collective-permute-start | bytes 2359304 | tf_op jit(solution)/shard_map/ppermute | solution.py:129
  256.6 3.4 fusion.23
  260.0 71.2 %collective-permute-done.5 = bf16[1024,384]{1,0:T(8,128)(2,1)} collective-permute-done((bf16[1024,384]{1,0:T(8,128)(2,1)}, bf16[1024,384]{1,0:T(8,128)(2,1)}, u32[]{:S(2)}, u32[]{:S(2)}) %collective-permute-start.5) | collective-permute-done | bytes 786464 | tf_op jit(solution)/shard_map/ppermute | solution.py:129
  331.2 2.4 fusion.27
  333.5 1.8 fusion.37
  (58 shorter events, 5.0 us)
Async XLA Ops:
  7.2 28.9 %copy-start = (bf16[2,64,4096]{2,1,0:T(8,128)(2,1)S(1)}, bf16[2,64,4096]{2,1,0:T(8,128)(2,1)}, u32[]{:S(2)}) copy-start(bf16[2,64,4096]{2,1,0:T(8,128)(2,1)} %param.8) | copy-start | bytes 3145732
  12.2 5.0 %copy-start.5 = (bf16[1,1024,384]{2,1,0:T(8,128)(2,1)S(1)}, bf16[1,1024,384]{2,1,0:T(8,128)(2,1)}, u32[]{:S(2)}) copy-start(bf16[1,1024,384]{2,1,0:T(8,128)(2,1)} %param.13) | copy-start | bytes 2359300
  12.2 24.6 %copy-start.7 = (s32[2,64,8]{1,2,0:T(8,128)S(1)}, s32[2,64,8]{1,2,0:T(8,128)}, u32[]{:S(2)}) copy-start(s32[2,64,8]{1,2,0:T(8,128)} %param.10) | copy-start | bytes 12292
  12.2 24.6 %copy-start.8 = (s32[2,64,8]{1,2,0:T(8,128)S(1)}, s32[2,64,8]{1,2,0:T(8,128)}, u32[]{:S(2)}) copy-start(s32[2,64,8]{1,2,0:T(8,128)} %param.9) | copy-start | bytes 12292
  12.2 24.7 %copy-start.9 = (f32[2,64,8]{1,2,0:T(8,128)S(1)}, f32[2,64,8]{1,2,0:T(8,128)}, u32[]{:S(2)}) copy-start(f32[2,64,8]{1,2,0:T(8,128)} %param.11) | copy-start | bytes 12292
  12.2 84.5 %all-to-all-start.2 = ((bf16[4,1152,384]{2,1,0:T(8,128)(2,1)}), bf16[4,1152,384]{2,1,0:T(8,128)(2,1)}, u32[]{:S(2)}, u32[]{:S(2)}) async-start(bf16[4,1152,384]{2,1,0:T(8,128)(2,1)} %broadcast_in_dim.73), calls=%async_computation.2 | async-start | bytes 7077888 | tf_op jit(solution)/shard_map/all_to_all | solution.py:76
  17.2 142.6 %all-gather.2.cloned.1.call-start = ((), (), s32[]{:S(2)}) async-start(), calls=%async_computation.7 | async-start | bytes 2359296 | tf_op jit(solution)/shard_map/all_gather | solution.py:42
  17.2 128.6 %collective-permute-start = (bf16[1024,384]{1,0:T(8,128)(2,1)S(1)}, bf16[1024,384]{1,0:T(8,128)(2,1)S(1)}, u32[]{:S(2)}, u32[]{:S(2)}) collective-permute-start(bf16[1024,384]{1,0:T(8,128)(2,1)S(1)} %bitcast.71), channel_id=1, source_target_pairs={{0,128},{128,0},{1,129},{129,1},{2,130},{130,2},{3,131},{131,3},{4... | collective-permute-start | bytes 2359304 | tf_op jit(solution)/shard_map/ppermute | solution.py:105
  26.0 68.0 %collective-permute-start.1 = (bf16[1024,384]{1,0:T(8,128)(2,1)S(1)}, bf16[1024,384]{1,0:T(8,128)(2,1)S(1)}, u32[]{:S(2)}, u32[]{:S(2)}) collective-permute-start(bf16[1024,384]{1,0:T(8,128)(2,1)S(1)} %bitcast.72), channel_id=1, source_target_pairs={{0,256},{256,0},{1,257},{257,1},{2,258},{258,2},{3,259},{259,3},{4... | collective-permute-start | bytes 2359304 | tf_op jit(solution)/shard_map/ppermute | solution.py:47
  93.9 57.2 %collective-permute-start.2 = (bf16[1024,384]{1,0:T(8,128)(2,1)S(1)}, bf16[1024,384]{1,0:T(8,128)(2,1)}, u32[]{:S(2)}, u32[]{:S(2)}) collective-permute-start(bf16[1024,384]{1,0:T(8,128)(2,1)S(1)} %collective-permute-done.1), channel_id=1, source_target_pairs={{0,128},{128,0},{1,129},{129,1},{2,130},{130,2},{3,131},{131,3},{4... | collective-permute-start | bytes 2359304 | tf_op jit(solution)/shard_map/ppermute | solution.py:106
  96.8 58.6 %all-to-all-start.1 = ((f32[8,2,2,72]{3,2,1,0:T(2,128)}), f32[8,2,2,72]{3,2,1,0:T(2,128)S(1)}, u32[]{:S(2)}, u32[]{:S(2)}) async-start(f32[8,2,2,72]{3,2,1,0:T(2,128)} %copy.40), calls=%async_computation.1 | async-start | bytes 32768 | tf_op jit(solution)/shard_map/all_to_all | solution.py:53
  155.4 32.3 %all-to-all-start.3 = ((bf16[4,288,1024]{2,1,0:T(8,128)(2,1)}), bf16[4,288,1024]{2,1,0:T(8,128)(2,1)S(1)}, u32[]{:S(2)}, u32[]{:S(2)}) async-start(bf16[4,288,1024]{2,1,0:T(8,128)(2,1)} %bitcast.10), calls=%async_computation.3 | async-start | bytes 4718592 | tf_op jit(solution)/shard_map/all_to_all | solution.py:115
  187.7 1.4 copy-start.3
  189.1 31.3 %all-to-all-start.4 = ((bf16[4,288,1024]{2,1,0:T(8,128)(2,1)}), bf16[4,288,1024]{2,1,0:T(8,128)(2,1)S(1)}, u32[]{:S(2)}, u32[]{:S(2)}) async-start(bf16[4,288,1024]{2,1,0:T(8,128)(2,1)} %bitcast.69), calls=%async_computation.5 | async-start | bytes 4718592 | tf_op jit(solution)/shard_map/all_to_all | solution.py:94
  192.7 140.8 %reduce-scatter.2.cloned.1.call-start = ((), (), s32[]{:S(2)}) async-start(), calls=%async_computation.6 | async-start | bytes 2359296 | tf_op jit(solution)/shard_map/reduce_scatter | solution.py:145
  192.9 4.7 %copy-start.4 = (bf16[4,288,1024]{2,1,0:T(8,128)(2,1)S(1)}, bf16[4,288,1024]{2,1,0:T(8,128)(2,1)}, u32[]{:S(2)}) copy-start(bf16[4,288,1024]{2,1,0:T(8,128)(2,1)} %copy-done.3) | copy-start | bytes 7077892
  220.4 4.2 %copy-start.1 = (bf16[4,288,1024]{2,1,0:T(8,128)(2,1)}, bf16[4,288,1024]{2,1,0:T(8,128)(2,1)S(1)}, u32[]{:S(2)}) copy-start(bf16[4,288,1024]{2,1,0:T(8,128)(2,1)S(1)} %all-to-all-done.4) | copy-start | bytes 7077892
  224.6 18.7 %collective-permute-start.4 = (bf16[1024,384]{1,0:T(8,128)(2,1)}, bf16[1024,384]{1,0:T(8,128)(2,1)}, u32[]{:S(2)}, u32[]{:S(2)}) collective-permute-start(bf16[1024,384]{1,0:T(8,128)(2,1)} %convolution_convert_fusion), channel_id=1, source_target_pairs={{0,128},{128,0},{1,129},{129,1},{2,130},{130,2},{3,131},{131,3},{4... | collective-permute-start | bytes 2359304 | tf_op jit(solution)/shard_map/ppermute | solution.py:126
  232.1 24.2 %all-to-all-start = ((bf16[4,128,1024]{2,1,0:T(8,128)(2,1)}), bf16[4,128,1024]{2,1,0:T(8,128)(2,1)S(1)}, u32[]{:S(2)}, u32[]{:S(2)}) async-start(bf16[4,128,1024]{2,1,0:T(8,128)(2,1)} %copy.37), calls=%async_computation | async-start | bytes 2097152 | tf_op jit(solution)/shard_map/all_to_all | solution.py:85
  236.6 6.6 %copy-start.2 = (bf16[4,288,1024]{2,1,0:T(8,128)(2,1)S(1)}, bf16[4,288,1024]{2,1,0:T(8,128)(2,1)}, u32[]{:S(2)}) copy-start(bf16[4,288,1024]{2,1,0:T(8,128)(2,1)} %copy-done.1) | copy-start | bytes 7077892
  241.1 18.9 %collective-permute-start.3 = (bf16[1024,384]{1,0:T(8,128)(2,1)}, bf16[1024,384]{1,0:T(8,128)(2,1)S(1)}, u32[]{:S(2)}, u32[]{:S(2)}) collective-permute-start(bf16[1024,384]{1,0:T(8,128)(2,1)} %convolution_convert_fusion.1), channel_id=1, source_target_pairs={{0,128},{128,0},{1,129},{129,1},{2,130},{130,2},{3,131},{131,3},{4... | collective-permute-start | bytes 2359304 | tf_op jit(solution)/shard_map/ppermute | solution.py:127
  247.1 84.0 %collective-permute-start.5 = (bf16[1024,384]{1,0:T(8,128)(2,1)}, bf16[1024,384]{1,0:T(8,128)(2,1)}, u32[]{:S(2)}, u32[]{:S(2)}) collective-permute-start(bf16[1024,384]{1,0:T(8,128)(2,1)} %add_convert_fusion.1), channel_id=1, source_target_pairs={{0,256},{256,0},{1,257},{257,1},{2,258},{258,2},{3,259},{259,3},{4... | collective-permute-start | bytes 2359304 | tf_op jit(solution)/shard_map/ppermute | solution.py:129
  260.0 73.6 %copy-start.6 = (bf16[2,64,1024]{2,1,0:T(8,128)(2,1)S(1)}, bf16[2,64,1024]{2,1,0:T(8,128)(2,1)}, u32[]{:S(2)}) copy-start(bf16[2,64,1024]{2,1,0:T(8,128)(2,1)} %param.15) | copy-start | bytes 786436
Sparse Core Ops, SparseCore 0:
  36.9 109.0 all-gather.1
  201.9 81.9 reduce-scatter.1

commit v2 on v1

v2 whole, which is shorter than its diff:
```python
import jax
import jax.numpy as jnp
from jax import lax
from jax.experimental import pallas as pl
from jax.experimental.pallas import tpu as pltpu
from jax.sharding import Mesh, PartitionSpec as P

AXES = ("zh", "co", "zl", "y", "x")
SIZES = (2, 2, 8, 4, 4)
SWAP = [(0, 1), (1, 0)]
BF16, F32, I32 = jnp.bfloat16, jnp.float32, jnp.int32
VMEM = 48 * 1024 * 1024


def dot(a, b, over):
    return lax.dot_general(a, b, ((over[:1], over[1:]), ((), ())), preferred_element_type=F32)


def call(body, grid, in_specs, out_spec, out_shape, prefetch, flops, scratch=()):
    return pl.pallas_call(
        body,
        grid_spec=pltpu.PrefetchScalarGridSpec(
            num_scalar_prefetch=prefetch,
            grid=grid,
            in_specs=in_specs,
            out_specs=out_spec,
            scratch_shapes=scratch,
        ),
        out_shape=out_shape,
        compiler_params=pltpu.CompilerParams(vmem_limit_bytes=VMEM),
        cost_estimate=pl.CostEstimate(flops=flops, bytes_accessed=1 << 23, transcendentals=0),
    )


def pick_rows(half, line, table, far):
    batches, tok, width = line.shape[1:]
    width //= 2
    rows = table.shape[1]
    part = rows // SIZES[3]

    def body(zh_ref, line_ref, table_ref, out_ref):
        source = line_ref[...].reshape(8 * tok, width)
        seat = table_ref[0, :, 0:1].astype(I32)
        hit = seat == lax.broadcasted_iota(I32, (rows, 8 * tok), 1)
        taken = dot(jnp.where(hit, 1.0, 0.0).astype(BF16), source, (1, 0))
        taken = (taken * table_ref[0, :, 1:2]).astype(BF16)
        out_ref[...] = taken.reshape(out_ref.shape)

    return call(
        body,
        (2, batches),
        [
            pl.BlockSpec((8, 1, tok, width), lambda k, m, zh: (zh[0] ^ half, m, 0, k)),
            pl.BlockSpec((1, rows, 2), lambda k, m, zh: (half * 4 + k * 2 + m, 0, 0)),
        ],
        pl.BlockSpec((4, 1, 1, part, width), lambda k, m, zh: (0, k, m, 0, 0)),
        jax.ShapeDtypeStruct((4, 2, batches, part, width), BF16),
        1,
        8 * rows * 8 * tok * width,
    )(far, line, table)


def rows_back(near, other, weight):
    pairs, quarters, rows, ff = near.shape
    width = weight.shape[1]
    part = rows // 2

    def body(near_ref, other_ref, weight_ref, out_ref):
        for k, ref in enumerate((near_ref, other_ref)):
            total = dot(ref[0, 0], weight_ref[0], (1, 1)) + dot(ref[0, 1], weight_ref[1], (1, 1))
            total = total.astype(BF16)
            out_ref[0, k] = total[:part]
            out_ref[1, k] = total[part:]

    piece = pl.BlockSpec((1, quarters, rows, ff), lambda h: (h, 0, 0, 0))
    return call(
        body,
        (pairs,),
        [piece, piece, pl.BlockSpec(weight.shape, lambda h: (0, 0, 0))],
        pl.BlockSpec((2, 2, part, width), lambda h: (h, 0, 0, 0)),
        jax.ShapeDtypeStruct((4, 2, part, width), BF16),
        0,
        8 * pairs * rows * ff * width,
    )(near, other, weight)


def combine(near, far_rows, table, far, tok):
    _, _, batches, part, width = near.shape
    rows = 4 * part

    def body(zh_ref, near_ref, far_ref, table_ref, out_ref):
        seat = table_ref[0, 0:1, :].astype(I32)
        hit = seat == lax.broadcasted_iota(I32, (8 * tok, rows), 0)
        gate = jnp.where(hit, table_ref[0, 1:2, :], 0.0)
        high = gate.astype(BF16)
        low = (gate - high.astype(F32)).astype(BF16)

        def put(ref):
            source = ref[...].reshape(rows, width)
            total = dot(high, source, (1, 0)) + dot(low, source, (1, 0))
            out_ref[...] = total.astype(BF16).reshape(out_ref.shape)

        pl.when(pl.program_id(0) == 0)(lambda: put(near_ref))
        pl.when(pl.program_id(0) == 1)(lambda: put(far_ref))

    block = (4, 1, 1, part, width)
    return call(
        body,
        (2, 2, batches),
        [
            pl.BlockSpec(
                block,
                lambda j, k, m, zh: (0, jnp.where(j == 0, k, 1), jnp.where(j == 0, m, 1), 0, 0),
            ),
            pl.BlockSpec(
                block,
                lambda j, k, m, zh: (0, jnp.where(j == 0, 0, k), jnp.where(j == 0, 0, m), 0, 0),
            ),
            pl.BlockSpec((1, 2, rows), lambda j, k, m, zh: (j * 4 + k * 2 + m, 0, 0)),
        ],
        pl.BlockSpec((1, 8, 1, tok, width), lambda j, k, m, zh: (zh[0] ^ j, 0, m, 0, k)),
        jax.ShapeDtypeStruct((2, 8, batches, tok, 2 * width), BF16),
        1,
        32 * rows * 8 * tok * width,
    )(far, near, far_rows, table)


def weight_sum(inbound, near, other, so_far, scale, kind):
    count, _, part, width = inbound.shape
    quarters, ff = near.shape[1], near.shape[3]

    def body(in_ref, near_ref, other_ref, *refs):
        out_ref, total = refs[-2:]

        @pl.when(pl.program_id(0) == 0)
        def _():
            total[...] = jnp.zeros_like(total) if so_far is None else refs[0][...]

        for q in range(quarters):
            total[q] += dot(in_ref[0, 0], near_ref[0, q], (0, 0)) + dot(
                in_ref[0, 1], other_ref[0, q], (0, 0)
            )

        @pl.when(pl.program_id(0) == count - 1)
        def _():
            out_ref[...] = (total[...] * scale).astype(kind)

    piece = pl.BlockSpec((1, quarters, part, ff), lambda y: (y // 2, 0, y % 2, 0))
    whole = pl.BlockSpec((quarters, width, ff), lambda y: (0, 0, 0))
    extra = () if so_far is None else (so_far,)
    return call(
        body,
        (count,),
        [pl.BlockSpec((1, 2, part, width), lambda y: (y, 0, 0, 0)), piece, piece]
        + [whole] * len(extra),
        whole,
        jax.ShapeDtypeStruct((quarters, width, ff), kind),
        0,
        4 * count * part * width * quarters * ff,
        (pltpu.VMEM((quarters, width, ff), F32),),
    )(inbound, near, other, *extra)


def slot_tables(expert_ids, slot_index, gate_weights, capacity, places):
    rows = expert_ids.shape[1]
    position = jnp.where(slot_index >= 0, expert_ids * capacity + slot_index, -1)
    matches = position[..., None] == jnp.arange(places, dtype=I32)
    token = jnp.arange(1, rows + 1, dtype=F32)[None, :, None, None]
    held = jnp.sum(jnp.where(matches, token, 0.0), axis=(1, 2)) - 1.0
    gate = jnp.sum(jnp.where(matches, gate_weights[..., None], 0.0), axis=(1, 2))
    return held, gate


def by(flag, a, b):
    return jnp.where(flag == 0, a, b), jnp.where(flag == 0, b, a)


def on_device(
    tokens,
    expert_ids,
    slot_index,
    gate_weights,
    up_gradient,
    up_weight,
    attention_partial,
    residual_gradient,
):
    nzl, ny, nx = (lax.axis_size(a) for a in ("zl", "y", "x"))
    zh, co, x = (lax.axis_index(a) for a in ("zh", "co", "x"))
    batches, tok, width = tokens.shape
    quarter, eighth = width // nx, width // nx // 2
    buffer_rows, ff = up_gradient.shape[3:]
    capacity = buffer_rows // (nzl * ny)
    rows = batches * buffer_rows
    far = zh.astype(I32).reshape(1)

    def gather(v):
        return lax.all_to_all(
            jnp.broadcast_to(v, (nx,) + v.shape), "x", split_axis=0, concat_axis=0, tiled=True
        ).reshape((2, 2) + v.shape)

    def along_y(v):
        shape = v.shape
        v = v.reshape(ny, -1, shape[-1])
        return lax.all_to_all(v, "y", split_axis=0, concat_axis=0, tiled=True).reshape(shape)

    own_part = lax.dynamic_slice_in_dim(tokens, x * quarter, quarter, 2)
    own_part = own_part.reshape(batches * tok, 2, eighth)
    mine, theirs = by(co, own_part[:, 0], own_part[:, 1])
    line = jnp.concatenate([mine, lax.ppermute(theirs, "co", SWAP)], axis=1)
    line = lax.all_gather(line, ("zh", "zl"), axis=0, tiled=True)
    line = line.reshape(2 * nzl, batches, tok, quarter)

    r = jnp.arange(rows, dtype=I32)
    r_batch = (r // (capacity * nzl)) % batches
    source_row = (
        (r_batch * nzl + (r // capacity) % nzl) * ny + r // (capacity * nzl * batches)
    ) * capacity + r % capacity
    order = (source_row[:, None] == r[None, :]).astype(BF16)
    hidden = dot(order, up_gradient.reshape(rows, ff), (1, 0)).astype(BF16)
    halves = hidden.reshape(2, rows // 2, ff)
    xh = x // 2
    keep, send = by(xh, halves[0], halves[1])
    taken = lax.ppermute(send, "x", [(i, (i + 2) % nx) for i in range(nx)])
    stay, leave = by(xh ^ zh, keep, taken)
    crossed = lax.ppermute(leave, "zh", SWAP)

    held, gate = slot_tables(expert_ids, slot_index, gate_weights, capacity, nzl * ny * capacity)
    table = jnp.stack([held, gate]).reshape(2, batches, nzl, ny * capacity)
    table = table.transpose(2, 0, 1, 3)
    table = jnp.stack([table, lax.ppermute(table, "co", SWAP)], axis=1)
    table = lax.all_to_all(
        jnp.concatenate([table, table]), ("zh", "zl"), split_axis=0, concat_axis=0, tiled=True
    ).reshape(2, nzl, 2, 2, batches, ny, capacity)
    table = jnp.where(zh == 0, table, table[::-1])
    table = table.transpose(3, 0, 2, 4, 5, 1, 6)
    start = jnp.arange(nzl, dtype=F32)[:, None] * tok
    seats = jnp.where(table[0] >= 0, table[0] + start, -1.0)
    table = jnp.stack([seats, table[1]]).reshape(2, 4 * batches, buffer_rows)
    lying, standing = table.transpose(1, 0, 2), table.transpose(1, 2, 0)

    cut = up_weight.reshape(2, eighth, ff)
    mine, theirs = by(co, cut[0], cut[1])
    weight = jnp.stack(by(co, mine, lax.ppermute(theirs, "co", SWAP)))

    near = gather(stay)
    near_other = lax.ppermute(near, "co", SWAP)
    back_near = along_y(rows_back(near, near_other, weight))
    wide = gather(crossed)
    wide_other = lax.ppermute(wide, "co", SWAP)
    back_far = along_y(rows_back(wide, wide_other, weight))

    inbound = along_y(pick_rows(0, line, standing, far))
    inbound_far = along_y(pick_rows(1, line, standing, far))

    split = (4, 2, batches, nzl * capacity, eighth)
    spread = combine(back_near.reshape(split), back_far.reshape(split), lying, far, tok)
    expert_part = lax.psum_scatter(
        spread.reshape(2 * nzl * batches * tok, quarter),
        ("zh", "zl"),
        scatter_dimension=0,
        tiled=True,
    )

    split = (4, 2, batches * nzl * capacity, eighth)
    total = weight_sum(inbound.reshape(split), near, near_other, None, 1.0, F32)
    total = weight_sum(
        inbound_far.reshape(split), wide, wide_other, total, 1.0 / (2 * SIZES[1]), BF16
    )
    mine, theirs = by(co, total[0], total[1])
    weight_gradient = jnp.concatenate(by(co, mine, lax.ppermute(theirs, "co", SWAP)))

    shares = attention_partial.reshape(batches * tok, nx, quarter).transpose(1, 0, 2)
    shares = lax.all_to_all(shares, "x", split_axis=0, concat_axis=0, tiled=True)
    base = residual_gradient.reshape(batches * tok, quarter).astype(F32) + jnp.sum(
        shares.astype(F32), axis=0
    )
    other = lax.ppermute(expert_part[:, eighth:], "co", SWAP)
    expert_part = jnp.concatenate(by(co, expert_part[:, :eighth], other), axis=1)
    token_gradient = (base + expert_part.astype(F32)).astype(BF16)
    return (token_gradient.reshape(batches, tok, quarter), weight_gradient[None])


def solution(mesh):
    split = Mesh(mesh.devices.reshape(SIZES), AXES)
    dp, ep, tp = ("zh", "co"), ("zl", "y"), "x"
    return jax.shard_map(
        on_device,
        mesh=split,
        in_specs=(
            P(None, dp + ep, None),
            P(None, dp + ep, None),
            P(None, dp + ep, None),
            P(None, dp + ep, None),
            P(dp, None, ep, None, tp),
            P(ep, tp, dp),
            P(tp, None, dp + ep, None),
            P(None, dp + ep, tp),
        ),
        out_specs=(P(None, dp + ep, tp), P(ep, tp, dp)),
        check_vma=False,
    )
```

time: 346 us -> 336 us (0.971)
  the two profiles are of different devices: /device:TPU:1 before, /device:TPU:163 now
where the time goes in v2:
time: 336 us; the launch traced here: 334 us
  waiting for transfers between devices  142 us (42%)
  starting transfers between devices  93.9 us (28%)
  Pallas kernels  44.8 us (13%)
  local copies, waits for them, and re-layouts  22.9 us (7%)
  between operations  14.5 us (4%)
  other arithmetic  12.9 us (4%)
    all_to_all x4, waiting for transfers between devices, along_y(): lax.all_to_all(v, 'y', split_axis=0, concat_axis=0, tiled=True)  87.4 us
    ppermute x1, waiting for transfers between devices, on_device(): crossed = lax.ppermute(leave, 'zh', SWAP)  23.7 us
    all_to_all x1, starting transfers between devices, on_device(): lax.all_to_all(jnp.concatenate([table, table]), ('zh', 'zl'), split_axis=...  22.2 us
    all_to_all x2, waiting for transfers between devices, gather(): lax.all_to_all(jnp.broadcast_to(v, (nx,) + v.shape), 'x', split_axis=0, c...  19.4 us
    all_to_all x4, starting transfers between devices, along_y(): lax.all_to_all(v, 'y', split_axis=0, concat_axis=0, tiled=True)  17.8 us
    pallas_call x1, Pallas kernels, combine(): call(body, (2, 2, batches), [pl.BlockSpec(block, lambda j, k, m, zh: (0,...  13.9 us
    pallas_call x2, Pallas kernels, weight_sum(): call(body, (count,), [pl.BlockSpec((1, 2, part, width), lambda y: (y, 0,...  12.7 us
    ppermute x1, waiting for transfers between devices, on_device(): taken = lax.ppermute(send, 'x', [(i, (i + 2) % nx) for i in range(nx)])  10.6 us
  transfers between devices with their start and end apart: 19, of which 10 were waited for; matrix products, arithmetic and copies ran while one was open for 8% of the time, Pallas kernels for 13%

profile of v2, /device:TPU:163, one launch (start us, length us, event | category | flops | bytes accessed | tf_op | source)
XLA Modules:
  0.0 334.1 jit_solution(16718630574354174853)
XLA Ops:
  9.3 2.6 collective-permute-start.7
  11.9 2.8 fusion.1
  14.8 3.8 %collective-permute-start = (bf16[576,384]{1,0:T(8,128)(2,1)S(1)}, bf16[576,384]{1,0:T(8,128)(2,1)S(1)}, u32[]{:S(2)}, u32[]{:S(2)}) collective-permute-start(bf16[576,384]{1,0:T(8,128)(2,1)S(1)} %broadcast_select_fusion.2), channel_id=1, source_target_pairs={{0,2},{1,3},{2,0},{3,1},{4,6},{5,7},{6,4},{7,5},{8,10},{9,11},{10,... | collective-permute-start | bytes 1327112 | tf_op jit(solution)/shard_map/ppermute | solution.py:224
  19.4 10.6 %collective-permute-done = bf16[576,384]{1,0:T(8,128)(2,1)S(1)} collective-permute-done((bf16[576,384]{1,0:T(8,128)(2,1)S(1)}, bf16[576,384]{1,0:T(8,128)(2,1)S(1)}, u32[]{:S(2)}, u32[]{:S(2)}) %collective-permute-start) | collective-permute-done | bytes 442400 | tf_op jit(solution)/shard_map/ppermute | solution.py:224
  31.5 4.3 %all-to-all-start.1 = ((bf16[4,576,384]{2,1,0:T(8,128)(2,1)}), bf16[4,576,384]{2,1,0:T(8,128)(2,1)S(1)}, u32[]{:S(2)}, u32[]{:S(2)}) async-start(bf16[4,576,384]{2,1,0:T(8,128)(2,1)} %broadcast_in_dim.47), calls=%async_computation.1 | async-start | bytes 3538944 | tf_op jit(solution)/shard_map/all_to_all | solution.py:198
  35.8 9.7 %collective-permute-start.3 = (bf16[576,384]{1,0:T(8,128)(2,1)S(1)}, bf16[576,384]{1,0:T(8,128)(2,1)}, u32[]{:S(2)}, u32[]{:S(2)}) collective-permute-start(bf16[576,384]{1,0:T(8,128)(2,1)S(1)} %get-tuple-element.4), channel_id=1, source_target_pairs={{0,256},{256,0},{1,257},{257,1},{2,258},{258,2},{3,259},{259,3},{4... | collective-permute-start | bytes 1327112 | tf_op jit(solution)/shard_map/ppermute | solution.py:226
  45.5 11.0 %all-to-all-done.1 = bf16[4,576,384]{2,1,0:T(8,128)(2,1)S(1)} async-done(((bf16[4,576,384]{2,1,0:T(8,128)(2,1)}), bf16[4,576,384]{2,1,0:T(8,128)(2,1)S(1)}, u32[]{:S(2)}, u32[]{:S(2)}) %all-to-all-start.1) | async-done | bytes 1769504 | tf_op jit(solution)/shard_map/all_to_all | solution.py:198
  56.5 3.8 %collective-permute-start.1 = (bf16[2,2,576,384]{3,2,1,0:T(8,128)(2,1)S(1)}, bf16[2,2,576,384]{3,2,1,0:T(8,128)(2,1)}, u32[]{:S(2)}, u32[]{:S(2)}) collective-permute-start(bf16[2,2,576,384]{3,2,1,0:T(8,128)(2,1)S(1)} %bitcast.69), channel_id=1, source_target_pairs={{0,128},{128,0},{1,129},{129,1},{2,130},{130,2},{3,131},{131,3},{4... | collective-permute-start | bytes 5308424 | tf_op jit(solution)/shard_map/ppermute | solution.py:247
  64.2 23.7 %collective-permute-done.3 = bf16[576,384]{1,0:T(8,128)(2,1)} collective-permute-done((bf16[576,384]{1,0:T(8,128)(2,1)S(1)}, bf16[576,384]{1,0:T(8,128)(2,1)}, u32[]{:S(2)}, u32[]{:S(2)}) %collective-permute-start.3) | collective-permute-done | bytes 442400 | tf_op jit(solution)/shard_map/ppermute | solution.py:226
  90.4 4.5 %all-to-all-start.3 = ((bf16[4,576,384]{2,1,0:T(8,128)(2,1)}), bf16[4,576,384]{2,1,0:T(8,128)(2,1)}, u32[]{:S(2)}, u32[]{:S(2)}) async-start(bf16[4,576,384]{2,1,0:T(8,128)(2,1)} %broadcast_in_dim.48), calls=%async_computation.3 | async-start | bytes 3538944 | tf_op jit(solution)/shard_map/all_to_all | solution.py:198
  96.0 5.2 %collective-permute-start.5 = (f32[8,2,2,72]{3,0,2,1:T(8,128)S(1)}, f32[8,2,2,72]{3,0,2,1:T(8,128)S(1)}, u32[]{:S(2)}, u32[]{:S(2)}) collective-permute-start(f32[8,2,2,72]{3,0,2,1:T(8,128)S(1)} %bitcast.85), channel_id=1, source_target_pairs={{0,128},{128,0},{1,129},{129,1},{2,130},{130,2},{3,131},{131,3},{4... | collective-permute-start | bytes 27656 | tf_op jit(solution)/shard_map/ppermute | solution.py:231
  105.0 8.4 %all-to-all-done.3 = bf16[4,576,384]{2,1,0:T(8,128)(2,1)} async-done(((bf16[4,576,384]{2,1,0:T(8,128)(2,1)}), bf16[4,576,384]{2,1,0:T(8,128)(2,1)}, u32[]{:S(2)}, u32[]{:S(2)}) %all-to-all-start.3) | async-done | bytes 1769504 | tf_op jit(solution)/shard_map/all_to_all | solution.py:198
  113.4 22.2 %all-to-all-start.5 = ((f32[16,2,2,2,72]{4,3,2,1,0:T(2,128)}), f32[16,2,2,2,72]{4,3,2,1,0:T(2,128)S(1)}, u32[]{:S(2)}, u32[]{:S(2)}) async-start(f32[16,2,2,2,72]{4,3,2,1,0:T(2,128)} %copy.58), calls=%async_computation.5 | async-start | bytes 131072 | tf_op jit(solution)/shard_map/all_to_all | solution.py:232
  135.6 4.4 %collective-permute-start.4 = (bf16[2,2,576,384]{3,2,1,0:T(8,128)(2,1)}, bf16[2,2,576,384]{3,2,1,0:T(8,128)(2,1)}, u32[]{:S(2)}, u32[]{:S(2)}) collective-permute-start(bf16[2,2,576,384]{3,2,1,0:T(8,128)(2,1)} %bitcast.11.near_ref), channel_id=1, source_target_pairs={{0,128},{128,0},{1,129},{129,1},{2,130},{130,2},{3,131},{131,3},{4... | collective-permute-start | bytes 5308424 | tf_op jit(solution)/shard_map/ppermute | solution.py:250
  141.2 5.1 %shard_map.95 = bf16[4,2,288,512]{3,2,1,0:T(8,128)(2,1)} custom-call(bf16[2,2,576,384]{3,2,1,0:T(8,128)(2,1)S(1)} %bitcast.70, bf16[2,2,576,384]{3,2,1,0:T(8,128)(2,1)} %collective-permute-done.1.other_ref, bf16[2,512,384]{2,1,0:T(8,128)(2,1)S(1)} %copy-done.5), custom_call_target="tpu_custom_call" | custom-call | flops 1811939328 | bytes 8388608 | tf_op jit(solution)/shard_map/pallas_call | solution.py:76
  146.3 3.9 %all-to-all-start.2 = ((bf16[4,576,512]{2,1,0:T(8,128)(2,1)}), bf16[4,576,512]{2,1,0:T(8,128)(2,1)S(1)}, u32[]{:S(2)}, u32[]{:S(2)}) async-start(bf16[4,576,512]{2,1,0:T(8,128)(2,1)} %bitcast.79), calls=%async_computation.2 | async-start | bytes 4718592 | tf_op jit(solution)/shard_map/all_to_all | solution.py:205
  151.4 5.3 %shard_map.96 = bf16[4,2,288,512]{3,2,1,0:T(8,128)(2,1)} custom-call(bf16[2,2,576,384]{3,2,1,0:T(8,128)(2,1)} %bitcast.11.near_ref, bf16[2,2,576,384]{3,2,1,0:T(8,128)(2,1)} %collective-permute-done.4.other_ref, bf16[2,512,384]{2,1,0:T(8,128)(2,1)S(1)} %copy-done.6), custom_call_target="tpu_custom_call" | custom-call | flops 1811939328 | bytes 8388608 | tf_op jit(solution)/shard_map/pallas_call | solution.py:76
  156.7 22.5 %all-to-all-done.2 = bf16[4,576,512]{2,1,0:T(8,128)(2,1)S(1)} async-done(((bf16[4,576,512]{2,1,0:T(8,128)(2,1)}), bf16[4,576,512]{2,1,0:T(8,128)(2,1)S(1)}, u32[]{:S(2)}, u32[]{:S(2)}) %all-to-all-start.2) | async-done | bytes 2359328 | tf_op jit(solution)/shard_map/all_to_all | solution.py:205
  179.2 4.5 %all-to-all-start.4 = ((bf16[4,576,512]{2,1,0:T(8,128)(2,1)}), bf16[4,576,512]{2,1,0:T(8,128)(2,1)}, u32[]{:S(2)}, u32[]{:S(2)}) async-start(bf16[4,576,512]{2,1,0:T(8,128)(2,1)} %bitcast.78), calls=%async_computation.4 | async-start | bytes 4718592 | tf_op jit(solution)/shard_map/all_to_all | solution.py:205
  190.7 21.2 %all-to-all-done.4 = bf16[4,576,512]{2,1,0:T(8,128)(2,1)} async-done(((bf16[4,576,512]{2,1,0:T(8,128)(2,1)}), bf16[4,576,512]{2,1,0:T(8,128)(2,1)}, u32[]{:S(2)}, u32[]{:S(2)}) %all-to-all-start.4) | async-done | bytes 2359328 | tf_op jit(solution)/shard_map/all_to_all | solution.py:205
  211.9 13.9 %shard_map.97 = bf16[2,8,2,64,1024]{4,3,2,1,0:T(8,128)(2,1)} custom-call(s32[1]{0:T(128)} %bitcast.2.zh_ref, bf16[4,2,2,144,512]{4,3,2,1,0:T(8,128)(2,1)S(1)} %bitcast.72, bf16[4,2,2,144,512]{4,3,2,1,0:T(8,128)(2,1)} %bitcast.13.far_ref, f32[8,2,576]{2,1,0:T(2,128)S(1)} %bitcast.73), custom_call_target="tpu_custom_call" | custom-call | flops 4831838208 | bytes 8388608 | tf_op jit(solution)/shard_map/pallas_call | solution.py:107
  226.5 3.9 %shard_map.99 = bf16[4,2,2,144,512]{4,3,2,1,0:T(8,128)(2,1)S(1)} custom-call(s32[1]{0:T(128)} %bitcast.2.zh_ref, bf16[16,2,64,1024]{3,2,1,0:T(8,128)(2,1)} %bitcast.74, f32[8,576,2]{2,1,0:T(8,128)S(1)} %bitcast.65), custom_call_target="tpu_custom_call" | custom-call | flops 1207959552 | bytes 8388608 | tf_op jit(solution)/shard_map/pallas_call | solution.py:49
  231.8 4.5 %all-to-all-start.7 = ((bf16[4,576,512]{2,1,0:T(8,128)(2,1)}), bf16[4,576,512]{2,1,0:T(8,128)(2,1)}, u32[]{:S(2)}, u32[]{:S(2)}) async-start(bf16[4,576,512]{2,1,0:T(8,128)(2,1)} %bitcast.68), calls=%async_computation.8 | async-start | bytes 4718592 | tf_op jit(solution)/shard_map/all_to_all | solution.py:205
  236.4 3.9 %shard_map.98 = bf16[4,2,2,144,512]{4,3,2,1,0:T(8,128)(2,1)S(1)} custom-call(s32[1]{0:T(128)} %bitcast.2.zh_ref, bf16[16,2,64,1024]{3,2,1,0:T(8,128)(2,1)} %bitcast.75, f32[8,576,2]{2,1,0:T(8,128)S(1)} %bitcast.66), custom_call_target="tpu_custom_call" | custom-call | flops 1207959552 | bytes 8388608 | tf_op jit(solution)/shard_map/pallas_call | solution.py:49
  241.8 21.8 %all-to-all-done.7 = bf16[4,576,512]{2,1,0:T(8,128)(2,1)} async-done(((bf16[4,576,512]{2,1,0:T(8,128)(2,1)}), bf16[4,576,512]{2,1,0:T(8,128)(2,1)}, u32[]{:S(2)}, u32[]{:S(2)}) %all-to-all-start.7) | async-done | bytes 2359328 | tf_op jit(solution)/shard_map/all_to_all | solution.py:205
  263.6 4.8 %all-to-all-start.6 = ((bf16[4,576,512]{2,1,0:T(8,128)(2,1)}), bf16[4,576,512]{2,1,0:T(8,128)(2,1)}, u32[]{:S(2)}, u32[]{:S(2)}) async-start(bf16[4,576,512]{2,1,0:T(8,128)(2,1)} %bitcast.67), calls=%async_computation.7 | async-start | bytes 4718592 | tf_op jit(solution)/shard_map/all_to_all | solution.py:205
  270.0 2.6 copy.55
  272.6 21.9 %all-to-all-done.6 = bf16[4,576,512]{2,1,0:T(8,128)(2,1)} async-done(((bf16[4,576,512]{2,1,0:T(8,128)(2,1)}), bf16[4,576,512]{2,1,0:T(8,128)(2,1)}, u32[]{:S(2)}, u32[]{:S(2)}) %all-to-all-start.6) | async-done | bytes 2359328 | tf_op jit(solution)/shard_map/all_to_all | solution.py:205
  294.5 5.4 %all-to-all-start = ((bf16[4,128,1024]{2,1,0:T(8,128)(2,1)}), bf16[4,128,1024]{2,1,0:T(8,128)(2,1)}, u32[]{:S(2)}, u32[]{:S(2)}) async-start(bf16[4,128,1024]{2,1,0:T(8,128)(2,1)} %copy.55), calls=%async_computation | async-start | bytes 2097152 | tf_op jit(solution)/shard_map/all_to_all | solution.py:274
  299.9 6.3 %shard_map.100.refs_0_ = f32[2,512,384]{2,1,0:T(8,128)S(1)} custom-call(bf16[4,2,288,512]{3,2,1,0:T(8,128)(2,1)} %bitcast.27.in_ref, bf16[2,2,576,384]{3,2,1,0:T(8,128)(2,1)S(1)} %bitcast.71, bf16[2,2,576,384]{3,2,1,0:T(8,128)(2,1)} %collective-permute-done.1.other_ref), custom_call_target="tpu_custom_call" | custom-call | flops 1811939328 | bytes 8388608 | tf_op jit(solution)/shard_map/pallas_call | solution.py:151
  306.2 6.5 %shard_map.101 = bf16[2,512,384]{2,1,0:T(8,128)(2,1)S(1)} custom-call(bf16[4,2,288,512]{3,2,1,0:T(8,128)(2,1)} %bitcast.25.in_ref, bf16[2,2,576,384]{3,2,1,0:T(8,128)(2,1)} %bitcast.11.near_ref, bf16[2,2,576,384]{3,2,1,0:T(8,128)(2,1)} %collective-permute-done.4.other_ref, f32[2,512,384]{2,1,0:T(8,128)S(1)} %shard_map.100.refs_0_), custom_call_target="tpu_custom_call" | custom-call | flops 1811939328 | bytes 8388608 | tf_op jit(solution)/shard_map/pallas_call | solution.py:151
  312.7 6.1 %collective-permute-start.8 = (bf16[512,384]{1,0:T(8,128)(2,1)S(1)}, bf16[512,384]{1,0:T(8,128)(2,1)S(1)}, u32[]{:S(2)}, u32[]{:S(2)}) collective-permute-start(bf16[512,384]{1,0:T(8,128)(2,1)S(1)} %select_bitcast_fusion), channel_id=1, source_target_pairs={{0,128},{128,0},{1,129},{129,1},{2,130},{130,2},{3,131},{131,3},{4... | collective-permute-start | bytes 1179656 | tf_op jit(solution)/shard_map/ppermute | solution.py:271
  (86 shorter events, 38.4 us)
Async XLA Ops:
  7.2 1.2 copy-start
  7.2 219.3 %all-gather.2.cloned.1.call-start = ((), (), s32[]{:S(2)}) async-start(), calls=%async_computation.10 | async-start | bytes 4456448 | tf_op jit(solution)/shard_map/all_gather | solution.py:211
  9.3 9.3 %collective-permute-start.7 = (bf16[128,512]{1,0:T(8,128)(2,1)S(1)}, bf16[128,512]{1,0:T(8,128)(2,1)S(1)}, u32[]{:S(2)}, u32[]{:S(2)}) collective-permute-start(bf16[128,512]{1,0:T(8,128)(2,1)S(1)} %bitcast.84), channel_id=1, source_target_pairs={{0,128},{128,0},{1,129},{129,1},{2,130},{130,2},{3,131},{131,3},{4... | collective-permute-start | bytes 393224 | tf_op jit(solution)/shard_map/ppermute | solution.py:210
  14.8 15.2 %collective-permute-start = (bf16[576,384]{1,0:T(8,128)(2,1)S(1)}, bf16[576,384]{1,0:T(8,128)(2,1)S(1)}, u32[]{:S(2)}, u32[]{:S(2)}) collective-permute-start(bf16[576,384]{1,0:T(8,128)(2,1)S(1)} %broadcast_select_fusion.2), channel_id=1, source_target_pairs={{0,2},{1,3},{2,0},{3,1},{4,6},{5,7},{6,4},{7,5},{8,10},{9,11},{10,... | collective-permute-start | bytes 1327112 | tf_op jit(solution)/shard_map/ppermute | solution.py:224
  31.5 25.0 %all-to-all-start.1 = ((bf16[4,576,384]{2,1,0:T(8,128)(2,1)}), bf16[4,576,384]{2,1,0:T(8,128)(2,1)S(1)}, u32[]{:S(2)}, u32[]{:S(2)}) async-start(bf16[4,576,384]{2,1,0:T(8,128)(2,1)} %broadcast_in_dim.47), calls=%async_computation.1 | async-start | bytes 3538944 | tf_op jit(solution)/shard_map/all_to_all | solution.py:198
  35.8 52.2 %collective-permute-start.3 = (bf16[576,384]{1,0:T(8,128)(2,1)S(1)}, bf16[576,384]{1,0:T(8,128)(2,1)}, u32[]{:S(2)}, u32[]{:S(2)}) collective-permute-start(bf16[576,384]{1,0:T(8,128)(2,1)S(1)} %get-tuple-element.4), channel_id=1, source_target_pairs={{0,256},{256,0},{1,257},{257,1},{2,258},{258,2},{3,259},{259,3},{4... | collective-permute-start | bytes 1327112 | tf_op jit(solution)/shard_map/ppermute | solution.py:226
  56.5 83.6 %copy-start.3 = (bf16[4,576,384]{2,1,0:T(8,128)(2,1)}, bf16[4,576,384]{2,1,0:T(8,128)(2,1)S(1)}, u32[]{:S(2)}) copy-start(bf16[4,576,384]{2,1,0:T(8,128)(2,1)S(1)} %all-to-all-done.1) | copy-start | bytes 5308420
  56.5 83.6 %collective-permute-start.1 = (bf16[2,2,576,384]{3,2,1,0:T(8,128)(2,1)S(1)}, bf16[2,2,576,384]{3,2,1,0:T(8,128)(2,1)}, u32[]{:S(2)}, u32[]{:S(2)}) collective-permute-start(bf16[2,2,576,384]{3,2,1,0:T(8,128)(2,1)S(1)} %bitcast.69), channel_id=1, source_target_pairs={{0,128},{128,0},{1,129},{129,1},{2,130},{130,2},{3,131},{131,3},{4... | collective-permute-start | bytes 5308424 | tf_op jit(solution)/shard_map/ppermute | solution.py:247
  62.2 32.7 %copy-start.8 = (s32[2,64,8]{1,2,0:T(8,128)S(1)}, s32[2,64,8]{1,2,0:T(8,128)}, u32[]{:S(2)}) copy-start(s32[2,64,8]{1,2,0:T(8,128)} %param.10) | copy-start | bytes 12292
  62.2 32.7 %copy-start.9 = (s32[2,64,8]{1,2,0:T(8,128)S(1)}, s32[2,64,8]{1,2,0:T(8,128)}, u32[]{:S(2)}) copy-start(s32[2,64,8]{1,2,0:T(8,128)} %param.9) | copy-start | bytes 12292
  62.2 40.5 %collective-permute-start.2 = (bf16[512,384]{1,0:T(8,128)(2,1)}, bf16[512,384]{1,0:T(8,128)(2,1)}, u32[]{:S(2)}, u32[]{:S(2)}) collective-permute-start(bf16[512,384]{1,0:T(8,128)(2,1)} %select_bitcast_fusion.1), channel_id=1, source_target_pairs={{0,128},{128,0},{1,129},{129,1},{2,130},{130,2},{3,131},{131,3},{4... | collective-permute-start | bytes 1179656 | tf_op jit(solution)/shard_map/ppermute | solution.py:244
  90.4 4.6 %copy-start.10 = (f32[2,64,8]{1,2,0:T(8,128)S(1)}, f32[2,64,8]{1,2,0:T(8,128)}, u32[]{:S(2)}) copy-start(f32[2,64,8]{1,2,0:T(8,128)} %param.11) | copy-start | bytes 12292
  90.4 23.0 %all-to-all-start.3 = ((bf16[4,576,384]{2,1,0:T(8,128)(2,1)}), bf16[4,576,384]{2,1,0:T(8,128)(2,1)}, u32[]{:S(2)}, u32[]{:S(2)}) async-start(bf16[4,576,384]{2,1,0:T(8,128)(2,1)} %broadcast_in_dim.48), calls=%async_computation.3 | async-start | bytes 3538944 | tf_op jit(solution)/shard_map/all_to_all | solution.py:198
  96.0 6.0 %collective-permute-start.5 = (f32[8,2,2,72]{3,0,2,1:T(8,128)S(1)}, f32[8,2,2,72]{3,0,2,1:T(8,128)S(1)}, u32[]{:S(2)}, u32[]{:S(2)}) collective-permute-start(f32[8,2,2,72]{3,0,2,1:T(8,128)S(1)} %bitcast.85), channel_id=1, source_target_pairs={{0,128},{128,0},{1,129},{129,1},{2,130},{130,2},{3,131},{131,3},{4... | collective-permute-start | bytes 27656 | tf_op jit(solution)/shard_map/ppermute | solution.py:231
  113.4 32.9 %all-to-all-start.5 = ((f32[16,2,2,2,72]{4,3,2,1,0:T(2,128)}), f32[16,2,2,2,72]{4,3,2,1,0:T(2,128)S(1)}, u32[]{:S(2)}, u32[]{:S(2)}) async-start(f32[16,2,2,2,72]{4,3,2,1,0:T(2,128)} %copy.58), calls=%async_computation.5 | async-start | bytes 131072 | tf_op jit(solution)/shard_map/all_to_all | solution.py:232
  135.6 14.6 %collective-permute-start.4 = (bf16[2,2,576,384]{3,2,1,0:T(8,128)(2,1)}, bf16[2,2,576,384]{3,2,1,0:T(8,128)(2,1)}, u32[]{:S(2)}, u32[]{:S(2)}) collective-permute-start(bf16[2,2,576,384]{3,2,1,0:T(8,128)(2,1)} %bitcast.11.near_ref), channel_id=1, source_target_pairs={{0,128},{128,0},{1,129},{129,1},{2,130},{130,2},{3,131},{131,3},{4... | collective-permute-start | bytes 5308424 | tf_op jit(solution)/shard_map/ppermute | solution.py:250
  140.0 1.1 copy-start.5
  146.3 32.9 %all-to-all-start.2 = ((bf16[4,576,512]{2,1,0:T(8,128)(2,1)}), bf16[4,576,512]{2,1,0:T(8,128)(2,1)S(1)}, u32[]{:S(2)}, u32[]{:S(2)}) async-start(bf16[4,576,512]{2,1,0:T(8,128)(2,1)} %bitcast.79), calls=%async_computation.2 | async-start | bytes 4718592 | tf_op jit(solution)/shard_map/all_to_all | solution.py:205
  150.2 1.1 copy-start.6
  179.2 32.7 %all-to-all-start.4 = ((bf16[4,576,512]{2,1,0:T(8,128)(2,1)}), bf16[4,576,512]{2,1,0:T(8,128)(2,1)}, u32[]{:S(2)}, u32[]{:S(2)}) async-start(bf16[4,576,512]{2,1,0:T(8,128)(2,1)} %bitcast.78), calls=%async_computation.4 | async-start | bytes 4718592 | tf_op jit(solution)/shard_map/all_to_all | solution.py:205
  183.8 136.6 %reduce-scatter.2.cloned.1.call-start = ((), (), s32[]{:S(2)}) async-start(), calls=%async_computation.9 | async-start | bytes 4456448 | tf_op jit(solution)/shard_map/reduce_scatter | solution.py:258
  230.4 1.4 copy-start.2
  231.8 31.8 %all-to-all-start.7 = ((bf16[4,576,512]{2,1,0:T(8,128)(2,1)}), bf16[4,576,512]{2,1,0:T(8,128)(2,1)}, u32[]{:S(2)}, u32[]{:S(2)}) async-start(bf16[4,576,512]{2,1,0:T(8,128)(2,1)} %bitcast.68), calls=%async_computation.8 | async-start | bytes 4718592 | tf_op jit(solution)/shard_map/all_to_all | solution.py:205
  240.3 1.5 copy-start.1
  263.6 4.8 %copy-start.7 = (bf16[1,2,64,4096]{3,2,1,0:T(8,128)(2,1)S(1)}, bf16[1,2,64,4096]{3,2,1,0:T(8,128)(2,1)}, u32[]{:S(2)}) copy-start(bf16[1,2,64,4096]{3,2,1,0:T(8,128)(2,1)} %param.14) | copy-start | bytes 3145732
  263.6 30.9 %all-to-all-start.6 = ((bf16[4,576,512]{2,1,0:T(8,128)(2,1)}), bf16[4,576,512]{2,1,0:T(8,128)(2,1)}, u32[]{:S(2)}, u32[]{:S(2)}) async-start(bf16[4,576,512]{2,1,0:T(8,128)(2,1)} %bitcast.67), calls=%async_computation.7 | async-start | bytes 4718592 | tf_op jit(solution)/shard_map/all_to_all | solution.py:205
  270.0 29.9 %copy-start.4 = (bf16[4,576,384]{2,1,0:T(8,128)(2,1)S(1)}, bf16[4,576,384]{2,1,0:T(8,128)(2,1)}, u32[]{:S(2)}) copy-start(bf16[4,576,384]{2,1,0:T(8,128)(2,1)} %copy-done.3) | copy-start | bytes 5308420
  294.5 24.3 %all-to-all-start = ((bf16[4,128,1024]{2,1,0:T(8,128)(2,1)}), bf16[4,128,1024]{2,1,0:T(8,128)(2,1)}, u32[]{:S(2)}, u32[]{:S(2)}) async-start(bf16[4,128,1024]{2,1,0:T(8,128)(2,1)} %copy.55), calls=%async_computation | async-start | bytes 2097152 | tf_op jit(solution)/shard_map/all_to_all | solution.py:274
  312.7 7.5 %collective-permute-start.8 = (bf16[512,384]{1,0:T(8,128)(2,1)S(1)}, bf16[512,384]{1,0:T(8,128)(2,1)S(1)}, u32[]{:S(2)}, u32[]{:S(2)}) collective-permute-start(bf16[512,384]{1,0:T(8,128)(2,1)S(1)} %select_bitcast_fusion), channel_id=1, source_target_pairs={{0,128},{128,0},{1,129},{129,1},{2,130},{130,2},{3,131},{131,3},{4... | collective-permute-start | bytes 1179656 | tf_op jit(solution)/shard_map/ppermute | solution.py:271
  321.3 3.2 collective-permute-start.6
Sparse Core Ops, SparseCore 0:
  19.5 106.0 all-gather.1
  225.9 68.6 reduce-scatter.1

commit v3 on v2

v3 whole, which is shorter than its diff:
```python
import jax
import jax.numpy as jnp
from jax import lax
from jax.experimental import pallas as pl
from jax.experimental.pallas import tpu as pltpu
from jax.sharding import Mesh, PartitionSpec as P

AXES = ("zh", "co", "zl", "y", "x")
SIZES = (2, 2, 8, 4, 4)
SWAP = [(0, 1), (1, 0)]
BF16, F32, I32 = jnp.bfloat16, jnp.float32, jnp.int32
VMEM = 48 * 1024 * 1024


def dot(a, b, over):
    return lax.dot_general(a, b, ((over[:1], over[1:]), ((), ())), preferred_element_type=F32)


def call(body, grid, in_specs, out_spec, out_shape, prefetch, flops, scratch=(), aliases={}):
    return pl.pallas_call(
        body,
        grid_spec=pltpu.PrefetchScalarGridSpec(
            num_scalar_prefetch=prefetch,
            grid=grid,
            in_specs=in_specs,
            out_specs=out_spec,
            scratch_shapes=scratch,
        ),
        out_shape=out_shape,
        input_output_aliases=aliases,
        compiler_params=pltpu.CompilerParams(vmem_limit_bytes=VMEM),
        cost_estimate=pl.CostEstimate(flops=flops, bytes_accessed=1 << 23, transcendentals=0),
    )


def pick_rows(half, line, table, far):
    batches, tok, width = line.shape[1:]
    width //= 2
    rows = table.shape[1]
    part = rows // 4

    def body(zh_ref, line_ref, table_ref, *out_refs):
        source = line_ref[...].reshape(8 * tok, width)
        seat = table_ref[0, :, 0:1].astype(I32)
        hit = seat == lax.broadcasted_iota(I32, (rows, 8 * tok), 1)
        taken = dot(jnp.where(hit, 1.0, 0.0).astype(BF16), source, (1, 0))
        taken = (taken * table_ref[0, :, 1:2]).astype(BF16)
        for d, ref in enumerate(out_refs):
            ref[0, 0] = taken[d * part : (d + 1) * part]

    return call(
        body,
        (2, batches),
        [
            pl.BlockSpec((8, 1, tok, width), lambda k, m, zh: (zh[0] ^ half, m, 0, k)),
            pl.BlockSpec((1, rows, 2), lambda k, m, zh: (half * 4 + k * 2 + m, 0, 0)),
        ],
        [pl.BlockSpec((1, 1, part, width), lambda k, m, zh: (k, m, 0, 0))] * 4,
        [jax.ShapeDtypeStruct((2, batches, part, width), BF16)] * 4,
        1,
        8 * rows * 8 * tok * width,
    )(far, line, table)


def rows_back(near, other, weight, here):
    _, quarters, rows, ff = near.shape
    width = weight.shape[1]
    part = rows // 2

    def body(y_ref, near_ref, other_ref, weight_ref, *out_refs):
        for d, out_ref in enumerate(out_refs):

            @pl.when(pl.program_id(0) == d)
            def _():
                for k, ref in enumerate((near_ref, other_ref)):
                    total = dot(ref[0, 0], weight_ref[0], (1, 1))
                    total += dot(ref[0, 1], weight_ref[1], (1, 1))
                    out_ref[k] = total.astype(BF16)

    def place(d, y):
        source = (y[0] + d) & 3
        return (source >> 1, 0, source & 1, 0)

    piece = pl.BlockSpec((1, quarters, part, ff), place)
    return call(
        body,
        (4,),
        [piece, piece, pl.BlockSpec(weight.shape, lambda d, y: (0, 0, 0))],
        [pl.BlockSpec((2, part, width), lambda d, y: (0, 0, 0))] * 4,
        [jax.ShapeDtypeStruct((2, part, width), BF16)] * 4,
        1,
        16 * part * quarters * ff * width,
    )(here, near, other, weight)


def combine(half, returned, table, far, tok, so_far):
    returned = [returned[d] for d in (0, 3, 2, 1)]
    _, batches, part, width = returned[0].shape
    rows = 4 * part

    def body(zh_ref, *refs):
        out_ref, table_ref = refs[-1], refs[4]
        seat = table_ref[0, 0:1, :].astype(I32)
        hit = seat == lax.broadcasted_iota(I32, (8 * tok, rows), 0)
        gate = jnp.where(hit, table_ref[0, 1:2, :], 0.0)
        high = gate.astype(BF16)
        low = (gate - high.astype(F32)).astype(BF16)
        source = jnp.concatenate([ref[0, 0] for ref in refs[:4]], axis=0)
        total = dot(high, source, (1, 0)) + dot(low, source, (1, 0))
        out_ref[...] = total.astype(BF16).reshape(out_ref.shape)

    extra = () if so_far is None else (so_far,)
    return call(
        body,
        (2, batches),
        [pl.BlockSpec((1, 1, part, width), lambda k, m, zh: (k, m, 0, 0))] * 4
        + [pl.BlockSpec((1, 2, rows), lambda k, m, zh: (half * 4 + k * 2 + m, 0, 0))]
        + [pl.BlockSpec(memory_space=pl.ANY)] * len(extra),
        pl.BlockSpec((1, 8, 1, tok, width), lambda k, m, zh: (zh[0] ^ half, 0, m, 0, k)),
        jax.ShapeDtypeStruct((2, 8, batches, tok, 2 * width), BF16),
        1,
        16 * rows * 8 * tok * width,
        aliases={6: 0} if extra else {},
    )(far, *returned, table, *extra)


def weight_sum(inbound, near, other, here, so_far, scale, kind):
    _, part, width = inbound[0].shape
    quarters, ff = near.shape[1], near.shape[3]

    def body(y_ref, *refs):
        near_ref, other_ref = refs[4:6]
        out_ref, total = refs[-2:]

        @pl.when(pl.program_id(0) == 0)
        def _():
            total[...] = jnp.zeros_like(total) if so_far is None else refs[6][...]

        for d in range(4):

            @pl.when(pl.program_id(0) == d)
            def _():
                for q in range(quarters):
                    total[q] += dot(refs[d][0], near_ref[0, q], (0, 0)) + dot(
                        refs[d][1], other_ref[0, q], (0, 0)
                    )

        @pl.when(pl.program_id(0) == 3)
        def _():
            out_ref[...] = (total[...] * scale).astype(kind)

    def place(d, y):
        source = (y[0] - d) & 3
        return (source >> 1, 0, source & 1, 0)

    piece = pl.BlockSpec((1, quarters, part, ff), place)
    whole = pl.BlockSpec((quarters, width, ff), lambda d, y: (0, 0, 0))
    extra = () if so_far is None else (so_far,)
    return call(
        body,
        (4,),
        [pl.BlockSpec((2, part, width), lambda d, y: (0, 0, 0))] * 4
        + [piece, piece]
        + [whole] * len(extra),
        whole,
        jax.ShapeDtypeStruct((quarters, width, ff), kind),
        1,
        16 * part * width * quarters * ff,
        scratch=(pltpu.VMEM((quarters, width, ff), F32),),
    )(here, *inbound, near, other, *extra)


def slot_tables(expert_ids, slot_index, gate_weights, capacity, places):
    rows = expert_ids.shape[1]
    position = jnp.where(slot_index >= 0, expert_ids * capacity + slot_index, -1)
    matches = position[..., None] == jnp.arange(places, dtype=I32)
    token = jnp.arange(1, rows + 1, dtype=F32)[None, :, None, None]
    held = jnp.sum(jnp.where(matches, token, 0.0), axis=(1, 2)) - 1.0
    gate = jnp.sum(jnp.where(matches, gate_weights[..., None], 0.0), axis=(1, 2))
    return held, gate


def by(flag, a, b):
    return jnp.where(flag == 0, a, b), jnp.where(flag == 0, b, a)


def on_device(
    tokens,
    expert_ids,
    slot_index,
    gate_weights,
    up_gradient,
    up_weight,
    attention_partial,
    residual_gradient,
):
    nzl, ny, nx = (lax.axis_size(a) for a in ("zl", "y", "x"))
    zh, co, x = (lax.axis_index(a) for a in ("zh", "co", "x"))
    batches, tok, width = tokens.shape
    quarter, eighth = width // nx, width // nx // 2
    buffer_rows, ff = up_gradient.shape[3:]
    capacity = buffer_rows // (nzl * ny)
    rows = batches * buffer_rows
    far = zh.astype(I32).reshape(1)
    y = lax.axis_index("y")
    here = y.astype(I32).reshape(1)

    def gather(v):
        return lax.all_to_all(
            jnp.broadcast_to(v, (nx,) + v.shape), "x", split_axis=0, concat_axis=0, tiled=True
        ).reshape((2, 2) + v.shape)

    def along_y(parts, shape):
        moved = [
            v if d == 0 else lax.ppermute(v, "y", [(i, (i + d) % ny) for i in range(ny)])
            for d, v in enumerate(parts)
        ]
        return [v.reshape(shape) for v in moved]

    own_part = lax.dynamic_slice_in_dim(tokens, x * quarter, quarter, 2)
    own_part = own_part.reshape(batches * tok, 2, eighth)
    mine, theirs = by(co, own_part[:, 0], own_part[:, 1])
    line = jnp.concatenate([mine, lax.ppermute(theirs, "co", SWAP)], axis=1)
    line = lax.all_gather(line, ("zh", "zl"), axis=0, tiled=True)
    line = line.reshape(2 * nzl, batches, tok, quarter)

    r = jnp.arange(rows, dtype=I32)
    r_batch = (r // (capacity * nzl)) % batches
    source_row = (
        (r_batch * nzl + (r // capacity) % nzl) * ny + r // (capacity * nzl * batches)
    ) * capacity + r % capacity
    order = (source_row[:, None] == r[None, :]).astype(BF16)
    hidden = dot(order, up_gradient.reshape(rows, ff), (1, 0)).astype(BF16)
    halves = hidden.reshape(2, rows // 2, ff)
    xh = x // 2
    keep, send = by(xh, halves[0], halves[1])
    taken = lax.ppermute(send, "x", [(i, (i + 2) % nx) for i in range(nx)])
    stay, leave = by(xh ^ zh, keep, taken)
    crossed = lax.ppermute(leave, "zh", SWAP)
    near = gather(stay)

    expert_ids, slot_index, gate_weights, leave = lax.optimization_barrier(
        (expert_ids, slot_index, gate_weights, leave)
    )
    held, gate = slot_tables(expert_ids, slot_index, gate_weights, capacity, nzl * ny * capacity)
    table = jnp.stack([held, gate]).reshape(2, batches, nzl, ny * capacity)
    table = table.transpose(2, 0, 1, 3)
    table = jnp.stack([table, lax.ppermute(table, "co", SWAP)], axis=1)
    table = lax.all_to_all(
        jnp.concatenate([table, table]), ("zh", "zl"), split_axis=0, concat_axis=0, tiled=True
    ).reshape(2, nzl, 2, 2, batches, ny, capacity)
    table = jnp.where(zh == 0, table, table[::-1])
    table = lax.dynamic_slice_in_dim(jnp.concatenate([table, table], axis=5), y, ny, 5)
    table = table.transpose(3, 0, 2, 4, 5, 1, 6)
    start = jnp.arange(nzl, dtype=F32)[:, None] * tok
    seats = jnp.where(table[0] >= 0, table[0] + start, -1.0)
    table = jnp.stack([seats, table[1]]).reshape(2, 4 * batches, buffer_rows)
    lying, standing = table.transpose(1, 0, 2), table.transpose(1, 2, 0)

    cut = up_weight.reshape(2, eighth, ff)
    mine, theirs = by(co, cut[0], cut[1])
    weight = jnp.stack(by(co, mine, lax.ppermute(theirs, "co", SWAP)))

    near_other = lax.ppermute(near, "co", SWAP)
    back = rows_back(near, near_other, weight, here)
    crossed, back, lying, standing = lax.optimization_barrier((crossed, back, lying, standing))
    wide = gather(crossed)
    split = (2, batches, nzl * capacity, eighth)
    spread = combine(0, along_y(back, split), lying, far, tok, None)
    wide_other = lax.ppermute(wide, "co", SWAP)
    back = rows_back(wide, wide_other, weight, here)
    attention_partial, back = lax.optimization_barrier((attention_partial, back))
    spread = combine(1, along_y(back, split), lying, far, tok, spread)
    line, _ = lax.optimization_barrier((line, spread))
    expert_part = lax.psum_scatter(
        spread.reshape(2 * nzl * batches * tok, quarter),
        ("zh", "zl"),
        scatter_dimension=0,
        tiled=True,
    )

    split = (2, batches * nzl * capacity, eighth)
    inbound = along_y(pick_rows(0, line, standing, far), split)
    inbound_far = along_y(pick_rows(1, line, standing, far), split)
    total = weight_sum(inbound, near, near_other, here, None, 1.0, F32)
    total = weight_sum(inbound_far, wide, wide_other, here, total, 1.0 / (2 * SIZES[1]), BF16)
    mine, theirs = by(co, total[0], total[1])
    weight_gradient = jnp.concatenate(by(co, mine, lax.ppermute(theirs, "co", SWAP)))

    shares = attention_partial.reshape(batches * tok, nx, quarter).transpose(1, 0, 2)
    shares = lax.all_to_all(shares, "x", split_axis=0, concat_axis=0, tiled=True)
    base = residual_gradient.reshape(batches * tok, quarter).astype(F32) + jnp.sum(
        shares.astype(F32), axis=0
    )
    other = lax.ppermute(expert_part[:, eighth:], "co", SWAP)
    expert_part = jnp.concatenate(by(co, expert_part[:, :eighth], other), axis=1)
    token_gradient = (base + expert_part.astype(F32)).astype(BF16)
    return (token_gradient.reshape(batches, tok, quarter), weight_gradient[None])


def solution(mesh):
    split = Mesh(mesh.devices.reshape(SIZES), AXES)
    dp, ep, tp = ("zh", "co"), ("zl", "y"), "x"
    return jax.shard_map(
        on_device,
        mesh=split,
        in_specs=(
            P(None, dp + ep, None),
            P(None, dp + ep, None),
            P(None, dp + ep, None),
            P(None, dp + ep, None),
            P(dp, None, ep, None, tp),
            P(ep, tp, dp),
            P(tp, None, dp + ep, None),
            P(None, dp + ep, tp),
        ),
        out_specs=(P(None, dp + ep, tp), P(ep, tp, dp)),
        check_vma=False,
    )
```

time: 336 us -> 324 us (0.964)
  the two profiles are of different devices: /device:TPU:163 before, /device:TPU:1 now
where the time goes in v3:
time: 324 us; the launch traced here: 323 us
  starting transfers between devices  109 us (34%)
  waiting for transfers between devices  102 us (31%)
  Pallas kernels  41 us (13%)
  blocking collectives  23.3 us (7%)
  local copies, waits for them, and re-layouts  20 us (6%)
  between operations  14.7 us (5%)
  other arithmetic  9.86 us (3%)
    ppermute x12, waiting for transfers between devices, along_y(): lax.ppermute(v, 'y', [(i, (i + d) % ny) for i in range(ny)])  48.6 us
    ppermute x1, waiting for transfers between devices, on_device(): crossed = lax.ppermute(leave, 'zh', SWAP)  38.6 us
    ppermute x12, starting transfers between devices, along_y(): lax.ppermute(v, 'y', [(i, (i + d) % ny) for i in range(ny)])  35.8 us
    all_to_all x1, blocking collectives, gather(): lax.all_to_all(jnp.broadcast_to(v, (nx,) + v.shape), 'x', split_axis=0, c...  23.3 us
    all_to_all x1, starting transfers between devices, on_device(): lax.all_to_all(jnp.concatenate([table, table]), ('zh', 'zl'), split_axis=...  15.4 us
    pallas_call x2, Pallas kernels, weight_sum(): call(body, (4,), [pl.BlockSpec((2, part, width), lambda d, y: (0, 0, 0))]...  12.4 us
    all_to_all x1, waiting for transfers between devices, gather(): lax.all_to_all(jnp.broadcast_to(v, (nx,) + v.shape), 'x', split_axis=0, c...  12.1 us
    ppermute x1, starting transfers between devices, on_device(): crossed = lax.ppermute(leave, 'zh', SWAP)  12 us
  transfers between devices with their start and end apart: 26, of which 12 were waited for; matrix products, arithmetic and copies ran while one was open for 6% of the time, Pallas kernels for 13%

profile of v3, /device:TPU:1, one launch (start us, length us, event | category | flops | bytes accessed | tf_op | source)
XLA Modules:
  0.0 322.6 jit_solution(2800015044729051569)
XLA Ops:
  10.2 5.5 %collective-permute-start = (bf16[576,384]{1,0:T(8,128)(2,1)S(1)}, bf16[576,384]{1,0:T(8,128)(2,1)S(1)}, u32[]{:S(2)}, u32[]{:S(2)}) collective-permute-start(bf16[576,384]{1,0:T(8,128)(2,1)S(1)} %broadcast_select_fusion.3), channel_id=1, source_target_pairs={{0,2},{1,3},{2,0},{3,1},{4,6},{5,7},{6,4},{7,5},{8,10},{9,11},{10,... | collective-permute-start | bytes 1327112 | tf_op jit(solution)/shard_map/ppermute | solution.py:237
  16.6 5.2 %collective-permute-start.13 = (bf16[128,512]{1,0:T(8,128)(2,1)S(1)}, bf16[128,512]{1,0:T(8,128)(2,1)S(1)}, u32[]{:S(2)}, u32[]{:S(2)}) collective-permute-start(bf16[128,512]{1,0:T(8,128)(2,1)S(1)} %bitcast.103), channel_id=1, source_target_pairs={{0,128},{128,0},{1,129},{129,1},{2,130},{130,2},{3,131},{131,3},{4... | collective-permute-start | bytes 393224 | tf_op jit(solution)/shard_map/ppermute | solution.py:223
  25.9 5.8 %all-to-all-start = ((bf16[4,576,384]{2,1,0:T(8,128)(2,1)}), bf16[4,576,384]{2,1,0:T(8,128)(2,1)}, u32[]{:S(2)}, u32[]{:S(2)}) async-start(bf16[4,576,384]{2,1,0:T(8,128)(2,1)} %broadcast_in_dim.47), calls=%async_computation | async-start | bytes 3538944 | tf_op jit(solution)/shard_map/all_to_all | solution.py:209
  31.7 5.9 %collective-permute-start.3 = (bf16[512,384]{1,0:T(8,128)(2,1)S(1)}, bf16[512,384]{1,0:T(8,128)(2,1)S(1)}, u32[]{:S(2)}, u32[]{:S(2)}) collective-permute-start(bf16[512,384]{1,0:T(8,128)(2,1)S(1)} %select_bitcast_fusion.1), channel_id=1, source_target_pairs={{0,128},{128,0},{1,129},{129,1},{2,130},{130,2},{3,131},{131,3},{4... | collective-permute-start | bytes 1179656 | tf_op jit(solution)/shard_map/ppermute | solution.py:262
  38.6 12.1 %all-to-all-done = bf16[4,576,384]{2,1,0:T(8,128)(2,1)} async-done(((bf16[4,576,384]{2,1,0:T(8,128)(2,1)}), bf16[4,576,384]{2,1,0:T(8,128)(2,1)}, u32[]{:S(2)}, u32[]{:S(2)}) %all-to-all-start) | async-done | bytes 1769504 | tf_op jit(solution)/shard_map/all_to_all | solution.py:209
  50.7 6.9 %collective-permute-start.2 = (bf16[2,2,576,384]{3,2,1,0:T(8,128)(2,1)}, bf16[2,2,576,384]{3,2,1,0:T(8,128)(2,1)}, u32[]{:S(2)}, u32[]{:S(2)}) collective-permute-start(bf16[2,2,576,384]{3,2,1,0:T(8,128)(2,1)} %bitcast.2.near_ref.refs_4_), channel_id=1, source_target_pairs={{0,128},{128,0},{1,129},{129,1},{2,130},{130,2},{3,131},{131,3},{4... | collective-permute-start | bytes 5308424 | tf_op jit(solution)/shard_map/ppermute | solution.py:264
  61.6 15.4 %all-to-all-start.1 = ((f32[16,2,2,2,72]{4,3,2,1,0:T(2,128)}), f32[16,2,2,2,72]{4,3,2,1,0:T(2,128)S(1)}, u32[]{:S(2)}, u32[]{:S(2)}) async-start(f32[16,2,2,2,72]{4,3,2,1,0:T(2,128)} %copy.62), calls=%async_computation.1 | async-start | bytes 131072 | tf_op jit(solution)/shard_map/all_to_all | solution.py:249
  78.2 12.0 %collective-permute-start.1 = (bf16[576,384]{1,0:T(8,128)(2,1)}, bf16[576,384]{1,0:T(8,128)(2,1)}, u32[]{:S(2)}, u32[]{:S(2)}) collective-permute-start(bf16[576,384]{1,0:T(8,128)(2,1)} %get-tuple-element.69), channel_id=1, source_target_pairs={{0,256},{256,0},{1,257},{257,1},{2,258},{258,2},{3,259},{259,3},{4... | collective-permute-start | bytes 1327112 | tf_op jit(solution)/shard_map/ppermute | solution.py:239
  92.9 4.9 %shard_map.95 = (bf16[2,288,512]{2,1,0:T(8,128)(2,1)S(1)}, bf16[2,288,512]{2,1,0:T(8,128)(2,1)S(1)}, bf16[2,288,512]{2,1,0:T(8,128)(2,1)S(1)}, bf16[2,288,512]{2,1,0:T(8,128)(2,1)S(1)}) custom-call(s32[1]{0:T(128)} %bitcast.y_ref, bf16[2,2,576,384]{3,2,1,0:T(8,128)(2,1)} %bitcast.2.near_ref.refs_4_, ...), custom_call_target="tpu_custom_call" | custom-call | flops 1811939328 | bytes 8388608 | tf_op jit(solution)/shard_map/pallas_call | solution.py:85
  97.9 38.6 %collective-permute-done.1 = bf16[576,384]{1,0:T(8,128)(2,1)} collective-permute-done((bf16[576,384]{1,0:T(8,128)(2,1)}, bf16[576,384]{1,0:T(8,128)(2,1)}, u32[]{:S(2)}, u32[]{:S(2)}) %collective-permute-start.1) | collective-permute-done | bytes 442400 | tf_op jit(solution)/shard_map/ppermute | solution.py:239
  137.7 23.3 %all_to_all.20 = bf16[4,576,384]{2,1,0:T(8,128)(2,1)S(1)} all-to-all(bf16[4,576,384]{2,1,0:T(8,128)(2,1)S(1)} %broadcast_in_dim.53), channel_id=1, replica_groups=mesh['zh'=2,'co'=2,'zl'=8,'y'=4,'x'=4] {'x'}, dimensions={0} | all-to-all | bytes 3538944 | tf_op jit(solution)/shard_map/all_to_all | solution.py:209
  160.9 4.8 %collective-permute-start.5 = (bf16[2,2,576,384]{3,2,1,0:T(8,128)(2,1)S(1)}, bf16[2,2,576,384]{3,2,1,0:T(8,128)(2,1)S(1)}, u32[]{:S(2)}, u32[]{:S(2)}) collective-permute-start(bf16[2,2,576,384]{3,2,1,0:T(8,128)(2,1)S(1)} %bitcast.76), channel_id=1, source_target_pairs={{0,128},{128,0},{1,129},{129,1},{2,130},{130,2},{3,131},{131,3},{4... | collective-permute-start | bytes 5308424 | tf_op jit(solution)/shard_map/ppermute | solution.py:270
  165.8 5.2 %collective-permute-start.9 = (bf16[2,288,512]{2,1,0:T(8,128)(2,1)S(1)}, bf16[2,288,512]{2,1,0:T(8,128)(2,1)S(1)}, u32[]{:S(2)}, u32[]{:S(2)}) collective-permute-start(bf16[2,288,512]{2,1,0:T(8,128)(2,1)S(1)} %get-tuple-element.53), channel_id=1, source_target_pairs={{0,12},{4,0},{8,4},{12,8},{1,13},{5,1},{9,5},{13,9},{2,14},{6,2},{... | collective-permute-start | bytes 1769480 | tf_op jit(solution)/shard_map/ppermute | solution.py:215
  176.6 4.7 %shard_map.96 = (bf16[2,288,512]{2,1,0:T(8,128)(2,1)S(1)}, bf16[2,288,512]{2,1,0:T(8,128)(2,1)S(1)}, bf16[2,288,512]{2,1,0:T(8,128)(2,1)S(1)}, bf16[2,288,512]{2,1,0:T(8,128)(2,1)S(1)}) custom-call(s32[1]{0:T(128)} %bitcast.y_ref, bf16[2,2,576,384]{3,2,1,0:T(8,128)(2,1)S(1)} %bitcast.77, bf16[2,2,576,384]{3,2,1,0:T(8,128)(2,1)} %copy-done.12, ...), custom_call_target="tpu_custom_call" | custom-call | flops 1811939328 | bytes 8388608 | tf_op jit(solution)/shard_map/pallas_call | solution.py:85
  181.4 4.0 %collective-permute-start.6 = (bf16[2,288,512]{2,1,0:T(8,128)(2,1)S(1)}, bf16[2,288,512]{2,1,0:T(8,128)(2,1)S(1)}, u32[]{:S(2)}, u32[]{:S(2)}) collective-permute-start(bf16[2,288,512]{2,1,0:T(8,128)(2,1)S(1)} %get-tuple-element.48), channel_id=1, source_target_pairs={{0,12},{4,0},{8,4},{12,8},{1,13},{5,1},{9,5},{13,9},{2,14},{6,2},{... | collective-permute-start | bytes 1769480 | tf_op jit(solution)/shard_map/ppermute | solution.py:215
  185.4 3.7 %collective-permute-start.7 = (bf16[2,288,512]{2,1,0:T(8,128)(2,1)S(1)}, bf16[2,288,512]{2,1,0:T(8,128)(2,1)S(1)}, u32[]{:S(2)}, u32[]{:S(2)}) collective-permute-start(bf16[2,288,512]{2,1,0:T(8,128)(2,1)S(1)} %get-tuple-element.49), channel_id=1, source_target_pairs={{0,8},{4,12},{8,0},{12,4},{1,9},{5,13},{9,1},{13,5},{2,10},{6,14},... | collective-permute-start | bytes 1769480 | tf_op jit(solution)/shard_map/ppermute | solution.py:215
  189.0 7.1 %collective-permute-done.9 = bf16[2,288,512]{2,1,0:T(8,128)(2,1)S(1)} collective-permute-done((bf16[2,288,512]{2,1,0:T(8,128)(2,1)S(1)}, bf16[2,288,512]{2,1,0:T(8,128)(2,1)S(1)}, u32[]{:S(2)}, u32[]{:S(2)}) %collective-permute-start.9) | collective-permute-done | bytes 589856 | tf_op jit(solution)/shard_map/ppermute | solution.py:215
  198.3 4.6 %collective-permute-done.11 = bf16[2,288,512]{2,1,0:T(8,128)(2,1)S(1)} collective-permute-done((bf16[2,288,512]{2,1,0:T(8,128)(2,1)S(1)}, bf16[2,288,512]{2,1,0:T(8,128)(2,1)S(1)}, u32[]{:S(2)}, u32[]{:S(2)}) %collective-permute-start.11) | collective-permute-done | bytes 589856 | tf_op jit(solution)/shard_map/ppermute | solution.py:215
  202.9 4.9 %shard_map.97.refs_5_ = bf16[2,8,2,64,1024]{4,3,2,1,0:T(8,128)(2,1)} custom-call(s32[1]{0:T(128)} %bitcast.16.zh_ref, bf16[2,2,144,512]{3,2,1,0:T(8,128)(2,1)S(1)} %bitcast.94, bf16[2,2,144,512]{3,2,1,0:T(8,128)(2,1)S(1)} %bitcast.91, bf16[2,2,144,512]{3,2,1,0:T(8,128)(2,1)S(1)} %bitcast.92, bf16[2,2,144,512]{3,2,1,0:T(8,128)(2,1)S(1)} %bitcast.93, ...), custom_call_target="tpu_custom_call" | custom-call | flops 2415919104 | bytes 8388608 | tf_op jit(solution)/shard_map/pallas_call | solution.py:113
  207.8 13.8 %collective-permute-done.6 = bf16[2,288,512]{2,1,0:T(8,128)(2,1)S(1)} collective-permute-done((bf16[2,288,512]{2,1,0:T(8,128)(2,1)S(1)}, bf16[2,288,512]{2,1,0:T(8,128)(2,1)S(1)}, u32[]{:S(2)}, u32[]{:S(2)}) %collective-permute-start.6) | collective-permute-done | bytes 589856 | tf_op jit(solution)/shard_map/ppermute | solution.py:215
  221.6 5.9 %collective-permute-done.8 = bf16[2,288,512]{2,1,0:T(8,128)(2,1)S(1)} collective-permute-done((bf16[2,288,512]{2,1,0:T(8,128)(2,1)S(1)}, bf16[2,288,512]{2,1,0:T(8,128)(2,1)S(1)}, u32[]{:S(2)}, u32[]{:S(2)}) %collective-permute-start.8) | collective-permute-done | bytes 589856 | tf_op jit(solution)/shard_map/ppermute | solution.py:215
  227.5 4.9 %shard_map.98 = bf16[2,8,2,64,1024]{4,3,2,1,0:T(8,128)(2,1)} custom-call(s32[1]{0:T(128)} %bitcast.16.zh_ref, bf16[2,2,144,512]{3,2,1,0:T(8,128)(2,1)S(1)} %bitcast.82, bf16[2,2,144,512]{3,2,1,0:T(8,128)(2,1)S(1)} %bitcast.84, bf16[2,2,144,512]{3,2,1,0:T(8,128)(2,1)S(1)} %bitcast.85, ...), custom_call_target="tpu_custom_call", output_to_operand_aliasing={{}: (6, {})} | custom-call | flops 2415919104 | bytes 8388608 | tf_op jit(solution)/shard_map/pallas_call | solution.py:113
  232.4 4.6 %shard_map.100 = (bf16[2,2,144,512]{3,2,1,0:T(8,128)(2,1)S(1)}, bf16[2,2,144,512]{3,2,1,0:T(8,128)(2,1)S(1)}, bf16[2,2,144,512]{3,2,1,0:T(8,128)(2,1)}, bf16[2,2,144,512]{3,2,1,0:T(8,128)(2,1)}) custom-call(s32[1]{0:T(128)} %bitcast.16.zh_ref, bf16[16,2,64,1024]{3,2,1,0:T(8,128)(2,1)} %bitcast.96, f32[8,576,2]{2,1,0:T(8,128)S(1)} %bitcast.74), custom_call_target="tpu_custom_call" | custom-call | flops 1207959552 | bytes 8388608 | tf_op jit(solution)/shard_map/pallas_call | solution.py:51
  242.6 3.6 %collective-permute-start.19 = (bf16[2,2,144,512]{3,2,1,0:T(8,128)(2,1)}, bf16[2,2,144,512]{3,2,1,0:T(8,128)(2,1)}, u32[]{:S(2)}, u32[]{:S(2)}) collective-permute-start(bf16[2,2,144,512]{3,2,1,0:T(8,128)(2,1)} %get-tuple-element.65), channel_id=1, source_target_pairs={{0,12},{4,0},{8,4},{12,8},{1,13},{5,1},{9,5},{13,9},{2,14},{6,2},{... | collective-permute-start | bytes 1769480 | tf_op jit(solution)/shard_map/ppermute | solution.py:215
  246.3 4.6 %shard_map.99 = (bf16[2,2,144,512]{3,2,1,0:T(8,128)(2,1)S(1)}, bf16[2,2,144,512]{3,2,1,0:T(8,128)(2,1)}, bf16[2,2,144,512]{3,2,1,0:T(8,128)(2,1)}, bf16[2,2,144,512]{3,2,1,0:T(8,128)(2,1)}) custom-call(s32[1]{0:T(128)} %bitcast.16.zh_ref, bf16[16,2,64,1024]{3,2,1,0:T(8,128)(2,1)} %bitcast.97, f32[8,576,2]{2,1,0:T(8,128)S(1)} %bitcast.75), custom_call_target="tpu_custom_call" | custom-call | flops 1207959552 | bytes 8388608 | tf_op jit(solution)/shard_map/pallas_call | solution.py:51
  254.2 3.7 %collective-permute-start.15 = (bf16[2,2,144,512]{3,2,1,0:T(8,128)(2,1)}, bf16[2,2,144,512]{3,2,1,0:T(8,128)(2,1)S(1)}, u32[]{:S(2)}, u32[]{:S(2)}) collective-permute-start(bf16[2,2,144,512]{3,2,1,0:T(8,128)(2,1)} %get-tuple-element.60), channel_id=1, source_target_pairs={{0,8},{4,12},{8,0},{12,4},{1,9},{5,13},{9,1},{13,5},{2,10},{6,14},... | collective-permute-start | bytes 1769480 | tf_op jit(solution)/shard_map/ppermute | solution.py:215
  257.9 9.2 %collective-permute-done.17 = bf16[2,2,144,512]{3,2,1,0:T(8,128)(2,1)S(1)} collective-permute-done((bf16[2,2,144,512]{3,2,1,0:T(8,128)(2,1)S(1)}, bf16[2,2,144,512]{3,2,1,0:T(8,128)(2,1)S(1)}, u32[]{:S(2)}, u32[]{:S(2)}) %collective-permute-start.17) | collective-permute-done | bytes 589856 | tf_op jit(solution)/shard_map/ppermute | solution.py:215
  275.0 4.2 %all-to-all-start.3 = ((bf16[4,128,1024]{2,1,0:T(8,128)(2,1)}), bf16[4,128,1024]{2,1,0:T(8,128)(2,1)}, u32[]{:S(2)}, u32[]{:S(2)}) async-start(bf16[4,128,1024]{2,1,0:T(8,128)(2,1)} %copy.68), calls=%async_computation.3 | async-start | bytes 2097152 | tf_op jit(solution)/shard_map/all_to_all | solution.py:291
  281.5 6.4 %shard_map.101.refs_6_ = f32[2,512,384]{2,1,0:T(8,128)S(1)} custom-call(s32[1]{0:T(128)} %bitcast.y_ref, bf16[2,288,512]{2,1,0:T(8,128)(2,1)S(1)} %bitcast.87, bf16[2,288,512]{2,1,0:T(8,128)(2,1)S(1)} %bitcast.88, bf16[2,288,512]{2,1,0:T(8,128)(2,1)} %bitcast.35.refs_2_, bf16[2,288,512]{2,1,0:T(8,128)(2,1)} %bitcast.36.refs_3_, ...), custom_call_target="tpu_custom_call" | custom-call | flops 1811939328 | bytes 8388608 | tf_op jit(solution)/shard_map/pallas_call | solution.py:159
  287.9 5.5 %collective-permute-done.14 = bf16[2,2,144,512]{3,2,1,0:T(8,128)(2,1)S(1)} collective-permute-done((bf16[2,2,144,512]{3,2,1,0:T(8,128)(2,1)}, bf16[2,2,144,512]{3,2,1,0:T(8,128)(2,1)S(1)}, u32[]{:S(2)}, u32[]{:S(2)}) %collective-permute-start.14) | collective-permute-done | bytes 589856 | tf_op jit(solution)/shard_map/ppermute | solution.py:215
  297.7 6.0 %shard_map.102 = bf16[2,512,384]{2,1,0:T(8,128)(2,1)S(1)} custom-call(s32[1]{0:T(128)} %bitcast.y_ref, bf16[2,288,512]{2,1,0:T(8,128)(2,1)S(1)} %bitcast.79, bf16[2,288,512]{2,1,0:T(8,128)(2,1)S(1)} %bitcast.80, bf16[2,288,512]{2,1,0:T(8,128)(2,1)S(1)} %bitcast.81, bf16[2,288,512]{2,1,0:T(8,128)(2,1)S(1)} %bitcast.83, bf16[2,2,576,384]{3,2,1,0:T(8,128)(2,1)} %bitcast.78, ...), custom_call_target="tpu_custom_call" | custom-call | flops 1811939328 | bytes 8388608 | tf_op jit(solution)/shard_map/pallas_call | solution.py:159
  303.7 3.5 %collective-permute-start.20 = (bf16[512,384]{1,0:T(8,128)(2,1)S(1)}, bf16[512,384]{1,0:T(8,128)(2,1)}, u32[]{:S(2)}, u32[]{:S(2)}) collective-permute-start(bf16[512,384]{1,0:T(8,128)(2,1)S(1)} %select_bitcast_fusion), channel_id=1, source_target_pairs={{0,128},{128,0},{1,129},{129,1},{2,130},{130,2},{3,131},{131,3},{4... | collective-permute-start | bytes 1179656 | tf_op jit(solution)/shard_map/ppermute | solution.py:288
  (115 shorter events, 57.4 us)
Async XLA Ops:
  7.2 8.6 %copy-start = (bf16[2,64,4096]{2,1,0:T(8,128)(2,1)S(1)}, bf16[2,64,4096]{2,1,0:T(8,128)(2,1)}, u32[]{:S(2)}) copy-start(bf16[2,64,4096]{2,1,0:T(8,128)(2,1)} %param.8) | copy-start | bytes 3145732
  7.2 225.3 %all-gather.2.cloned.1.call-start = ((), (), s32[]{:S(2)}) async-start(), calls=%async_computation.6 | async-start | bytes 4456448 | tf_op jit(solution)/shard_map/all_gather | solution.py:224
  10.2 13.3 %collective-permute-start = (bf16[576,384]{1,0:T(8,128)(2,1)S(1)}, bf16[576,384]{1,0:T(8,128)(2,1)S(1)}, u32[]{:S(2)}, u32[]{:S(2)}) collective-permute-start(bf16[576,384]{1,0:T(8,128)(2,1)S(1)} %broadcast_select_fusion.3), channel_id=1, source_target_pairs={{0,2},{1,3},{2,0},{3,1},{4,6},{5,7},{6,4},{7,5},{8,10},{9,11},{10,... | collective-permute-start | bytes 1327112 | tf_op jit(solution)/shard_map/ppermute | solution.py:237
  16.6 6.2 %collective-permute-start.13 = (bf16[128,512]{1,0:T(8,128)(2,1)S(1)}, bf16[128,512]{1,0:T(8,128)(2,1)S(1)}, u32[]{:S(2)}, u32[]{:S(2)}) collective-permute-start(bf16[128,512]{1,0:T(8,128)(2,1)S(1)} %bitcast.103), channel_id=1, source_target_pairs={{0,128},{128,0},{1,129},{129,1},{2,130},{130,2},{3,131},{131,3},{4... | collective-permute-start | bytes 393224 | tf_op jit(solution)/shard_map/ppermute | solution.py:223
  25.9 11.8 %copy-start.14 = (f32[2,64,8]{1,2,0:T(8,128)S(1)}, f32[2,64,8]{1,2,0:T(8,128)}, u32[]{:S(2)}) copy-start(f32[2,64,8]{1,2,0:T(8,128)} %param.11) | copy-start | bytes 12292
  25.9 11.9 %copy-start.15 = (s32[2,64,8]{1,2,0:T(8,128)S(1)}, s32[2,64,8]{1,2,0:T(8,128)}, u32[]{:S(2)}) copy-start(s32[2,64,8]{1,2,0:T(8,128)} %param.10) | copy-start | bytes 12292
  25.9 11.9 %copy-start.16 = (s32[2,64,8]{1,2,0:T(8,128)S(1)}, s32[2,64,8]{1,2,0:T(8,128)}, u32[]{:S(2)}) copy-start(s32[2,64,8]{1,2,0:T(8,128)} %param.9) | copy-start | bytes 12292
  25.9 24.8 %all-to-all-start = ((bf16[4,576,384]{2,1,0:T(8,128)(2,1)}), bf16[4,576,384]{2,1,0:T(8,128)(2,1)}, u32[]{:S(2)}, u32[]{:S(2)}) async-start(bf16[4,576,384]{2,1,0:T(8,128)(2,1)} %broadcast_in_dim.47), calls=%async_computation | async-start | bytes 3538944 | tf_op jit(solution)/shard_map/all_to_all | solution.py:209
  31.7 45.3 %collective-permute-start.3 = (bf16[512,384]{1,0:T(8,128)(2,1)S(1)}, bf16[512,384]{1,0:T(8,128)(2,1)S(1)}, u32[]{:S(2)}, u32[]{:S(2)}) collective-permute-start(bf16[512,384]{1,0:T(8,128)(2,1)S(1)} %select_bitcast_fusion.1), channel_id=1, source_target_pairs={{0,128},{128,0},{1,129},{129,1},{2,130},{130,2},{3,131},{131,3},{4... | collective-permute-start | bytes 1179656 | tf_op jit(solution)/shard_map/ppermute | solution.py:262
  50.7 41.1 %collective-permute-start.2 = (bf16[2,2,576,384]{3,2,1,0:T(8,128)(2,1)}, bf16[2,2,576,384]{3,2,1,0:T(8,128)(2,1)}, u32[]{:S(2)}, u32[]{:S(2)}) collective-permute-start(bf16[2,2,576,384]{3,2,1,0:T(8,128)(2,1)} %bitcast.2.near_ref.refs_4_), channel_id=1, source_target_pairs={{0,128},{128,0},{1,129},{129,1},{2,130},{130,2},{3,131},{131,3},{4... | collective-permute-start | bytes 5308424 | tf_op jit(solution)/shard_map/ppermute | solution.py:264
  57.8 3.1 collective-permute-start.4
  61.6 28.5 %all-to-all-start.1 = ((f32[16,2,2,2,72]{4,3,2,1,0:T(2,128)}), f32[16,2,2,2,72]{4,3,2,1,0:T(2,128)S(1)}, u32[]{:S(2)}, u32[]{:S(2)}) async-start(f32[16,2,2,2,72]{4,3,2,1,0:T(2,128)} %copy.62), calls=%async_computation.1 | async-start | bytes 131072 | tf_op jit(solution)/shard_map/all_to_all | solution.py:249
  77.0 232.9 %reduce-scatter.2.cloned.1.call-start = ((), (), s32[]{:S(2)}) async-start(), calls=%async_computation.5 | async-start | bytes 4456448 | tf_op jit(solution)/shard_map/reduce_scatter | solution.py:275
  78.2 58.3 %collective-permute-start.1 = (bf16[576,384]{1,0:T(8,128)(2,1)}, bf16[576,384]{1,0:T(8,128)(2,1)}, u32[]{:S(2)}, u32[]{:S(2)}) collective-permute-start(bf16[576,384]{1,0:T(8,128)(2,1)} %get-tuple-element.69), channel_id=1, source_target_pairs={{0,256},{256,0},{1,257},{257,1},{2,258},{258,2},{3,259},{259,3},{4... | collective-permute-start | bytes 1327112 | tf_op jit(solution)/shard_map/ppermute | solution.py:239
  160.9 20.4 %copy-start.1 = (bf16[4,576,384]{2,1,0:T(8,128)(2,1)}, bf16[4,576,384]{2,1,0:T(8,128)(2,1)S(1)}, u32[]{:S(2)}) copy-start(bf16[4,576,384]{2,1,0:T(8,128)(2,1)S(1)} %all_to_all.20) | copy-start | bytes 5308420
  160.9 14.4 %collective-permute-start.5 = (bf16[2,2,576,384]{3,2,1,0:T(8,128)(2,1)S(1)}, bf16[2,2,576,384]{3,2,1,0:T(8,128)(2,1)S(1)}, u32[]{:S(2)}, u32[]{:S(2)}) collective-permute-start(bf16[2,2,576,384]{3,2,1,0:T(8,128)(2,1)S(1)} %bitcast.76), channel_id=1, source_target_pairs={{0,128},{128,0},{1,129},{129,1},{2,130},{130,2},{3,131},{131,3},{4... | collective-permute-start | bytes 5308424 | tf_op jit(solution)/shard_map/ppermute | solution.py:270
  165.8 30.4 %collective-permute-start.9 = (bf16[2,288,512]{2,1,0:T(8,128)(2,1)S(1)}, bf16[2,288,512]{2,1,0:T(8,128)(2,1)S(1)}, u32[]{:S(2)}, u32[]{:S(2)}) collective-permute-start(bf16[2,288,512]{2,1,0:T(8,128)(2,1)S(1)} %get-tuple-element.53), channel_id=1, source_target_pairs={{0,12},{4,0},{8,4},{12,8},{1,13},{5,1},{9,5},{13,9},{2,14},{6,2},{... | collective-permute-start | bytes 1769480 | tf_op jit(solution)/shard_map/ppermute | solution.py:215
  171.0 27.3 %collective-permute-start.10 = (bf16[2,288,512]{2,1,0:T(8,128)(2,1)S(1)}, bf16[2,288,512]{2,1,0:T(8,128)(2,1)S(1)}, u32[]{:S(2)}, u32[]{:S(2)}) collective-permute-start(bf16[2,288,512]{2,1,0:T(8,128)(2,1)S(1)} %get-tuple-element.54), channel_id=1, source_target_pairs={{0,8},{4,12},{8,0},{12,4},{1,9},{5,13},{9,1},{13,5},{2,10},{6,14},... | collective-permute-start | bytes 1769480 | tf_op jit(solution)/shard_map/ppermute | solution.py:215
  172.9 30.0 %collective-permute-start.11 = (bf16[2,288,512]{2,1,0:T(8,128)(2,1)S(1)}, bf16[2,288,512]{2,1,0:T(8,128)(2,1)S(1)}, u32[]{:S(2)}, u32[]{:S(2)}) collective-permute-start(bf16[2,288,512]{2,1,0:T(8,128)(2,1)S(1)} %get-tuple-element.55), channel_id=1, source_target_pairs={{0,4},{4,8},{8,12},{12,0},{1,5},{5,9},{9,13},{13,1},{2,6},{6,10},{... | collective-permute-start | bytes 1769480 | tf_op jit(solution)/shard_map/ppermute | solution.py:215
  181.4 40.2 %collective-permute-start.6 = (bf16[2,288,512]{2,1,0:T(8,128)(2,1)S(1)}, bf16[2,288,512]{2,1,0:T(8,128)(2,1)S(1)}, u32[]{:S(2)}, u32[]{:S(2)}) collective-permute-start(bf16[2,288,512]{2,1,0:T(8,128)(2,1)S(1)} %get-tuple-element.48), channel_id=1, source_target_pairs={{0,12},{4,0},{8,4},{12,8},{1,13},{5,1},{9,5},{13,9},{2,14},{6,2},{... | collective-permute-start | bytes 1769480 | tf_op jit(solution)/shard_map/ppermute | solution.py:215
  185.4 36.2 %collective-permute-start.7 = (bf16[2,288,512]{2,1,0:T(8,128)(2,1)S(1)}, bf16[2,288,512]{2,1,0:T(8,128)(2,1)S(1)}, u32[]{:S(2)}, u32[]{:S(2)}) collective-permute-start(bf16[2,288,512]{2,1,0:T(8,128)(2,1)S(1)} %get-tuple-element.49), channel_id=1, source_target_pairs={{0,8},{4,12},{8,0},{12,4},{1,9},{5,13},{9,1},{13,5},{2,10},{6,14},... | collective-permute-start | bytes 1769480 | tf_op jit(solution)/shard_map/ppermute | solution.py:215
  196.2 31.3 %collective-permute-start.8 = (bf16[2,288,512]{2,1,0:T(8,128)(2,1)S(1)}, bf16[2,288,512]{2,1,0:T(8,128)(2,1)S(1)}, u32[]{:S(2)}, u32[]{:S(2)}) collective-permute-start(bf16[2,288,512]{2,1,0:T(8,128)(2,1)S(1)} %get-tuple-element.50), channel_id=1, source_target_pairs={{0,4},{4,8},{8,12},{12,0},{1,5},{5,9},{9,13},{13,1},{2,6},{6,10},{... | collective-permute-start | bytes 1769480 | tf_op jit(solution)/shard_map/ppermute | solution.py:215
  237.8 29.2 %collective-permute-start.17 = (bf16[2,2,144,512]{3,2,1,0:T(8,128)(2,1)S(1)}, bf16[2,2,144,512]{3,2,1,0:T(8,128)(2,1)S(1)}, u32[]{:S(2)}, u32[]{:S(2)}) collective-permute-start(bf16[2,2,144,512]{3,2,1,0:T(8,128)(2,1)S(1)} %get-tuple-element.63), channel_id=1, source_target_pairs={{0,4},{4,8},{8,12},{12,0},{1,5},{5,9},{9,13},{13,1},{2,6},{6,10},{... | collective-permute-start | bytes 1769480 | tf_op jit(solution)/shard_map/ppermute | solution.py:215
  239.8 39.5 %collective-permute-start.18 = (bf16[2,2,144,512]{3,2,1,0:T(8,128)(2,1)}, bf16[2,2,144,512]{3,2,1,0:T(8,128)(2,1)}, u32[]{:S(2)}, u32[]{:S(2)}) collective-permute-start(bf16[2,2,144,512]{3,2,1,0:T(8,128)(2,1)} %get-tuple-element.64), channel_id=1, source_target_pairs={{0,8},{4,12},{8,0},{12,4},{1,9},{5,13},{9,1},{13,5},{2,10},{6,14},... | collective-permute-start | bytes 1769480 | tf_op jit(solution)/shard_map/ppermute | solution.py:215
  242.6 36.6 %collective-permute-start.19 = (bf16[2,2,144,512]{3,2,1,0:T(8,128)(2,1)}, bf16[2,2,144,512]{3,2,1,0:T(8,128)(2,1)}, u32[]{:S(2)}, u32[]{:S(2)}) collective-permute-start(bf16[2,2,144,512]{3,2,1,0:T(8,128)(2,1)} %get-tuple-element.65), channel_id=1, source_target_pairs={{0,12},{4,0},{8,4},{12,8},{1,13},{5,1},{9,5},{13,9},{2,14},{6,2},{... | collective-permute-start | bytes 1769480 | tf_op jit(solution)/shard_map/ppermute | solution.py:215
  251.7 41.7 %collective-permute-start.14 = (bf16[2,2,144,512]{3,2,1,0:T(8,128)(2,1)}, bf16[2,2,144,512]{3,2,1,0:T(8,128)(2,1)S(1)}, u32[]{:S(2)}, u32[]{:S(2)}) collective-permute-start(bf16[2,2,144,512]{3,2,1,0:T(8,128)(2,1)} %get-tuple-element.59), channel_id=1, source_target_pairs={{0,4},{4,8},{8,12},{12,0},{1,5},{5,9},{9,13},{13,1},{2,6},{6,10},{... | collective-permute-start | bytes 1769480 | tf_op jit(solution)/shard_map/ppermute | solution.py:215
  254.2 39.2 %collective-permute-start.15 = (bf16[2,2,144,512]{3,2,1,0:T(8,128)(2,1)}, bf16[2,2,144,512]{3,2,1,0:T(8,128)(2,1)S(1)}, u32[]{:S(2)}, u32[]{:S(2)}) collective-permute-start(bf16[2,2,144,512]{3,2,1,0:T(8,128)(2,1)} %get-tuple-element.60), channel_id=1, source_target_pairs={{0,8},{4,12},{8,0},{12,4},{1,9},{5,13},{9,1},{13,5},{2,10},{6,14},... | collective-permute-start | bytes 1769480 | tf_op jit(solution)/shard_map/ppermute | solution.py:215
  267.9 27.9 %collective-permute-start.16 = (bf16[2,2,144,512]{3,2,1,0:T(8,128)(2,1)}, bf16[2,2,144,512]{3,2,1,0:T(8,128)(2,1)S(1)}, u32[]{:S(2)}, u32[]{:S(2)}) collective-permute-start(bf16[2,2,144,512]{3,2,1,0:T(8,128)(2,1)} %get-tuple-element.61), channel_id=1, source_target_pairs={{0,12},{4,0},{8,4},{12,8},{1,13},{5,1},{9,5},{13,9},{2,14},{6,2},{... | collective-permute-start | bytes 1769480 | tf_op jit(solution)/shard_map/ppermute | solution.py:215
  275.0 32.2 %all-to-all-start.3 = ((bf16[4,128,1024]{2,1,0:T(8,128)(2,1)}), bf16[4,128,1024]{2,1,0:T(8,128)(2,1)}, u32[]{:S(2)}, u32[]{:S(2)}) async-start(bf16[4,128,1024]{2,1,0:T(8,128)(2,1)} %copy.68), calls=%async_computation.3 | async-start | bytes 2097152 | tf_op jit(solution)/shard_map/all_to_all | solution.py:291
  281.5 15.2 %copy-start.4 = (bf16[2,2,144,512]{3,2,1,0:T(8,128)(2,1)S(1)}, bf16[2,2,144,512]{3,2,1,0:T(8,128)(2,1)}, u32[]{:S(2)}) copy-start(bf16[2,2,144,512]{3,2,1,0:T(8,128)(2,1)} %copy-done.3) | copy-start | bytes 1769476
  303.7 5.0 %collective-permute-start.20 = (bf16[512,384]{1,0:T(8,128)(2,1)S(1)}, bf16[512,384]{1,0:T(8,128)(2,1)}, u32[]{:S(2)}, u32[]{:S(2)}) collective-permute-start(bf16[512,384]{1,0:T(8,128)(2,1)S(1)} %select_bitcast_fusion), channel_id=1, source_target_pairs={{0,128},{128,0},{1,129},{129,1},{2,130},{130,2},{3,131},{131,3},{4... | collective-permute-start | bytes 1179656 | tf_op jit(solution)/shard_map/ppermute | solution.py:288
  310.8 3.2 %collective-permute-start.12 = (bf16[128,512]{1,0:T(8,128)(2,1)S(1)}, bf16[128,512]{1,0:T(8,128)(2,1)S(1)}, u32[]{:S(2)}, u32[]{:S(2)}) collective-permute-start(bf16[128,512]{1,0:T(8,128)(2,1)S(1)} %slice.58), channel_id=1, source_target_pairs={{0,128},{128,0},{1,129},{129,1},{2,130},{130,2},{3,131},{131,3},{4... | collective-permute-start | bytes 393224 | tf_op jit(solution)/shard_map/ppermute | solution.py:295
  (11 other events, 20.9 us)
Sparse Core Ops, SparseCore 0:
  23.7 86.8 all-gather.1
  232.5 64.2 reduce-scatter.1

commit v4 on v3

--- a/solution.py
+++ b/solution.py
@@ -239,13 +239,23 @@
     crossed = lax.ppermute(leave, "zh", SWAP)
     near = gather(stay)
 
-    expert_ids, slot_index, gate_weights, leave = lax.optimization_barrier(
-        (expert_ids, slot_index, gate_weights, leave)
-    )
+    cut = up_weight.reshape(2, eighth, ff)
+    mine, theirs = by(co, cut[0], cut[1])
+    weight = jnp.stack(by(co, mine, lax.ppermute(theirs, "co", SWAP)))
+
+    near_other = lax.ppermute(near, "co", SWAP)
+    back = rows_back(near, near_other, weight, here)
+    crossed, expert_ids, slot_index, gate_weights = lax.optimization_barrier(
+        (crossed, expert_ids, slot_index, gate_weights)
+    )
+    wide = gather(crossed)
+    wide, back = lax.optimization_barrier((wide, back))
+
     held, gate = slot_tables(expert_ids, slot_index, gate_weights, capacity, nzl * ny * capacity)
     table = jnp.stack([held, gate]).reshape(2, batches, nzl, ny * capacity)
     table = table.transpose(2, 0, 1, 3)
     table = jnp.stack([table, lax.ppermute(table, "co", SWAP)], axis=1)
+    table, wide = lax.optimization_barrier((table, wide))
     table = lax.all_to_all(
         jnp.concatenate([table, table]), ("zh", "zl"), split_axis=0, concat_axis=0, tiled=True
     ).reshape(2, nzl, 2, 2, batches, ny, capacity)
@@ -257,14 +267,6 @@
     table = jnp.stack([seats, table[1]]).reshape(2, 4 * batches, buffer_rows)
     lying, standing = table.transpose(1, 0, 2), table.transpose(1, 2, 0)
 
-    cut = up_weight.reshape(2, eighth, ff)
-    mine, theirs = by(co, cut[0], cut[1])
-    weight = jnp.stack(by(co, mine, lax.ppermute(theirs, "co", SWAP)))
-
-    near_other = lax.ppermute(near, "co", SWAP)
-    back = rows_back(near, near_other, weight, here)
-    crossed, back, lying, standing = lax.optimization_barrier((crossed, back, lying, standing))
-    wide = gather(crossed)
     split = (2, batches, nzl * capacity, eighth)
     spread = combine(0, along_y(back, split), lying, far, tok, None)
     wide_other = lax.ppermute(wide, "co", SWAP)

time: 324 us -> 301 us (0.929)
  blocking collectives: 23.3 us -> 0 us
  waiting for transfers between devices: 102 us -> 88.6 us
  local copies, waits for them, and re-layouts: 20 us -> 29.4 us
  Pallas kernels: 41 us -> 44.7 us
    all_to_all x1 -> x0, blocking collectives: 23.3 us -> none  [gather(): lax.all_to_all(jnp.broadcast_to(v, (nx,) + v.shape), 'x', split_axis=0, c...]
    ppermute x12, waiting for transfers between devices: 48.6 us -> 35.4 us  [along_y(): lax.ppermute(v, 'y', [(i, (i + d) % ny) for i in range(ny)])]
    ppermute x1, waiting for transfers between devices: 0.01 us -> 12.9 us  [on_device(): taken = lax.ppermute(send, 'x', [(i, (i + 2) % nx) for i in range(nx)])]
    ppermute x1, waiting for transfers between devices: 38.6 us -> 30.2 us  [on_device(): crossed = lax.ppermute(leave, 'zh', SWAP)]
    all_to_all x1 -> x2, waiting for transfers between devices: 12.1 us -> 6.71 us  [gather(): lax.all_to_all(jnp.broadcast_to(v, (nx,) + v.shape), 'x', split_axis=0, c...]
    unnamed x38 -> x46, local copies, waits for them, and re-layouts: 8.9 us -> 13.3 us
    ppermute x1, starting transfers between devices: 1.92 us -> 5.5 us  [on_device(): table = jnp.stack([table, lax.ppermute(table, 'co', SWAP)], axis=1)]
    ppermute x1, starting transfers between devices: 5.22 us -> 8.79 us  [on_device(): line = jnp.concatenate([mine, lax.ppermute(theirs, 'co', SWAP)], axis=1)]
  transfers between devices with their start and end apart: 26 -> 27, of which waited for: 12 -> 13; matrix products, arithmetic and copies ran while one was open for 6% -> 9% of each run, Pallas kernels for 13% -> 15%
where the time goes in v4:
time: 301 us; the launch traced here: 299 us
  starting transfers between devices  107 us (36%)
  waiting for transfers between devices  88.6 us (29%)
  Pallas kernels  44.7 us (15%)
  local copies, waits for them, and re-layouts  29.4 us (10%)
  between operations  14.7 us (5%)
  other arithmetic  13 us (4%)
    ppermute x12, waiting for transfers between devices, along_y(): lax.ppermute(v, 'y', [(i, (i + d) % ny) for i in range(ny)])  35.4 us
    ppermute x12, starting transfers between devices, along_y(): lax.ppermute(v, 'y', [(i, (i + d) % ny) for i in range(ny)])  35 us
    ppermute x1, waiting for transfers between devices, on_device(): crossed = lax.ppermute(leave, 'zh', SWAP)  30.2 us
    all_to_all x1, starting transfers between devices, on_device(): lax.all_to_all(jnp.concatenate([table, table]), ('zh', 'zl'), split_axis=...  13.3 us
    unnamed x46, local copies, waits for them, and re-layouts  13.3 us
    ppermute x1, waiting for transfers between devices, on_device(): taken = lax.ppermute(send, 'x', [(i, (i + 2) % nx) for i in range(nx)])  12.9 us
    pallas_call x2, Pallas kernels, weight_sum(): call(body, (4,), [pl.BlockSpec((2, part, width), lambda d, y: (0, 0, 0))]...  12.8 us
    pallas_call x2, Pallas kernels, rows_back(): call(body, (4,), [piece, piece, pl.BlockSpec(weight.shape, lambda d, y: (...  11.9 us
  transfers between devices with their start and end apart: 27, of which 13 were waited for; matrix products, arithmetic and copies ran while one was open for 9% of the time, Pallas kernels for 15%

profile of v4, /device:TPU:1, one launch (start us, length us, event | category | flops | bytes accessed | tf_op | source)
XLA Modules:
  0.0 299.4 jit_solution(16315586448763279295)
XLA Ops:
  9.3 8.8 %collective-permute-start.13 = (bf16[128,512]{1,0:T(8,128)(2,1)S(1)}, bf16[128,512]{1,0:T(8,128)(2,1)S(1)}, u32[]{:S(2)}, u32[]{:S(2)}) collective-permute-start(bf16[128,512]{1,0:T(8,128)(2,1)S(1)} %bitcast.99), channel_id=1, source_target_pairs={{0,128},{128,0},{1,129},{129,1},{2,130},{130,2},{3,131},{131,3},{4... | collective-permute-start | bytes 393224 | tf_op jit(solution)/shard_map/ppermute | solution.py:223
  23.5 12.9 %collective-permute-done = bf16[576,384]{1,0:T(8,128)(2,1)S(1)} collective-permute-done((bf16[576,384]{1,0:T(8,128)(2,1)S(1)}, bf16[576,384]{1,0:T(8,128)(2,1)S(1)}, u32[]{:S(2)}, u32[]{:S(2)}) %collective-permute-start) | collective-permute-done | bytes 442400 | tf_op jit(solution)/shard_map/ppermute | solution.py:237
  37.9 3.6 %all-to-all-start.1 = ((bf16[4,576,384]{2,1,0:T(8,128)(2,1)}), bf16[4,576,384]{2,1,0:T(8,128)(2,1)S(1)}, u32[]{:S(2)}, u32[]{:S(2)}) async-start(bf16[4,576,384]{2,1,0:T(8,128)(2,1)} %broadcast_in_dim.52), calls=%async_computation.1 | async-start | bytes 3538944 | tf_op jit(solution)/shard_map/all_to_all | solution.py:209
  41.5 10.5 %collective-permute-start.1 = (bf16[576,384]{1,0:T(8,128)(2,1)S(1)}, bf16[576,384]{1,0:T(8,128)(2,1)}, u32[]{:S(2)}, u32[]{:S(2)}) collective-permute-start(bf16[576,384]{1,0:T(8,128)(2,1)S(1)} %get-tuple-element.71), channel_id=1, source_target_pairs={{0,256},{256,0},{1,257},{257,1},{2,258},{258,2},{3,259},{259,3},{4... | collective-permute-start | bytes 1327112 | tf_op jit(solution)/shard_map/ppermute | solution.py:239
  53.9 3.6 %collective-permute-start.4 = (bf16[512,384]{1,0:T(8,128)(2,1)}, bf16[512,384]{1,0:T(8,128)(2,1)}, u32[]{:S(2)}, u32[]{:S(2)}) collective-permute-start(bf16[512,384]{1,0:T(8,128)(2,1)} %select_bitcast_fusion.1), channel_id=1, source_target_pairs={{0,128},{128,0},{1,129},{129,1},{2,130},{130,2},{3,131},{131,3},{4... | collective-permute-start | bytes 1179656 | tf_op jit(solution)/shard_map/ppermute | solution.py:244
  57.5 5.7 %all-to-all-done.1 = bf16[4,576,384]{2,1,0:T(8,128)(2,1)S(1)} async-done(((bf16[4,576,384]{2,1,0:T(8,128)(2,1)}), bf16[4,576,384]{2,1,0:T(8,128)(2,1)S(1)}, u32[]{:S(2)}, u32[]{:S(2)}) %all-to-all-start.1) | async-done | bytes 1769504 | tf_op jit(solution)/shard_map/all_to_all | solution.py:209
  63.2 3.9 %collective-permute-start.3 = (bf16[2,2,576,384]{3,2,1,0:T(8,128)(2,1)S(1)}, bf16[2,2,576,384]{3,2,1,0:T(8,128)(2,1)}, u32[]{:S(2)}, u32[]{:S(2)}) collective-permute-start(bf16[2,2,576,384]{3,2,1,0:T(8,128)(2,1)S(1)} %bitcast.76), channel_id=1, source_target_pairs={{0,128},{128,0},{1,129},{129,1},{2,130},{130,2},{3,131},{131,3},{4... | collective-permute-start | bytes 5308424 | tf_op jit(solution)/shard_map/ppermute | solution.py:246
  67.1 30.2 %collective-permute-done.1 = bf16[576,384]{1,0:T(8,128)(2,1)} collective-permute-done((bf16[576,384]{1,0:T(8,128)(2,1)S(1)}, bf16[576,384]{1,0:T(8,128)(2,1)}, u32[]{:S(2)}, u32[]{:S(2)}) %collective-permute-start.1) | collective-permute-done | bytes 442400 | tf_op jit(solution)/shard_map/ppermute | solution.py:239
  99.8 4.5 %all-to-all-start = ((bf16[4,576,384]{2,1,0:T(8,128)(2,1)}), bf16[4,576,384]{2,1,0:T(8,128)(2,1)}, u32[]{:S(2)}, u32[]{:S(2)}) async-start(bf16[4,576,384]{2,1,0:T(8,128)(2,1)} %broadcast_in_dim.51), calls=%async_computation | async-start | bytes 3538944 | tf_op jit(solution)/shard_map/all_to_all | solution.py:209
  107.5 5.5 %collective-permute-start.2 = (f32[8,2,2,72]{3,0,2,1:T(8,128)S(1)}, f32[8,2,2,72]{3,0,2,1:T(8,128)S(1)}, u32[]{:S(2)}, u32[]{:S(2)}) collective-permute-start(f32[8,2,2,72]{3,0,2,1:T(8,128)S(1)} %bitcast.100), channel_id=1, source_target_pairs={{0,128},{128,0},{1,129},{129,1},{2,130},{130,2},{3,131},{131,3},{4... | collective-permute-start | bytes 27656 | tf_op jit(solution)/shard_map/ppermute | solution.py:257
  114.2 5.8 %shard_map.95 = (bf16[2,288,512]{2,1,0:T(8,128)(2,1)S(1)}, bf16[2,288,512]{2,1,0:T(8,128)(2,1)}, bf16[2,288,512]{2,1,0:T(8,128)(2,1)}, bf16[2,288,512]{2,1,0:T(8,128)(2,1)S(1)}) custom-call(s32[1]{0:T(128)} %bitcast.y_ref, bf16[2,2,576,384]{3,2,1,0:T(8,128)(2,1)S(1)} %bitcast.77, bf16[2,2,576,384]{3,2,1,0:T(8,128)(2,1)} %collective-permute-done.3.other_ref.refs_5_, ...), custom_call_target="tpu_custom_call" | custom-call | flops 1811939328 | bytes 8388608 | tf_op jit(solution)/shard_map/pallas_call | solution.py:85
  123.6 6.5 %collective-permute-start.5 = (bf16[2,2,576,384]{3,2,1,0:T(8,128)(2,1)}, bf16[2,2,576,384]{3,2,1,0:T(8,128)(2,1)}, u32[]{:S(2)}, u32[]{:S(2)}) collective-permute-start(bf16[2,2,576,384]{3,2,1,0:T(8,128)(2,1)} %bitcast.5.near_ref.refs_4_), channel_id=1, source_target_pairs={{0,128},{128,0},{1,129},{129,1},{2,130},{130,2},{3,131},{131,3},{4... | collective-permute-start | bytes 5308424 | tf_op jit(solution)/shard_map/ppermute | solution.py:272
  130.8 13.3 %all-to-all-start.3 = ((f32[16,2,2,2,72]{4,3,2,1,0:T(2,128)}), f32[16,2,2,2,72]{4,3,2,1,0:T(2,128)S(1)}, u32[]{:S(2)}, u32[]{:S(2)}) async-start(f32[16,2,2,2,72]{4,3,2,1,0:T(2,128)} %copy.63), calls=%async_computation.3 | async-start | bytes 131072 | tf_op jit(solution)/shard_map/all_to_all | solution.py:259
  144.1 4.1 %collective-permute-start.9 = (bf16[2,288,512]{2,1,0:T(8,128)(2,1)}, bf16[2,288,512]{2,1,0:T(8,128)(2,1)S(1)}, u32[]{:S(2)}, u32[]{:S(2)}) collective-permute-start(bf16[2,288,512]{2,1,0:T(8,128)(2,1)} %copy-done.13), channel_id=1, source_target_pairs={{0,12},{4,0},{8,4},{12,8},{1,13},{5,1},{9,5},{13,9},{2,14},{6,2},{... | collective-permute-start | bytes 1769480 | tf_op jit(solution)/shard_map/ppermute | solution.py:215
  150.6 2.8 collective-permute-start.11
  157.4 6.1 %shard_map.96 = (bf16[2,288,512]{2,1,0:T(8,128)(2,1)S(1)}, bf16[2,288,512]{2,1,0:T(8,128)(2,1)}, bf16[2,288,512]{2,1,0:T(8,128)(2,1)}, bf16[2,288,512]{2,1,0:T(8,128)(2,1)}) custom-call(s32[1]{0:T(128)} %bitcast.y_ref, bf16[2,2,576,384]{3,2,1,0:T(8,128)(2,1)} %bitcast.5.near_ref.refs_4_, bf16[2,2,576,384]{3,2,1,0:T(8,128)(2,1)} %collective-permute-done.5.other_ref.refs_5_, ...), custom_call_target="tpu_custom_call" | custom-call | flops 1811939328 | bytes 8388608 | tf_op jit(solution)/shard_map/pallas_call | solution.py:85
  163.5 4.1 %collective-permute-start.6 = (bf16[2,288,512]{2,1,0:T(8,128)(2,1)}, bf16[2,288,512]{2,1,0:T(8,128)(2,1)S(1)}, u32[]{:S(2)}, u32[]{:S(2)}) collective-permute-start(bf16[2,288,512]{2,1,0:T(8,128)(2,1)} %get-tuple-element.51), channel_id=1, source_target_pairs={{0,12},{4,0},{8,4},{12,8},{1,13},{5,1},{9,5},{13,9},{2,14},{6,2},{... | collective-permute-start | bytes 1769480 | tf_op jit(solution)/shard_map/ppermute | solution.py:215
  170.8 2.9 collective-permute-start.8
  182.9 6.0 %shard_map.97.refs_5_ = bf16[2,8,2,64,1024]{4,3,2,1,0:T(8,128)(2,1)} custom-call(s32[1]{0:T(128)} %bitcast.13.zh_ref, bf16[2,2,144,512]{3,2,1,0:T(8,128)(2,1)S(1)} %bitcast.90, bf16[2,2,144,512]{3,2,1,0:T(8,128)(2,1)S(1)} %bitcast.89, bf16[2,2,144,512]{3,2,1,0:T(8,128)(2,1)} %bitcast.22.refs_2_, bf16[2,2,144,512]{3,2,1,0:T(8,128)(2,1)} %bitcast.23.refs_3_, ...), custom_call_target="tpu_custom_call" | custom-call | flops 2415919104 | bytes 8388608 | tf_op jit(solution)/shard_map/pallas_call | solution.py:113
  191.6 13.4 %collective-permute-done.8 = bf16[2,288,512]{2,1,0:T(8,128)(2,1)S(1)} collective-permute-done((bf16[2,288,512]{2,1,0:T(8,128)(2,1)}, bf16[2,288,512]{2,1,0:T(8,128)(2,1)S(1)}, u32[]{:S(2)}, u32[]{:S(2)}) %collective-permute-start.8) | collective-permute-done | bytes 589856 | tf_op jit(solution)/shard_map/ppermute | solution.py:215
  205.0 4.9 %shard_map.98 = bf16[2,8,2,64,1024]{4,3,2,1,0:T(8,128)(2,1)} custom-call(s32[1]{0:T(128)} %bitcast.13.zh_ref, bf16[2,2,144,512]{3,2,1,0:T(8,128)(2,1)S(1)} %bitcast.79, bf16[2,2,144,512]{3,2,1,0:T(8,128)(2,1)S(1)} %bitcast.81, bf16[2,2,144,512]{3,2,1,0:T(8,128)(2,1)S(1)} %bitcast.82, ...), custom_call_target="tpu_custom_call", output_to_operand_aliasing={{}: (6, {})} | custom-call | flops 2415919104 | bytes 8388608 | tf_op jit(solution)/shard_map/pallas_call | solution.py:113
  210.7 4.6 %shard_map.100 = (bf16[2,2,144,512]{3,2,1,0:T(8,128)(2,1)S(1)}, bf16[2,2,144,512]{3,2,1,0:T(8,128)(2,1)S(1)}, bf16[2,2,144,512]{3,2,1,0:T(8,128)(2,1)}, bf16[2,2,144,512]{3,2,1,0:T(8,128)(2,1)}) custom-call(s32[1]{0:T(128)} %bitcast.13.zh_ref, bf16[16,2,64,1024]{3,2,1,0:T(8,128)(2,1)} %bitcast.92, f32[8,576,2]{2,1,0:T(8,128)S(1)} %bitcast.74), custom_call_target="tpu_custom_call" | custom-call | flops 1207959552 | bytes 8388608 | tf_op jit(solution)/shard_map/pallas_call | solution.py:51
  220.5 3.9 %collective-permute-start.19 = (bf16[2,2,144,512]{3,2,1,0:T(8,128)(2,1)}, bf16[2,2,144,512]{3,2,1,0:T(8,128)(2,1)}, u32[]{:S(2)}, u32[]{:S(2)}) collective-permute-start(bf16[2,2,144,512]{3,2,1,0:T(8,128)(2,1)} %get-tuple-element.67), channel_id=1, source_target_pairs={{0,12},{4,0},{8,4},{12,8},{1,13},{5,1},{9,5},{13,9},{2,14},{6,2},{... | collective-permute-start | bytes 1769480 | tf_op jit(solution)/shard_map/ppermute | solution.py:215
  224.5 4.6 %shard_map.99 = (bf16[2,2,144,512]{3,2,1,0:T(8,128)(2,1)S(1)}, bf16[2,2,144,512]{3,2,1,0:T(8,128)(2,1)}, bf16[2,2,144,512]{3,2,1,0:T(8,128)(2,1)}, bf16[2,2,144,512]{3,2,1,0:T(8,128)(2,1)}) custom-call(s32[1]{0:T(128)} %bitcast.13.zh_ref, bf16[16,2,64,1024]{3,2,1,0:T(8,128)(2,1)} %bitcast.93, f32[8,576,2]{2,1,0:T(8,128)S(1)} %bitcast.75), custom_call_target="tpu_custom_call" | custom-call | flops 1207959552 | bytes 8388608 | tf_op jit(solution)/shard_map/pallas_call | solution.py:51
  232.3 3.7 %collective-permute-start.15 = (bf16[2,2,144,512]{3,2,1,0:T(8,128)(2,1)}, bf16[2,2,144,512]{3,2,1,0:T(8,128)(2,1)}, u32[]{:S(2)}, u32[]{:S(2)}) collective-permute-start(bf16[2,2,144,512]{3,2,1,0:T(8,128)(2,1)} %get-tuple-element.62), channel_id=1, source_target_pairs={{0,8},{4,12},{8,0},{12,4},{1,9},{5,13},{9,1},{13,5},{2,10},{6,14},... | collective-permute-start | bytes 1769480 | tf_op jit(solution)/shard_map/ppermute | solution.py:215
  236.0 9.2 %collective-permute-done.17 = bf16[2,2,144,512]{3,2,1,0:T(8,128)(2,1)S(1)} collective-permute-done((bf16[2,2,144,512]{3,2,1,0:T(8,128)(2,1)S(1)}, bf16[2,2,144,512]{3,2,1,0:T(8,128)(2,1)S(1)}, u32[]{:S(2)}, u32[]{:S(2)}) %collective-permute-start.17) | collective-permute-done | bytes 589856 | tf_op jit(solution)/shard_map/ppermute | solution.py:215
  250.6 2.7 copy.62
  253.3 4.2 %all-to-all-start.2 = ((bf16[4,128,1024]{2,1,0:T(8,128)(2,1)}), bf16[4,128,1024]{2,1,0:T(8,128)(2,1)}, u32[]{:S(2)}, u32[]{:S(2)}) async-start(bf16[4,128,1024]{2,1,0:T(8,128)(2,1)} %copy.62), calls=%async_computation.2 | async-start | bytes 2097152 | tf_op jit(solution)/shard_map/all_to_all | solution.py:293
  259.7 6.4 %shard_map.101.refs_6_ = f32[2,512,384]{2,1,0:T(8,128)S(1)} custom-call(s32[1]{0:T(128)} %bitcast.y_ref, bf16[2,288,512]{2,1,0:T(8,128)(2,1)S(1)} %bitcast.85, bf16[2,288,512]{2,1,0:T(8,128)(2,1)S(1)} %bitcast.86, bf16[2,288,512]{2,1,0:T(8,128)(2,1)} %bitcast.35.refs_2_, bf16[2,288,512]{2,1,0:T(8,128)(2,1)} %bitcast.36.refs_3_, ...), custom_call_target="tpu_custom_call" | custom-call | flops 1811939328 | bytes 8388608 | tf_op jit(solution)/shard_map/pallas_call | solution.py:159
  266.1 5.4 %collective-permute-done.14 = bf16[2,2,144,512]{3,2,1,0:T(8,128)(2,1)S(1)} collective-permute-done((bf16[2,2,144,512]{3,2,1,0:T(8,128)(2,1)}, bf16[2,2,144,512]{3,2,1,0:T(8,128)(2,1)S(1)}, u32[]{:S(2)}, u32[]{:S(2)}) %collective-permute-start.14) | collective-permute-done | bytes 589856 | tf_op jit(solution)/shard_map/ppermute | solution.py:215
  274.0 6.4 %shard_map.102 = bf16[2,512,384]{2,1,0:T(8,128)(2,1)S(1)} custom-call(s32[1]{0:T(128)} %bitcast.y_ref, bf16[2,288,512]{2,1,0:T(8,128)(2,1)S(1)} %bitcast.80, bf16[2,288,512]{2,1,0:T(8,128)(2,1)S(1)} %bitcast.83, bf16[2,288,512]{2,1,0:T(8,128)(2,1)} %bitcast.31.refs_2_, bf16[2,288,512]{2,1,0:T(8,128)(2,1)} %bitcast.32.refs_3_, ...), custom_call_target="tpu_custom_call" | custom-call | flops 1811939328 | bytes 8388608 | tf_op jit(solution)/shard_map/pallas_call | solution.py:159
  280.4 3.6 %collective-permute-start.20 = (bf16[512,384]{1,0:T(8,128)(2,1)S(1)}, bf16[512,384]{1,0:T(8,128)(2,1)}, u32[]{:S(2)}, u32[]{:S(2)}) collective-permute-start(bf16[512,384]{1,0:T(8,128)(2,1)S(1)} %select_bitcast_fusion), channel_id=1, source_target_pairs={{0,128},{128,0},{1,129},{129,1},{2,130},{130,2},{3,131},{131,3},{4... | collective-permute-start | bytes 1179656 | tf_op jit(solution)/shard_map/ppermute | solution.py:290
  (125 shorter events, 70.9 us)
Async XLA Ops:
  7.2 12.6 %copy-start.20 = (bf16[1,2,1,576,384]{4,3,2,1,0:T(8,128)(2,1)S(1)}, bf16[1,2,1,576,384]{4,3,2,1,0:T(8,128)(2,1)}, u32[]{:S(2)}) copy-start(bf16[1,2,1,576,384]{4,3,2,1,0:T(8,128)(2,1)} %param.12) | copy-start | bytes 2654212
  7.2 203.5 %all-gather.2.cloned.1.call-start = ((), (), s32[]{:S(2)}) async-start(), calls=%async_computation.6 | async-start | bytes 4456448 | tf_op jit(solution)/shard_map/all_gather | solution.py:224
  9.3 9.8 %collective-permute-start.13 = (bf16[128,512]{1,0:T(8,128)(2,1)S(1)}, bf16[128,512]{1,0:T(8,128)(2,1)S(1)}, u32[]{:S(2)}, u32[]{:S(2)}) collective-permute-start(bf16[128,512]{1,0:T(8,128)(2,1)S(1)} %bitcast.99), channel_id=1, source_target_pairs={{0,128},{128,0},{1,129},{129,1},{2,130},{130,2},{3,131},{131,3},{4... | collective-permute-start | bytes 393224 | tf_op jit(solution)/shard_map/ppermute | solution.py:223
  21.5 14.8 %collective-permute-start = (bf16[576,384]{1,0:T(8,128)(2,1)S(1)}, bf16[576,384]{1,0:T(8,128)(2,1)S(1)}, u32[]{:S(2)}, u32[]{:S(2)}) collective-permute-start(bf16[576,384]{1,0:T(8,128)(2,1)S(1)} %broadcast_select_fusion.3), channel_id=1, source_target_pairs={{0,2},{1,3},{2,0},{3,1},{4,6},{5,7},{6,4},{7,5},{8,10},{9,11},{10,... | collective-permute-start | bytes 1327112 | tf_op jit(solution)/shard_map/ppermute | solution.py:237
  37.9 25.3 %all-to-all-start.1 = ((bf16[4,576,384]{2,1,0:T(8,128)(2,1)}), bf16[4,576,384]{2,1,0:T(8,128)(2,1)S(1)}, u32[]{:S(2)}, u32[]{:S(2)}) async-start(bf16[4,576,384]{2,1,0:T(8,128)(2,1)} %broadcast_in_dim.52), calls=%async_computation.1 | async-start | bytes 3538944 | tf_op jit(solution)/shard_map/all_to_all | solution.py:209
  41.5 55.9 %collective-permute-start.1 = (bf16[576,384]{1,0:T(8,128)(2,1)S(1)}, bf16[576,384]{1,0:T(8,128)(2,1)}, u32[]{:S(2)}, u32[]{:S(2)}) collective-permute-start(bf16[576,384]{1,0:T(8,128)(2,1)S(1)} %get-tuple-element.71), channel_id=1, source_target_pairs={{0,256},{256,0},{1,257},{257,1},{2,258},{258,2},{3,259},{259,3},{4... | collective-permute-start | bytes 1327112 | tf_op jit(solution)/shard_map/ppermute | solution.py:239
  53.9 50.5 %collective-permute-start.4 = (bf16[512,384]{1,0:T(8,128)(2,1)}, bf16[512,384]{1,0:T(8,128)(2,1)}, u32[]{:S(2)}, u32[]{:S(2)}) collective-permute-start(bf16[512,384]{1,0:T(8,128)(2,1)} %select_bitcast_fusion.1), channel_id=1, source_target_pairs={{0,128},{128,0},{1,129},{129,1},{2,130},{130,2},{3,131},{131,3},{4... | collective-permute-start | bytes 1179656 | tf_op jit(solution)/shard_map/ppermute | solution.py:244
  63.2 51.0 %copy-start.1 = (bf16[4,576,384]{2,1,0:T(8,128)(2,1)}, bf16[4,576,384]{2,1,0:T(8,128)(2,1)S(1)}, u32[]{:S(2)}) copy-start(bf16[4,576,384]{2,1,0:T(8,128)(2,1)S(1)} %all-to-all-done.1) | copy-start | bytes 5308420
  63.2 51.0 %collective-permute-start.3 = (bf16[2,2,576,384]{3,2,1,0:T(8,128)(2,1)S(1)}, bf16[2,2,576,384]{3,2,1,0:T(8,128)(2,1)}, u32[]{:S(2)}, u32[]{:S(2)}) collective-permute-start(bf16[2,2,576,384]{3,2,1,0:T(8,128)(2,1)S(1)} %bitcast.76), channel_id=1, source_target_pairs={{0,128},{128,0},{1,129},{129,1},{2,130},{130,2},{3,131},{131,3},{4... | collective-permute-start | bytes 5308424 | tf_op jit(solution)/shard_map/ppermute | solution.py:246
  99.8 6.7 %copy-start.19 = (s32[2,64,8]{1,2,0:T(8,128)S(1)}, s32[2,64,8]{1,2,0:T(8,128)}, u32[]{:S(2)}) copy-start(s32[2,64,8]{1,2,0:T(8,128)} %param.9) | copy-start | bytes 12292
  99.8 23.8 %all-to-all-start = ((bf16[4,576,384]{2,1,0:T(8,128)(2,1)}), bf16[4,576,384]{2,1,0:T(8,128)(2,1)}, u32[]{:S(2)}, u32[]{:S(2)}) async-start(bf16[4,576,384]{2,1,0:T(8,128)(2,1)} %broadcast_in_dim.51), calls=%async_computation | async-start | bytes 3538944 | tf_op jit(solution)/shard_map/all_to_all | solution.py:209
  107.5 6.6 %collective-permute-start.2 = (f32[8,2,2,72]{3,0,2,1:T(8,128)S(1)}, f32[8,2,2,72]{3,0,2,1:T(8,128)S(1)}, u32[]{:S(2)}, u32[]{:S(2)}) collective-permute-start(f32[8,2,2,72]{3,0,2,1:T(8,128)S(1)} %bitcast.100), channel_id=1, source_target_pairs={{0,128},{128,0},{1,129},{129,1},{2,130},{130,2},{3,131},{131,3},{4... | collective-permute-start | bytes 27656 | tf_op jit(solution)/shard_map/ppermute | solution.py:257
  123.6 32.6 %collective-permute-start.5 = (bf16[2,2,576,384]{3,2,1,0:T(8,128)(2,1)}, bf16[2,2,576,384]{3,2,1,0:T(8,128)(2,1)}, u32[]{:S(2)}, u32[]{:S(2)}) collective-permute-start(bf16[2,2,576,384]{3,2,1,0:T(8,128)(2,1)} %bitcast.5.near_ref.refs_4_), channel_id=1, source_target_pairs={{0,128},{128,0},{1,129},{129,1},{2,130},{130,2},{3,131},{131,3},{4... | collective-permute-start | bytes 5308424 | tf_op jit(solution)/shard_map/ppermute | solution.py:272
  130.8 25.0 %all-to-all-start.3 = ((f32[16,2,2,2,72]{4,3,2,1,0:T(2,128)}), f32[16,2,2,2,72]{4,3,2,1,0:T(2,128)S(1)}, u32[]{:S(2)}, u32[]{:S(2)}) async-start(f32[16,2,2,2,72]{4,3,2,1,0:T(2,128)} %copy.63), calls=%async_computation.3 | async-start | bytes 131072 | tf_op jit(solution)/shard_map/all_to_all | solution.py:259
  144.1 142.6 %reduce-scatter.2.cloned.1.call-start = ((), (), s32[]{:S(2)}) async-start(), calls=%async_computation.5 | async-start | bytes 4456448 | tf_op jit(solution)/shard_map/reduce_scatter | solution.py:277
  144.1 25.8 %collective-permute-start.9 = (bf16[2,288,512]{2,1,0:T(8,128)(2,1)}, bf16[2,288,512]{2,1,0:T(8,128)(2,1)S(1)}, u32[]{:S(2)}, u32[]{:S(2)}) collective-permute-start(bf16[2,288,512]{2,1,0:T(8,128)(2,1)} %copy-done.13), channel_id=1, source_target_pairs={{0,12},{4,0},{8,4},{12,8},{1,13},{5,1},{9,5},{13,9},{2,14},{6,2},{... | collective-permute-start | bytes 1769480 | tf_op jit(solution)/shard_map/ppermute | solution.py:215
  148.3 30.3 %collective-permute-start.10 = (bf16[2,288,512]{2,1,0:T(8,128)(2,1)}, bf16[2,288,512]{2,1,0:T(8,128)(2,1)}, u32[]{:S(2)}, u32[]{:S(2)}) collective-permute-start(bf16[2,288,512]{2,1,0:T(8,128)(2,1)} %get-tuple-element.57), channel_id=1, source_target_pairs={{0,8},{4,12},{8,0},{12,4},{1,9},{5,13},{9,1},{13,5},{2,10},{6,14},... | collective-permute-start | bytes 1769480 | tf_op jit(solution)/shard_map/ppermute | solution.py:215
  150.6 30.2 %collective-permute-start.11 = (bf16[2,288,512]{2,1,0:T(8,128)(2,1)}, bf16[2,288,512]{2,1,0:T(8,128)(2,1)}, u32[]{:S(2)}, u32[]{:S(2)}) collective-permute-start(bf16[2,288,512]{2,1,0:T(8,128)(2,1)} %get-tuple-element.58), channel_id=1, source_target_pairs={{0,4},{4,8},{8,12},{12,0},{1,5},{5,9},{9,13},{13,1},{2,6},{6,10},{... | collective-permute-start | bytes 1769480 | tf_op jit(solution)/shard_map/ppermute | solution.py:215
  163.5 25.5 %collective-permute-start.6 = (bf16[2,288,512]{2,1,0:T(8,128)(2,1)}, bf16[2,288,512]{2,1,0:T(8,128)(2,1)S(1)}, u32[]{:S(2)}, u32[]{:S(2)}) collective-permute-start(bf16[2,288,512]{2,1,0:T(8,128)(2,1)} %get-tuple-element.51), channel_id=1, source_target_pairs={{0,12},{4,0},{8,4},{12,8},{1,13},{5,1},{9,5},{13,9},{2,14},{6,2},{... | collective-permute-start | bytes 1769480 | tf_op jit(solution)/shard_map/ppermute | solution.py:215
  167.6 24.0 %collective-permute-start.7 = (bf16[2,288,512]{2,1,0:T(8,128)(2,1)}, bf16[2,288,512]{2,1,0:T(8,128)(2,1)S(1)}, u32[]{:S(2)}, u32[]{:S(2)}) collective-permute-start(bf16[2,288,512]{2,1,0:T(8,128)(2,1)} %get-tuple-element.52), channel_id=1, source_target_pairs={{0,8},{4,12},{8,0},{12,4},{1,9},{5,13},{9,1},{13,5},{2,10},{6,14},... | collective-permute-start | bytes 1769480 | tf_op jit(solution)/shard_map/ppermute | solution.py:215
  170.8 34.2 %collective-permute-start.8 = (bf16[2,288,512]{2,1,0:T(8,128)(2,1)}, bf16[2,288,512]{2,1,0:T(8,128)(2,1)S(1)}, u32[]{:S(2)}, u32[]{:S(2)}) collective-permute-start(bf16[2,288,512]{2,1,0:T(8,128)(2,1)} %get-tuple-element.53), channel_id=1, source_target_pairs={{0,4},{4,8},{8,12},{12,0},{1,5},{5,9},{9,13},{13,1},{2,6},{6,10},{... | collective-permute-start | bytes 1769480 | tf_op jit(solution)/shard_map/ppermute | solution.py:215
  216.0 29.2 %collective-permute-start.17 = (bf16[2,2,144,512]{3,2,1,0:T(8,128)(2,1)S(1)}, bf16[2,2,144,512]{3,2,1,0:T(8,128)(2,1)S(1)}, u32[]{:S(2)}, u32[]{:S(2)}) collective-permute-start(bf16[2,2,144,512]{3,2,1,0:T(8,128)(2,1)S(1)} %get-tuple-element.65), channel_id=1, source_target_pairs={{0,4},{4,8},{8,12},{12,0},{1,5},{5,9},{9,13},{13,1},{2,6},{6,10},{... | collective-permute-start | bytes 1769480 | tf_op jit(solution)/shard_map/ppermute | solution.py:215
  218.0 39.6 %collective-permute-start.18 = (bf16[2,2,144,512]{3,2,1,0:T(8,128)(2,1)}, bf16[2,2,144,512]{3,2,1,0:T(8,128)(2,1)}, u32[]{:S(2)}, u32[]{:S(2)}) collective-permute-start(bf16[2,2,144,512]{3,2,1,0:T(8,128)(2,1)} %get-tuple-element.66), channel_id=1, source_target_pairs={{0,8},{4,12},{8,0},{12,4},{1,9},{5,13},{9,1},{13,5},{2,10},{6,14},... | collective-permute-start | bytes 1769480 | tf_op jit(solution)/shard_map/ppermute | solution.py:215
  220.5 37.0 %collective-permute-start.19 = (bf16[2,2,144,512]{3,2,1,0:T(8,128)(2,1)}, bf16[2,2,144,512]{3,2,1,0:T(8,128)(2,1)}, u32[]{:S(2)}, u32[]{:S(2)}) collective-permute-start(bf16[2,2,144,512]{3,2,1,0:T(8,128)(2,1)} %get-tuple-element.67), channel_id=1, source_target_pairs={{0,12},{4,0},{8,4},{12,8},{1,13},{5,1},{9,5},{13,9},{2,14},{6,2},{... | collective-permute-start | bytes 1769480 | tf_op jit(solution)/shard_map/ppermute | solution.py:215
  229.8 41.6 %collective-permute-start.14 = (bf16[2,2,144,512]{3,2,1,0:T(8,128)(2,1)}, bf16[2,2,144,512]{3,2,1,0:T(8,128)(2,1)S(1)}, u32[]{:S(2)}, u32[]{:S(2)}) collective-permute-start(bf16[2,2,144,512]{3,2,1,0:T(8,128)(2,1)} %get-tuple-element.61), channel_id=1, source_target_pairs={{0,4},{4,8},{8,12},{12,0},{1,5},{5,9},{9,13},{13,1},{2,6},{6,10},{... | collective-permute-start | bytes 1769480 | tf_op jit(solution)/shard_map/ppermute | solution.py:215
  232.3 39.2 %collective-permute-start.15 = (bf16[2,2,144,512]{3,2,1,0:T(8,128)(2,1)}, bf16[2,2,144,512]{3,2,1,0:T(8,128)(2,1)}, u32[]{:S(2)}, u32[]{:S(2)}) collective-permute-start(bf16[2,2,144,512]{3,2,1,0:T(8,128)(2,1)} %get-tuple-element.62), channel_id=1, source_target_pairs={{0,8},{4,12},{8,0},{12,4},{1,9},{5,13},{9,1},{13,5},{2,10},{6,14},... | collective-permute-start | bytes 1769480 | tf_op jit(solution)/shard_map/ppermute | solution.py:215
  246.0 27.9 %collective-permute-start.16 = (bf16[2,2,144,512]{3,2,1,0:T(8,128)(2,1)}, bf16[2,2,144,512]{3,2,1,0:T(8,128)(2,1)}, u32[]{:S(2)}, u32[]{:S(2)}) collective-permute-start(bf16[2,2,144,512]{3,2,1,0:T(8,128)(2,1)} %get-tuple-element.63), channel_id=1, source_target_pairs={{0,12},{4,0},{8,4},{12,8},{1,13},{5,1},{9,5},{13,9},{2,14},{6,2},{... | collective-permute-start | bytes 1769480 | tf_op jit(solution)/shard_map/ppermute | solution.py:215
  250.6 7.0 %copy-start.2 = (bf16[4,576,384]{2,1,0:T(8,128)(2,1)S(1)}, bf16[4,576,384]{2,1,0:T(8,128)(2,1)}, u32[]{:S(2)}) copy-start(bf16[4,576,384]{2,1,0:T(8,128)(2,1)} %copy-done.1) | copy-start | bytes 5308420
  253.3 30.8 %all-to-all-start.2 = ((bf16[4,128,1024]{2,1,0:T(8,128)(2,1)}), bf16[4,128,1024]{2,1,0:T(8,128)(2,1)}, u32[]{:S(2)}, u32[]{:S(2)}) async-start(bf16[4,128,1024]{2,1,0:T(8,128)(2,1)} %copy.62), calls=%async_computation.2 | async-start | bytes 2097152 | tf_op jit(solution)/shard_map/all_to_all | solution.py:293
  259.7 14.3 %copy-start.6 = (bf16[2,2,144,512]{3,2,1,0:T(8,128)(2,1)S(1)}, bf16[2,2,144,512]{3,2,1,0:T(8,128)(2,1)}, u32[]{:S(2)}) copy-start(bf16[2,2,144,512]{3,2,1,0:T(8,128)(2,1)} %copy-done.5) | copy-start | bytes 1769476
  280.4 5.1 %collective-permute-start.20 = (bf16[512,384]{1,0:T(8,128)(2,1)S(1)}, bf16[512,384]{1,0:T(8,128)(2,1)}, u32[]{:S(2)}, u32[]{:S(2)}) collective-permute-start(bf16[512,384]{1,0:T(8,128)(2,1)S(1)} %select_bitcast_fusion), channel_id=1, source_target_pairs={{0,128},{128,0},{1,129},{129,1},{2,130},{130,2},{3,131},{131,3},{4... | collective-permute-start | bytes 1179656 | tf_op jit(solution)/shard_map/ppermute | solution.py:290
  287.6 3.2 %collective-permute-start.12 = (bf16[128,512]{1,0:T(8,128)(2,1)S(1)}, bf16[128,512]{1,0:T(8,128)(2,1)S(1)}, u32[]{:S(2)}, u32[]{:S(2)}) collective-permute-start(bf16[128,512]{1,0:T(8,128)(2,1)S(1)} %slice.58), channel_id=1, source_target_pairs={{0,128},{128,0},{1,129},{129,1},{2,130},{130,2},{3,131},{131,3},{4... | collective-permute-start | bytes 393224 | tf_op jit(solution)/shard_map/ppermute | solution.py:297
  (16 other events, 32.2 us)
Sparse Core Ops, SparseCore 0:
  19.9 105.8 all-gather.1
  210.0 67.1 reduce-scatter.1

commit v5 on v4

--- a/solution.py
+++ b/solution.py
@@ -33,9 +33,8 @@
     )
 
 
-def pick_rows(half, line, table, far):
-    batches, tok, width = line.shape[1:]
-    width //= 2
+def pick_rows(half, line, table, far, width):
+    batches, tok = line.shape[1:3]
     rows = table.shape[1]
     part = rows // 4
 
@@ -63,40 +62,43 @@
 
 
 def rows_back(near, other, weight, here):
-    _, quarters, rows, ff = near.shape
+    _, quarters, batches, _, part, ff = near.shape
     width = weight.shape[1]
-    part = rows // 2
+    shape = (2, batches, part, width)
 
     def body(y_ref, near_ref, other_ref, weight_ref, *out_refs):
         for d, out_ref in enumerate(out_refs):
 
             @pl.when(pl.program_id(0) == d)
             def _():
-                for k, ref in enumerate((near_ref, other_ref)):
-                    total = dot(ref[0, 0], weight_ref[0], (1, 1))
-                    total += dot(ref[0, 1], weight_ref[1], (1, 1))
-                    out_ref[k] = total.astype(BF16)
+                total = 0.0
+                for q in range(quarters):
+                    rows = jnp.concatenate(
+                        [ref[0, q, m, 0] for ref in (near_ref, other_ref) for m in range(batches)]
+                    )
+                    total += dot(rows, weight_ref[q], (1, 1))
+                out_ref[...] = total.astype(BF16).reshape(shape)
 
     def place(d, y):
         source = (y[0] + d) & 3
-        return (source >> 1, 0, source & 1, 0)
-
-    piece = pl.BlockSpec((1, quarters, part, ff), place)
+        return (source >> 1, 0, 0, source & 1, 0, 0)
+
+    piece = pl.BlockSpec((1, quarters, batches, 1, part, ff), place)
     return call(
         body,
         (4,),
         [piece, piece, pl.BlockSpec(weight.shape, lambda d, y: (0, 0, 0))],
-        [pl.BlockSpec((2, part, width), lambda d, y: (0, 0, 0))] * 4,
-        [jax.ShapeDtypeStruct((2, part, width), BF16)] * 4,
+        [pl.BlockSpec(shape, lambda d, y: (0, 0, 0, 0))] * 4,
+        [jax.ShapeDtypeStruct(shape, BF16)] * 4,
         1,
-        16 * part * quarters * ff * width,
+        16 * batches * part * quarters * ff * width,
     )(here, near, other, weight)
 
 
-def combine(half, returned, table, far, tok, so_far):
+def combine(half, first, returned, table, far, shape, so_far):
     returned = [returned[d] for d in (0, 3, 2, 1)]
     _, batches, part, width = returned[0].shape
-    rows = 4 * part
+    rows, tok = 4 * part, shape[3]
 
     def body(zh_ref, *refs):
         out_ref, table_ref = refs[-1], refs[4]
@@ -114,19 +116,19 @@
         body,
         (2, batches),
         [pl.BlockSpec((1, 1, part, width), lambda k, m, zh: (k, m, 0, 0))] * 4
-        + [pl.BlockSpec((1, 2, rows), lambda k, m, zh: (half * 4 + k * 2 + m, 0, 0))]
+        + [pl.BlockSpec((1, 2, rows), lambda k, m, zh: (half * 4 + k * 2 + m + first, 0, 0))]
         + [pl.BlockSpec(memory_space=pl.ANY)] * len(extra),
-        pl.BlockSpec((1, 8, 1, tok, width), lambda k, m, zh: (zh[0] ^ half, 0, m, 0, k)),
-        jax.ShapeDtypeStruct((2, 8, batches, tok, 2 * width), BF16),
+        pl.BlockSpec((1, 8, 1, tok, width), lambda k, m, zh: (zh[0] ^ half, 0, m + first, 0, k)),
+        jax.ShapeDtypeStruct(shape, BF16),
         1,
-        16 * rows * 8 * tok * width,
+        8 * batches * rows * 8 * tok * width,
         aliases={6: 0} if extra else {},
     )(far, *returned, table, *extra)
 
 
-def weight_sum(inbound, near, other, here, so_far, scale, kind):
-    _, part, width = inbound[0].shape
-    quarters, ff = near.shape[1], near.shape[3]
+def weight_sum(first, inbound, near, other, here, so_far, scale, kind):
+    _, quarters, batches, _, part, ff = near.shape
+    width = inbound[0].shape[3]
 
     def body(y_ref, *refs):
         near_ref, other_ref = refs[4:6]
@@ -140,10 +142,12 @@
 
             @pl.when(pl.program_id(0) == d)
             def _():
+                source = refs[d][...].reshape(2 * batches * part, width)
                 for q in range(quarters):
-                    total[q] += dot(refs[d][0], near_ref[0, q], (0, 0)) + dot(
-                        refs[d][1], other_ref[0, q], (0, 0)
+                    rows = jnp.concatenate(
+                        [ref[0, q, m, 0] for ref in (near_ref, other_ref) for m in range(batches)]
                     )
+                    total[q] += dot(source, rows, (0, 0))
 
         @pl.when(pl.program_id(0) == 3)
         def _():
@@ -151,21 +155,21 @@
 
     def place(d, y):
         source = (y[0] - d) & 3
-        return (source >> 1, 0, source & 1, 0)
-
-    piece = pl.BlockSpec((1, quarters, part, ff), place)
+        return (source >> 1, 0, 0, source & 1, 0, 0)
+
+    piece = pl.BlockSpec((1, quarters, batches, 1, part, ff), place)
     whole = pl.BlockSpec((quarters, width, ff), lambda d, y: (0, 0, 0))
     extra = () if so_far is None else (so_far,)
     return call(
         body,
         (4,),
-        [pl.BlockSpec((2, part, width), lambda d, y: (0, 0, 0))] * 4
+        [pl.BlockSpec((2, batches, part, width), lambda d, y: (0, first, 0, 0))] * 4
         + [piece, piece]
         + [whole] * len(extra),
         whole,
         jax.ShapeDtypeStruct((quarters, width, ff), kind),
         1,
-        16 * part * width * quarters * ff,
+        16 * batches * part * width * quarters * ff,
         scratch=(pltpu.VMEM((quarters, width, ff), F32),),
     )(here, *inbound, near, other, *extra)
 
@@ -205,39 +209,50 @@
     y = lax.axis_index("y")
     here = y.astype(I32).reshape(1)
 
+    part = nzl * capacity
+
     def gather(v):
-        return lax.all_to_all(
+        v = lax.all_to_all(
             jnp.broadcast_to(v, (nx,) + v.shape), "x", split_axis=0, concat_axis=0, tiled=True
-        ).reshape((2, 2) + v.shape)
-
-    def along_y(parts, shape):
-        moved = [
+        )
+        return v.reshape(2, 2, -1, 2, part, ff)
+
+    def along_y(parts):
+        return [
             v if d == 0 else lax.ppermute(v, "y", [(i, (i + d) % ny) for i in range(ny)])
             for d, v in enumerate(parts)
         ]
-        return [v.reshape(shape) for v in moved]
+
+    r = jnp.arange(rows, dtype=I32)
+    source_row = (
+        ((r // (part * ny)) * nzl + (r // capacity) % nzl) * ny + (r // part) % ny
+    ) * capacity + r % capacity
+    order = (source_row[:, None] == r[None, :]).astype(BF16)
+    hidden = dot(order, up_gradient.reshape(rows, ff), (1, 0)).astype(BF16)
+    halves = hidden.reshape(batches, 2, 2 * part, ff)
+    xh = x // 2
+    keep, send = by(xh, halves[:, 0], halves[:, 1])
+    taken = lax.ppermute(send, "x", [(i, (i + 2) % nx) for i in range(nx)])
+    stay, leave = by(xh ^ zh, keep, taken)
+    near = gather(stay)
+
+    expert_ids, slot_index, gate_weights, send = lax.optimization_barrier(
+        (expert_ids, slot_index, gate_weights, send)
+    )
+    held, gate = slot_tables(expert_ids, slot_index, gate_weights, capacity, nzl * ny * capacity)
+    high = lax.reduce_precision(gate, 8, 7)
+    middle = lax.reduce_precision(gate - high, 8, 7)
+    table = jnp.stack([held, high, middle, gate - high - middle])
+    table = table.reshape(4, batches, nzl, 2, 2 * capacity).transpose(2, 0, 1, 3, 4)
+    table = table.reshape(batches * tok, 2 * capacity).astype(BF16)
+    table = jnp.pad(table, ((0, 0), (0, 64 - 2 * capacity)))
 
     own_part = lax.dynamic_slice_in_dim(tokens, x * quarter, quarter, 2)
     own_part = own_part.reshape(batches * tok, 2, eighth)
     mine, theirs = by(co, own_part[:, 0], own_part[:, 1])
-    line = jnp.concatenate([mine, lax.ppermute(theirs, "co", SWAP)], axis=1)
+    theirs = lax.ppermute(jnp.concatenate([theirs, table], axis=1), "co", SWAP)
+    line = jnp.concatenate([mine, theirs[:, :eighth], table, theirs[:, eighth:]], axis=1)
     line = lax.all_gather(line, ("zh", "zl"), axis=0, tiled=True)
-    line = line.reshape(2 * nzl, batches, tok, quarter)
-
-    r = jnp.arange(rows, dtype=I32)
-    r_batch = (r // (capacity * nzl)) % batches
-    source_row = (
-        (r_batch * nzl + (r // capacity) % nzl) * ny + r // (capacity * nzl * batches)
-    ) * capacity + r % capacity
-    order = (source_row[:, None] == r[None, :]).astype(BF16)
-    hidden = dot(order, up_gradient.reshape(rows, ff), (1, 0)).astype(BF16)
-    halves = hidden.reshape(2, rows // 2, ff)
-    xh = x // 2
-    keep, send = by(xh, halves[0], halves[1])
-    taken = lax.ppermute(send, "x", [(i, (i + 2) % nx) for i in range(nx)])
-    stay, leave = by(xh ^ zh, keep, taken)
-    crossed = lax.ppermute(leave, "zh", SWAP)
-    near = gather(stay)
 
     cut = up_weight.reshape(2, eighth, ff)
     mine, theirs = by(co, cut[0], cut[1])
@@ -245,35 +260,38 @@
 
     near_other = lax.ppermute(near, "co", SWAP)
     back = rows_back(near, near_other, weight, here)
-    crossed, expert_ids, slot_index, gate_weights = lax.optimization_barrier(
-        (crossed, expert_ids, slot_index, gate_weights)
-    )
-    wide = gather(crossed)
-    wide, back = lax.optimization_barrier((wide, back))
-
-    held, gate = slot_tables(expert_ids, slot_index, gate_weights, capacity, nzl * ny * capacity)
-    table = jnp.stack([held, gate]).reshape(2, batches, nzl, ny * capacity)
-    table = table.transpose(2, 0, 1, 3)
-    table = jnp.stack([table, lax.ppermute(table, "co", SWAP)], axis=1)
-    table, wide = lax.optimization_barrier((table, wide))
-    table = lax.all_to_all(
-        jnp.concatenate([table, table]), ("zh", "zl"), split_axis=0, concat_axis=0, tiled=True
-    ).reshape(2, nzl, 2, 2, batches, ny, capacity)
-    table = jnp.where(zh == 0, table, table[::-1])
-    table = lax.dynamic_slice_in_dim(jnp.concatenate([table, table], axis=5), y, ny, 5)
-    table = table.transpose(3, 0, 2, 4, 5, 1, 6)
+    wide, wide_other, wide_back = [], [], []
+    for m in range(batches):
+        crossed = lax.ppermute(leave[m], "zh", SWAP)
+        if m + 1 < batches:
+            crossed, leave = lax.optimization_barrier((crossed, leave))
+        wide.append(gather(crossed))
+        if m == 0:
+            wide[0], back = lax.optimization_barrier((wide[0], back))
+        wide_other.append(lax.ppermute(wide[m], "co", SWAP))
+        wide_back.append(rows_back(wide[m], wide_other[m], weight, here))
+
+    column = lax.dynamic_slice(
+        line.reshape(2 * nzl, batches * tok, -1),
+        (0, lax.axis_index("zl") * 16, quarter),
+        (2 * nzl, 16, 128),
+    ).reshape(2, nzl, 4, batches, 2, 2, 64)[..., : 2 * capacity]
+    column = jnp.where(zh == 0, column, column[::-1]).astype(F32)
+    column = column.reshape(2, nzl, 4, batches, 2, 2, 2, capacity)
+    column = column.transpose(2, 0, 5, 3, 4, 6, 1, 7).reshape(
+        4, 4 * batches, ny, nzl, capacity
+    )
+    column = lax.dynamic_slice_in_dim(jnp.concatenate([column, column], axis=2), y, ny, 2)
     start = jnp.arange(nzl, dtype=F32)[:, None] * tok
-    seats = jnp.where(table[0] >= 0, table[0] + start, -1.0)
-    table = jnp.stack([seats, table[1]]).reshape(2, 4 * batches, buffer_rows)
-    lying, standing = table.transpose(1, 0, 2), table.transpose(1, 2, 0)
-
-    split = (2, batches, nzl * capacity, eighth)
-    spread = combine(0, along_y(back, split), lying, far, tok, None)
-    wide_other = lax.ppermute(wide, "co", SWAP)
-    back = rows_back(wide, wide_other, weight, here)
-    attention_partial, back = lax.optimization_barrier((attention_partial, back))
-    spread = combine(1, along_y(back, split), lying, far, tok, spread)
-    line, _ = lax.optimization_barrier((line, spread))
+    seats = jnp.where(column[0] >= 0, column[0] + start, -1.0)
+    column = jnp.stack([seats, column[1] + (column[2] + column[3])])
+    column = column.reshape(2, 4 * batches, buffer_rows)
+    lying, standing = column.transpose(1, 0, 2), column.transpose(1, 2, 0)
+
+    shape = (2, nzl, batches, tok, quarter)
+    spread = combine(0, 0, along_y(back), lying, far, shape, None)
+    for m in range(batches):
+        spread = combine(1, m, along_y(wide_back[m]), lying, far, shape, spread)
     expert_part = lax.psum_scatter(
         spread.reshape(2 * nzl * batches * tok, quarter),
         ("zh", "zl"),
@@ -281,11 +299,26 @@
         tiled=True,
     )
 
-    split = (2, batches * nzl * capacity, eighth)
-    inbound = along_y(pick_rows(0, line, standing, far), split)
-    inbound_far = along_y(pick_rows(1, line, standing, far), split)
-    total = weight_sum(inbound, near, near_other, here, None, 1.0, F32)
-    total = weight_sum(inbound_far, wide, wide_other, here, total, 1.0 / (2 * SIZES[1]), BF16)
+    line = line.reshape(2 * nzl, batches, tok, -1)
+    line, attention_partial, last = lax.optimization_barrier(
+        (line, attention_partial, wide_back[-1])
+    )
+    inbound = along_y(pick_rows(0, line, standing, far, eighth))
+    line, _ = lax.optimization_barrier((line, spread))
+    inbound_far = along_y(pick_rows(1, line, standing, far, eighth))
+    total = weight_sum(0, inbound, near, near_other, here, None, 1.0, F32)
+    for m in range(batches):
+        last = m + 1 == batches
+        total = weight_sum(
+            m,
+            inbound_far,
+            wide[m],
+            wide_other[m],
+            here,
+            total,
+            1.0 / (2 * SIZES[1]) if last else 1.0,
+            BF16 if last else F32,
+        )
     mine, theirs = by(co, total[0], total[1])
     weight_gradient = jnp.concatenate(by(co, mine, lax.ppermute(theirs, "co", SWAP)))
 

time: 301 us -> 320 us (1.063)
  starting transfers between devices: 107 us -> 120 us
  waiting for transfers between devices: 88.6 us -> 81.1 us
  local copies, waits for them, and re-layouts: 29.4 us -> 35.4 us
  Pallas kernels: 44.7 us -> 49.5 us
    all_to_all x1 -> x0, starting transfers between devices: 13.3 us -> none  [on_device(): lax.all_to_all(jnp.concatenate([table, table]), ('zh', 'zl'), split_axis=...]
    ppermute x12 -> x15, starting transfers between devices: 35 us -> 46.2 us  [along_y(): lax.ppermute(v, 'y', [(i, (i + d) % ny) for i in range(ny)])]
    ppermute x12 -> x15, waiting for transfers between devices: 35.4 us -> 24.4 us  [along_y(): lax.ppermute(v, 'y', [(i, (i + d) % ny) for i in range(ny)])]
    ppermute x4 -> x5, starting transfers between devices: 31.2 us -> 40.9 us  [the longest x2 24.6 us: on_device(): crossed = lax.ppermute(leave[m], 'zh', SWAP)]
    all_to_all x2 -> x3, waiting for transfers between devices: 6.71 us -> 15.7 us  [gather(): lax.all_to_all(jnp.broadcast_to(v, (nx,) + v.shape), 'x', split_axis=0, c...]
    all_to_all x2 -> x3, starting transfers between devices: 8.11 us -> 12 us  [gather(): lax.all_to_all(jnp.broadcast_to(v, (nx,) + v.shape), 'x', split_axis=0, c...]
    unnamed x46 -> x55, local copies, waits for them, and re-layouts: 13.3 us -> 17.1 us
    ppermute x4 -> x5, waiting for transfers between devices: 31.2 us -> 27.9 us  [the longest x2 26.9 us: on_device(): crossed = lax.ppermute(leave[m], 'zh', SWAP)]
  transfers between devices with their start and end apart: 27 -> 31, of which waited for: 13 -> 11; matrix products, arithmetic and copies ran while one was open for 9% -> 8% of each run, Pallas kernels for 15% -> 15%
where the time goes in v5:
time: 320 us; the launch traced here: 316 us
  starting transfers between devices  120 us (38%)
  waiting for transfers between devices  81.1 us (25%)
  Pallas kernels  49.5 us (15%)
  local copies, waits for them, and re-layouts  35.4 us (11%)
  between operations  15 us (5%)
  other arithmetic  12.1 us (4%)
    ppermute x15, starting transfers between devices, along_y(): lax.ppermute(v, 'y', [(i, (i + d) % ny) for i in range(ny)])  46.2 us
    ppermute x2, waiting for transfers between devices, on_device(): crossed = lax.ppermute(leave[m], 'zh', SWAP)  26.9 us
    ppermute x2, starting transfers between devices, on_device(): crossed = lax.ppermute(leave[m], 'zh', SWAP)  24.6 us
    ppermute x15, waiting for transfers between devices, along_y(): lax.ppermute(v, 'y', [(i, (i + d) % ny) for i in range(ny)])  24.4 us
    unnamed x55, local copies, waits for them, and re-layouts  17.1 us
    all_to_all x3, waiting for transfers between devices, gather(): lax.all_to_all(jnp.broadcast_to(v, (nx,) + v.shape), 'x', split_axis=0, c...  15.7 us
    pallas_call x3, Pallas kernels, weight_sum(): call(body, (4,), [pl.BlockSpec((2, batches, part, width), lambda d, y: (0...  15.7 us
    pallas_call x3, Pallas kernels, rows_back(): call(body, (4,), [piece, piece, pl.BlockSpec(weight.shape, lambda d, y: (...  14.3 us
  transfers between devices with their start and end apart: 31, of which 11 were waited for; matrix products, arithmetic and copies ran while one was open for 8% of the time, Pallas kernels for 15%

profile of v5, /device:TPU:1, one launch (start us, length us, event | category | flops | bytes accessed | tf_op | source)
XLA Modules:
  0.0 315.7 jit_solution(11809476122512382078)
XLA Ops:
  12.4 8.8 %collective-permute-start = (bf16[128,576]{1,0:T(8,128)(2,1)S(1)}, bf16[128,576]{1,0:T(8,128)(2,1)S(1)}, u32[]{:S(2)}, u32[]{:S(2)}) collective-permute-start(bf16[128,576]{1,0:T(8,128)(2,1)S(1)} %pad_maximum_fusion.1), channel_id=1, source_target_pairs={{0,128},{128,0},{1,129},{129,1},{2,130},{130,2},{3,131},{131,3},{4... | collective-permute-start | bytes 442376 | tf_op jit(solution)/shard_map/ppermute | solution.py:253
  25.1 13.0 %collective-permute-done.1 = bf16[2,288,384]{2,1,0:T(8,128)(2,1)} collective-permute-done((bf16[2,288,384]{2,1,0:T(8,128)(2,1)S(1)}, bf16[2,288,384]{2,1,0:T(8,128)(2,1)}, u32[]{:S(2)}, u32[]{:S(2)}) %collective-permute-start.1) | collective-permute-done | bytes 442400 | tf_op jit(solution)/shard_map/ppermute | solution.py:235
  44.2 10.4 %collective-permute-start.2 = (bf16[288,384]{1,0:T(8,128)(2,1)S(1)}, bf16[288,384]{1,0:T(8,128)(2,1)}, u32[]{:S(2)}, u32[]{:S(2)}) collective-permute-start(bf16[288,384]{1,0:T(8,128)(2,1)S(1)} %slice_bitcast_fusion), channel_id=1, source_target_pairs={{0,256},{256,0},{1,257},{257,1},{2,258},{258,2},{3,259},{259,3},{4... | collective-permute-start | bytes 663560 | tf_op jit(solution)/shard_map/ppermute | solution.py:265
  54.6 11.3 %all-to-all-done.3 = bf16[4,2,288,384]{3,2,1,0:T(8,128)(2,1)S(1)} async-done(((bf16[4,2,288,384]{3,2,1,0:T(8,128)(2,1)}), bf16[4,2,288,384]{3,2,1,0:T(8,128)(2,1)S(1)}, u32[]{:S(2)}, u32[]{:S(2)}) %all-to-all-start.3) | async-done | bytes 1769504 | tf_op jit(solution)/shard_map/all_to_all | solution.py:215
  65.9 3.9 %collective-permute-start.9 = (bf16[2,2,2,2,144,384]{5,4,3,2,1,0:T(8,128)(2,1)S(1)}, bf16[2,2,2,2,144,384]{5,4,3,2,1,0:T(8,128)(2,1)}, u32[]{:S(2)}, u32[]{:S(2)}) collective-permute-start(bf16[2,2,2,2,144,384]{5,4,3,2,1,0:T(8,128)(2,1)S(1)} %bitcast.92), channel_id=1, source_target_pairs={{0,128},{128,0},{1,129},{129,1},{2,130},{130,2},{3,131},{131,3},{4... | collective-permute-start | bytes 5308424 | tf_op jit(solution)/shard_map/ppermute | solution.py:261
  69.8 6.1 %collective-permute-done.2 = bf16[288,384]{1,0:T(8,128)(2,1)} collective-permute-done((bf16[288,384]{1,0:T(8,128)(2,1)S(1)}, bf16[288,384]{1,0:T(8,128)(2,1)}, u32[]{:S(2)}, u32[]{:S(2)}) %collective-permute-start.2) | collective-permute-done | bytes 221216 | tf_op jit(solution)/shard_map/ppermute | solution.py:265
  75.9 14.2 %collective-permute-start.3 = (bf16[288,384]{1,0:T(8,128)(2,1)S(1)}, bf16[288,384]{1,0:T(8,128)(2,1)S(1)}, u32[]{:S(2)}, u32[]{:S(2)}) collective-permute-start(bf16[288,384]{1,0:T(8,128)(2,1)S(1)} %slice_bitcast_fusion.1), channel_id=1, source_target_pairs={{0,256},{256,0},{1,257},{257,1},{2,258},{258,2},{3,259},{259,3},{4... | collective-permute-start | bytes 663560 | tf_op jit(solution)/shard_map/ppermute | solution.py:265
  90.1 20.9 %collective-permute-done.3 = bf16[288,384]{1,0:T(8,128)(2,1)S(1)} collective-permute-done((bf16[288,384]{1,0:T(8,128)(2,1)S(1)}, bf16[288,384]{1,0:T(8,128)(2,1)S(1)}, u32[]{:S(2)}, u32[]{:S(2)}) %collective-permute-start.3) | collective-permute-done | bytes 221216 | tf_op jit(solution)/shard_map/ppermute | solution.py:265
  112.0 4.2 %all-to-all-start = ((bf16[4,288,384]{2,1,0:T(8,128)(2,1)}), bf16[4,288,384]{2,1,0:T(8,128)(2,1)}, u32[]{:S(2)}, u32[]{:S(2)}) async-start(bf16[4,288,384]{2,1,0:T(8,128)(2,1)} %broadcast_in_dim.54), calls=%async_computation | async-start | bytes 1769472 | tf_op jit(solution)/shard_map/all_to_all | solution.py:215
  118.1 4.3 %collective-permute-start.5 = (bf16[512,384]{1,0:T(8,128)(2,1)}, bf16[512,384]{1,0:T(8,128)(2,1)S(1)}, u32[]{:S(2)}, u32[]{:S(2)}) collective-permute-start(bf16[512,384]{1,0:T(8,128)(2,1)} %select_bitcast_fusion.1), channel_id=1, source_target_pairs={{0,128},{128,0},{1,129},{129,1},{2,130},{130,2},{3,131},{131,3},{4... | collective-permute-start | bytes 1179656 | tf_op jit(solution)/shard_map/ppermute | solution.py:259
  122.5 4.4 %all-to-all-done = bf16[4,288,384]{2,1,0:T(8,128)(2,1)} async-done(((bf16[4,288,384]{2,1,0:T(8,128)(2,1)}), bf16[4,288,384]{2,1,0:T(8,128)(2,1)}, u32[]{:S(2)}, u32[]{:S(2)}) %all-to-all-start) | async-done | bytes 884768 | tf_op jit(solution)/shard_map/all_to_all | solution.py:215
  128.8 4.2 %all-to-all-start.2 = ((bf16[4,288,384]{2,1,0:T(8,128)(2,1)}), bf16[4,288,384]{2,1,0:T(8,128)(2,1)}, u32[]{:S(2)}, u32[]{:S(2)}) async-start(bf16[4,288,384]{2,1,0:T(8,128)(2,1)} %broadcast_in_dim.56), calls=%async_computation.2 | async-start | bytes 1769472 | tf_op jit(solution)/shard_map/all_to_all | solution.py:215
  134.4 5.6 %collective-permute-start.4 = (bf16[2,2,1,2,144,384]{5,4,3,2,1,0:T(8,128)(2,1)}, bf16[2,2,1,2,144,384]{5,4,3,2,1,0:T(8,128)(2,1)}, u32[]{:S(2)}, u32[]{:S(2)}) collective-permute-start(bf16[2,2,1,2,144,384]{5,4,3,2,1,0:T(8,128)(2,1)} %bitcast.13.near_ref.refs_4_), channel_id=1, source_target_pairs={{0,128},{128,0},{1,129},{129,1},{2,130},{130,2},{3,131},{131,3},{4... | collective-permute-start | bytes 2654216 | tf_op jit(solution)/shard_map/ppermute | solution.py:271
  140.0 5.9 %shard_map.96 = (bf16[2,2,144,512]{3,2,1,0:T(8,128)(2,1)S(1)}, bf16[2,2,144,512]{3,2,1,0:T(8,128)(2,1)}, bf16[2,2,144,512]{3,2,1,0:T(8,128)(2,1)}, bf16[2,2,144,512]{3,2,1,0:T(8,128)(2,1)}) custom-call(s32[1]{0:T(128)} %bitcast.7.y_ref, bf16[2,2,2,2,144,384]{5,4,3,2,1,0:T(8,128)(2,1)S(1)} %bitcast.93, ...), custom_call_target="tpu_custom_call" | custom-call | flops 1811939328 | bytes 8388608 | tf_op jit(solution)/shard_map/pallas_call | solution.py:87
  150.8 3.8 %shard_map.95 = (bf16[2,1,144,512]{3,2,1,0:T(8,128)(2,1)S(1)}, bf16[2,1,144,512]{3,2,1,0:T(8,128)(2,1)S(1)}, bf16[2,1,144,512]{3,2,1,0:T(8,128)(2,1)S(1)}, bf16[2,1,144,512]{3,2,1,0:T(8,128)(2,1)S(1)}) custom-call(s32[1]{0:T(128)} %bitcast.7.y_ref, bf16[2,2,1,2,144,384]{5,4,3,2,1,0:T(8,128)(2,1)} %bitcast.13.near_ref.refs_4_, ...), custom_call_target="tpu_custom_call" | custom-call | flops 905969664 | bytes 8388608 | tf_op jit(solution)/shard_map/pallas_call | solution.py:87
  156.0 4.5 %collective-permute-start.14 = (bf16[2,2,144,512]{3,2,1,0:T(8,128)(2,1)}, bf16[2,2,144,512]{3,2,1,0:T(8,128)(2,1)}, u32[]{:S(2)}, u32[]{:S(2)}) collective-permute-start(bf16[2,2,144,512]{3,2,1,0:T(8,128)(2,1)} %get-tuple-element.55), channel_id=1, source_target_pairs={{0,12},{4,0},{8,4},{12,8},{1,13},{5,1},{9,5},{13,9},{2,14},{6,2},{... | collective-permute-start | bytes 1769480 | tf_op jit(solution)/shard_map/ppermute | solution.py:222
  166.2 4.6 %shard_map.97 = (bf16[2,1,144,512]{3,2,1,0:T(8,128)(2,1)S(1)}, bf16[2,1,144,512]{3,2,1,0:T(8,128)(2,1)S(1)}, bf16[2,1,144,512]{3,2,1,0:T(8,128)(2,1)}, bf16[2,1,144,512]{3,2,1,0:T(8,128)(2,1)}) custom-call(s32[1]{0:T(128)} %bitcast.7.y_ref, bf16[2,2,1,2,144,384]{5,4,3,2,1,0:T(8,128)(2,1)} %bitcast.25.near_ref.refs_4_, ...), custom_call_target="tpu_custom_call" | custom-call | flops 905969664 | bytes 8388608 | tf_op jit(solution)/shard_map/pallas_call | solution.py:87
  171.5 3.7 %collective-permute-start.11 = (bf16[2,1,144,512]{3,2,1,0:T(8,128)(2,1)}, bf16[2,1,144,512]{3,2,1,0:T(8,128)(2,1)S(1)}, u32[]{:S(2)}, u32[]{:S(2)}) collective-permute-start(bf16[2,1,144,512]{3,2,1,0:T(8,128)(2,1)} %get-tuple-element.51), channel_id=1, source_target_pairs={{0,12},{4,0},{8,4},{12,8},{1,13},{5,1},{9,5},{13,9},{2,14},{6,2},{... | collective-permute-start | bytes 884744 | tf_op jit(solution)/shard_map/ppermute | solution.py:222
  186.5 5.9 %collective-permute-start.6 = (bf16[2,1,144,512]{3,2,1,0:T(8,128)(2,1)}, bf16[2,1,144,512]{3,2,1,0:T(8,128)(2,1)S(1)}, u32[]{:S(2)}, u32[]{:S(2)}) collective-permute-start(bf16[2,1,144,512]{3,2,1,0:T(8,128)(2,1)} %copy-done.18), channel_id=1, source_target_pairs={{0,12},{4,0},{8,4},{12,8},{1,13},{5,1},{9,5},{13,9},{2,14},{6,2},{... | collective-permute-start | bytes 884744 | tf_op jit(solution)/shard_map/ppermute | solution.py:222
  199.6 6.2 %shard_map.98.refs_5_ = bf16[2,8,2,64,1024]{4,3,2,1,0:T(8,128)(2,1)} custom-call(s32[1]{0:T(128)} %bitcast.20.zh_ref, bf16[2,2,144,512]{3,2,1,0:T(8,128)(2,1)S(1)} %copy-done.21, bf16[2,2,144,512]{3,2,1,0:T(8,128)(2,1)} %collective-permute-done.14.refs_1_, bf16[2,2,144,512]{3,2,1,0:T(8,128)(2,1)} %collective-permute-done.15.refs_2_, ...), custom_call_target="tpu_custom_call" | custom-call | flops 2415919104 | bytes 8388608 | tf_op jit(solution)/shard_map/pallas_call | solution.py:115
  210.1 7.1 %collective-permute-done.8.refs_3_ = bf16[2,1,144,512]{3,2,1,0:T(8,128)(2,1)S(1)} collective-permute-done((bf16[2,1,144,512]{3,2,1,0:T(8,128)(2,1)S(1)}, bf16[2,1,144,512]{3,2,1,0:T(8,128)(2,1)S(1)}, u32[]{:S(2)}, u32[]{:S(2)}) %collective-permute-start.8) | collective-permute-done | bytes 294944 | tf_op jit(solution)/shard_map/ppermute | solution.py:222
  221.9 4.6 %shard_map.102 = (bf16[2,2,144,512]{3,2,1,0:T(8,128)(2,1)S(1)}, bf16[2,2,144,512]{3,2,1,0:T(8,128)(2,1)S(1)}, bf16[2,2,144,512]{3,2,1,0:T(8,128)(2,1)}, bf16[2,2,144,512]{3,2,1,0:T(8,128)(2,1)}) custom-call(s32[1]{0:T(128)} %bitcast.20.zh_ref, bf16[16,2,64,1152]{3,2,1,0:T(8,128)(2,1)} %bitcast.99, f32[8,576,2]{2,1,0:T(8,128)S(1)} %bitcast.90), custom_call_target="tpu_custom_call" | custom-call | flops 1207959552 | bytes 8388608 | tf_op jit(solution)/shard_map/pallas_call | solution.py:50
  232.2 4.0 %collective-permute-start.23 = (bf16[2,2,144,512]{3,2,1,0:T(8,128)(2,1)}, bf16[2,2,144,512]{3,2,1,0:T(8,128)(2,1)}, u32[]{:S(2)}, u32[]{:S(2)}) collective-permute-start(bf16[2,2,144,512]{3,2,1,0:T(8,128)(2,1)} %get-tuple-element.67), channel_id=1, source_target_pairs={{0,12},{4,0},{8,4},{12,8},{1,13},{5,1},{9,5},{13,9},{2,14},{6,2},{... | collective-permute-start | bytes 1769480 | tf_op jit(solution)/shard_map/ppermute | solution.py:222
  236.2 4.6 %shard_map.101 = (bf16[2,2,144,512]{3,2,1,0:T(8,128)(2,1)S(1)}, bf16[2,2,144,512]{3,2,1,0:T(8,128)(2,1)}, bf16[2,2,144,512]{3,2,1,0:T(8,128)(2,1)}, bf16[2,2,144,512]{3,2,1,0:T(8,128)(2,1)}) custom-call(s32[1]{0:T(128)} %bitcast.20.zh_ref, bf16[16,2,64,1152]{3,2,1,0:T(8,128)(2,1)} %bitcast.100, f32[8,576,2]{2,1,0:T(8,128)S(1)} %bitcast.91), custom_call_target="tpu_custom_call" | custom-call | flops 1207959552 | bytes 8388608 | tf_op jit(solution)/shard_map/pallas_call | solution.py:50
  243.7 3.7 %collective-permute-start.19 = (bf16[2,2,144,512]{3,2,1,0:T(8,128)(2,1)}, bf16[2,2,144,512]{3,2,1,0:T(8,128)(2,1)}, u32[]{:S(2)}, u32[]{:S(2)}) collective-permute-start(bf16[2,2,144,512]{3,2,1,0:T(8,128)(2,1)} %get-tuple-element.62), channel_id=1, source_target_pairs={{0,8},{4,12},{8,0},{12,4},{1,9},{5,13},{9,1},{13,5},{2,10},{6,14},... | collective-permute-start | bytes 1769480 | tf_op jit(solution)/shard_map/ppermute | solution.py:222
  247.4 8.9 %collective-permute-done.21.refs_1_ = bf16[2,2,144,512]{3,2,1,0:T(8,128)(2,1)S(1)} collective-permute-done((bf16[2,2,144,512]{3,2,1,0:T(8,128)(2,1)S(1)}, bf16[2,2,144,512]{3,2,1,0:T(8,128)(2,1)S(1)}, u32[]{:S(2)}, u32[]{:S(2)}) %collective-permute-start.21) | collective-permute-done | bytes 589856 | tf_op jit(solution)/shard_map/ppermute | solution.py:222
  264.3 4.4 %all-to-all-start.1 = ((bf16[4,128,1024]{2,1,0:T(8,128)(2,1)}), bf16[4,128,1024]{2,1,0:T(8,128)(2,1)}, u32[]{:S(2)}, u32[]{:S(2)}) async-start(bf16[4,128,1024]{2,1,0:T(8,128)(2,1)} %copy.124), calls=%async_computation.1 | async-start | bytes 2097152 | tf_op jit(solution)/shard_map/all_to_all | solution.py:326
  270.9 5.6 %shard_map.103.refs_6_ = f32[2,512,384]{2,1,0:T(8,128)S(1)} custom-call(s32[1]{0:T(128)} %bitcast.7.y_ref, bf16[2,2,144,512]{3,2,1,0:T(8,128)(2,1)S(1)} %copy-done.14, bf16[2,2,144,512]{3,2,1,0:T(8,128)(2,1)S(1)} %copy-done.16, bf16[2,2,144,512]{3,2,1,0:T(8,128)(2,1)} %collective-permute-done.22.refs_2_, ...), custom_call_target="tpu_custom_call" | custom-call | flops 1811939328 | bytes 8388608 | tf_op jit(solution)/shard_map/pallas_call | solution.py:163
  277.7 5.0 %collective-permute-done.18.refs_1_ = bf16[2,2,144,512]{3,2,1,0:T(8,128)(2,1)S(1)} collective-permute-done((bf16[2,2,144,512]{3,2,1,0:T(8,128)(2,1)}, bf16[2,2,144,512]{3,2,1,0:T(8,128)(2,1)S(1)}, u32[]{:S(2)}, u32[]{:S(2)}) %collective-permute-start.18) | collective-permute-done | bytes 589856 | tf_op jit(solution)/shard_map/ppermute | solution.py:222
  285.3 4.9 %shard_map.104.refs_6_ = f32[2,512,384]{2,1,0:T(8,128)S(1)} custom-call(s32[1]{0:T(128)} %bitcast.7.y_ref, bf16[2,2,144,512]{3,2,1,0:T(8,128)(2,1)S(1)} %copy-done.8, bf16[2,2,144,512]{3,2,1,0:T(8,128)(2,1)S(1)} %collective-permute-done.18.refs_1_, bf16[2,2,144,512]{3,2,1,0:T(8,128)(2,1)} %collective-permute-done.19.refs_2_, ...), custom_call_target="tpu_custom_call" | custom-call | flops 905969664 | bytes 8388608 | tf_op jit(solution)/shard_map/pallas_call | solution.py:163
  291.3 5.1 %shard_map.105 = bf16[2,512,384]{2,1,0:T(8,128)(2,1)S(1)} custom-call(s32[1]{0:T(128)} %bitcast.7.y_ref, bf16[2,2,144,512]{3,2,1,0:T(8,128)(2,1)S(1)} %copy-done.8, bf16[2,2,144,512]{3,2,1,0:T(8,128)(2,1)S(1)} %collective-permute-done.18.refs_1_, bf16[2,2,144,512]{3,2,1,0:T(8,128)(2,1)} %collective-permute-done.19.refs_2_, ...), custom_call_target="tpu_custom_call" | custom-call | flops 905969664 | bytes 8388608 | tf_op jit(solution)/shard_map/pallas_call | solution.py:163
  296.6 3.8 %collective-permute-start.24 = (bf16[512,384]{1,0:T(8,128)(2,1)S(1)}, bf16[512,384]{1,0:T(8,128)(2,1)}, u32[]{:S(2)}, u32[]{:S(2)}) collective-permute-start(bf16[512,384]{1,0:T(8,128)(2,1)S(1)} %select_bitcast_fusion), channel_id=1, source_target_pairs={{0,128},{128,0},{1,129},{129,1},{2,130},{130,2},{3,131},{131,3},{4... | collective-permute-start | bytes 1179656 | tf_op jit(solution)/shard_map/ppermute | solution.py:323
  (153 shorter events, 93.0 us)
Async XLA Ops:
  7.2 170.8 %all-gather.2.cloned.1.call-start = ((), (), s32[]{:S(2)}) async-start(), calls=%async_computation.5 | async-start | bytes 5013504 | tf_op jit(solution)/shard_map/all_gather | solution.py:255
  12.4 9.8 %collective-permute-start = (bf16[128,576]{1,0:T(8,128)(2,1)S(1)}, bf16[128,576]{1,0:T(8,128)(2,1)S(1)}, u32[]{:S(2)}, u32[]{:S(2)}) collective-permute-start(bf16[128,576]{1,0:T(8,128)(2,1)S(1)} %pad_maximum_fusion.1), channel_id=1, source_target_pairs={{0,128},{128,0},{1,129},{129,1},{2,130},{130,2},{3,131},{131,3},{4... | collective-permute-start | bytes 442376 | tf_op jit(solution)/shard_map/ppermute | solution.py:253
  23.1 14.9 %collective-permute-start.1 = (bf16[2,288,384]{2,1,0:T(8,128)(2,1)S(1)}, bf16[2,288,384]{2,1,0:T(8,128)(2,1)}, u32[]{:S(2)}, u32[]{:S(2)}) collective-permute-start(bf16[2,288,384]{2,1,0:T(8,128)(2,1)S(1)} %fusion.4), channel_id=1, source_target_pairs={{0,2},{1,3},{2,0},{3,1},{4,6},{5,7},{6,4},{7,5},{8,10},{9,11},{10,... | collective-permute-start | bytes 1327112 | tf_op jit(solution)/shard_map/ppermute | solution.py:235
  40.5 25.4 %all-to-all-start.3 = ((bf16[4,2,288,384]{3,2,1,0:T(8,128)(2,1)}), bf16[4,2,288,384]{3,2,1,0:T(8,128)(2,1)S(1)}, u32[]{:S(2)}, u32[]{:S(2)}) async-start(bf16[4,2,288,384]{3,2,1,0:T(8,128)(2,1)} %broadcast_in_dim.57), calls=%async_computation.3 | async-start | bytes 3538944 | tf_op jit(solution)/shard_map/all_to_all | solution.py:215
  44.2 31.7 %collective-permute-start.2 = (bf16[288,384]{1,0:T(8,128)(2,1)S(1)}, bf16[288,384]{1,0:T(8,128)(2,1)}, u32[]{:S(2)}, u32[]{:S(2)}) collective-permute-start(bf16[288,384]{1,0:T(8,128)(2,1)S(1)} %slice_bitcast_fusion), channel_id=1, source_target_pairs={{0,256},{256,0},{1,257},{257,1},{2,258},{258,2},{3,259},{259,3},{4... | collective-permute-start | bytes 663560 | tf_op jit(solution)/shard_map/ppermute | solution.py:265
  65.9 74.1 %copy-start.3 = (bf16[4,2,288,384]{3,2,1,0:T(8,128)(2,1)}, bf16[4,2,288,384]{3,2,1,0:T(8,128)(2,1)S(1)}, u32[]{:S(2)}) copy-start(bf16[4,2,288,384]{3,2,1,0:T(8,128)(2,1)S(1)} %all-to-all-done.3) | copy-start | bytes 5308420
  65.9 74.1 %collective-permute-start.9 = (bf16[2,2,2,2,144,384]{5,4,3,2,1,0:T(8,128)(2,1)S(1)}, bf16[2,2,2,2,144,384]{5,4,3,2,1,0:T(8,128)(2,1)}, u32[]{:S(2)}, u32[]{:S(2)}) collective-permute-start(bf16[2,2,2,2,144,384]{5,4,3,2,1,0:T(8,128)(2,1)S(1)} %bitcast.92), channel_id=1, source_target_pairs={{0,128},{128,0},{1,129},{129,1},{2,130},{130,2},{3,131},{131,3},{4... | collective-permute-start | bytes 5308424 | tf_op jit(solution)/shard_map/ppermute | solution.py:261
  75.9 35.1 %collective-permute-start.3 = (bf16[288,384]{1,0:T(8,128)(2,1)S(1)}, bf16[288,384]{1,0:T(8,128)(2,1)S(1)}, u32[]{:S(2)}, u32[]{:S(2)}) collective-permute-start(bf16[288,384]{1,0:T(8,128)(2,1)S(1)} %slice_bitcast_fusion.1), channel_id=1, source_target_pairs={{0,256},{256,0},{1,257},{257,1},{2,258},{258,2},{3,259},{259,3},{4... | collective-permute-start | bytes 663560 | tf_op jit(solution)/shard_map/ppermute | solution.py:265
  112.0 14.9 %all-to-all-start = ((bf16[4,288,384]{2,1,0:T(8,128)(2,1)}), bf16[4,288,384]{2,1,0:T(8,128)(2,1)}, u32[]{:S(2)}, u32[]{:S(2)}) async-start(bf16[4,288,384]{2,1,0:T(8,128)(2,1)} %broadcast_in_dim.54), calls=%async_computation | async-start | bytes 1769472 | tf_op jit(solution)/shard_map/all_to_all | solution.py:215
  118.1 15.0 %collective-permute-start.5 = (bf16[512,384]{1,0:T(8,128)(2,1)}, bf16[512,384]{1,0:T(8,128)(2,1)S(1)}, u32[]{:S(2)}, u32[]{:S(2)}) collective-permute-start(bf16[512,384]{1,0:T(8,128)(2,1)} %select_bitcast_fusion.1), channel_id=1, source_target_pairs={{0,128},{128,0},{1,129},{129,1},{2,130},{130,2},{3,131},{131,3},{4... | collective-permute-start | bytes 1179656 | tf_op jit(solution)/shard_map/ppermute | solution.py:259
  128.8 18.8 %all-to-all-start.2 = ((bf16[4,288,384]{2,1,0:T(8,128)(2,1)}), bf16[4,288,384]{2,1,0:T(8,128)(2,1)}, u32[]{:S(2)}, u32[]{:S(2)}) async-start(bf16[4,288,384]{2,1,0:T(8,128)(2,1)} %broadcast_in_dim.56), calls=%async_computation.2 | async-start | bytes 1769472 | tf_op jit(solution)/shard_map/all_to_all | solution.py:215
  133.1 169.9 %reduce-scatter.2.cloned.1.call-start = ((), (), s32[]{:S(2)}) async-start(), calls=%async_computation.6 | async-start | bytes 4456448 | tf_op jit(solution)/shard_map/reduce_scatter | solution.py:295
  134.4 15.2 %collective-permute-start.4 = (bf16[2,2,1,2,144,384]{5,4,3,2,1,0:T(8,128)(2,1)}, bf16[2,2,1,2,144,384]{5,4,3,2,1,0:T(8,128)(2,1)}, u32[]{:S(2)}, u32[]{:S(2)}) collective-permute-start(bf16[2,2,1,2,144,384]{5,4,3,2,1,0:T(8,128)(2,1)} %bitcast.13.near_ref.refs_4_), channel_id=1, source_target_pairs={{0,128},{128,0},{1,129},{129,1},{2,130},{130,2},{3,131},{131,3},{4... | collective-permute-start | bytes 2654216 | tf_op jit(solution)/shard_map/ppermute | solution.py:271
  147.7 18.5 %collective-permute-start.10 = (bf16[2,2,1,2,144,384]{5,4,3,2,1,0:T(8,128)(2,1)}, bf16[2,2,1,2,144,384]{5,4,3,2,1,0:T(8,128)(2,1)S(1)}, u32[]{:S(2)}, u32[]{:S(2)}) collective-permute-start(bf16[2,2,1,2,144,384]{5,4,3,2,1,0:T(8,128)(2,1)} %bitcast.25.near_ref.refs_4_), channel_id=1, source_target_pairs={{0,128},{128,0},{1,129},{129,1},{2,130},{130,2},{3,131},{131,3},{4... | collective-permute-start | bytes 2654216 | tf_op jit(solution)/shard_map/ppermute | solution.py:271
  156.0 28.6 %collective-permute-start.14 = (bf16[2,2,144,512]{3,2,1,0:T(8,128)(2,1)}, bf16[2,2,144,512]{3,2,1,0:T(8,128)(2,1)}, u32[]{:S(2)}, u32[]{:S(2)}) collective-permute-start(bf16[2,2,144,512]{3,2,1,0:T(8,128)(2,1)} %get-tuple-element.55), channel_id=1, source_target_pairs={{0,12},{4,0},{8,4},{12,8},{1,13},{5,1},{9,5},{13,9},{2,14},{6,2},{... | collective-permute-start | bytes 1769480 | tf_op jit(solution)/shard_map/ppermute | solution.py:222
  160.5 26.0 %collective-permute-start.15 = (bf16[2,2,144,512]{3,2,1,0:T(8,128)(2,1)}, bf16[2,2,144,512]{3,2,1,0:T(8,128)(2,1)}, u32[]{:S(2)}, u32[]{:S(2)}) collective-permute-start(bf16[2,2,144,512]{3,2,1,0:T(8,128)(2,1)} %get-tuple-element.56), channel_id=1, source_target_pairs={{0,8},{4,12},{8,0},{12,4},{1,9},{5,13},{9,1},{13,5},{2,10},{6,14},... | collective-permute-start | bytes 1769480 | tf_op jit(solution)/shard_map/ppermute | solution.py:222
  163.4 29.9 %collective-permute-start.16 = (bf16[2,2,144,512]{3,2,1,0:T(8,128)(2,1)}, bf16[2,2,144,512]{3,2,1,0:T(8,128)(2,1)}, u32[]{:S(2)}, u32[]{:S(2)}) collective-permute-start(bf16[2,2,144,512]{3,2,1,0:T(8,128)(2,1)} %get-tuple-element.57), channel_id=1, source_target_pairs={{0,4},{4,8},{8,12},{12,0},{1,5},{5,9},{9,13},{13,1},{2,6},{6,10},{... | collective-permute-start | bytes 1769480 | tf_op jit(solution)/shard_map/ppermute | solution.py:222
  171.5 24.3 %collective-permute-start.11 = (bf16[2,1,144,512]{3,2,1,0:T(8,128)(2,1)}, bf16[2,1,144,512]{3,2,1,0:T(8,128)(2,1)S(1)}, u32[]{:S(2)}, u32[]{:S(2)}) collective-permute-start(bf16[2,1,144,512]{3,2,1,0:T(8,128)(2,1)} %get-tuple-element.51), channel_id=1, source_target_pairs={{0,12},{4,0},{8,4},{12,8},{1,13},{5,1},{9,5},{13,9},{2,14},{6,2},{... | collective-permute-start | bytes 884744 | tf_op jit(solution)/shard_map/ppermute | solution.py:222
  175.2 30.6 %collective-permute-start.12 = (bf16[2,1,144,512]{3,2,1,0:T(8,128)(2,1)}, bf16[2,1,144,512]{3,2,1,0:T(8,128)(2,1)S(1)}, u32[]{:S(2)}, u32[]{:S(2)}) collective-permute-start(bf16[2,1,144,512]{3,2,1,0:T(8,128)(2,1)} %get-tuple-element.52), channel_id=1, source_target_pairs={{0,8},{4,12},{8,0},{12,4},{1,9},{5,13},{9,1},{13,5},{2,10},{6,14},... | collective-permute-start | bytes 884744 | tf_op jit(solution)/shard_map/ppermute | solution.py:222
  184.6 21.3 %collective-permute-start.13 = (bf16[2,1,144,512]{3,2,1,0:T(8,128)(2,1)}, bf16[2,1,144,512]{3,2,1,0:T(8,128)(2,1)S(1)}, u32[]{:S(2)}, u32[]{:S(2)}) collective-permute-start(bf16[2,1,144,512]{3,2,1,0:T(8,128)(2,1)} %copy-done.19), channel_id=1, source_target_pairs={{0,4},{4,8},{8,12},{12,0},{1,5},{5,9},{9,13},{13,1},{2,6},{6,10},{... | collective-permute-start | bytes 884744 | tf_op jit(solution)/shard_map/ppermute | solution.py:222
  186.5 23.5 %collective-permute-start.6 = (bf16[2,1,144,512]{3,2,1,0:T(8,128)(2,1)}, bf16[2,1,144,512]{3,2,1,0:T(8,128)(2,1)S(1)}, u32[]{:S(2)}, u32[]{:S(2)}) collective-permute-start(bf16[2,1,144,512]{3,2,1,0:T(8,128)(2,1)} %copy-done.18), channel_id=1, source_target_pairs={{0,12},{4,0},{8,4},{12,8},{1,13},{5,1},{9,5},{13,9},{2,14},{6,2},{... | collective-permute-start | bytes 884744 | tf_op jit(solution)/shard_map/ppermute | solution.py:222
  193.3 16.8 %collective-permute-start.7 = (bf16[2,1,144,512]{3,2,1,0:T(8,128)(2,1)}, bf16[2,1,144,512]{3,2,1,0:T(8,128)(2,1)S(1)}, u32[]{:S(2)}, u32[]{:S(2)}) collective-permute-start(bf16[2,1,144,512]{3,2,1,0:T(8,128)(2,1)} %copy-done.17), channel_id=1, source_target_pairs={{0,8},{4,12},{8,0},{12,4},{1,9},{5,13},{9,1},{13,5},{2,10},{6,14},... | collective-permute-start | bytes 884744 | tf_op jit(solution)/shard_map/ppermute | solution.py:222
  195.8 21.4 %collective-permute-start.8 = (bf16[2,1,144,512]{3,2,1,0:T(8,128)(2,1)S(1)}, bf16[2,1,144,512]{3,2,1,0:T(8,128)(2,1)S(1)}, u32[]{:S(2)}, u32[]{:S(2)}) collective-permute-start(bf16[2,1,144,512]{3,2,1,0:T(8,128)(2,1)S(1)} %get-tuple-element.40), channel_id=1, source_target_pairs={{0,4},{4,8},{8,12},{12,0},{1,5},{5,9},{9,13},{13,1},{2,6},{6,10},{... | collective-permute-start | bytes 884744 | tf_op jit(solution)/shard_map/ppermute | solution.py:222
  227.3 28.9 %collective-permute-start.21 = (bf16[2,2,144,512]{3,2,1,0:T(8,128)(2,1)S(1)}, bf16[2,2,144,512]{3,2,1,0:T(8,128)(2,1)S(1)}, u32[]{:S(2)}, u32[]{:S(2)}) collective-permute-start(bf16[2,2,144,512]{3,2,1,0:T(8,128)(2,1)S(1)} %get-tuple-element.65), channel_id=1, source_target_pairs={{0,4},{4,8},{8,12},{12,0},{1,5},{5,9},{9,13},{13,1},{2,6},{6,10},{... | collective-permute-start | bytes 1769480 | tf_op jit(solution)/shard_map/ppermute | solution.py:222
  229.2 39.5 %collective-permute-start.22 = (bf16[2,2,144,512]{3,2,1,0:T(8,128)(2,1)}, bf16[2,2,144,512]{3,2,1,0:T(8,128)(2,1)}, u32[]{:S(2)}, u32[]{:S(2)}) collective-permute-start(bf16[2,2,144,512]{3,2,1,0:T(8,128)(2,1)} %get-tuple-element.66), channel_id=1, source_target_pairs={{0,8},{4,12},{8,0},{12,4},{1,9},{5,13},{9,1},{13,5},{2,10},{6,14},... | collective-permute-start | bytes 1769480 | tf_op jit(solution)/shard_map/ppermute | solution.py:222
  232.2 36.5 %collective-permute-start.23 = (bf16[2,2,144,512]{3,2,1,0:T(8,128)(2,1)}, bf16[2,2,144,512]{3,2,1,0:T(8,128)(2,1)}, u32[]{:S(2)}, u32[]{:S(2)}) collective-permute-start(bf16[2,2,144,512]{3,2,1,0:T(8,128)(2,1)} %get-tuple-element.67), channel_id=1, source_target_pairs={{0,12},{4,0},{8,4},{12,8},{1,13},{5,1},{9,5},{13,9},{2,14},{6,2},{... | collective-permute-start | bytes 1769480 | tf_op jit(solution)/shard_map/ppermute | solution.py:222
  241.6 41.1 %collective-permute-start.18 = (bf16[2,2,144,512]{3,2,1,0:T(8,128)(2,1)}, bf16[2,2,144,512]{3,2,1,0:T(8,128)(2,1)S(1)}, u32[]{:S(2)}, u32[]{:S(2)}) collective-permute-start(bf16[2,2,144,512]{3,2,1,0:T(8,128)(2,1)} %get-tuple-element.61), channel_id=1, source_target_pairs={{0,4},{4,8},{8,12},{12,0},{1,5},{5,9},{9,13},{13,1},{2,6},{6,10},{... | collective-permute-start | bytes 1769480 | tf_op jit(solution)/shard_map/ppermute | solution.py:222
  243.7 39.1 %collective-permute-start.19 = (bf16[2,2,144,512]{3,2,1,0:T(8,128)(2,1)}, bf16[2,2,144,512]{3,2,1,0:T(8,128)(2,1)}, u32[]{:S(2)}, u32[]{:S(2)}) collective-permute-start(bf16[2,2,144,512]{3,2,1,0:T(8,128)(2,1)} %get-tuple-element.62), channel_id=1, source_target_pairs={{0,8},{4,12},{8,0},{12,4},{1,9},{5,13},{9,1},{13,5},{2,10},{6,14},... | collective-permute-start | bytes 1769480 | tf_op jit(solution)/shard_map/ppermute | solution.py:222
  257.1 28.2 %collective-permute-start.20 = (bf16[2,2,144,512]{3,2,1,0:T(8,128)(2,1)}, bf16[2,2,144,512]{3,2,1,0:T(8,128)(2,1)}, u32[]{:S(2)}, u32[]{:S(2)}) collective-permute-start(bf16[2,2,144,512]{3,2,1,0:T(8,128)(2,1)} %get-tuple-element.63), channel_id=1, source_target_pairs={{0,12},{4,0},{8,4},{12,8},{1,13},{5,1},{9,5},{13,9},{2,14},{6,2},{... | collective-permute-start | bytes 1769480 | tf_op jit(solution)/shard_map/ppermute | solution.py:222
  264.3 36.1 %all-to-all-start.1 = ((bf16[4,128,1024]{2,1,0:T(8,128)(2,1)}), bf16[4,128,1024]{2,1,0:T(8,128)(2,1)}, u32[]{:S(2)}, u32[]{:S(2)}) async-start(bf16[4,128,1024]{2,1,0:T(8,128)(2,1)} %copy.124), calls=%async_computation.1 | async-start | bytes 2097152 | tf_op jit(solution)/shard_map/all_to_all | solution.py:326
  296.6 5.3 %collective-permute-start.24 = (bf16[512,384]{1,0:T(8,128)(2,1)S(1)}, bf16[512,384]{1,0:T(8,128)(2,1)}, u32[]{:S(2)}, u32[]{:S(2)}) collective-permute-start(bf16[512,384]{1,0:T(8,128)(2,1)S(1)} %select_bitcast_fusion), channel_id=1, source_target_pairs={{0,128},{128,0},{1,129},{129,1},{2,130},{130,2},{3,131},{131,3},{4... | collective-permute-start | bytes 1179656 | tf_op jit(solution)/shard_map/ppermute | solution.py:323
  303.9 3.2 %collective-permute-start.17 = (bf16[128,512]{1,0:T(8,128)(2,1)S(1)}, bf16[128,512]{1,0:T(8,128)(2,1)S(1)}, u32[]{:S(2)}, u32[]{:S(2)}) collective-permute-start(bf16[128,512]{1,0:T(8,128)(2,1)S(1)} %slice.92), channel_id=1, source_target_pairs={{0,128},{128,0},{1,129},{129,1},{2,130},{130,2},{3,131},{131,3},{4... | collective-permute-start | bytes 393224 | tf_op jit(solution)/shard_map/ppermute | solution.py:330
  (25 other events, 94.4 us)
Sparse Core Ops, SparseCore 0:
  23.2 108.6 all-gather.1
  221.3 71.1 reduce-scatter.1

commit v6 on v2

--- a/solution.py
+++ b/solution.py
@@ -16,7 +16,7 @@
     return lax.dot_general(a, b, ((over[:1], over[1:]), ((), ())), preferred_element_type=F32)
 
 
-def call(body, grid, in_specs, out_spec, out_shape, prefetch, flops, scratch=()):
+def call(body, grid, in_specs, out_spec, out_shape, prefetch, flops, scratch=(), aliases={}):
     return pl.pallas_call(
         body,
         grid_spec=pltpu.PrefetchScalarGridSpec(
@@ -27,14 +27,14 @@
             scratch_shapes=scratch,
         ),
         out_shape=out_shape,
+        input_output_aliases=aliases,
         compiler_params=pltpu.CompilerParams(vmem_limit_bytes=VMEM),
         cost_estimate=pl.CostEstimate(flops=flops, bytes_accessed=1 << 23, transcendentals=0),
     )
 
 
-def pick_rows(half, line, table, far):
-    batches, tok, width = line.shape[1:]
-    width //= 2
+def pick_rows(half, line, table, far, width):
+    batches, tok = line.shape[1:3]
     rows = table.shape[1]
     part = rows // SIZES[3]
 
@@ -84,45 +84,36 @@
     )(near, other, weight)
 
 
-def combine(near, far_rows, table, far, tok):
-    _, _, batches, part, width = near.shape
+def combine(half, returned, table, far, tok, so_far):
+    _, _, batches, part, width = returned.shape
     rows = 4 * part
 
-    def body(zh_ref, near_ref, far_ref, table_ref, out_ref):
+    def body(zh_ref, back_ref, table_ref, *refs):
+        out_ref = refs[-1]
         seat = table_ref[0, 0:1, :].astype(I32)
         hit = seat == lax.broadcasted_iota(I32, (8 * tok, rows), 0)
         gate = jnp.where(hit, table_ref[0, 1:2, :], 0.0)
         high = gate.astype(BF16)
         low = (gate - high.astype(F32)).astype(BF16)
-
-        def put(ref):
-            source = ref[...].reshape(rows, width)
-            total = dot(high, source, (1, 0)) + dot(low, source, (1, 0))
-            out_ref[...] = total.astype(BF16).reshape(out_ref.shape)
-
-        pl.when(pl.program_id(0) == 0)(lambda: put(near_ref))
-        pl.when(pl.program_id(0) == 1)(lambda: put(far_ref))
-
-    block = (4, 1, 1, part, width)
+        source = back_ref[...].reshape(rows, width)
+        total = dot(high, source, (1, 0)) + dot(low, source, (1, 0))
+        out_ref[...] = total.astype(BF16).reshape(out_ref.shape)
+
+    extra = () if so_far is None else (so_far,)
     return call(
         body,
-        (2, 2, batches),
+        (2, batches),
         [
-            pl.BlockSpec(
-                block,
-                lambda j, k, m, zh: (0, jnp.where(j == 0, k, 1), jnp.where(j == 0, m, 1), 0, 0),
-            ),
-            pl.BlockSpec(
-                block,
-                lambda j, k, m, zh: (0, jnp.where(j == 0, 0, k), jnp.where(j == 0, 0, m), 0, 0),
-            ),
-            pl.BlockSpec((1, 2, rows), lambda j, k, m, zh: (j * 4 + k * 2 + m, 0, 0)),
-        ],
-        pl.BlockSpec((1, 8, 1, tok, width), lambda j, k, m, zh: (zh[0] ^ j, 0, m, 0, k)),
+            pl.BlockSpec((4, 1, 1, part, width), lambda k, m, zh: (0, k, m, 0, 0)),
+            pl.BlockSpec((1, 2, rows), lambda k, m, zh: (half * 4 + k * 2 + m, 0, 0)),
+        ]
+        + [pl.BlockSpec(memory_space=pl.ANY)] * len(extra),
+        pl.BlockSpec((1, 8, 1, tok, width), lambda k, m, zh: (zh[0] ^ half, 0, m, 0, k)),
         jax.ShapeDtypeStruct((2, 8, batches, tok, 2 * width), BF16),
         1,
-        32 * rows * 8 * tok * width,
-    )(far, near, far_rows, table)
+        16 * rows * 8 * tok * width,
+        aliases={3: 0} if extra else {},
+    )(far, returned, table, *extra)
 
 
 def weight_sum(inbound, near, other, so_far, scale, kind):
@@ -204,12 +195,9 @@
         v = v.reshape(ny, -1, shape[-1])
         return lax.all_to_all(v, "y", split_axis=0, concat_axis=0, tiled=True).reshape(shape)
 
-    own_part = lax.dynamic_slice_in_dim(tokens, x * quarter, quarter, 2)
-    own_part = own_part.reshape(batches * tok, 2, eighth)
-    mine, theirs = by(co, own_part[:, 0], own_part[:, 1])
-    line = jnp.concatenate([mine, lax.ppermute(theirs, "co", SWAP)], axis=1)
-    line = lax.all_gather(line, ("zh", "zl"), axis=0, tiled=True)
-    line = line.reshape(2 * nzl, batches, tok, quarter)
+    cut = up_weight.reshape(2, eighth, ff)
+    mine, theirs = by(co, cut[0], cut[1])
+    weight = jnp.stack(by(co, mine, lax.ppermute(theirs, "co", SWAP)))
 
     r = jnp.arange(rows, dtype=I32)
     r_batch = (r // (capacity * nzl)) % batches
@@ -223,38 +211,56 @@
     keep, send = by(xh, halves[0], halves[1])
     taken = lax.ppermute(send, "x", [(i, (i + 2) % nx) for i in range(nx)])
     stay, leave = by(xh ^ zh, keep, taken)
+    stay, weight = lax.optimization_barrier((stay, weight))
     crossed = lax.ppermute(leave, "zh", SWAP)
-
+    near = gather(stay)
+
+    expert_ids, slot_index, gate_weights, send = lax.optimization_barrier(
+        (expert_ids, slot_index, gate_weights, send)
+    )
     held, gate = slot_tables(expert_ids, slot_index, gate_weights, capacity, nzl * ny * capacity)
-    table = jnp.stack([held, gate]).reshape(2, batches, nzl, ny * capacity)
-    table = table.transpose(2, 0, 1, 3)
-    table = jnp.stack([table, lax.ppermute(table, "co", SWAP)], axis=1)
-    table = lax.all_to_all(
-        jnp.concatenate([table, table]), ("zh", "zl"), split_axis=0, concat_axis=0, tiled=True
-    ).reshape(2, nzl, 2, 2, batches, ny, capacity)
-    table = jnp.where(zh == 0, table, table[::-1])
-    table = table.transpose(3, 0, 2, 4, 5, 1, 6)
+    high = lax.reduce_precision(gate, 8, 7)
+    middle = lax.reduce_precision(gate - high, 8, 7)
+    table = jnp.stack([held, high, middle, gate - high - middle])
+    table = table.reshape(4, batches, nzl, 2, 2 * capacity).transpose(2, 0, 1, 3, 4)
+    table = table.reshape(batches * tok, 2 * capacity).astype(BF16)
+    table = jnp.pad(table, ((0, 0), (0, 64 - 2 * capacity)))
+
+    own_part = lax.dynamic_slice_in_dim(tokens, x * quarter, quarter, 2)
+    own_part = own_part.reshape(batches * tok, 2, eighth)
+    mine, theirs = by(co, own_part[:, 0], own_part[:, 1])
+    theirs = lax.ppermute(jnp.concatenate([theirs, table], axis=1), "co", SWAP)
+    line = jnp.concatenate([mine, theirs[:, :eighth], table, theirs[:, eighth:]], axis=1)
+    line, near = lax.optimization_barrier((line, near))
+    line = lax.all_gather(line, ("zh", "zl"), axis=0, tiled=True)
+
+    near_other = lax.ppermute(near, "co", SWAP)
+    back = rows_back(near, near_other, weight)
+    wide = gather(crossed)
+    wide, back = lax.optimization_barrier((wide, back))
+    back = along_y(back)
+    wide_other = lax.ppermute(wide, "co", SWAP)
+    wide_back = rows_back(wide, wide_other, weight)
+    wide_back, back = lax.optimization_barrier((wide_back, back))
+    wide_back = along_y(wide_back)
+
+    column = lax.dynamic_slice(
+        line.reshape(2 * nzl, batches * tok, -1),
+        (0, lax.axis_index("zl") * 16, quarter),
+        (2 * nzl, 16, 128),
+    ).reshape(2, nzl, 4, batches, 2, 2, 64)[..., : 2 * capacity]
+    column = jnp.where(zh == 0, column, column[::-1]).astype(F32)
+    column = column.reshape(2, nzl, 4, batches, 2, 2, 2, capacity)
+    column = column.transpose(2, 0, 5, 3, 4, 6, 1, 7)
     start = jnp.arange(nzl, dtype=F32)[:, None] * tok
-    seats = jnp.where(table[0] >= 0, table[0] + start, -1.0)
-    table = jnp.stack([seats, table[1]]).reshape(2, 4 * batches, buffer_rows)
-    lying, standing = table.transpose(1, 0, 2), table.transpose(1, 2, 0)
-
-    cut = up_weight.reshape(2, eighth, ff)
-    mine, theirs = by(co, cut[0], cut[1])
-    weight = jnp.stack(by(co, mine, lax.ppermute(theirs, "co", SWAP)))
-
-    near = gather(stay)
-    near_other = lax.ppermute(near, "co", SWAP)
-    back_near = along_y(rows_back(near, near_other, weight))
-    wide = gather(crossed)
-    wide_other = lax.ppermute(wide, "co", SWAP)
-    back_far = along_y(rows_back(wide, wide_other, weight))
-
-    inbound = along_y(pick_rows(0, line, standing, far))
-    inbound_far = along_y(pick_rows(1, line, standing, far))
+    seats = jnp.where(column[0] >= 0, column[0] + start, -1.0)
+    column = jnp.stack([seats, column[1] + (column[2] + column[3])])
+    column = column.reshape(2, 4 * batches, buffer_rows)
+    lying, standing = column.transpose(1, 0, 2), column.transpose(1, 2, 0)
 
     split = (4, 2, batches, nzl * capacity, eighth)
-    spread = combine(back_near.reshape(split), back_far.reshape(split), lying, far, tok)
+    spread = combine(0, back.reshape(split), lying, far, tok, None)
+    spread = combine(1, wide_back.reshape(split), lying, far, tok, spread)
     expert_part = lax.psum_scatter(
         spread.reshape(2 * nzl * batches * tok, quarter),
         ("zh", "zl"),
@@ -262,6 +268,13 @@
         tiled=True,
     )
 
+    line = line.reshape(2 * nzl, batches, tok, -1)
+    line, wide_back = lax.optimization_barrier((line, wide_back))
+    inbound = along_y(pick_rows(0, line, standing, far, eighth))
+    line, inbound, attention_partial = lax.optimization_barrier(
+        (line, inbound, attention_partial)
+    )
+    inbound_far = along_y(pick_rows(1, line, standing, far, eighth))
     split = (4, 2, batches * nzl * capacity, eighth)
     total = weight_sum(inbound.reshape(split), near, near_other, None, 1.0, F32)
     total = weight_sum(

time: 336 us -> 339 us (level)
  the two profiles are of different devices: /device:TPU:163 before, /device:TPU:1 now
where the time goes in v6:
time: 339 us; the launch traced here: 337 us
  waiting for transfers between devices  137 us (40%)
  starting transfers between devices  63.6 us (19%)
  Pallas kernels  41.1 us (12%)
  local copies, waits for them, and re-layouts  30.9 us (9%)
  blocking collectives  30.7 us (9%)
  other arithmetic  15.4 us (5%)
  between operations  14.6 us (4%)
    all_to_all x3, waiting for transfers between devices, along_y(): lax.all_to_all(v, 'y', split_axis=0, concat_axis=0, tiled=True)  55.4 us
    ppermute x1, waiting for transfers between devices, on_device(): crossed = lax.ppermute(leave, 'zh', SWAP)  44.3 us
    all_to_all x1, blocking collectives, along_y(): lax.all_to_all(v, 'y', split_axis=0, concat_axis=0, tiled=True)  30.7 us
    all_to_all x2, waiting for transfers between devices, gather(): lax.all_to_all(jnp.broadcast_to(v, (nx,) + v.shape), 'x', split_axis=0, c...  28.2 us
    pallas_call x2, Pallas kernels, weight_sum(): call(body, (count,), [pl.BlockSpec((1, 2, part, width), lambda y: (y, 0,...  12.8 us
    all_to_all x3, starting transfers between devices, along_y(): lax.all_to_all(v, 'y', split_axis=0, concat_axis=0, tiled=True)  12.1 us
    ppermute x1, starting transfers between devices, on_device(): crossed = lax.ppermute(leave, 'zh', SWAP)  10.5 us
    pallas_call x2, Pallas kernels, rows_back(): call(body, (pairs,), [piece, piece, pl.BlockSpec(weight.shape, lambda h:...  10.4 us
  transfers between devices with their start and end apart: 16, of which 9 were waited for; matrix products, arithmetic and copies ran while one was open for 10% of the time, Pallas kernels for 11%

profile of v6, /device:TPU:1, one launch (start us, length us, event | category | flops | bytes accessed | tf_op | source)
XLA Modules:
  0.0 336.6 jit_solution(26770203264744365)
XLA Ops:
  9.2 8.8 %collective-permute-start.2 = (bf16[512,384]{1,0:T(8,128)(2,1)}, bf16[512,384]{1,0:T(8,128)(2,1)S(1)}, u32[]{:S(2)}, u32[]{:S(2)}) collective-permute-start(bf16[512,384]{1,0:T(8,128)(2,1)} %select_bitcast_fusion.1), channel_id=1, source_target_pairs={{0,128},{128,0},{1,129},{129,1},{2,130},{130,2},{3,131},{131,3},{4... | collective-permute-start | bytes 1179656 | tf_op jit(solution)/shard_map/ppermute | solution.py:200
  18.1 2.9 fusion.1
  28.0 8.3 %collective-permute-done.1 = bf16[576,384]{1,0:T(8,128)(2,1)} collective-permute-done((bf16[576,384]{1,0:T(8,128)(2,1)S(1)}, bf16[576,384]{1,0:T(8,128)(2,1)}, u32[]{:S(2)}, u32[]{:S(2)}) %collective-permute-start.1) | collective-permute-done | bytes 442400 | tf_op jit(solution)/shard_map/ppermute | solution.py:212
  39.6 3.6 %all-to-all-start = ((bf16[4,576,384]{2,1,0:T(8,128)(2,1)}), bf16[4,576,384]{2,1,0:T(8,128)(2,1)S(1)}, u32[]{:S(2)}, u32[]{:S(2)}) async-start(bf16[4,576,384]{2,1,0:T(8,128)(2,1)} %broadcast_in_dim.51), calls=%async_computation | async-start | bytes 3538944 | tf_op jit(solution)/shard_map/all_to_all | solution.py:189
  46.5 2.7 collective-permute-start
  52.5 12.8 %all-to-all-done = bf16[4,576,384]{2,1,0:T(8,128)(2,1)S(1)} async-done(((bf16[4,576,384]{2,1,0:T(8,128)(2,1)}), bf16[4,576,384]{2,1,0:T(8,128)(2,1)S(1)}, u32[]{:S(2)}, u32[]{:S(2)}) %all-to-all-start) | async-done | bytes 1769504 | tf_op jit(solution)/shard_map/all_to_all | solution.py:189
  65.3 3.6 %collective-permute-start.4 = (bf16[2,2,576,384]{3,2,1,0:T(8,128)(2,1)S(1)}, bf16[2,2,576,384]{3,2,1,0:T(8,128)(2,1)}, u32[]{:S(2)}, u32[]{:S(2)}) collective-permute-start(bf16[2,2,576,384]{3,2,1,0:T(8,128)(2,1)S(1)} %bitcast.72), channel_id=1, source_target_pairs={{0,128},{128,0},{1,129},{129,1},{2,130},{130,2},{3,131},{131,3},{4... | collective-permute-start | bytes 5308424 | tf_op jit(solution)/shard_map/ppermute | solution.py:237
  68.9 10.5 %collective-permute-start.3 = (bf16[576,384]{1,0:T(8,128)(2,1)S(1)}, bf16[576,384]{1,0:T(8,128)(2,1)S(1)}, u32[]{:S(2)}, u32[]{:S(2)}) collective-permute-start(bf16[576,384]{1,0:T(8,128)(2,1)S(1)} %copy-done.10), channel_id=1, source_target_pairs={{0,256},{256,0},{1,257},{257,1},{2,258},{258,2},{3,259},{259,3},{4... | collective-permute-start | bytes 1327112 | tf_op jit(solution)/shard_map/ppermute | solution.py:215
  79.4 44.3 %collective-permute-done.3 = bf16[576,384]{1,0:T(8,128)(2,1)S(1)} collective-permute-done((bf16[576,384]{1,0:T(8,128)(2,1)S(1)}, bf16[576,384]{1,0:T(8,128)(2,1)S(1)}, u32[]{:S(2)}, u32[]{:S(2)}) %collective-permute-start.3) | collective-permute-done | bytes 442400 | tf_op jit(solution)/shard_map/ppermute | solution.py:215
  125.2 4.4 %all-to-all-start.3 = ((bf16[4,576,384]{2,1,0:T(8,128)(2,1)}), bf16[4,576,384]{2,1,0:T(8,128)(2,1)}, u32[]{:S(2)}, u32[]{:S(2)}) async-start(bf16[4,576,384]{2,1,0:T(8,128)(2,1)} %broadcast_in_dim.53), calls=%async_computation.3 | async-start | bytes 3538944 | tf_op jit(solution)/shard_map/all_to_all | solution.py:189
  130.7 5.0 %shard_map.96 = bf16[4,2,288,512]{3,2,1,0:T(8,128)(2,1)} custom-call(bf16[2,2,576,384]{3,2,1,0:T(8,128)(2,1)S(1)} %bitcast.73, bf16[2,2,576,384]{3,2,1,0:T(8,128)(2,1)} %collective-permute-done.4.other_ref, bf16[2,512,384]{2,1,0:T(8,128)(2,1)S(1)} %copy-done.6), custom_call_target="tpu_custom_call" | custom-call | flops 1811939328 | bytes 8388608 | tf_op jit(solution)/shard_map/pallas_call | solution.py:76
  135.8 15.4 %all-to-all-done.3 = bf16[4,576,384]{2,1,0:T(8,128)(2,1)} async-done(((bf16[4,576,384]{2,1,0:T(8,128)(2,1)}), bf16[4,576,384]{2,1,0:T(8,128)(2,1)}, u32[]{:S(2)}, u32[]{:S(2)}) %all-to-all-start.3) | async-done | bytes 1769504 | tf_op jit(solution)/shard_map/all_to_all | solution.py:189
  151.2 4.1 %collective-permute-start.5 = (bf16[2,2,576,384]{3,2,1,0:T(8,128)(2,1)}, bf16[2,2,576,384]{3,2,1,0:T(8,128)(2,1)}, u32[]{:S(2)}, u32[]{:S(2)}) collective-permute-start(bf16[2,2,576,384]{3,2,1,0:T(8,128)(2,1)} %bitcast.17.near_ref), channel_id=1, source_target_pairs={{0,128},{128,0},{1,129},{129,1},{2,130},{130,2},{3,131},{131,3},{4... | collective-permute-start | bytes 5308424 | tf_op jit(solution)/shard_map/ppermute | solution.py:242
  155.3 3.6 %all-to-all-start.4 = ((bf16[4,576,512]{2,1,0:T(8,128)(2,1)}), bf16[4,576,512]{2,1,0:T(8,128)(2,1)S(1)}, u32[]{:S(2)}, u32[]{:S(2)}) async-start(bf16[4,576,512]{2,1,0:T(8,128)(2,1)} %bitcast.85), calls=%async_computation.4 | async-start | bytes 4718592 | tf_op jit(solution)/shard_map/all_to_all | solution.py:196
  160.1 5.3 %shard_map.97 = bf16[4,2,288,512]{3,2,1,0:T(8,128)(2,1)} custom-call(bf16[2,2,576,384]{3,2,1,0:T(8,128)(2,1)} %bitcast.17.near_ref, bf16[2,2,576,384]{3,2,1,0:T(8,128)(2,1)} %collective-permute-done.5.other_ref, bf16[2,512,384]{2,1,0:T(8,128)(2,1)S(1)} %copy-done.7), custom_call_target="tpu_custom_call" | custom-call | flops 1811939328 | bytes 8388608 | tf_op jit(solution)/shard_map/pallas_call | solution.py:76
  165.4 22.8 %all-to-all-done.4 = bf16[4,576,512]{2,1,0:T(8,128)(2,1)S(1)} async-done(((bf16[4,576,512]{2,1,0:T(8,128)(2,1)}), bf16[4,576,512]{2,1,0:T(8,128)(2,1)S(1)}, u32[]{:S(2)}, u32[]{:S(2)}) %all-to-all-start.4) | async-done | bytes 2359328 | tf_op jit(solution)/shard_map/all_to_all | solution.py:196
  189.7 3.6 %all-to-all-start.5 = ((bf16[4,576,512]{2,1,0:T(8,128)(2,1)}), bf16[4,576,512]{2,1,0:T(8,128)(2,1)S(1)}, u32[]{:S(2)}, u32[]{:S(2)}) async-start(bf16[4,576,512]{2,1,0:T(8,128)(2,1)} %bitcast.84), calls=%async_computation.5 | async-start | bytes 4718592 | tf_op jit(solution)/shard_map/all_to_all | solution.py:196
  196.6 2.1 reshape.245
  206.2 5.1 %shard_map.98.refs_0_ = bf16[2,8,2,64,1024]{4,3,2,1,0:T(8,128)(2,1)} custom-call(s32[1]{0:T(128)} %bitcast.9.zh_ref, bf16[4,2,2,144,512]{4,3,2,1,0:T(8,128)(2,1)S(1)} %bitcast.75, f32[8,2,576]{2,1,0:T(2,128)S(1)} %bitcast.76), custom_call_target="tpu_custom_call" | custom-call | flops 2415919104 | bytes 8388608 | tf_op jit(solution)/shard_map/pallas_call | solution.py:103
  211.2 10.4 %all-to-all-done.5 = bf16[4,576,512]{2,1,0:T(8,128)(2,1)S(1)} async-done(((bf16[4,576,512]{2,1,0:T(8,128)(2,1)}), bf16[4,576,512]{2,1,0:T(8,128)(2,1)S(1)}, u32[]{:S(2)}, u32[]{:S(2)}) %all-to-all-start.5) | async-done | bytes 2359328 | tf_op jit(solution)/shard_map/all_to_all | solution.py:196
  221.7 5.1 %shard_map.99 = bf16[2,8,2,64,1024]{4,3,2,1,0:T(8,128)(2,1)} custom-call(s32[1]{0:T(128)} %bitcast.9.zh_ref, bf16[4,2,2,144,512]{4,3,2,1,0:T(8,128)(2,1)S(1)} %bitcast.69, f32[8,2,576]{2,1,0:T(2,128)S(1)} %bitcast.77, bf16[2,8,2,64,1024]{4,3,2,1,0:T(8,128)(2,1)} %shard_map.98.refs_0_), custom_call_target="tpu_custom_call", output_to_operand_aliasing={{}: (3, {})} | custom-call | flops 2415919104 | bytes 8388608 | tf_op jit(solution)/shard_map/pallas_call | solution.py:103
  227.5 3.9 %shard_map.95 = bf16[4,2,2,144,512]{4,3,2,1,0:T(8,128)(2,1)S(1)} custom-call(s32[1]{0:T(128)} %bitcast.9.zh_ref, bf16[16,2,64,1152]{3,2,1,0:T(8,128)(2,1)} %bitcast.79, f32[8,576,2]{2,1,0:T(8,128)S(1)} %bitcast.67), custom_call_target="tpu_custom_call" | custom-call | flops 1207959552 | bytes 8388608 | tf_op jit(solution)/shard_map/pallas_call | solution.py:49
  231.4 30.7 %all_to_all.35 = bf16[4,576,512]{2,1,0:T(8,128)(2,1)} all-to-all(bf16[4,576,512]{2,1,0:T(8,128)(2,1)S(1)} %bitcast.71), channel_id=1, replica_groups=mesh['zh'=2,'co'=2,'zl'=8,'y'=4,'x'=4] {'y'}, dimensions={0} | all-to-all | bytes 4718592 | tf_op jit(solution)/shard_map/all_to_all | solution.py:196
  262.2 3.9 %shard_map.100 = bf16[4,2,2,144,512]{4,3,2,1,0:T(8,128)(2,1)S(1)} custom-call(s32[1]{0:T(128)} %bitcast.9.zh_ref, bf16[16,2,64,1152]{3,2,1,0:T(8,128)(2,1)} %bitcast.80, f32[8,576,2]{2,1,0:T(8,128)S(1)} %bitcast.68), custom_call_target="tpu_custom_call" | custom-call | flops 1207959552 | bytes 8388608 | tf_op jit(solution)/shard_map/pallas_call | solution.py:49
  267.5 4.8 %all-to-all-start.6 = ((bf16[4,576,512]{2,1,0:T(8,128)(2,1)}), bf16[4,576,512]{2,1,0:T(8,128)(2,1)}, u32[]{:S(2)}, u32[]{:S(2)}) async-start(bf16[4,576,512]{2,1,0:T(8,128)(2,1)} %bitcast.70), calls=%async_computation.7 | async-start | bytes 4718592 | tf_op jit(solution)/shard_map/all_to_all | solution.py:196
  273.9 2.7 copy.95
  276.6 22.2 %all-to-all-done.6 = bf16[4,576,512]{2,1,0:T(8,128)(2,1)} async-done(((bf16[4,576,512]{2,1,0:T(8,128)(2,1)}), bf16[4,576,512]{2,1,0:T(8,128)(2,1)}, u32[]{:S(2)}, u32[]{:S(2)}) %all-to-all-start.6) | async-done | bytes 2359328 | tf_op jit(solution)/shard_map/all_to_all | solution.py:196
  298.8 4.3 %all-to-all-start.2 = ((bf16[4,128,1024]{2,1,0:T(8,128)(2,1)}), bf16[4,128,1024]{2,1,0:T(8,128)(2,1)}, u32[]{:S(2)}, u32[]{:S(2)}) async-start(bf16[4,128,1024]{2,1,0:T(8,128)(2,1)} %copy.95), calls=%async_computation.2 | async-start | bytes 2097152 | tf_op jit(solution)/shard_map/all_to_all | solution.py:287
  303.1 6.3 %shard_map.101.refs_0_ = f32[2,512,384]{2,1,0:T(8,128)S(1)} custom-call(bf16[4,2,288,512]{3,2,1,0:T(8,128)(2,1)} %bitcast.82, bf16[2,2,576,384]{3,2,1,0:T(8,128)(2,1)S(1)} %bitcast.74, bf16[2,2,576,384]{3,2,1,0:T(8,128)(2,1)} %collective-permute-done.4.other_ref), custom_call_target="tpu_custom_call" | custom-call | flops 1811939328 | bytes 8388608 | tf_op jit(solution)/shard_map/pallas_call | solution.py:142
  309.4 6.5 %shard_map.102 = bf16[2,512,384]{2,1,0:T(8,128)(2,1)S(1)} custom-call(bf16[4,2,288,512]{3,2,1,0:T(8,128)(2,1)} %bitcast.28.in_ref, bf16[2,2,576,384]{3,2,1,0:T(8,128)(2,1)} %bitcast.17.near_ref, bf16[2,2,576,384]{3,2,1,0:T(8,128)(2,1)} %collective-permute-done.5.other_ref, f32[2,512,384]{2,1,0:T(8,128)S(1)} %shard_map.101.refs_0_), custom_call_target="tpu_custom_call" | custom-call | flops 1811939328 | bytes 8388608 | tf_op jit(solution)/shard_map/pallas_call | solution.py:142
  315.9 5.4 %collective-permute-start.7 = (bf16[512,384]{1,0:T(8,128)(2,1)S(1)}, bf16[512,384]{1,0:T(8,128)(2,1)S(1)}, u32[]{:S(2)}, u32[]{:S(2)}) collective-permute-start(bf16[512,384]{1,0:T(8,128)(2,1)S(1)} %select_bitcast_fusion), channel_id=1, source_target_pairs={{0,128},{128,0},{1,129},{129,1},{2,130},{130,2},{3,131},{131,3},{4... | collective-permute-start | bytes 1179656 | tf_op jit(solution)/shard_map/ppermute | solution.py:284
  323.9 2.1 collective-permute-start.6
  (98 shorter events, 44.7 us)
Async XLA Ops:
  7.2 37.7 %copy-start = (bf16[2,64,4096]{2,1,0:T(8,128)(2,1)S(1)}, bf16[2,64,4096]{2,1,0:T(8,128)(2,1)}, u32[]{:S(2)}) copy-start(bf16[2,64,4096]{2,1,0:T(8,128)(2,1)} %param.8) | copy-start | bytes 3145732
  9.2 17.8 %collective-permute-start.2 = (bf16[512,384]{1,0:T(8,128)(2,1)}, bf16[512,384]{1,0:T(8,128)(2,1)S(1)}, u32[]{:S(2)}, u32[]{:S(2)}) collective-permute-start(bf16[512,384]{1,0:T(8,128)(2,1)} %select_bitcast_fusion.1), channel_id=1, source_target_pairs={{0,128},{128,0},{1,129},{129,1},{2,130},{130,2},{3,131},{131,3},{4... | collective-permute-start | bytes 1179656 | tf_op jit(solution)/shard_map/ppermute | solution.py:200
  18.0 4.9 %copy-start.13 = (s32[2,64,8]{1,2,0:T(8,128)S(1)}, s32[2,64,8]{1,2,0:T(8,128)}, u32[]{:S(2)}) copy-start(s32[2,64,8]{1,2,0:T(8,128)} %param.10) | copy-start | bytes 12292
  18.0 4.9 %copy-start.14 = (s32[2,64,8]{1,2,0:T(8,128)S(1)}, s32[2,64,8]{1,2,0:T(8,128)}, u32[]{:S(2)}) copy-start(s32[2,64,8]{1,2,0:T(8,128)} %param.9) | copy-start | bytes 12292
  18.0 8.9 %copy-start.8 = (bf16[1,1024,384]{2,1,0:T(8,128)(2,1)S(1)}, bf16[1,1024,384]{2,1,0:T(8,128)(2,1)}, u32[]{:S(2)}) copy-start(bf16[1,1024,384]{2,1,0:T(8,128)(2,1)} %param.13) | copy-start | bytes 2359300
  21.0 15.3 %collective-permute-start.1 = (bf16[576,384]{1,0:T(8,128)(2,1)S(1)}, bf16[576,384]{1,0:T(8,128)(2,1)}, u32[]{:S(2)}, u32[]{:S(2)}) collective-permute-start(bf16[576,384]{1,0:T(8,128)(2,1)S(1)} %broadcast_select_fusion.5), channel_id=1, source_target_pairs={{0,2},{1,3},{2,0},{3,1},{4,6},{5,7},{6,4},{7,5},{8,10},{9,11},{10,... | collective-permute-start | bytes 1327112 | tf_op jit(solution)/shard_map/ppermute | solution.py:212
  38.2 5.0 %copy-start.11 = (s32[2,64,8]{2,1,0:T(8,128)S(1)}, s32[2,64,8]{2,1,0:T(8,128)}, u32[]{:S(2)}) copy-start(s32[2,64,8]{2,1,0:T(8,128)} %copy.85) | copy-start | bytes 12292
  38.2 5.0 %copy-start.12 = (f32[2,64,8]{2,1,0:T(8,128)S(1)}, f32[2,64,8]{2,1,0:T(8,128)}, u32[]{:S(2)}) copy-start(f32[2,64,8]{2,1,0:T(8,128)} %copy.86) | copy-start | bytes 12292
  38.2 5.1 %copy-start.15 = (f32[64]{0:T(128)S(1)}, f32[64]{0:T(128)}, u32[]{:S(2)}) copy-start(f32[64]{0:T(128)} %iota_add_fusion) | copy-start | bytes 772
  39.6 25.6 %all-to-all-start = ((bf16[4,576,384]{2,1,0:T(8,128)(2,1)}), bf16[4,576,384]{2,1,0:T(8,128)(2,1)S(1)}, u32[]{:S(2)}, u32[]{:S(2)}) async-start(bf16[4,576,384]{2,1,0:T(8,128)(2,1)} %broadcast_in_dim.51), calls=%async_computation | async-start | bytes 3538944 | tf_op jit(solution)/shard_map/all_to_all | solution.py:189
  43.2 150.2 %all-gather.2.cloned.1.call-start = ((), (), s32[]{:S(2)}) async-start(), calls=%async_computation.8 | async-start | bytes 5013504 | tf_op jit(solution)/shard_map/all_gather | solution.py:235
  45.1 23.8 %copy-start.10 = (bf16[576,384]{1,0:T(8,128)(2,1)S(1)}, bf16[576,384]{1,0:T(8,128)(2,1)}, u32[]{:S(2)}) copy-start(bf16[576,384]{1,0:T(8,128)(2,1)} %get-tuple-element.32) | copy-start | bytes 1327108
  46.5 3.7 %collective-permute-start = (bf16[128,576]{1,0:T(8,128)(2,1)S(1)}, bf16[128,576]{1,0:T(8,128)(2,1)S(1)}, u32[]{:S(2)}, u32[]{:S(2)}) collective-permute-start(bf16[128,576]{1,0:T(8,128)(2,1)S(1)} %pad_maximum_fusion.1), channel_id=1, source_target_pairs={{0,128},{128,0},{1,129},{129,1},{2,130},{130,2},{3,131},{131,3},{4... | collective-permute-start | bytes 442376 | tf_op jit(solution)/shard_map/ppermute | solution.py:232
  65.2 64.3 %copy-start.2 = (bf16[4,576,384]{2,1,0:T(8,128)(2,1)}, bf16[4,576,384]{2,1,0:T(8,128)(2,1)S(1)}, u32[]{:S(2)}) copy-start(bf16[4,576,384]{2,1,0:T(8,128)(2,1)S(1)} %all-to-all-done) | copy-start | bytes 5308420
  65.3 64.3 %collective-permute-start.4 = (bf16[2,2,576,384]{3,2,1,0:T(8,128)(2,1)S(1)}, bf16[2,2,576,384]{3,2,1,0:T(8,128)(2,1)}, u32[]{:S(2)}, u32[]{:S(2)}) collective-permute-start(bf16[2,2,576,384]{3,2,1,0:T(8,128)(2,1)S(1)} %bitcast.72), channel_id=1, source_target_pairs={{0,128},{128,0},{1,129},{129,1},{2,130},{130,2},{3,131},{131,3},{4... | collective-permute-start | bytes 5308424 | tf_op jit(solution)/shard_map/ppermute | solution.py:237
  68.9 54.8 %collective-permute-start.3 = (bf16[576,384]{1,0:T(8,128)(2,1)S(1)}, bf16[576,384]{1,0:T(8,128)(2,1)S(1)}, u32[]{:S(2)}, u32[]{:S(2)}) collective-permute-start(bf16[576,384]{1,0:T(8,128)(2,1)S(1)} %copy-done.10), channel_id=1, source_target_pairs={{0,256},{256,0},{1,257},{257,1},{2,258},{258,2},{3,259},{259,3},{4... | collective-permute-start | bytes 1327112 | tf_op jit(solution)/shard_map/ppermute | solution.py:215
  125.2 26.1 %all-to-all-start.3 = ((bf16[4,576,384]{2,1,0:T(8,128)(2,1)}), bf16[4,576,384]{2,1,0:T(8,128)(2,1)}, u32[]{:S(2)}, u32[]{:S(2)}) async-start(bf16[4,576,384]{2,1,0:T(8,128)(2,1)} %broadcast_in_dim.53), calls=%async_computation.3 | async-start | bytes 3538944 | tf_op jit(solution)/shard_map/all_to_all | solution.py:189
  129.6 1.1 copy-start.6
  151.2 7.7 %collective-permute-start.5 = (bf16[2,2,576,384]{3,2,1,0:T(8,128)(2,1)}, bf16[2,2,576,384]{3,2,1,0:T(8,128)(2,1)}, u32[]{:S(2)}, u32[]{:S(2)}) collective-permute-start(bf16[2,2,576,384]{3,2,1,0:T(8,128)(2,1)} %bitcast.17.near_ref), channel_id=1, source_target_pairs={{0,128},{128,0},{1,129},{129,1},{2,130},{130,2},{3,131},{131,3},{4... | collective-permute-start | bytes 5308424 | tf_op jit(solution)/shard_map/ppermute | solution.py:242
  155.3 32.9 %all-to-all-start.4 = ((bf16[4,576,512]{2,1,0:T(8,128)(2,1)}), bf16[4,576,512]{2,1,0:T(8,128)(2,1)S(1)}, u32[]{:S(2)}, u32[]{:S(2)}) async-start(bf16[4,576,512]{2,1,0:T(8,128)(2,1)} %bitcast.85), calls=%async_computation.4 | async-start | bytes 4718592 | tf_op jit(solution)/shard_map/all_to_all | solution.py:196
  159.0 1.1 copy-start.7
  188.2 1.5 copy-start.4
  189.7 32.0 %all-to-all-start.5 = ((bf16[4,576,512]{2,1,0:T(8,128)(2,1)}), bf16[4,576,512]{2,1,0:T(8,128)(2,1)S(1)}, u32[]{:S(2)}, u32[]{:S(2)}) async-start(bf16[4,576,512]{2,1,0:T(8,128)(2,1)} %bitcast.84), calls=%async_computation.5 | async-start | bytes 4718592 | tf_op jit(solution)/shard_map/all_to_all | solution.py:196
  193.3 129.7 %reduce-scatter.2.cloned.1.call-start = ((), (), s32[]{:S(2)}) async-start(), calls=%async_computation.9 | async-start | bytes 4456448 | tf_op jit(solution)/shard_map/reduce_scatter | solution.py:264
  204.5 1.7 copy-start.5
  266.1 1.4 copy-start.1
  267.5 4.8 %copy-start.9 = (bf16[1,2,64,4096]{3,2,1,0:T(8,128)(2,1)S(1)}, bf16[1,2,64,4096]{3,2,1,0:T(8,128)(2,1)}, u32[]{:S(2)}) copy-start(bf16[1,2,64,4096]{3,2,1,0:T(8,128)(2,1)} %param.14) | copy-start | bytes 3145732
  267.5 31.3 %all-to-all-start.6 = ((bf16[4,576,512]{2,1,0:T(8,128)(2,1)}), bf16[4,576,512]{2,1,0:T(8,128)(2,1)}, u32[]{:S(2)}, u32[]{:S(2)}) async-start(bf16[4,576,512]{2,1,0:T(8,128)(2,1)} %bitcast.70), calls=%async_computation.7 | async-start | bytes 4718592 | tf_op jit(solution)/shard_map/all_to_all | solution.py:196
  273.9 29.1 %copy-start.3 = (bf16[4,576,384]{2,1,0:T(8,128)(2,1)S(1)}, bf16[4,576,384]{2,1,0:T(8,128)(2,1)}, u32[]{:S(2)}) copy-start(bf16[4,576,384]{2,1,0:T(8,128)(2,1)} %copy-done.2) | copy-start | bytes 5308420
  298.8 22.6 %all-to-all-start.2 = ((bf16[4,128,1024]{2,1,0:T(8,128)(2,1)}), bf16[4,128,1024]{2,1,0:T(8,128)(2,1)}, u32[]{:S(2)}, u32[]{:S(2)}) async-start(bf16[4,128,1024]{2,1,0:T(8,128)(2,1)} %copy.95), calls=%async_computation.2 | async-start | bytes 2097152 | tf_op jit(solution)/shard_map/all_to_all | solution.py:287
  315.9 6.9 %collective-permute-start.7 = (bf16[512,384]{1,0:T(8,128)(2,1)S(1)}, bf16[512,384]{1,0:T(8,128)(2,1)S(1)}, u32[]{:S(2)}, u32[]{:S(2)}) collective-permute-start(bf16[512,384]{1,0:T(8,128)(2,1)S(1)} %select_bitcast_fusion), channel_id=1, source_target_pairs={{0,128},{128,0},{1,129},{129,1},{2,130},{130,2},{3,131},{131,3},{4... | collective-permute-start | bytes 1179656 | tf_op jit(solution)/shard_map/ppermute | solution.py:284
  323.9 3.2 collective-permute-start.6
Sparse Core Ops, SparseCore 0:
  65.4 103.1 all-gather.1
  226.9 71.0 reduce-scatter.1

commit v7 on v3

--- a/solution.py
+++ b/solution.py
@@ -33,9 +33,8 @@
     )
 
 
-def pick_rows(half, line, table, far):
-    batches, tok, width = line.shape[1:]
-    width //= 2
+def pick_rows(half, line, table, far, width):
+    batches, tok = line.shape[1:3]
     rows = table.shape[1]
     part = rows // 4
 
@@ -217,12 +216,9 @@
         ]
         return [v.reshape(shape) for v in moved]
 
-    own_part = lax.dynamic_slice_in_dim(tokens, x * quarter, quarter, 2)
-    own_part = own_part.reshape(batches * tok, 2, eighth)
-    mine, theirs = by(co, own_part[:, 0], own_part[:, 1])
-    line = jnp.concatenate([mine, lax.ppermute(theirs, "co", SWAP)], axis=1)
-    line = lax.all_gather(line, ("zh", "zl"), axis=0, tiled=True)
-    line = line.reshape(2 * nzl, batches, tok, quarter)
+    cut = up_weight.reshape(2, eighth, ff)
+    mine, theirs = by(co, cut[0], cut[1])
+    weight = jnp.stack(by(co, mine, lax.ppermute(theirs, "co", SWAP)))
 
     r = jnp.arange(rows, dtype=I32)
     r_batch = (r // (capacity * nzl)) % batches
@@ -239,39 +235,52 @@
     crossed = lax.ppermute(leave, "zh", SWAP)
     near = gather(stay)
 
-    expert_ids, slot_index, gate_weights, leave = lax.optimization_barrier(
-        (expert_ids, slot_index, gate_weights, leave)
+    expert_ids, slot_index, gate_weights, send = lax.optimization_barrier(
+        (expert_ids, slot_index, gate_weights, send)
     )
     held, gate = slot_tables(expert_ids, slot_index, gate_weights, capacity, nzl * ny * capacity)
-    table = jnp.stack([held, gate]).reshape(2, batches, nzl, ny * capacity)
-    table = table.transpose(2, 0, 1, 3)
-    table = jnp.stack([table, lax.ppermute(table, "co", SWAP)], axis=1)
-    table = lax.all_to_all(
-        jnp.concatenate([table, table]), ("zh", "zl"), split_axis=0, concat_axis=0, tiled=True
-    ).reshape(2, nzl, 2, 2, batches, ny, capacity)
-    table = jnp.where(zh == 0, table, table[::-1])
-    table = lax.dynamic_slice_in_dim(jnp.concatenate([table, table], axis=5), y, ny, 5)
-    table = table.transpose(3, 0, 2, 4, 5, 1, 6)
-    start = jnp.arange(nzl, dtype=F32)[:, None] * tok
-    seats = jnp.where(table[0] >= 0, table[0] + start, -1.0)
-    table = jnp.stack([seats, table[1]]).reshape(2, 4 * batches, buffer_rows)
-    lying, standing = table.transpose(1, 0, 2), table.transpose(1, 2, 0)
-
-    cut = up_weight.reshape(2, eighth, ff)
-    mine, theirs = by(co, cut[0], cut[1])
-    weight = jnp.stack(by(co, mine, lax.ppermute(theirs, "co", SWAP)))
-
+    high = lax.reduce_precision(gate, 8, 7)
+    middle = lax.reduce_precision(gate - high, 8, 7)
+    table = jnp.stack([held, high, middle, gate - high - middle])
+    table = table.reshape(4, batches, nzl, 2, 2 * capacity).transpose(2, 0, 1, 3, 4)
+    table = table.reshape(batches * tok, 2 * capacity).astype(BF16)
+    table = jnp.pad(table, ((0, 0), (0, 64 - 2 * capacity)))
+
+    own_part = lax.dynamic_slice_in_dim(tokens, x * quarter, quarter, 2)
+    own_part = own_part.reshape(batches * tok, 2, eighth)
+    mine, theirs = by(co, own_part[:, 0], own_part[:, 1])
+    theirs = lax.ppermute(jnp.concatenate([theirs, table], axis=1), "co", SWAP)
+    line = jnp.concatenate([mine, theirs[:, :eighth], table, theirs[:, eighth:]], axis=1)
+    line = lax.all_gather(line, ("zh", "zl"), axis=0, tiled=True)
+
+    split = (2, batches, nzl * capacity, eighth)
+    near, crossed = lax.optimization_barrier((near, crossed))
     near_other = lax.ppermute(near, "co", SWAP)
     back = rows_back(near, near_other, weight, here)
-    crossed, back, lying, standing = lax.optimization_barrier((crossed, back, lying, standing))
     wide = gather(crossed)
-    split = (2, batches, nzl * capacity, eighth)
-    spread = combine(0, along_y(back, split), lying, far, tok, None)
+    wide, back = lax.optimization_barrier((wide, along_y(back, split)))
     wide_other = lax.ppermute(wide, "co", SWAP)
-    back = rows_back(wide, wide_other, weight, here)
-    attention_partial, back = lax.optimization_barrier((attention_partial, back))
-    spread = combine(1, along_y(back, split), lying, far, tok, spread)
-    line, _ = lax.optimization_barrier((line, spread))
+    wide_back = rows_back(wide, wide_other, weight, here)
+
+    column = lax.dynamic_slice(
+        line.reshape(2 * nzl, batches * tok, -1),
+        (0, lax.axis_index("zl") * 16, quarter),
+        (2 * nzl, 16, 128),
+    ).reshape(2, nzl, 4, batches, 2, 2, 64)[..., : 2 * capacity]
+    column = jnp.where(zh == 0, column, column[::-1]).astype(F32)
+    column = column.reshape(2, nzl, 4, batches, 2, 2, 2, capacity)
+    column = column.transpose(2, 0, 5, 3, 4, 6, 1, 7).reshape(
+        4, 4 * batches, ny, nzl, capacity
+    )
+    column = lax.dynamic_slice_in_dim(jnp.concatenate([column, column], axis=2), y, ny, 2)
+    start = jnp.arange(nzl, dtype=F32)[:, None] * tok
+    seats = jnp.where(column[0] >= 0, column[0] + start, -1.0)
+    column = jnp.stack([seats, column[1] + (column[2] + column[3])])
+    column = column.reshape(2, 4 * batches, buffer_rows)
+    lying, standing = column.transpose(1, 0, 2), column.transpose(1, 2, 0)
+
+    spread = combine(0, back, lying, far, tok, None)
+    spread = combine(1, along_y(wide_back, split), lying, far, tok, spread)
     expert_part = lax.psum_scatter(
         spread.reshape(2 * nzl * batches * tok, quarter),
         ("zh", "zl"),
@@ -279,9 +288,11 @@
         tiled=True,
     )
 
+    line = line.reshape(2 * nzl, batches, tok, -1)
+    line, attention_partial, _ = lax.optimization_barrier((line, attention_partial, spread))
     split = (2, batches * nzl * capacity, eighth)
-    inbound = along_y(pick_rows(0, line, standing, far), split)
-    inbound_far = along_y(pick_rows(1, line, standing, far), split)
+    inbound = along_y(pick_rows(0, line, standing, far, eighth), split)
+    inbound_far = along_y(pick_rows(1, line, standing, far, eighth), split)
     total = weight_sum(inbound, near, near_other, here, None, 1.0, F32)
     total = weight_sum(inbound_far, wide, wide_other, here, total, 1.0 / (2 * SIZES[1]), BF16)
     mine, theirs = by(co, total[0], total[1])

time: 324 us -> 305 us (0.941)
  blocking collectives: 23.3 us -> 0 us
  starting transfers between devices: 109 us -> 88.8 us
  local copies, waits for them, and re-layouts: 20 us -> 31 us
  waiting for transfers between devices: 102 us -> 110 us
    all_to_all x1 -> x0, blocking collectives: 23.3 us -> none  [gather(): lax.all_to_all(jnp.broadcast_to(v, (nx,) + v.shape), 'x', split_axis=0, c...]
    all_to_all x1 -> x0, starting transfers between devices: 15.4 us -> none  [on_device(): lax.all_to_all(jnp.concatenate([table, table]), ('zh', 'zl'), split_axis=...]
    ppermute x1, waiting for transfers between devices: 0.01 us -> 12.8 us  [on_device(): taken = lax.ppermute(send, 'x', [(i, (i + 2) % nx) for i in range(nx)])]
    all_to_all x1 -> x2, waiting for transfers between devices: 12.1 us -> 4.39 us  [gather(): lax.all_to_all(jnp.broadcast_to(v, (nx,) + v.shape), 'x', split_axis=0, c...]
    ppermute x1, waiting for transfers between devices: 38.6 us -> 45.2 us  [on_device(): crossed = lax.ppermute(leave, 'zh', SWAP)]
    ppermute x12, waiting for transfers between devices: 48.6 us -> 42.8 us  [along_y(): lax.ppermute(v, 'y', [(i, (i + d) % ny) for i in range(ny)])]
    ppermute x1, starting transfers between devices: 5.93 us -> 1.91 us  [on_device(): weight = jnp.stack(by(co, mine, lax.ppermute(theirs, 'co', SWAP)))]
    ppermute x1, waiting for transfers between devices: 0.01 us -> 3.62 us  [on_device(): wide_other = lax.ppermute(wide, 'co', SWAP)]
  transfers between devices with their start and end apart: 26 -> 25, of which waited for: 12 -> 12; matrix products, arithmetic and copies ran while one was open for 6% -> 9% of each run, Pallas kernels for 13% -> 13%
where the time goes in v7:
time: 305 us; the launch traced here: 303 us
  waiting for transfers between devices  110 us (36%)
  starting transfers between devices  88.8 us (29%)
  Pallas kernels  43.8 us (14%)
  local copies, waits for them, and re-layouts  31 us (10%)
  between operations  14.7 us (5%)
  other arithmetic  12 us (4%)
    ppermute x1, waiting for transfers between devices, on_device(): crossed = lax.ppermute(leave, 'zh', SWAP)  45.2 us
    ppermute x12, waiting for transfers between devices, along_y(): lax.ppermute(v, 'y', [(i, (i + d) % ny) for i in range(ny)])  42.8 us
    ppermute x12, starting transfers between devices, along_y(): lax.ppermute(v, 'y', [(i, (i + d) % ny) for i in range(ny)])  35.4 us
    ppermute x1, waiting for transfers between devices, on_device(): taken = lax.ppermute(send, 'x', [(i, (i + 2) % nx) for i in range(nx)])  12.8 us
    pallas_call x2, Pallas kernels, weight_sum(): call(body, (4,), [pl.BlockSpec((2, part, width), lambda d, y: (0, 0, 0))]...  12.7 us
    unnamed x49, local copies, waits for them, and re-layouts  12.4 us
    pallas_call x2, Pallas kernels, rows_back(): call(body, (4,), [piece, piece, pl.BlockSpec(weight.shape, lambda d, y: (...  12.1 us
    ppermute x1, starting transfers between devices, on_device(): crossed = lax.ppermute(leave, 'zh', SWAP)  10.5 us
  transfers between devices with their start and end apart: 25, of which 12 were waited for; matrix products, arithmetic and copies ran while one was open for 9% of the time, Pallas kernels for 13%

profile of v7, /device:TPU:1, one launch (start us, length us, event | category | flops | bytes accessed | tf_op | source)
XLA Modules:
  0.0 303.1 jit_solution(10845628812548939806)
XLA Ops:
  7.3 2.9 fusion.1
  12.4 8.8 %collective-permute-start = (bf16[128,576]{1,0:T(8,128)(2,1)S(1)}, bf16[128,576]{1,0:T(8,128)(2,1)S(1)}, u32[]{:S(2)}, u32[]{:S(2)}) collective-permute-start(bf16[128,576]{1,0:T(8,128)(2,1)S(1)} %pad_maximum_fusion.1), channel_id=1, source_target_pairs={{0,128},{128,0},{1,129},{129,1},{2,130},{130,2},{3,131},{131,3},{4... | collective-permute-start | bytes 442376 | tf_op jit(solution)/shard_map/ppermute | solution.py:252
  25.1 12.8 %collective-permute-done.1 = bf16[576,384]{1,0:T(8,128)(2,1)S(1)} collective-permute-done((bf16[576,384]{1,0:T(8,128)(2,1)S(1)}, bf16[576,384]{1,0:T(8,128)(2,1)S(1)}, u32[]{:S(2)}, u32[]{:S(2)}) %collective-permute-start.1) | collective-permute-done | bytes 442400 | tf_op jit(solution)/shard_map/ppermute | solution.py:233
  40.2 3.6 %all-to-all-start = ((bf16[4,576,384]{2,1,0:T(8,128)(2,1)}), bf16[4,576,384]{2,1,0:T(8,128)(2,1)S(1)}, u32[]{:S(2)}, u32[]{:S(2)}) async-start(bf16[4,576,384]{2,1,0:T(8,128)(2,1)} %broadcast_in_dim.51), calls=%async_computation | async-start | bytes 3538944 | tf_op jit(solution)/shard_map/all_to_all | solution.py:208
  43.8 10.5 %collective-permute-start.2 = (bf16[576,384]{1,0:T(8,128)(2,1)}, bf16[576,384]{1,0:T(8,128)(2,1)S(1)}, u32[]{:S(2)}, u32[]{:S(2)}) collective-permute-start(bf16[576,384]{1,0:T(8,128)(2,1)} %get-tuple-element.60), channel_id=1, source_target_pairs={{0,256},{256,0},{1,257},{257,1},{2,258},{258,2},{3,259},{259,3},{4... | collective-permute-start | bytes 1327112 | tf_op jit(solution)/shard_map/ppermute | solution.py:235
  54.2 45.2 %collective-permute-done.2 = bf16[576,384]{1,0:T(8,128)(2,1)S(1)} collective-permute-done((bf16[576,384]{1,0:T(8,128)(2,1)}, bf16[576,384]{1,0:T(8,128)(2,1)S(1)}, u32[]{:S(2)}, u32[]{:S(2)}) %collective-permute-start.2) | collective-permute-done | bytes 442400 | tf_op jit(solution)/shard_map/ppermute | solution.py:235
  99.4 4.3 %collective-permute-start.3 = (bf16[2,2,576,384]{3,2,1,0:T(8,128)(2,1)S(1)}, bf16[2,2,576,384]{3,2,1,0:T(8,128)(2,1)}, u32[]{:S(2)}, u32[]{:S(2)}) collective-permute-start(bf16[2,2,576,384]{3,2,1,0:T(8,128)(2,1)S(1)} %bitcast.77), channel_id=1, source_target_pairs={{0,128},{128,0},{1,129},{129,1},{2,130},{130,2},{3,131},{131,3},{4... | collective-permute-start | bytes 5308424 | tf_op jit(solution)/shard_map/ppermute | solution.py:258
  109.0 5.4 %all-to-all-start.1 = ((bf16[4,576,384]{2,1,0:T(8,128)(2,1)}), bf16[4,576,384]{2,1,0:T(8,128)(2,1)}, u32[]{:S(2)}, u32[]{:S(2)}) async-start(bf16[4,576,384]{2,1,0:T(8,128)(2,1)} %broadcast_in_dim.52), calls=%async_computation.1 | async-start | bytes 3538944 | tf_op jit(solution)/shard_map/all_to_all | solution.py:208
  115.9 6.0 %shard_map.95 = (bf16[2,288,512]{2,1,0:T(8,128)(2,1)S(1)}, bf16[2,288,512]{2,1,0:T(8,128)(2,1)}, bf16[2,288,512]{2,1,0:T(8,128)(2,1)}, bf16[2,288,512]{2,1,0:T(8,128)(2,1)S(1)}) custom-call(s32[1]{0:T(128)} %bitcast.5.y_ref, bf16[2,2,576,384]{3,2,1,0:T(8,128)(2,1)S(1)} %bitcast.78, bf16[2,2,576,384]{3,2,1,0:T(8,128)(2,1)} %collective-permute-done.3.other_ref.refs_5_, ...), custom_call_target="tpu_custom_call" | custom-call | flops 1811939328 | bytes 8388608 | tf_op jit(solution)/shard_map/pallas_call | solution.py:84
  125.0 4.5 %collective-permute-start.6 = (bf16[2,288,512]{2,1,0:T(8,128)(2,1)}, bf16[2,288,512]{2,1,0:T(8,128)(2,1)S(1)}, u32[]{:S(2)}, u32[]{:S(2)}) collective-permute-start(bf16[2,288,512]{2,1,0:T(8,128)(2,1)} %get-tuple-element.37), channel_id=1, source_target_pairs={{0,8},{4,12},{8,0},{12,4},{1,9},{5,13},{9,1},{13,5},{2,10},{6,14},... | collective-permute-start | bytes 1769480 | tf_op jit(solution)/shard_map/ppermute | solution.py:214
  129.5 3.0 collective-permute-start.7
  132.5 4.4 %all-to-all-done.1 = bf16[4,576,384]{2,1,0:T(8,128)(2,1)} async-done(((bf16[4,576,384]{2,1,0:T(8,128)(2,1)}), bf16[4,576,384]{2,1,0:T(8,128)(2,1)}, u32[]{:S(2)}, u32[]{:S(2)}) %all-to-all-start.1) | async-done | bytes 1769504 | tf_op jit(solution)/shard_map/all_to_all | solution.py:208
  136.9 3.2 %collective-permute-done.5 = bf16[2,288,512]{2,1,0:T(8,128)(2,1)S(1)} collective-permute-done((bf16[2,288,512]{2,1,0:T(8,128)(2,1)}, bf16[2,288,512]{2,1,0:T(8,128)(2,1)S(1)}, u32[]{:S(2)}, u32[]{:S(2)}) %collective-permute-start.5) | collective-permute-done | bytes 589856 | tf_op jit(solution)/shard_map/ppermute | solution.py:214
  140.9 12.1 %collective-permute-done.6 = bf16[2,288,512]{2,1,0:T(8,128)(2,1)S(1)} collective-permute-done((bf16[2,288,512]{2,1,0:T(8,128)(2,1)}, bf16[2,288,512]{2,1,0:T(8,128)(2,1)S(1)}, u32[]{:S(2)}, u32[]{:S(2)}) %collective-permute-start.6) | collective-permute-done | bytes 589856 | tf_op jit(solution)/shard_map/ppermute | solution.py:214
  155.4 3.5 %collective-permute-start.8 = (bf16[2,2,576,384]{3,2,1,0:T(8,128)(2,1)}, bf16[2,2,576,384]{3,2,1,0:T(8,128)(2,1)}, u32[]{:S(2)}, u32[]{:S(2)}) collective-permute-start(bf16[2,2,576,384]{3,2,1,0:T(8,128)(2,1)} %bitcast.7.near_ref.refs_4_), channel_id=1, source_target_pairs={{0,128},{128,0},{1,129},{129,1},{2,130},{130,2},{3,131},{131,3},{4... | collective-permute-start | bytes 5308424 | tf_op jit(solution)/shard_map/ppermute | solution.py:262
  158.9 3.6 %collective-permute-done.8.other_ref.refs_5_ = bf16[2,2,576,384]{3,2,1,0:T(8,128)(2,1)} collective-permute-done((bf16[2,2,576,384]{3,2,1,0:T(8,128)(2,1)}, bf16[2,2,576,384]{3,2,1,0:T(8,128)(2,1)}, u32[]{:S(2)}, u32[]{:S(2)}) %collective-permute-start.8) | collective-permute-done | bytes 1769504 | tf_op jit(solution)/shard_map/ppermute | solution.py:262
  163.6 6.1 %shard_map.96 = (bf16[2,288,512]{2,1,0:T(8,128)(2,1)S(1)}, bf16[2,288,512]{2,1,0:T(8,128)(2,1)}, bf16[2,288,512]{2,1,0:T(8,128)(2,1)}, bf16[2,288,512]{2,1,0:T(8,128)(2,1)}) custom-call(s32[1]{0:T(128)} %bitcast.5.y_ref, bf16[2,2,576,384]{3,2,1,0:T(8,128)(2,1)} %bitcast.7.near_ref.refs_4_, bf16[2,2,576,384]{3,2,1,0:T(8,128)(2,1)} %collective-permute-done.8.other_ref.refs_5_, ...), custom_call_target="tpu_custom_call" | custom-call | flops 1811939328 | bytes 8388608 | tf_op jit(solution)/shard_map/pallas_call | solution.py:84
  169.7 4.3 %collective-permute-start.9 = (bf16[2,288,512]{2,1,0:T(8,128)(2,1)}, bf16[2,288,512]{2,1,0:T(8,128)(2,1)S(1)}, u32[]{:S(2)}, u32[]{:S(2)}) collective-permute-start(bf16[2,288,512]{2,1,0:T(8,128)(2,1)} %get-tuple-element.41), channel_id=1, source_target_pairs={{0,12},{4,0},{8,4},{12,8},{1,13},{5,1},{9,5},{13,9},{2,14},{6,2},{... | collective-permute-start | bytes 1769480 | tf_op jit(solution)/shard_map/ppermute | solution.py:214
  192.3 4.9 %shard_map.97.refs_5_ = bf16[2,8,2,64,1024]{4,3,2,1,0:T(8,128)(2,1)} custom-call(s32[1]{0:T(128)} %bitcast.4.zh_ref, bf16[2,2,144,512]{3,2,1,0:T(8,128)(2,1)S(1)} %bitcast.93, bf16[2,2,144,512]{3,2,1,0:T(8,128)(2,1)S(1)} %bitcast.92, bf16[2,2,144,512]{3,2,1,0:T(8,128)(2,1)S(1)} %bitcast.91, bf16[2,2,144,512]{3,2,1,0:T(8,128)(2,1)S(1)} %bitcast.90, ...), custom_call_target="tpu_custom_call" | custom-call | flops 2415919104 | bytes 8388608 | tf_op jit(solution)/shard_map/pallas_call | solution.py:112
  197.2 8.3 %collective-permute-done.11 = bf16[2,288,512]{2,1,0:T(8,128)(2,1)S(1)} collective-permute-done((bf16[2,288,512]{2,1,0:T(8,128)(2,1)}, bf16[2,288,512]{2,1,0:T(8,128)(2,1)S(1)}, u32[]{:S(2)}, u32[]{:S(2)}) %collective-permute-start.11) | collective-permute-done | bytes 589856 | tf_op jit(solution)/shard_map/ppermute | solution.py:214
  205.5 4.9 %shard_map.98 = bf16[2,8,2,64,1024]{4,3,2,1,0:T(8,128)(2,1)} custom-call(s32[1]{0:T(128)} %bitcast.4.zh_ref, bf16[2,2,144,512]{3,2,1,0:T(8,128)(2,1)S(1)} %bitcast.80, bf16[2,2,144,512]{3,2,1,0:T(8,128)(2,1)S(1)} %bitcast.81, bf16[2,2,144,512]{3,2,1,0:T(8,128)(2,1)S(1)} %bitcast.82, ...), custom_call_target="tpu_custom_call", output_to_operand_aliasing={{}: (6, {})} | custom-call | flops 2415919104 | bytes 8388608 | tf_op jit(solution)/shard_map/pallas_call | solution.py:112
  211.1 4.6 %shard_map.100 = (bf16[2,2,144,512]{3,2,1,0:T(8,128)(2,1)S(1)}, bf16[2,2,144,512]{3,2,1,0:T(8,128)(2,1)S(1)}, bf16[2,2,144,512]{3,2,1,0:T(8,128)(2,1)}, bf16[2,2,144,512]{3,2,1,0:T(8,128)(2,1)}) custom-call(s32[1]{0:T(128)} %bitcast.4.zh_ref, bf16[16,2,64,1152]{3,2,1,0:T(8,128)(2,1)} %bitcast.95, f32[8,576,2]{2,1,0:T(8,128)S(1)} %bitcast.75), custom_call_target="tpu_custom_call" | custom-call | flops 1207959552 | bytes 8388608 | tf_op jit(solution)/shard_map/pallas_call | solution.py:50
  221.2 4.0 %collective-permute-start.18 = (bf16[2,2,144,512]{3,2,1,0:T(8,128)(2,1)}, bf16[2,2,144,512]{3,2,1,0:T(8,128)(2,1)}, u32[]{:S(2)}, u32[]{:S(2)}) collective-permute-start(bf16[2,2,144,512]{3,2,1,0:T(8,128)(2,1)} %get-tuple-element.57), channel_id=1, source_target_pairs={{0,12},{4,0},{8,4},{12,8},{1,13},{5,1},{9,5},{13,9},{2,14},{6,2},{... | collective-permute-start | bytes 1769480 | tf_op jit(solution)/shard_map/ppermute | solution.py:214
  225.1 4.6 %shard_map.99 = (bf16[2,2,144,512]{3,2,1,0:T(8,128)(2,1)S(1)}, bf16[2,2,144,512]{3,2,1,0:T(8,128)(2,1)}, bf16[2,2,144,512]{3,2,1,0:T(8,128)(2,1)}, bf16[2,2,144,512]{3,2,1,0:T(8,128)(2,1)}) custom-call(s32[1]{0:T(128)} %bitcast.4.zh_ref, bf16[16,2,64,1152]{3,2,1,0:T(8,128)(2,1)} %bitcast.96, f32[8,576,2]{2,1,0:T(8,128)S(1)} %bitcast.76), custom_call_target="tpu_custom_call" | custom-call | flops 1207959552 | bytes 8388608 | tf_op jit(solution)/shard_map/pallas_call | solution.py:50
  232.9 3.8 %collective-permute-start.14 = (bf16[2,2,144,512]{3,2,1,0:T(8,128)(2,1)}, bf16[2,2,144,512]{3,2,1,0:T(8,128)(2,1)}, u32[]{:S(2)}, u32[]{:S(2)}) collective-permute-start(bf16[2,2,144,512]{3,2,1,0:T(8,128)(2,1)} %get-tuple-element.52), channel_id=1, source_target_pairs={{0,8},{4,12},{8,0},{12,4},{1,9},{5,13},{9,1},{13,5},{2,10},{6,14},... | collective-permute-start | bytes 1769480 | tf_op jit(solution)/shard_map/ppermute | solution.py:214
  236.6 9.3 %collective-permute-done.16 = bf16[2,2,144,512]{3,2,1,0:T(8,128)(2,1)S(1)} collective-permute-done((bf16[2,2,144,512]{3,2,1,0:T(8,128)(2,1)S(1)}, bf16[2,2,144,512]{3,2,1,0:T(8,128)(2,1)S(1)}, u32[]{:S(2)}, u32[]{:S(2)}) %collective-permute-start.16) | collective-permute-done | bytes 589856 | tf_op jit(solution)/shard_map/ppermute | solution.py:214
  254.0 4.4 %all-to-all-start.2 = ((bf16[4,128,1024]{2,1,0:T(8,128)(2,1)}), bf16[4,128,1024]{2,1,0:T(8,128)(2,1)}, u32[]{:S(2)}, u32[]{:S(2)}) async-start(bf16[4,128,1024]{2,1,0:T(8,128)(2,1)} %copy.86), calls=%async_computation.2 | async-start | bytes 2097152 | tf_op jit(solution)/shard_map/all_to_all | solution.py:302
  260.6 6.4 %shard_map.101.refs_6_ = f32[2,512,384]{2,1,0:T(8,128)S(1)} custom-call(s32[1]{0:T(128)} %bitcast.5.y_ref, bf16[2,288,512]{2,1,0:T(8,128)(2,1)S(1)} %bitcast.86, bf16[2,288,512]{2,1,0:T(8,128)(2,1)S(1)} %bitcast.87, bf16[2,288,512]{2,1,0:T(8,128)(2,1)} %bitcast.36.refs_2_, bf16[2,288,512]{2,1,0:T(8,128)(2,1)} %bitcast.37.refs_3_, ...), custom_call_target="tpu_custom_call" | custom-call | flops 1811939328 | bytes 8388608 | tf_op jit(solution)/shard_map/pallas_call | solution.py:158
  267.0 5.1 %collective-permute-done.13 = bf16[2,2,144,512]{3,2,1,0:T(8,128)(2,1)S(1)} collective-permute-done((bf16[2,2,144,512]{3,2,1,0:T(8,128)(2,1)}, bf16[2,2,144,512]{3,2,1,0:T(8,128)(2,1)S(1)}, u32[]{:S(2)}, u32[]{:S(2)}) %collective-permute-start.13) | collective-permute-done | bytes 589856 | tf_op jit(solution)/shard_map/ppermute | solution.py:214
  274.5 6.4 %shard_map.102 = bf16[2,512,384]{2,1,0:T(8,128)(2,1)S(1)} custom-call(s32[1]{0:T(128)} %bitcast.5.y_ref, bf16[2,288,512]{2,1,0:T(8,128)(2,1)S(1)} %bitcast.83, bf16[2,288,512]{2,1,0:T(8,128)(2,1)S(1)} %bitcast.85, bf16[2,288,512]{2,1,0:T(8,128)(2,1)} %bitcast.32.refs_2_, bf16[2,288,512]{2,1,0:T(8,128)(2,1)} %bitcast.33.refs_3_, ...), custom_call_target="tpu_custom_call" | custom-call | flops 1811939328 | bytes 8388608 | tf_op jit(solution)/shard_map/pallas_call | solution.py:158
  281.0 3.6 %collective-permute-start.19 = (bf16[512,384]{1,0:T(8,128)(2,1)S(1)}, bf16[512,384]{1,0:T(8,128)(2,1)}, u32[]{:S(2)}, u32[]{:S(2)}) collective-permute-start(bf16[512,384]{1,0:T(8,128)(2,1)S(1)} %select_bitcast_fusion), channel_id=1, source_target_pairs={{0,128},{128,0},{1,129},{129,1},{2,130},{130,2},{3,131},{131,3},{4... | collective-permute-start | bytes 1179656 | tf_op jit(solution)/shard_map/ppermute | solution.py:299
  288.1 5.5 %collective-permute-start.12 = (bf16[128,512]{1,0:T(8,128)(2,1)S(1)}, bf16[128,512]{1,0:T(8,128)(2,1)S(1)}, u32[]{:S(2)}, u32[]{:S(2)}) collective-permute-start(bf16[128,512]{1,0:T(8,128)(2,1)S(1)} %slice.85), channel_id=1, source_target_pairs={{0,128},{128,0},{1,129},{129,1},{2,130},{130,2},{3,131},{131,3},{4... | collective-permute-start | bytes 393224 | tf_op jit(solution)/shard_map/ppermute | solution.py:306
  (129 shorter events, 68.7 us)
Async XLA Ops:
  7.2 171.7 %all-gather.2.cloned.1.call-start = ((), (), s32[]{:S(2)}) async-start(), calls=%async_computation.4 | async-start | bytes 5013504 | tf_op jit(solution)/shard_map/all_gather | solution.py:254
  12.4 9.8 %collective-permute-start = (bf16[128,576]{1,0:T(8,128)(2,1)S(1)}, bf16[128,576]{1,0:T(8,128)(2,1)S(1)}, u32[]{:S(2)}, u32[]{:S(2)}) collective-permute-start(bf16[128,576]{1,0:T(8,128)(2,1)S(1)} %pad_maximum_fusion.1), channel_id=1, source_target_pairs={{0,128},{128,0},{1,129},{129,1},{2,130},{130,2},{3,131},{131,3},{4... | collective-permute-start | bytes 442376 | tf_op jit(solution)/shard_map/ppermute | solution.py:252
  23.1 14.8 %collective-permute-start.1 = (bf16[576,384]{1,0:T(8,128)(2,1)S(1)}, bf16[576,384]{1,0:T(8,128)(2,1)S(1)}, u32[]{:S(2)}, u32[]{:S(2)}) collective-permute-start(bf16[576,384]{1,0:T(8,128)(2,1)S(1)} %broadcast_select_fusion.5), channel_id=1, source_target_pairs={{0,2},{1,3},{2,0},{3,1},{4,6},{5,7},{6,4},{7,5},{8,10},{9,11},{10,... | collective-permute-start | bytes 1327112 | tf_op jit(solution)/shard_map/ppermute | solution.py:233
  40.2 59.3 %all-to-all-start = ((bf16[4,576,384]{2,1,0:T(8,128)(2,1)}), bf16[4,576,384]{2,1,0:T(8,128)(2,1)S(1)}, u32[]{:S(2)}, u32[]{:S(2)}) async-start(bf16[4,576,384]{2,1,0:T(8,128)(2,1)} %broadcast_in_dim.51), calls=%async_computation | async-start | bytes 3538944 | tf_op jit(solution)/shard_map/all_to_all | solution.py:208
  43.8 55.7 %collective-permute-start.2 = (bf16[576,384]{1,0:T(8,128)(2,1)}, bf16[576,384]{1,0:T(8,128)(2,1)S(1)}, u32[]{:S(2)}, u32[]{:S(2)}) collective-permute-start(bf16[576,384]{1,0:T(8,128)(2,1)} %get-tuple-element.60), channel_id=1, source_target_pairs={{0,256},{256,0},{1,257},{257,1},{2,258},{258,2},{3,259},{259,3},{4... | collective-permute-start | bytes 1327112 | tf_op jit(solution)/shard_map/ppermute | solution.py:235
  99.4 16.4 %copy-start.1 = (bf16[4,576,384]{2,1,0:T(8,128)(2,1)}, bf16[4,576,384]{2,1,0:T(8,128)(2,1)S(1)}, u32[]{:S(2)}) copy-start(bf16[4,576,384]{2,1,0:T(8,128)(2,1)S(1)} %all-to-all-done) | copy-start | bytes 5308420
  99.4 16.4 %collective-permute-start.3 = (bf16[2,2,576,384]{3,2,1,0:T(8,128)(2,1)S(1)}, bf16[2,2,576,384]{3,2,1,0:T(8,128)(2,1)}, u32[]{:S(2)}, u32[]{:S(2)}) collective-permute-start(bf16[2,2,576,384]{3,2,1,0:T(8,128)(2,1)S(1)} %bitcast.77), channel_id=1, source_target_pairs={{0,128},{128,0},{1,129},{129,1},{2,130},{130,2},{3,131},{131,3},{4... | collective-permute-start | bytes 5308424 | tf_op jit(solution)/shard_map/ppermute | solution.py:258
  105.7 8.7 %collective-permute-start.4 = (bf16[512,384]{1,0:T(8,128)(2,1)}, bf16[512,384]{1,0:T(8,128)(2,1)}, u32[]{:S(2)}, u32[]{:S(2)}) collective-permute-start(bf16[512,384]{1,0:T(8,128)(2,1)} %select_bitcast_fusion.1), channel_id=1, source_target_pairs={{0,128},{128,0},{1,129},{129,1},{2,130},{130,2},{3,131},{131,3},{4... | collective-permute-start | bytes 1179656 | tf_op jit(solution)/shard_map/ppermute | solution.py:221
  109.0 27.9 %all-to-all-start.1 = ((bf16[4,576,384]{2,1,0:T(8,128)(2,1)}), bf16[4,576,384]{2,1,0:T(8,128)(2,1)}, u32[]{:S(2)}, u32[]{:S(2)}) async-start(bf16[4,576,384]{2,1,0:T(8,128)(2,1)} %broadcast_in_dim.52), calls=%async_computation.1 | async-start | bytes 3538944 | tf_op jit(solution)/shard_map/all_to_all | solution.py:208
  114.4 172.8 %reduce-scatter.2.cloned.1.call-start = ((), (), s32[]{:S(2)}) async-start(), calls=%async_computation.5 | async-start | bytes 4456448 | tf_op jit(solution)/shard_map/reduce_scatter | solution.py:284
  115.8 6.1 %copy-start.3 = (bf16[2,512,384]{2,1,0:T(8,128)(2,1)}, bf16[2,512,384]{2,1,0:T(8,128)(2,1)S(1)}, u32[]{:S(2)}) copy-start(bf16[2,512,384]{2,1,0:T(8,128)(2,1)S(1)} %pad_maximum_fusion.weight_ref) | copy-start | bytes 2359300
  122.7 17.4 %collective-permute-start.5 = (bf16[2,288,512]{2,1,0:T(8,128)(2,1)}, bf16[2,288,512]{2,1,0:T(8,128)(2,1)S(1)}, u32[]{:S(2)}, u32[]{:S(2)}) collective-permute-start(bf16[2,288,512]{2,1,0:T(8,128)(2,1)} %get-tuple-element.36), channel_id=1, source_target_pairs={{0,4},{4,8},{8,12},{12,0},{1,5},{5,9},{9,13},{13,1},{2,6},{6,10},{... | collective-permute-start | bytes 1769480 | tf_op jit(solution)/shard_map/ppermute | solution.py:214
  125.0 28.0 %collective-permute-start.6 = (bf16[2,288,512]{2,1,0:T(8,128)(2,1)}, bf16[2,288,512]{2,1,0:T(8,128)(2,1)S(1)}, u32[]{:S(2)}, u32[]{:S(2)}) collective-permute-start(bf16[2,288,512]{2,1,0:T(8,128)(2,1)} %get-tuple-element.37), channel_id=1, source_target_pairs={{0,8},{4,12},{8,0},{12,4},{1,9},{5,13},{9,1},{13,5},{2,10},{6,14},... | collective-permute-start | bytes 1769480 | tf_op jit(solution)/shard_map/ppermute | solution.py:214
  129.5 25.8 %collective-permute-start.7 = (bf16[2,288,512]{2,1,0:T(8,128)(2,1)S(1)}, bf16[2,288,512]{2,1,0:T(8,128)(2,1)S(1)}, u32[]{:S(2)}, u32[]{:S(2)}) collective-permute-start(bf16[2,288,512]{2,1,0:T(8,128)(2,1)S(1)} %get-tuple-element.38), channel_id=1, source_target_pairs={{0,12},{4,0},{8,4},{12,8},{1,13},{5,1},{9,5},{13,9},{2,14},{6,2},{... | collective-permute-start | bytes 1769480 | tf_op jit(solution)/shard_map/ppermute | solution.py:214
  153.1 16.6 %copy-start.13 = (bf16[2,288,512]{2,1,0:T(8,128)(2,1)}, bf16[2,288,512]{2,1,0:T(8,128)(2,1)S(1)}, u32[]{:S(2)}) copy-start(bf16[2,288,512]{2,1,0:T(8,128)(2,1)S(1)} %collective-permute-done.6) | copy-start | bytes 1769476
  155.4 14.3 %copy-start.15 = (bf16[2,288,512]{2,1,0:T(8,128)(2,1)}, bf16[2,288,512]{2,1,0:T(8,128)(2,1)S(1)}, u32[]{:S(2)}) copy-start(bf16[2,288,512]{2,1,0:T(8,128)(2,1)S(1)} %collective-permute-done.7) | copy-start | bytes 1769476
  155.4 7.1 %collective-permute-start.8 = (bf16[2,2,576,384]{3,2,1,0:T(8,128)(2,1)}, bf16[2,2,576,384]{3,2,1,0:T(8,128)(2,1)}, u32[]{:S(2)}, u32[]{:S(2)}) collective-permute-start(bf16[2,2,576,384]{3,2,1,0:T(8,128)(2,1)} %bitcast.7.near_ref.refs_4_), channel_id=1, source_target_pairs={{0,128},{128,0},{1,129},{129,1},{2,130},{130,2},{3,131},{131,3},{4... | collective-permute-start | bytes 5308424 | tf_op jit(solution)/shard_map/ppermute | solution.py:262
  169.7 27.4 %collective-permute-start.9 = (bf16[2,288,512]{2,1,0:T(8,128)(2,1)}, bf16[2,288,512]{2,1,0:T(8,128)(2,1)S(1)}, u32[]{:S(2)}, u32[]{:S(2)}) collective-permute-start(bf16[2,288,512]{2,1,0:T(8,128)(2,1)} %get-tuple-element.41), channel_id=1, source_target_pairs={{0,12},{4,0},{8,4},{12,8},{1,13},{5,1},{9,5},{13,9},{2,14},{6,2},{... | collective-permute-start | bytes 1769480 | tf_op jit(solution)/shard_map/ppermute | solution.py:214
  174.0 23.2 %collective-permute-start.10 = (bf16[2,288,512]{2,1,0:T(8,128)(2,1)}, bf16[2,288,512]{2,1,0:T(8,128)(2,1)S(1)}, u32[]{:S(2)}, u32[]{:S(2)}) collective-permute-start(bf16[2,288,512]{2,1,0:T(8,128)(2,1)} %get-tuple-element.42), channel_id=1, source_target_pairs={{0,8},{4,12},{8,0},{12,4},{1,9},{5,13},{9,1},{13,5},{2,10},{6,14},... | collective-permute-start | bytes 1769480 | tf_op jit(solution)/shard_map/ppermute | solution.py:214
  176.7 28.8 %collective-permute-start.11 = (bf16[2,288,512]{2,1,0:T(8,128)(2,1)}, bf16[2,288,512]{2,1,0:T(8,128)(2,1)S(1)}, u32[]{:S(2)}, u32[]{:S(2)}) collective-permute-start(bf16[2,288,512]{2,1,0:T(8,128)(2,1)} %get-tuple-element.43), channel_id=1, source_target_pairs={{0,4},{4,8},{8,12},{12,0},{1,5},{5,9},{9,13},{13,1},{2,6},{6,10},{... | collective-permute-start | bytes 1769480 | tf_op jit(solution)/shard_map/ppermute | solution.py:214
  216.5 29.4 %collective-permute-start.16 = (bf16[2,2,144,512]{3,2,1,0:T(8,128)(2,1)S(1)}, bf16[2,2,144,512]{3,2,1,0:T(8,128)(2,1)S(1)}, u32[]{:S(2)}, u32[]{:S(2)}) collective-permute-start(bf16[2,2,144,512]{3,2,1,0:T(8,128)(2,1)S(1)} %get-tuple-element.55), channel_id=1, source_target_pairs={{0,4},{4,8},{8,12},{12,0},{1,5},{5,9},{9,13},{13,1},{2,6},{6,10},{... | collective-permute-start | bytes 1769480 | tf_op jit(solution)/shard_map/ppermute | solution.py:214
  218.4 40.0 %collective-permute-start.17 = (bf16[2,2,144,512]{3,2,1,0:T(8,128)(2,1)}, bf16[2,2,144,512]{3,2,1,0:T(8,128)(2,1)}, u32[]{:S(2)}, u32[]{:S(2)}) collective-permute-start(bf16[2,2,144,512]{3,2,1,0:T(8,128)(2,1)} %get-tuple-element.56), channel_id=1, source_target_pairs={{0,8},{4,12},{8,0},{12,4},{1,9},{5,13},{9,1},{13,5},{2,10},{6,14},... | collective-permute-start | bytes 1769480 | tf_op jit(solution)/shard_map/ppermute | solution.py:214
  221.2 37.2 %collective-permute-start.18 = (bf16[2,2,144,512]{3,2,1,0:T(8,128)(2,1)}, bf16[2,2,144,512]{3,2,1,0:T(8,128)(2,1)}, u32[]{:S(2)}, u32[]{:S(2)}) collective-permute-start(bf16[2,2,144,512]{3,2,1,0:T(8,128)(2,1)} %get-tuple-element.57), channel_id=1, source_target_pairs={{0,12},{4,0},{8,4},{12,8},{1,13},{5,1},{9,5},{13,9},{2,14},{6,2},{... | collective-permute-start | bytes 1769480 | tf_op jit(solution)/shard_map/ppermute | solution.py:214
  230.6 41.5 %collective-permute-start.13 = (bf16[2,2,144,512]{3,2,1,0:T(8,128)(2,1)}, bf16[2,2,144,512]{3,2,1,0:T(8,128)(2,1)S(1)}, u32[]{:S(2)}, u32[]{:S(2)}) collective-permute-start(bf16[2,2,144,512]{3,2,1,0:T(8,128)(2,1)} %get-tuple-element.51), channel_id=1, source_target_pairs={{0,4},{4,8},{8,12},{12,0},{1,5},{5,9},{9,13},{13,1},{2,6},{6,10},{... | collective-permute-start | bytes 1769480 | tf_op jit(solution)/shard_map/ppermute | solution.py:214
  232.9 39.2 %collective-permute-start.14 = (bf16[2,2,144,512]{3,2,1,0:T(8,128)(2,1)}, bf16[2,2,144,512]{3,2,1,0:T(8,128)(2,1)}, u32[]{:S(2)}, u32[]{:S(2)}) collective-permute-start(bf16[2,2,144,512]{3,2,1,0:T(8,128)(2,1)} %get-tuple-element.52), channel_id=1, source_target_pairs={{0,8},{4,12},{8,0},{12,4},{1,9},{5,13},{9,1},{13,5},{2,10},{6,14},... | collective-permute-start | bytes 1769480 | tf_op jit(solution)/shard_map/ppermute | solution.py:214
  246.7 27.8 %collective-permute-start.15 = (bf16[2,2,144,512]{3,2,1,0:T(8,128)(2,1)}, bf16[2,2,144,512]{3,2,1,0:T(8,128)(2,1)}, u32[]{:S(2)}, u32[]{:S(2)}) collective-permute-start(bf16[2,2,144,512]{3,2,1,0:T(8,128)(2,1)} %get-tuple-element.53), channel_id=1, source_target_pairs={{0,12},{4,0},{8,4},{12,8},{1,13},{5,1},{9,5},{13,9},{2,14},{6,2},{... | collective-permute-start | bytes 1769480 | tf_op jit(solution)/shard_map/ppermute | solution.py:214
  251.3 7.1 %copy-start.2 = (bf16[4,576,384]{2,1,0:T(8,128)(2,1)S(1)}, bf16[4,576,384]{2,1,0:T(8,128)(2,1)}, u32[]{:S(2)}) copy-start(bf16[4,576,384]{2,1,0:T(8,128)(2,1)} %copy-done.1) | copy-start | bytes 5308420
  254.0 30.6 %all-to-all-start.2 = ((bf16[4,128,1024]{2,1,0:T(8,128)(2,1)}), bf16[4,128,1024]{2,1,0:T(8,128)(2,1)}, u32[]{:S(2)}, u32[]{:S(2)}) async-start(bf16[4,128,1024]{2,1,0:T(8,128)(2,1)} %copy.86), calls=%async_computation.2 | async-start | bytes 2097152 | tf_op jit(solution)/shard_map/all_to_all | solution.py:302
  260.6 14.0 %copy-start.6 = (bf16[2,2,144,512]{3,2,1,0:T(8,128)(2,1)S(1)}, bf16[2,2,144,512]{3,2,1,0:T(8,128)(2,1)}, u32[]{:S(2)}) copy-start(bf16[2,2,144,512]{3,2,1,0:T(8,128)(2,1)} %copy-done.5) | copy-start | bytes 1769476
  281.0 5.1 %collective-permute-start.19 = (bf16[512,384]{1,0:T(8,128)(2,1)S(1)}, bf16[512,384]{1,0:T(8,128)(2,1)}, u32[]{:S(2)}, u32[]{:S(2)}) collective-permute-start(bf16[512,384]{1,0:T(8,128)(2,1)S(1)} %select_bitcast_fusion), channel_id=1, source_target_pairs={{0,128},{128,0},{1,129},{129,1},{2,130},{130,2},{3,131},{131,3},{4... | collective-permute-start | bytes 1179656 | tf_op jit(solution)/shard_map/ppermute | solution.py:299
  286.0 9.5 %copy-start.19 = (bf16[2,64,1024]{2,1,0:T(8,128)(2,1)S(1)}, bf16[2,64,1024]{2,1,0:T(8,128)(2,1)}, u32[]{:S(2)}) copy-start(bf16[2,64,1024]{2,1,0:T(8,128)(2,1)} %param.15) | copy-start | bytes 786436
  288.1 6.4 %collective-permute-start.12 = (bf16[128,512]{1,0:T(8,128)(2,1)S(1)}, bf16[128,512]{1,0:T(8,128)(2,1)S(1)}, u32[]{:S(2)}, u32[]{:S(2)}) collective-permute-start(bf16[128,512]{1,0:T(8,128)(2,1)S(1)} %slice.85), channel_id=1, source_target_pairs={{0,128},{128,0},{1,129},{129,1},{2,130},{130,2},{3,131},{131,3},{4... | collective-permute-start | bytes 393224 | tf_op jit(solution)/shard_map/ppermute | solution.py:306
  (16 other events, 25.0 us)
Sparse Core Ops, SparseCore 0:
  23.2 108.5 all-gather.1
  210.5 70.8 reduce-scatter.1

commit v8 on v7

--- a/solution.py
+++ b/solution.py
@@ -231,6 +231,7 @@
     xh = x // 2
     keep, send = by(xh, halves[0], halves[1])
     taken = lax.ppermute(send, "x", [(i, (i + 2) % nx) for i in range(nx)])
+    taken, weight = lax.optimization_barrier((taken, weight))
     stay, leave = by(xh ^ zh, keep, taken)
     crossed = lax.ppermute(leave, "zh", SWAP)
     near = gather(stay)
@@ -251,6 +252,7 @@
     mine, theirs = by(co, own_part[:, 0], own_part[:, 1])
     theirs = lax.ppermute(jnp.concatenate([theirs, table], axis=1), "co", SWAP)
     line = jnp.concatenate([mine, theirs[:, :eighth], table, theirs[:, eighth:]], axis=1)
+    line, stay = lax.optimization_barrier((line, stay))
     line = lax.all_gather(line, ("zh", "zl"), axis=0, tiled=True)
 
     split = (2, batches, nzl * capacity, eighth)

time: 305 us -> 306 us (level)
    ppermute x1, starting transfers between devices: 8.8 us -> 1.91 us  [on_device(): theirs = lax.ppermute(jnp.concatenate([theirs, table], axis=1), 'co', SWAP)]
    ppermute x1, starting transfers between devices: 1.91 us -> 8.78 us  [on_device(): weight = jnp.stack(by(co, mine, lax.ppermute(theirs, 'co', SWAP)))]
    unnamed x49 -> x51, local copies, waits for them, and re-layouts: 12.4 us -> 13.6 us
  transfers between devices with their start and end apart: 25 -> 25, of which waited for: 12 -> 10; matrix products, arithmetic and copies ran while one was open for 9% -> 10% of each run, Pallas kernels for 13% -> 13%
where the time goes in v8:
time: 306 us; the launch traced here: 304 us
  waiting for transfers between devices  107 us (35%)
  starting transfers between devices  87.3 us (29%)
  Pallas kernels  43.6 us (14%)
  local copies, waits for them, and re-layouts  33.2 us (11%)
  between operations  14.7 us (5%)
  other arithmetic  14.4 us (5%)
    ppermute x1, waiting for transfers between devices, on_device(): crossed = lax.ppermute(leave, 'zh', SWAP)  44.5 us
    ppermute x12, waiting for transfers between devices, along_y(): lax.ppermute(v, 'y', [(i, (i + d) % ny) for i in range(ny)])  42.6 us
    ppermute x12, starting transfers between devices, along_y(): lax.ppermute(v, 'y', [(i, (i + d) % ny) for i in range(ny)])  33.7 us
    unnamed x51, local copies, waits for them, and re-layouts  13.6 us
    pallas_call x2, Pallas kernels, weight_sum(): call(body, (4,), [pl.BlockSpec((2, part, width), lambda d, y: (0, 0, 0))]...  12.7 us
    pallas_call x2, Pallas kernels, rows_back(): call(body, (4,), [piece, piece, pl.BlockSpec(weight.shape, lambda d, y: (...  11.9 us
    ppermute x1, starting transfers between devices, on_device(): crossed = lax.ppermute(leave, 'zh', SWAP)  10.5 us
    ppermute x1, waiting for transfers between devices, on_device(): taken = lax.ppermute(send, 'x', [(i, (i + 2) % nx) for i in range(nx)])  10 us
  transfers between devices with their start and end apart: 25, of which 10 were waited for; matrix products, arithmetic and copies ran while one was open for 10% of the time, Pallas kernels for 13%

profile of v8, /device:TPU:1, one launch (start us, length us, event | category | flops | bytes accessed | tf_op | source)
XLA Modules:
  0.0 303.6 jit_solution(7357054350037855341)
XLA Ops:
  9.2 8.8 %collective-permute-start.2 = (bf16[512,384]{1,0:T(8,128)(2,1)}, bf16[512,384]{1,0:T(8,128)(2,1)}, u32[]{:S(2)}, u32[]{:S(2)}) collective-permute-start(bf16[512,384]{1,0:T(8,128)(2,1)} %select_bitcast_fusion.1), channel_id=1, source_target_pairs={{0,128},{128,0},{1,129},{129,1},{2,130},{130,2},{3,131},{131,3},{4... | collective-permute-start | bytes 1179656 | tf_op jit(solution)/shard_map/ppermute | solution.py:221
  18.1 2.8 fusion.1
  31.4 10.0 %collective-permute-done.1 = bf16[576,384]{1,0:T(8,128)(2,1)} collective-permute-done((bf16[576,384]{1,0:T(8,128)(2,1)}, bf16[576,384]{1,0:T(8,128)(2,1)}, u32[]{:S(2)}, u32[]{:S(2)}) %collective-permute-start.1) | collective-permute-done | bytes 442400 | tf_op jit(solution)/shard_map/ppermute | solution.py:233
  44.0 3.6 %all-to-all-start = ((bf16[4,576,384]{2,1,0:T(8,128)(2,1)}), bf16[4,576,384]{2,1,0:T(8,128)(2,1)S(1)}, u32[]{:S(2)}, u32[]{:S(2)}) async-start(bf16[4,576,384]{2,1,0:T(8,128)(2,1)} %broadcast_in_dim.51), calls=%async_computation | async-start | bytes 3538944 | tf_op jit(solution)/shard_map/all_to_all | solution.py:208
  47.6 10.5 %collective-permute-start.3 = (bf16[576,384]{1,0:T(8,128)(2,1)S(1)}, bf16[576,384]{1,0:T(8,128)(2,1)}, u32[]{:S(2)}, u32[]{:S(2)}) collective-permute-start(bf16[576,384]{1,0:T(8,128)(2,1)S(1)} %get-tuple-element.66), channel_id=1, source_target_pairs={{0,256},{256,0},{1,257},{257,1},{2,258},{258,2},{3,259},{259,3},{4... | collective-permute-start | bytes 1327112 | tf_op jit(solution)/shard_map/ppermute | solution.py:236
  58.1 44.5 %collective-permute-done.3 = bf16[576,384]{1,0:T(8,128)(2,1)} collective-permute-done((bf16[576,384]{1,0:T(8,128)(2,1)S(1)}, bf16[576,384]{1,0:T(8,128)(2,1)}, u32[]{:S(2)}, u32[]{:S(2)}) %collective-permute-start.3) | collective-permute-done | bytes 442400 | tf_op jit(solution)/shard_map/ppermute | solution.py:236
  102.6 3.4 %collective-permute-start.4 = (bf16[2,2,576,384]{3,2,1,0:T(8,128)(2,1)S(1)}, bf16[2,2,576,384]{3,2,1,0:T(8,128)(2,1)}, u32[]{:S(2)}, u32[]{:S(2)}) collective-permute-start(bf16[2,2,576,384]{3,2,1,0:T(8,128)(2,1)S(1)} %bitcast.77), channel_id=1, source_target_pairs={{0,128},{128,0},{1,129},{129,1},{2,130},{130,2},{3,131},{131,3},{4... | collective-permute-start | bytes 5308424 | tf_op jit(solution)/shard_map/ppermute | solution.py:260
  108.4 4.4 %all-to-all-start.1 = ((bf16[4,576,384]{2,1,0:T(8,128)(2,1)}), bf16[4,576,384]{2,1,0:T(8,128)(2,1)}, u32[]{:S(2)}, u32[]{:S(2)}) async-start(bf16[4,576,384]{2,1,0:T(8,128)(2,1)} %broadcast_in_dim.52), calls=%async_computation.1 | async-start | bytes 3538944 | tf_op jit(solution)/shard_map/all_to_all | solution.py:208
  114.0 5.8 %shard_map.95 = (bf16[2,288,512]{2,1,0:T(8,128)(2,1)S(1)}, bf16[2,288,512]{2,1,0:T(8,128)(2,1)}, bf16[2,288,512]{2,1,0:T(8,128)(2,1)}, bf16[2,288,512]{2,1,0:T(8,128)(2,1)S(1)}) custom-call(s32[1]{0:T(128)} %bitcast.9.y_ref, bf16[2,2,576,384]{3,2,1,0:T(8,128)(2,1)S(1)} %bitcast.78, bf16[2,2,576,384]{3,2,1,0:T(8,128)(2,1)} %collective-permute-done.4.other_ref.refs_5_, ...), custom_call_target="tpu_custom_call" | custom-call | flops 1811939328 | bytes 8388608 | tf_op jit(solution)/shard_map/pallas_call | solution.py:84
  122.6 2.8 collective-permute-start.6
  125.4 3.7 %collective-permute-start.7 = (bf16[2,288,512]{2,1,0:T(8,128)(2,1)S(1)}, bf16[2,288,512]{2,1,0:T(8,128)(2,1)S(1)}, u32[]{:S(2)}, u32[]{:S(2)}) collective-permute-start(bf16[2,288,512]{2,1,0:T(8,128)(2,1)S(1)} %get-tuple-element.44), channel_id=1, source_target_pairs={{0,12},{4,0},{8,4},{12,8},{1,13},{5,1},{9,5},{13,9},{2,14},{6,2},{... | collective-permute-start | bytes 1769480 | tf_op jit(solution)/shard_map/ppermute | solution.py:214
  129.1 6.7 %all-to-all-done.1 = bf16[4,576,384]{2,1,0:T(8,128)(2,1)} async-done(((bf16[4,576,384]{2,1,0:T(8,128)(2,1)}), bf16[4,576,384]{2,1,0:T(8,128)(2,1)}, u32[]{:S(2)}, u32[]{:S(2)}) %all-to-all-start.1) | async-done | bytes 1769504 | tf_op jit(solution)/shard_map/all_to_all | solution.py:208
  135.8 15.6 %collective-permute-done.5 = bf16[2,288,512]{2,1,0:T(8,128)(2,1)S(1)} collective-permute-done((bf16[2,288,512]{2,1,0:T(8,128)(2,1)}, bf16[2,288,512]{2,1,0:T(8,128)(2,1)S(1)}, u32[]{:S(2)}, u32[]{:S(2)}) %collective-permute-start.5) | collective-permute-done | bytes 589856 | tf_op jit(solution)/shard_map/ppermute | solution.py:214
  153.6 3.2 %collective-permute-start.8 = (bf16[2,2,576,384]{3,2,1,0:T(8,128)(2,1)}, bf16[2,2,576,384]{3,2,1,0:T(8,128)(2,1)}, u32[]{:S(2)}, u32[]{:S(2)}) collective-permute-start(bf16[2,2,576,384]{3,2,1,0:T(8,128)(2,1)} %bitcast.11.near_ref.refs_4_), channel_id=1, source_target_pairs={{0,128},{128,0},{1,129},{129,1},{2,130},{130,2},{3,131},{131,3},{4... | collective-permute-start | bytes 5308424 | tf_op jit(solution)/shard_map/ppermute | solution.py:264
  156.8 3.6 %collective-permute-done.8.other_ref.refs_5_ = bf16[2,2,576,384]{3,2,1,0:T(8,128)(2,1)} collective-permute-done((bf16[2,2,576,384]{3,2,1,0:T(8,128)(2,1)}, bf16[2,2,576,384]{3,2,1,0:T(8,128)(2,1)}, u32[]{:S(2)}, u32[]{:S(2)}) %collective-permute-start.8) | collective-permute-done | bytes 1769504 | tf_op jit(solution)/shard_map/ppermute | solution.py:264
  161.6 6.1 %shard_map.96 = (bf16[2,288,512]{2,1,0:T(8,128)(2,1)S(1)}, bf16[2,288,512]{2,1,0:T(8,128)(2,1)}, bf16[2,288,512]{2,1,0:T(8,128)(2,1)}, bf16[2,288,512]{2,1,0:T(8,128)(2,1)}) custom-call(s32[1]{0:T(128)} %bitcast.9.y_ref, bf16[2,2,576,384]{3,2,1,0:T(8,128)(2,1)} %bitcast.11.near_ref.refs_4_, ...), custom_call_target="tpu_custom_call" | custom-call | flops 1811939328 | bytes 8388608 | tf_op jit(solution)/shard_map/pallas_call | solution.py:84
  167.7 4.3 %collective-permute-start.9 = (bf16[2,288,512]{2,1,0:T(8,128)(2,1)}, bf16[2,288,512]{2,1,0:T(8,128)(2,1)S(1)}, u32[]{:S(2)}, u32[]{:S(2)}) collective-permute-start(bf16[2,288,512]{2,1,0:T(8,128)(2,1)} %get-tuple-element.47), channel_id=1, source_target_pairs={{0,12},{4,0},{8,4},{12,8},{1,13},{5,1},{9,5},{13,9},{2,14},{6,2},{... | collective-permute-start | bytes 1769480 | tf_op jit(solution)/shard_map/ppermute | solution.py:214
  190.0 4.9 %shard_map.97.refs_5_ = bf16[2,8,2,64,1024]{4,3,2,1,0:T(8,128)(2,1)} custom-call(s32[1]{0:T(128)} %bitcast.8.zh_ref, bf16[2,2,144,512]{3,2,1,0:T(8,128)(2,1)S(1)} %bitcast.93, bf16[2,2,144,512]{3,2,1,0:T(8,128)(2,1)S(1)} %bitcast.92, bf16[2,2,144,512]{3,2,1,0:T(8,128)(2,1)S(1)} %bitcast.91, bf16[2,2,144,512]{3,2,1,0:T(8,128)(2,1)S(1)} %bitcast.90, ...), custom_call_target="tpu_custom_call" | custom-call | flops 2415919104 | bytes 8388608 | tf_op jit(solution)/shard_map/pallas_call | solution.py:112
  194.9 8.5 %collective-permute-done.11 = bf16[2,288,512]{2,1,0:T(8,128)(2,1)S(1)} collective-permute-done((bf16[2,288,512]{2,1,0:T(8,128)(2,1)}, bf16[2,288,512]{2,1,0:T(8,128)(2,1)S(1)}, u32[]{:S(2)}, u32[]{:S(2)}) %collective-permute-start.11) | collective-permute-done | bytes 589856 | tf_op jit(solution)/shard_map/ppermute | solution.py:214
  203.4 4.9 %shard_map.98 = bf16[2,8,2,64,1024]{4,3,2,1,0:T(8,128)(2,1)} custom-call(s32[1]{0:T(128)} %bitcast.8.zh_ref, bf16[2,2,144,512]{3,2,1,0:T(8,128)(2,1)S(1)} %bitcast.80, bf16[2,2,144,512]{3,2,1,0:T(8,128)(2,1)S(1)} %bitcast.81, bf16[2,2,144,512]{3,2,1,0:T(8,128)(2,1)S(1)} %bitcast.82, ...), custom_call_target="tpu_custom_call", output_to_operand_aliasing={{}: (6, {})} | custom-call | flops 2415919104 | bytes 8388608 | tf_op jit(solution)/shard_map/pallas_call | solution.py:112
  209.0 4.6 %shard_map.100 = (bf16[2,2,144,512]{3,2,1,0:T(8,128)(2,1)S(1)}, bf16[2,2,144,512]{3,2,1,0:T(8,128)(2,1)S(1)}, bf16[2,2,144,512]{3,2,1,0:T(8,128)(2,1)}, bf16[2,2,144,512]{3,2,1,0:T(8,128)(2,1)}) custom-call(s32[1]{0:T(128)} %bitcast.8.zh_ref, bf16[16,2,64,1152]{3,2,1,0:T(8,128)(2,1)} %bitcast.95, f32[8,576,2]{2,1,0:T(8,128)S(1)} %bitcast.75), custom_call_target="tpu_custom_call" | custom-call | flops 1207959552 | bytes 8388608 | tf_op jit(solution)/shard_map/pallas_call | solution.py:50
  218.9 4.0 %collective-permute-start.18 = (bf16[2,2,144,512]{3,2,1,0:T(8,128)(2,1)}, bf16[2,2,144,512]{3,2,1,0:T(8,128)(2,1)}, u32[]{:S(2)}, u32[]{:S(2)}) collective-permute-start(bf16[2,2,144,512]{3,2,1,0:T(8,128)(2,1)} %get-tuple-element.63), channel_id=1, source_target_pairs={{0,12},{4,0},{8,4},{12,8},{1,13},{5,1},{9,5},{13,9},{2,14},{6,2},{... | collective-permute-start | bytes 1769480 | tf_op jit(solution)/shard_map/ppermute | solution.py:214
  222.9 4.6 %shard_map.99 = (bf16[2,2,144,512]{3,2,1,0:T(8,128)(2,1)S(1)}, bf16[2,2,144,512]{3,2,1,0:T(8,128)(2,1)}, bf16[2,2,144,512]{3,2,1,0:T(8,128)(2,1)}, bf16[2,2,144,512]{3,2,1,0:T(8,128)(2,1)}) custom-call(s32[1]{0:T(128)} %bitcast.8.zh_ref, bf16[16,2,64,1152]{3,2,1,0:T(8,128)(2,1)} %bitcast.96, f32[8,576,2]{2,1,0:T(8,128)S(1)} %bitcast.76), custom_call_target="tpu_custom_call" | custom-call | flops 1207959552 | bytes 8388608 | tf_op jit(solution)/shard_map/pallas_call | solution.py:50
  230.8 3.7 %collective-permute-start.14 = (bf16[2,2,144,512]{3,2,1,0:T(8,128)(2,1)}, bf16[2,2,144,512]{3,2,1,0:T(8,128)(2,1)}, u32[]{:S(2)}, u32[]{:S(2)}) collective-permute-start(bf16[2,2,144,512]{3,2,1,0:T(8,128)(2,1)} %get-tuple-element.58), channel_id=1, source_target_pairs={{0,8},{4,12},{8,0},{12,4},{1,9},{5,13},{9,1},{13,5},{2,10},{6,14},... | collective-permute-start | bytes 1769480 | tf_op jit(solution)/shard_map/ppermute | solution.py:214
  234.5 9.4 %collective-permute-done.16 = bf16[2,2,144,512]{3,2,1,0:T(8,128)(2,1)S(1)} collective-permute-done((bf16[2,2,144,512]{3,2,1,0:T(8,128)(2,1)S(1)}, bf16[2,2,144,512]{3,2,1,0:T(8,128)(2,1)S(1)}, u32[]{:S(2)}, u32[]{:S(2)}) %collective-permute-start.16) | collective-permute-done | bytes 589856 | tf_op jit(solution)/shard_map/ppermute | solution.py:214
  249.3 2.7 copy.86
  251.9 4.3 %all-to-all-start.2 = ((bf16[4,128,1024]{2,1,0:T(8,128)(2,1)}), bf16[4,128,1024]{2,1,0:T(8,128)(2,1)}, u32[]{:S(2)}, u32[]{:S(2)}) async-start(bf16[4,128,1024]{2,1,0:T(8,128)(2,1)} %copy.86), calls=%async_computation.2 | async-start | bytes 2097152 | tf_op jit(solution)/shard_map/all_to_all | solution.py:304
  258.4 6.4 %shard_map.101.refs_6_ = f32[2,512,384]{2,1,0:T(8,128)S(1)} custom-call(s32[1]{0:T(128)} %bitcast.9.y_ref, bf16[2,288,512]{2,1,0:T(8,128)(2,1)S(1)} %bitcast.86, bf16[2,288,512]{2,1,0:T(8,128)(2,1)S(1)} %bitcast.87, bf16[2,288,512]{2,1,0:T(8,128)(2,1)} %bitcast.36.refs_2_, bf16[2,288,512]{2,1,0:T(8,128)(2,1)} %bitcast.37.refs_3_, ...), custom_call_target="tpu_custom_call" | custom-call | flops 1811939328 | bytes 8388608 | tf_op jit(solution)/shard_map/pallas_call | solution.py:158
  264.8 5.2 %collective-permute-done.13 = bf16[2,2,144,512]{3,2,1,0:T(8,128)(2,1)S(1)} collective-permute-done((bf16[2,2,144,512]{3,2,1,0:T(8,128)(2,1)}, bf16[2,2,144,512]{3,2,1,0:T(8,128)(2,1)S(1)}, u32[]{:S(2)}, u32[]{:S(2)}) %collective-permute-start.13) | collective-permute-done | bytes 589856 | tf_op jit(solution)/shard_map/ppermute | solution.py:214
  272.5 6.4 %shard_map.102 = bf16[2,512,384]{2,1,0:T(8,128)(2,1)S(1)} custom-call(s32[1]{0:T(128)} %bitcast.9.y_ref, bf16[2,288,512]{2,1,0:T(8,128)(2,1)S(1)} %bitcast.83, bf16[2,288,512]{2,1,0:T(8,128)(2,1)S(1)} %bitcast.85, bf16[2,288,512]{2,1,0:T(8,128)(2,1)} %bitcast.32.refs_2_, bf16[2,288,512]{2,1,0:T(8,128)(2,1)} %bitcast.33.refs_3_, ...), custom_call_target="tpu_custom_call" | custom-call | flops 1811939328 | bytes 8388608 | tf_op jit(solution)/shard_map/pallas_call | solution.py:158
  278.9 3.6 %collective-permute-start.19 = (bf16[512,384]{1,0:T(8,128)(2,1)S(1)}, bf16[512,384]{1,0:T(8,128)(2,1)}, u32[]{:S(2)}, u32[]{:S(2)}) collective-permute-start(bf16[512,384]{1,0:T(8,128)(2,1)S(1)} %select_bitcast_fusion), channel_id=1, source_target_pairs={{0,128},{128,0},{1,129},{129,1},{2,130},{130,2},{3,131},{131,3},{4... | collective-permute-start | bytes 1179656 | tf_op jit(solution)/shard_map/ppermute | solution.py:301
  286.0 8.0 %collective-permute-start.12 = (bf16[128,512]{1,0:T(8,128)(2,1)S(1)}, bf16[128,512]{1,0:T(8,128)(2,1)S(1)}, u32[]{:S(2)}, u32[]{:S(2)}) collective-permute-start(bf16[128,512]{1,0:T(8,128)(2,1)S(1)} %slice.85), channel_id=1, source_target_pairs={{0,128},{128,0},{1,129},{129,1},{2,130},{130,2},{3,131},{131,3},{4... | collective-permute-start | bytes 393224 | tf_op jit(solution)/shard_map/ppermute | solution.py:308
  (131 shorter events, 68.0 us)
Async XLA Ops:
  7.2 15.8 %copy-start = (bf16[2,64,4096]{2,1,0:T(8,128)(2,1)S(1)}, bf16[2,64,4096]{2,1,0:T(8,128)(2,1)}, u32[]{:S(2)}) copy-start(bf16[2,64,4096]{2,1,0:T(8,128)(2,1)} %param.8) | copy-start | bytes 3145732
  7.2 169.4 %all-gather.2.cloned.1.call-start = ((), (), s32[]{:S(2)}) async-start(), calls=%async_computation.4 | async-start | bytes 5013504 | tf_op jit(solution)/shard_map/all_gather | solution.py:256
  9.2 20.1 %collective-permute-start.2 = (bf16[512,384]{1,0:T(8,128)(2,1)}, bf16[512,384]{1,0:T(8,128)(2,1)}, u32[]{:S(2)}, u32[]{:S(2)}) collective-permute-start(bf16[512,384]{1,0:T(8,128)(2,1)} %select_bitcast_fusion.1), channel_id=1, source_target_pairs={{0,128},{128,0},{1,129},{129,1},{2,130},{130,2},{3,131},{131,3},{4... | collective-permute-start | bytes 1179656 | tf_op jit(solution)/shard_map/ppermute | solution.py:221
  21.9 7.5 %copy-start.19 = (bf16[1,1024,384]{2,1,0:T(8,128)(2,1)S(1)}, bf16[1,1024,384]{2,1,0:T(8,128)(2,1)}, u32[]{:S(2)}) copy-start(bf16[1,1024,384]{2,1,0:T(8,128)(2,1)} %param.13) | copy-start | bytes 2359300
  24.6 3.9 %collective-permute-start = (bf16[128,576]{1,0:T(8,128)(2,1)}, bf16[128,576]{1,0:T(8,128)(2,1)S(1)}, u32[]{:S(2)}, u32[]{:S(2)}) collective-permute-start(bf16[128,576]{1,0:T(8,128)(2,1)} %pad_maximum_fusion.1), channel_id=1, source_target_pairs={{0,128},{128,0},{1,129},{129,1},{2,130},{130,2},{3,131},{131,3},{4... | collective-permute-start | bytes 442376 | tf_op jit(solution)/shard_map/ppermute | solution.py:253
  26.5 14.9 %collective-permute-start.1 = (bf16[576,384]{1,0:T(8,128)(2,1)}, bf16[576,384]{1,0:T(8,128)(2,1)}, u32[]{:S(2)}, u32[]{:S(2)}) collective-permute-start(bf16[576,384]{1,0:T(8,128)(2,1)} %broadcast_select_fusion.5), channel_id=1, source_target_pairs={{0,2},{1,3},{2,0},{3,1},{4,6},{5,7},{6,4},{7,5},{8,10},{9,11},{10,... | collective-permute-start | bytes 1327112 | tf_op jit(solution)/shard_map/ppermute | solution.py:233
  44.0 58.6 %all-to-all-start = ((bf16[4,576,384]{2,1,0:T(8,128)(2,1)}), bf16[4,576,384]{2,1,0:T(8,128)(2,1)S(1)}, u32[]{:S(2)}, u32[]{:S(2)}) async-start(bf16[4,576,384]{2,1,0:T(8,128)(2,1)} %broadcast_in_dim.51), calls=%async_computation | async-start | bytes 3538944 | tf_op jit(solution)/shard_map/all_to_all | solution.py:208
  47.6 55.0 %collective-permute-start.3 = (bf16[576,384]{1,0:T(8,128)(2,1)S(1)}, bf16[576,384]{1,0:T(8,128)(2,1)}, u32[]{:S(2)}, u32[]{:S(2)}) collective-permute-start(bf16[576,384]{1,0:T(8,128)(2,1)S(1)} %get-tuple-element.66), channel_id=1, source_target_pairs={{0,256},{256,0},{1,257},{257,1},{2,258},{258,2},{3,259},{259,3},{4... | collective-permute-start | bytes 1327112 | tf_op jit(solution)/shard_map/ppermute | solution.py:236
  102.6 10.3 %copy-start.1 = (bf16[4,576,384]{2,1,0:T(8,128)(2,1)}, bf16[4,576,384]{2,1,0:T(8,128)(2,1)S(1)}, u32[]{:S(2)}) copy-start(bf16[4,576,384]{2,1,0:T(8,128)(2,1)S(1)} %all-to-all-done) | copy-start | bytes 5308420
  102.6 10.3 %collective-permute-start.4 = (bf16[2,2,576,384]{3,2,1,0:T(8,128)(2,1)S(1)}, bf16[2,2,576,384]{3,2,1,0:T(8,128)(2,1)}, u32[]{:S(2)}, u32[]{:S(2)}) collective-permute-start(bf16[2,2,576,384]{3,2,1,0:T(8,128)(2,1)S(1)} %bitcast.77), channel_id=1, source_target_pairs={{0,128},{128,0},{1,129},{129,1},{2,130},{130,2},{3,131},{131,3},{4... | collective-permute-start | bytes 5308424 | tf_op jit(solution)/shard_map/ppermute | solution.py:260
  108.4 27.4 %all-to-all-start.1 = ((bf16[4,576,384]{2,1,0:T(8,128)(2,1)}), bf16[4,576,384]{2,1,0:T(8,128)(2,1)}, u32[]{:S(2)}, u32[]{:S(2)}) async-start(bf16[4,576,384]{2,1,0:T(8,128)(2,1)} %broadcast_in_dim.52), calls=%async_computation.1 | async-start | bytes 3538944 | tf_op jit(solution)/shard_map/all_to_all | solution.py:208
  112.8 172.3 %reduce-scatter.2.cloned.1.call-start = ((), (), s32[]{:S(2)}) async-start(), calls=%async_computation.5 | async-start | bytes 4456448 | tf_op jit(solution)/shard_map/reduce_scatter | solution.py:286
  120.7 30.7 %collective-permute-start.5 = (bf16[2,288,512]{2,1,0:T(8,128)(2,1)}, bf16[2,288,512]{2,1,0:T(8,128)(2,1)S(1)}, u32[]{:S(2)}, u32[]{:S(2)}) collective-permute-start(bf16[2,288,512]{2,1,0:T(8,128)(2,1)} %get-tuple-element.42), channel_id=1, source_target_pairs={{0,4},{4,8},{8,12},{12,0},{1,5},{5,9},{9,13},{13,1},{2,6},{6,10},{... | collective-permute-start | bytes 1769480 | tf_op jit(solution)/shard_map/ppermute | solution.py:214
  122.6 29.7 %collective-permute-start.6 = (bf16[2,288,512]{2,1,0:T(8,128)(2,1)}, bf16[2,288,512]{2,1,0:T(8,128)(2,1)S(1)}, u32[]{:S(2)}, u32[]{:S(2)}) collective-permute-start(bf16[2,288,512]{2,1,0:T(8,128)(2,1)} %get-tuple-element.43), channel_id=1, source_target_pairs={{0,8},{4,12},{8,0},{12,4},{1,9},{5,13},{9,1},{13,5},{2,10},{6,14},... | collective-permute-start | bytes 1769480 | tf_op jit(solution)/shard_map/ppermute | solution.py:214
  125.4 28.2 %collective-permute-start.7 = (bf16[2,288,512]{2,1,0:T(8,128)(2,1)S(1)}, bf16[2,288,512]{2,1,0:T(8,128)(2,1)S(1)}, u32[]{:S(2)}, u32[]{:S(2)}) collective-permute-start(bf16[2,288,512]{2,1,0:T(8,128)(2,1)S(1)} %get-tuple-element.44), channel_id=1, source_target_pairs={{0,12},{4,0},{8,4},{12,8},{1,13},{5,1},{9,5},{13,9},{2,14},{6,2},{... | collective-permute-start | bytes 1769480 | tf_op jit(solution)/shard_map/ppermute | solution.py:214
  152.2 15.4 %copy-start.13 = (bf16[2,288,512]{2,1,0:T(8,128)(2,1)}, bf16[2,288,512]{2,1,0:T(8,128)(2,1)S(1)}, u32[]{:S(2)}) copy-start(bf16[2,288,512]{2,1,0:T(8,128)(2,1)S(1)} %collective-permute-done.6) | copy-start | bytes 1769476
  153.6 14.0 %copy-start.15 = (bf16[2,288,512]{2,1,0:T(8,128)(2,1)}, bf16[2,288,512]{2,1,0:T(8,128)(2,1)S(1)}, u32[]{:S(2)}) copy-start(bf16[2,288,512]{2,1,0:T(8,128)(2,1)S(1)} %collective-permute-done.7) | copy-start | bytes 1769476
  153.6 6.8 %collective-permute-start.8 = (bf16[2,2,576,384]{3,2,1,0:T(8,128)(2,1)}, bf16[2,2,576,384]{3,2,1,0:T(8,128)(2,1)}, u32[]{:S(2)}, u32[]{:S(2)}) collective-permute-start(bf16[2,2,576,384]{3,2,1,0:T(8,128)(2,1)} %bitcast.11.near_ref.refs_4_), channel_id=1, source_target_pairs={{0,128},{128,0},{1,129},{129,1},{2,130},{130,2},{3,131},{131,3},{4... | collective-permute-start | bytes 5308424 | tf_op jit(solution)/shard_map/ppermute | solution.py:264
  167.7 27.3 %collective-permute-start.9 = (bf16[2,288,512]{2,1,0:T(8,128)(2,1)}, bf16[2,288,512]{2,1,0:T(8,128)(2,1)S(1)}, u32[]{:S(2)}, u32[]{:S(2)}) collective-permute-start(bf16[2,288,512]{2,1,0:T(8,128)(2,1)} %get-tuple-element.47), channel_id=1, source_target_pairs={{0,12},{4,0},{8,4},{12,8},{1,13},{5,1},{9,5},{13,9},{2,14},{6,2},{... | collective-permute-start | bytes 1769480 | tf_op jit(solution)/shard_map/ppermute | solution.py:214
  171.9 23.0 %collective-permute-start.10 = (bf16[2,288,512]{2,1,0:T(8,128)(2,1)}, bf16[2,288,512]{2,1,0:T(8,128)(2,1)S(1)}, u32[]{:S(2)}, u32[]{:S(2)}) collective-permute-start(bf16[2,288,512]{2,1,0:T(8,128)(2,1)} %get-tuple-element.48), channel_id=1, source_target_pairs={{0,8},{4,12},{8,0},{12,4},{1,9},{5,13},{9,1},{13,5},{2,10},{6,14},... | collective-permute-start | bytes 1769480 | tf_op jit(solution)/shard_map/ppermute | solution.py:214
  173.9 29.6 %collective-permute-start.11 = (bf16[2,288,512]{2,1,0:T(8,128)(2,1)}, bf16[2,288,512]{2,1,0:T(8,128)(2,1)S(1)}, u32[]{:S(2)}, u32[]{:S(2)}) collective-permute-start(bf16[2,288,512]{2,1,0:T(8,128)(2,1)} %get-tuple-element.49), channel_id=1, source_target_pairs={{0,4},{4,8},{8,12},{12,0},{1,5},{5,9},{9,13},{13,1},{2,6},{6,10},{... | collective-permute-start | bytes 1769480 | tf_op jit(solution)/shard_map/ppermute | solution.py:214
  214.5 29.4 %collective-permute-start.16 = (bf16[2,2,144,512]{3,2,1,0:T(8,128)(2,1)S(1)}, bf16[2,2,144,512]{3,2,1,0:T(8,128)(2,1)S(1)}, u32[]{:S(2)}, u32[]{:S(2)}) collective-permute-start(bf16[2,2,144,512]{3,2,1,0:T(8,128)(2,1)S(1)} %get-tuple-element.61), channel_id=1, source_target_pairs={{0,4},{4,8},{8,12},{12,0},{1,5},{5,9},{9,13},{13,1},{2,6},{6,10},{... | collective-permute-start | bytes 1769480 | tf_op jit(solution)/shard_map/ppermute | solution.py:214
  216.4 39.8 %collective-permute-start.17 = (bf16[2,2,144,512]{3,2,1,0:T(8,128)(2,1)}, bf16[2,2,144,512]{3,2,1,0:T(8,128)(2,1)}, u32[]{:S(2)}, u32[]{:S(2)}) collective-permute-start(bf16[2,2,144,512]{3,2,1,0:T(8,128)(2,1)} %get-tuple-element.62), channel_id=1, source_target_pairs={{0,8},{4,12},{8,0},{12,4},{1,9},{5,13},{9,1},{13,5},{2,10},{6,14},... | collective-permute-start | bytes 1769480 | tf_op jit(solution)/shard_map/ppermute | solution.py:214
  218.9 37.4 %collective-permute-start.18 = (bf16[2,2,144,512]{3,2,1,0:T(8,128)(2,1)}, bf16[2,2,144,512]{3,2,1,0:T(8,128)(2,1)}, u32[]{:S(2)}, u32[]{:S(2)}) collective-permute-start(bf16[2,2,144,512]{3,2,1,0:T(8,128)(2,1)} %get-tuple-element.63), channel_id=1, source_target_pairs={{0,12},{4,0},{8,4},{12,8},{1,13},{5,1},{9,5},{13,9},{2,14},{6,2},{... | collective-permute-start | bytes 1769480 | tf_op jit(solution)/shard_map/ppermute | solution.py:214
  228.3 41.7 %collective-permute-start.13 = (bf16[2,2,144,512]{3,2,1,0:T(8,128)(2,1)}, bf16[2,2,144,512]{3,2,1,0:T(8,128)(2,1)S(1)}, u32[]{:S(2)}, u32[]{:S(2)}) collective-permute-start(bf16[2,2,144,512]{3,2,1,0:T(8,128)(2,1)} %get-tuple-element.57), channel_id=1, source_target_pairs={{0,4},{4,8},{8,12},{12,0},{1,5},{5,9},{9,13},{13,1},{2,6},{6,10},{... | collective-permute-start | bytes 1769480 | tf_op jit(solution)/shard_map/ppermute | solution.py:214
  230.8 39.2 %collective-permute-start.14 = (bf16[2,2,144,512]{3,2,1,0:T(8,128)(2,1)}, bf16[2,2,144,512]{3,2,1,0:T(8,128)(2,1)}, u32[]{:S(2)}, u32[]{:S(2)}) collective-permute-start(bf16[2,2,144,512]{3,2,1,0:T(8,128)(2,1)} %get-tuple-element.58), channel_id=1, source_target_pairs={{0,8},{4,12},{8,0},{12,4},{1,9},{5,13},{9,1},{13,5},{2,10},{6,14},... | collective-permute-start | bytes 1769480 | tf_op jit(solution)/shard_map/ppermute | solution.py:214
  244.7 27.8 %collective-permute-start.15 = (bf16[2,2,144,512]{3,2,1,0:T(8,128)(2,1)}, bf16[2,2,144,512]{3,2,1,0:T(8,128)(2,1)}, u32[]{:S(2)}, u32[]{:S(2)}) collective-permute-start(bf16[2,2,144,512]{3,2,1,0:T(8,128)(2,1)} %get-tuple-element.59), channel_id=1, source_target_pairs={{0,12},{4,0},{8,4},{12,8},{1,13},{5,1},{9,5},{13,9},{2,14},{6,2},{... | collective-permute-start | bytes 1769480 | tf_op jit(solution)/shard_map/ppermute | solution.py:214
  251.9 30.5 %all-to-all-start.2 = ((bf16[4,128,1024]{2,1,0:T(8,128)(2,1)}), bf16[4,128,1024]{2,1,0:T(8,128)(2,1)}, u32[]{:S(2)}, u32[]{:S(2)}) async-start(bf16[4,128,1024]{2,1,0:T(8,128)(2,1)} %copy.86), calls=%async_computation.2 | async-start | bytes 2097152 | tf_op jit(solution)/shard_map/all_to_all | solution.py:304
  258.4 14.1 %copy-start.6 = (bf16[2,2,144,512]{3,2,1,0:T(8,128)(2,1)S(1)}, bf16[2,2,144,512]{3,2,1,0:T(8,128)(2,1)}, u32[]{:S(2)}) copy-start(bf16[2,2,144,512]{3,2,1,0:T(8,128)(2,1)} %copy-done.5) | copy-start | bytes 1769476
  278.9 5.1 %collective-permute-start.19 = (bf16[512,384]{1,0:T(8,128)(2,1)S(1)}, bf16[512,384]{1,0:T(8,128)(2,1)}, u32[]{:S(2)}, u32[]{:S(2)}) collective-permute-start(bf16[512,384]{1,0:T(8,128)(2,1)S(1)} %select_bitcast_fusion), channel_id=1, source_target_pairs={{0,128},{128,0},{1,129},{129,1},{2,130},{130,2},{3,131},{131,3},{4... | collective-permute-start | bytes 1179656 | tf_op jit(solution)/shard_map/ppermute | solution.py:301
  283.9 12.0 %copy-start.20 = (bf16[2,64,1024]{2,1,0:T(8,128)(2,1)S(1)}, bf16[2,64,1024]{2,1,0:T(8,128)(2,1)}, u32[]{:S(2)}) copy-start(bf16[2,64,1024]{2,1,0:T(8,128)(2,1)} %param.15) | copy-start | bytes 786436
  286.0 9.0 %collective-permute-start.12 = (bf16[128,512]{1,0:T(8,128)(2,1)S(1)}, bf16[128,512]{1,0:T(8,128)(2,1)S(1)}, u32[]{:S(2)}, u32[]{:S(2)}) collective-permute-start(bf16[128,512]{1,0:T(8,128)(2,1)S(1)} %slice.85), channel_id=1, source_target_pairs={{0,128},{128,0},{1,129},{129,1},{2,130},{130,2},{3,131},{131,3},{4... | collective-permute-start | bytes 393224 | tf_op jit(solution)/shard_map/ppermute | solution.py:308
  (17 other events, 31.0 us)
Sparse Core Ops, SparseCore 0:
  42.7 104.4 all-gather.1
  208.5 73.3 reduce-scatter.1

commit v9 on v8

--- a/solution.py
+++ b/solution.py
@@ -61,50 +61,54 @@
     )(far, line, table)
 
 
-def rows_back(near, other, weight, here):
-    _, quarters, rows, ff = near.shape
+def quarters_of(part, ff, source, relative):
+    def spec(q):
+        def place(d, where):
+            block = source(d, where)
+            x = 2 * (block >> 1) + q
+            if relative:
+                x = (where[1] - x) & 3
+            return (x, block & 1, 0)
+
+        return pl.BlockSpec((1, part, ff), place)
+
+    return [spec(0), spec(1)]
+
+
+def rows_back(near, other, weight, where, relative):
+    _, rows, ff = near.shape
     width = weight.shape[1]
     part = rows // 2
 
-    def body(y_ref, near_ref, other_ref, weight_ref, *out_refs):
-        for d, out_ref in enumerate(out_refs):
-
-            @pl.when(pl.program_id(0) == d)
-            def _():
-                for k, ref in enumerate((near_ref, other_ref)):
-                    total = dot(ref[0, 0], weight_ref[0], (1, 1))
-                    total += dot(ref[0, 1], weight_ref[1], (1, 1))
-                    out_ref[k] = total.astype(BF16)
-
-    def place(d, y):
-        source = (y[0] + d) & 3
-        return (source >> 1, 0, source & 1, 0)
-
-    piece = pl.BlockSpec((1, quarters, part, ff), place)
+    def body(where_ref, near0, near1, other0, other1, weight_ref, out_ref):
+        for k, (first, second) in enumerate(((near0, near1), (other0, other1))):
+            total = dot(first[0], weight_ref[0], (1, 1)) + dot(second[0], weight_ref[1], (1, 1))
+            out_ref[0, k] = total.astype(BF16)
+
+    pieces = quarters_of(part, ff, lambda d, where: d, relative)
     return call(
         body,
         (4,),
-        [piece, piece, pl.BlockSpec(weight.shape, lambda d, y: (0, 0, 0))],
-        [pl.BlockSpec((2, part, width), lambda d, y: (0, 0, 0))] * 4,
-        [jax.ShapeDtypeStruct((2, part, width), BF16)] * 4,
+        pieces + pieces + [pl.BlockSpec(weight.shape, lambda d, where: (0, 0, 0))],
+        pl.BlockSpec((1, 2, part, width), lambda d, where: (d, 0, 0, 0)),
+        jax.ShapeDtypeStruct((4, 2, part, width), BF16),
         1,
-        16 * part * quarters * ff * width,
-    )(here, near, other, weight)
+        32 * part * ff * width,
+    )(where, near, near, other, other, weight)
 
 
 def combine(half, returned, table, far, tok, so_far):
-    returned = [returned[d] for d in (0, 3, 2, 1)]
-    _, batches, part, width = returned[0].shape
+    _, _, batches, part, width = returned.shape
     rows = 4 * part
 
-    def body(zh_ref, *refs):
-        out_ref, table_ref = refs[-1], refs[4]
+    def body(zh_ref, back_ref, table_ref, *refs):
+        out_ref = refs[-1]
         seat = table_ref[0, 0:1, :].astype(I32)
         hit = seat == lax.broadcasted_iota(I32, (8 * tok, rows), 0)
         gate = jnp.where(hit, table_ref[0, 1:2, :], 0.0)
         high = gate.astype(BF16)
         low = (gate - high.astype(F32)).astype(BF16)
-        source = jnp.concatenate([ref[0, 0] for ref in refs[:4]], axis=0)
+        source = back_ref[...].reshape(rows, width)
         total = dot(high, source, (1, 0)) + dot(low, source, (1, 0))
         out_ref[...] = total.astype(BF16).reshape(out_ref.shape)
 
@@ -112,61 +116,60 @@
     return call(
         body,
         (2, batches),
-        [pl.BlockSpec((1, 1, part, width), lambda k, m, zh: (k, m, 0, 0))] * 4
-        + [pl.BlockSpec((1, 2, rows), lambda k, m, zh: (half * 4 + k * 2 + m, 0, 0))]
+        [
+            pl.BlockSpec((4, 1, 1, part, width), lambda k, m, zh: (0, k, m, 0, 0)),
+            pl.BlockSpec((1, 2, rows), lambda k, m, zh: (half * 4 + k * 2 + m, 0, 0)),
+        ]
         + [pl.BlockSpec(memory_space=pl.ANY)] * len(extra),
         pl.BlockSpec((1, 8, 1, tok, width), lambda k, m, zh: (zh[0] ^ half, 0, m, 0, k)),
         jax.ShapeDtypeStruct((2, 8, batches, tok, 2 * width), BF16),
         1,
         16 * rows * 8 * tok * width,
-        aliases={6: 0} if extra else {},
-    )(far, *returned, table, *extra)
-
-
-def weight_sum(inbound, near, other, here, so_far, scale, kind):
+        aliases={3: 0} if extra else {},
+    )(far, returned, table, *extra)
+
+
+def weight_sum(inbound, near, other, where, relative, so_far, scale, kind):
     _, part, width = inbound[0].shape
-    quarters, ff = near.shape[1], near.shape[3]
-
-    def body(y_ref, *refs):
-        near_ref, other_ref = refs[4:6]
+    ff = near.shape[2]
+
+    def body(where_ref, *refs):
+        hidden = ((refs[4], refs[6]), (refs[5], refs[7]))
         out_ref, total = refs[-2:]
 
         @pl.when(pl.program_id(0) == 0)
         def _():
-            total[...] = jnp.zeros_like(total) if so_far is None else refs[6][...]
+            total[...] = jnp.zeros_like(total) if so_far is None else refs[8][...]
 
         for d in range(4):
 
             @pl.when(pl.program_id(0) == d)
             def _():
-                for q in range(quarters):
-                    total[q] += dot(refs[d][0], near_ref[0, q], (0, 0)) + dot(
-                        refs[d][1], other_ref[0, q], (0, 0)
+                for q, (first, second) in enumerate(hidden):
+                    total[q] += dot(refs[d][0], first[0], (0, 0)) + dot(
+                        refs[d][1], second[0], (0, 0)
                     )
 
         @pl.when(pl.program_id(0) == 3)
         def _():
             out_ref[...] = (total[...] * scale).astype(kind)
 
-    def place(d, y):
-        source = (y[0] - d) & 3
-        return (source >> 1, 0, source & 1, 0)
-
-    piece = pl.BlockSpec((1, quarters, part, ff), place)
-    whole = pl.BlockSpec((quarters, width, ff), lambda d, y: (0, 0, 0))
+    pieces = quarters_of(part, ff, lambda d, where: (where[0] - d) & 3, relative)
+    whole = pl.BlockSpec((2, width, ff), lambda d, where: (0, 0, 0))
     extra = () if so_far is None else (so_far,)
     return call(
         body,
         (4,),
-        [pl.BlockSpec((2, part, width), lambda d, y: (0, 0, 0))] * 4
-        + [piece, piece]
+        [pl.BlockSpec((2, part, width), lambda d, where: (0, 0, 0))] * 4
+        + pieces
+        + pieces
         + [whole] * len(extra),
         whole,
-        jax.ShapeDtypeStruct((quarters, width, ff), kind),
+        jax.ShapeDtypeStruct((2, width, ff), kind),
         1,
-        16 * part * width * quarters * ff,
-        scratch=(pltpu.VMEM((quarters, width, ff), F32),),
-    )(here, *inbound, near, other, *extra)
+        32 * part * width * ff,
+        scratch=(pltpu.VMEM((2, width, ff), F32),),
+    )(where, *inbound, near, near, other, other, *extra)
 
 
 def slot_tables(expert_ids, slot_index, gate_weights, capacity, places):
@@ -202,12 +205,23 @@
     rows = batches * buffer_rows
     far = zh.astype(I32).reshape(1)
     y = lax.axis_index("y")
-    here = y.astype(I32).reshape(1)
+    here = jnp.stack([y, x]).astype(I32)
 
     def gather(v):
         return lax.all_to_all(
             jnp.broadcast_to(v, (nx,) + v.shape), "x", split_axis=0, concat_axis=0, tiled=True
-        ).reshape((2, 2) + v.shape)
+        )
+
+    def gather_back(v):
+        return [v] + [
+            lax.ppermute(v, "x", [(i, (i + d) % nx) for i in range(nx)]) for d in (1, 2, 3)
+        ]
+
+    def swap_y(v):
+        shape = v.shape
+        v = v.reshape(ny, -1, shape[-1])
+        v = lax.all_to_all(v, "y", split_axis=0, concat_axis=0, tiled=True)
+        return v.reshape(4, 2, batches, nzl * capacity, eighth)
 
     def along_y(parts, shape):
         moved = [
@@ -215,10 +229,6 @@
             for d, v in enumerate(parts)
         ]
         return [v.reshape(shape) for v in moved]
-
-    cut = up_weight.reshape(2, eighth, ff)
-    mine, theirs = by(co, cut[0], cut[1])
-    weight = jnp.stack(by(co, mine, lax.ppermute(theirs, "co", SWAP)))
 
     r = jnp.arange(rows, dtype=I32)
     r_batch = (r // (capacity * nzl)) % batches
@@ -231,10 +241,13 @@
     xh = x // 2
     keep, send = by(xh, halves[0], halves[1])
     taken = lax.ppermute(send, "x", [(i, (i + 2) % nx) for i in range(nx)])
-    taken, weight = lax.optimization_barrier((taken, weight))
     stay, leave = by(xh ^ zh, keep, taken)
     crossed = lax.ppermute(leave, "zh", SWAP)
     near = gather(stay)
+
+    cut = up_weight.reshape(2, eighth, ff)
+    mine, theirs = by(co, cut[0], cut[1])
+    weight = jnp.stack(by(co, mine, lax.ppermute(theirs, "co", SWAP)))
 
     expert_ids, slot_index, gate_weights, send = lax.optimization_barrier(
         (expert_ids, slot_index, gate_weights, send)
@@ -255,14 +268,16 @@
     line, stay = lax.optimization_barrier((line, stay))
     line = lax.all_gather(line, ("zh", "zl"), axis=0, tiled=True)
 
-    split = (2, batches, nzl * capacity, eighth)
     near, crossed = lax.optimization_barrier((near, crossed))
     near_other = lax.ppermute(near, "co", SWAP)
-    back = rows_back(near, near_other, weight, here)
-    wide = gather(crossed)
-    wide, back = lax.optimization_barrier((wide, along_y(back, split)))
+    back = rows_back(near, near_other, weight, here, False)
+    *wide, _ = lax.optimization_barrier((*gather_back(crossed), back))
+    back = swap_y(back)
+    wide = jnp.stack(wide)
     wide_other = lax.ppermute(wide, "co", SWAP)
-    wide_back = rows_back(wide, wide_other, weight, here)
+    wide_back = rows_back(wide, wide_other, weight, here, True)
+    wide_back, back = lax.optimization_barrier((wide_back, back))
+    wide_back = swap_y(wide_back)
 
     column = lax.dynamic_slice(
         line.reshape(2 * nzl, batches * tok, -1),
@@ -274,15 +289,15 @@
     column = column.transpose(2, 0, 5, 3, 4, 6, 1, 7).reshape(
         4, 4 * batches, ny, nzl, capacity
     )
-    column = lax.dynamic_slice_in_dim(jnp.concatenate([column, column], axis=2), y, ny, 2)
     start = jnp.arange(nzl, dtype=F32)[:, None] * tok
     seats = jnp.where(column[0] >= 0, column[0] + start, -1.0)
     column = jnp.stack([seats, column[1] + (column[2] + column[3])])
-    column = column.reshape(2, 4 * batches, buffer_rows)
-    lying, standing = column.transpose(1, 0, 2), column.transpose(1, 2, 0)
+    lying = column.reshape(2, 4 * batches, buffer_rows).transpose(1, 0, 2)
+    column = lax.dynamic_slice_in_dim(jnp.concatenate([column, column], axis=2), y, ny, 2)
+    standing = column.reshape(2, 4 * batches, buffer_rows).transpose(1, 2, 0)
 
     spread = combine(0, back, lying, far, tok, None)
-    spread = combine(1, along_y(wide_back, split), lying, far, tok, spread)
+    spread = combine(1, wide_back, lying, far, tok, spread)
     expert_part = lax.psum_scatter(
         spread.reshape(2 * nzl * batches * tok, quarter),
         ("zh", "zl"),
@@ -295,8 +310,10 @@
     split = (2, batches * nzl * capacity, eighth)
     inbound = along_y(pick_rows(0, line, standing, far, eighth), split)
     inbound_far = along_y(pick_rows(1, line, standing, far, eighth), split)
-    total = weight_sum(inbound, near, near_other, here, None, 1.0, F32)
-    total = weight_sum(inbound_far, wide, wide_other, here, total, 1.0 / (2 * SIZES[1]), BF16)
+    total = weight_sum(inbound, near, near_other, here, False, None, 1.0, F32)
+    total = weight_sum(
+        inbound_far, wide, wide_other, here, True, total, 1.0 / (2 * SIZES[1]), BF16
+    )
     mine, theirs = by(co, total[0], total[1])
     weight_gradient = jnp.concatenate(by(co, mine, lax.ppermute(theirs, "co", SWAP)))
 

time: 306 us -> 302 us (0.987)
  starting transfers between devices: 87.3 us -> 104 us
  local copies, waits for them, and re-layouts: 33.2 us -> 19.8 us
  waiting for transfers between devices: 107 us -> 95.4 us
  Pallas kernels: 43.6 us -> 48.8 us
    all_to_all x0 -> x2, waiting for transfers between devices: none -> 40 us  [swap_y(): v = lax.all_to_all(v, 'y', split_axis=0, concat_axis=0, tiled=True)]
    ppermute x12 -> x6, waiting for transfers between devices: 42.6 us -> 15.3 us  [along_y(): lax.ppermute(v, 'y', [(i, (i + d) % ny) for i in range(ny)])]
    ppermute x12 -> x6, starting transfers between devices: 33.7 us -> 18.7 us  [along_y(): lax.ppermute(v, 'y', [(i, (i + d) % ny) for i in range(ny)])]
    ppermute x1, waiting for transfers between devices: 44.5 us -> 30.8 us  [on_device(): crossed = lax.ppermute(leave, 'zh', SWAP)]
    ppermute x0 -> x3, starting transfers between devices: none -> 11.4 us  [gather_back(): lax.ppermute(v, 'x', [(i, (i + d) % nx) for i in range(nx)])]
    ppermute x1, starting transfers between devices: 3.43 us -> 14.5 us  [on_device(): near_other = lax.ppermute(near, 'co', SWAP)]
    ppermute x1, waiting for transfers between devices: 10 us -> 0.01 us  [on_device(): taken = lax.ppermute(send, 'x', [(i, (i + 2) % nx) for i in range(nx)])]
    all_to_all x0 -> x2, starting transfers between devices: none -> 9.01 us  [swap_y(): v = lax.all_to_all(v, 'y', split_axis=0, concat_axis=0, tiled=True)]
  transfers between devices with their start and end apart: 25 -> 23, of which waited for: 10 -> 10; matrix products, arithmetic and copies ran while one was open for 10% -> 8% of each run, Pallas kernels for 13% -> 14%
where the time goes in v9:
time: 302 us; the launch traced here: 300 us
  starting transfers between devices  104 us (34%)
  waiting for transfers between devices  95.4 us (32%)
  Pallas kernels  48.8 us (16%)
  local copies, waits for them, and re-layouts  19.8 us (7%)
  between operations  14.7 us (5%)
  other arithmetic  14.1 us (5%)
    all_to_all x2, waiting for transfers between devices, swap_y(): v = lax.all_to_all(v, 'y', split_axis=0, concat_axis=0, tiled=True)  40 us
    ppermute x1, waiting for transfers between devices, on_device(): crossed = lax.ppermute(leave, 'zh', SWAP)  30.8 us
    ppermute x6, starting transfers between devices, along_y(): lax.ppermute(v, 'y', [(i, (i + d) % ny) for i in range(ny)])  18.7 us
    ppermute x6, waiting for transfers between devices, along_y(): lax.ppermute(v, 'y', [(i, (i + d) % ny) for i in range(ny)])  15.3 us
    ppermute x1, starting transfers between devices, on_device(): crossed = lax.ppermute(leave, 'zh', SWAP)  14.6 us
    ppermute x1, starting transfers between devices, on_device(): near_other = lax.ppermute(near, 'co', SWAP)  14.5 us
    pallas_call x2, Pallas kernels, weight_sum(): call(body, (4,), [pl.BlockSpec((2, part, width), lambda d, where: (0, 0,...  14.3 us
    pallas_call x2, Pallas kernels, rows_back(): call(body, (4,), pieces + pieces + [pl.BlockSpec(weight.shape, lambda d,...  12.8 us
  transfers between devices with their start and end apart: 23, of which 10 were waited for; matrix products, arithmetic and copies ran while one was open for 8% of the time, Pallas kernels for 14%

profile of v9, /device:TPU:1, one launch (start us, length us, event | category | flops | bytes accessed | tf_op | source)
XLA Modules:
  0.0 299.6 jit_solution(16935281962667941985)
XLA Ops:
  7.3 2.9 fusion.1
  10.3 5.5 %collective-permute-start.1 = (bf16[576,384]{1,0:T(8,128)(2,1)S(1)}, bf16[576,384]{1,0:T(8,128)(2,1)S(1)}, u32[]{:S(2)}, u32[]{:S(2)}) collective-permute-start(bf16[576,384]{1,0:T(8,128)(2,1)S(1)} %broadcast_select_fusion.5), channel_id=1, source_target_pairs={{0,2},{1,3},{2,0},{3,1},{4,6},{5,7},{6,4},{7,5},{8,10},{9,11},{10,... | collective-permute-start | bytes 1327112 | tf_op jit(solution)/shard_map/ppermute | solution.py:243
  18.6 5.2 %collective-permute-start = (bf16[128,576]{1,0:T(8,128)(2,1)}, bf16[128,576]{1,0:T(8,128)(2,1)S(1)}, u32[]{:S(2)}, u32[]{:S(2)}) collective-permute-start(bf16[128,576]{1,0:T(8,128)(2,1)} %pad_maximum_fusion.2), channel_id=1, source_target_pairs={{0,128},{128,0},{1,129},{129,1},{2,130},{130,2},{3,131},{131,3},{4... | collective-permute-start | bytes 442376 | tf_op jit(solution)/shard_map/ppermute | solution.py:266
  28.2 4.5 %all-to-all-start = ((bf16[4,576,384]{2,1,0:T(8,128)(2,1)}), bf16[4,576,384]{2,1,0:T(8,128)(2,1)S(1)}, u32[]{:S(2)}, u32[]{:S(2)}) async-start(bf16[4,576,384]{2,1,0:T(8,128)(2,1)} %broadcast_in_dim.50), calls=%async_computation | async-start | bytes 3538944 | tf_op jit(solution)/shard_map/all_to_all | solution.py:211
  32.7 14.6 %collective-permute-start.2 = (bf16[576,384]{1,0:T(8,128)(2,1)}, bf16[576,384]{1,0:T(8,128)(2,1)S(1)}, u32[]{:S(2)}, u32[]{:S(2)}) collective-permute-start(bf16[576,384]{1,0:T(8,128)(2,1)} %get-tuple-element.48), channel_id=1, source_target_pairs={{0,256},{256,0},{1,257},{257,1},{2,258},{258,2},{3,259},{259,3},{4... | collective-permute-start | bytes 1327112 | tf_op jit(solution)/shard_map/ppermute | solution.py:245
  47.3 30.8 %collective-permute-done.2 = bf16[576,384]{1,0:T(8,128)(2,1)S(1)} collective-permute-done((bf16[576,384]{1,0:T(8,128)(2,1)}, bf16[576,384]{1,0:T(8,128)(2,1)S(1)}, u32[]{:S(2)}, u32[]{:S(2)}) %collective-permute-start.2) | collective-permute-done | bytes 442400 | tf_op jit(solution)/shard_map/ppermute | solution.py:245
  78.1 14.5 %collective-permute-start.6 = (bf16[4,576,384]{2,1,0:T(8,128)(2,1)S(1)}, bf16[4,576,384]{2,1,0:T(8,128)(2,1)}, u32[]{:S(2)}, u32[]{:S(2)}) collective-permute-start(bf16[4,576,384]{2,1,0:T(8,128)(2,1)S(1)} %all-to-all-done.near0.near1.refs_4_.refs_5_), channel_id=1, source_target_pairs={{0,128},{128,0},{1,129},{129,1},{2,130},{130,2},{3,131},{131,3},{4... | collective-permute-start | bytes 5308424 | tf_op jit(solution)/shard_map/ppermute | solution.py:272
  96.6 3.9 %collective-permute-start.3 = (bf16[576,384]{1,0:T(8,128)(2,1)S(1)}, bf16[576,384]{1,0:T(8,128)(2,1)S(1)}, u32[]{:S(2)}, u32[]{:S(2)}) collective-permute-start(bf16[576,384]{1,0:T(8,128)(2,1)S(1)} %collective-permute-done.2), channel_id=1, source_target_pairs={{0,1},{1,2},{2,3},{3,0},{4,5},{5,6},{6,7},{7,4},{8,9},{9,10},{10,1... | collective-permute-start | bytes 1327112 | tf_op jit(solution)/shard_map/ppermute | solution.py:217
  100.5 4.3 %collective-permute-start.4 = (bf16[576,384]{1,0:T(8,128)(2,1)S(1)}, bf16[576,384]{1,0:T(8,128)(2,1)S(1)}, u32[]{:S(2)}, u32[]{:S(2)}) collective-permute-start(bf16[576,384]{1,0:T(8,128)(2,1)S(1)} %collective-permute-done.2), channel_id=1, source_target_pairs={{0,2},{1,3},{2,0},{3,1},{4,6},{5,7},{6,4},{7,5},{8,10},{9,11},{10,... | collective-permute-start | bytes 1327112 | tf_op jit(solution)/shard_map/ppermute | solution.py:217
  104.9 3.1 %collective-permute-start.5 = (bf16[576,384]{1,0:T(8,128)(2,1)S(1)}, bf16[576,384]{1,0:T(8,128)(2,1)S(1)}, u32[]{:S(2)}, u32[]{:S(2)}) collective-permute-start(bf16[576,384]{1,0:T(8,128)(2,1)S(1)} %collective-permute-done.2), channel_id=1, source_target_pairs={{0,3},{1,0},{2,1},{3,2},{4,7},{5,4},{6,5},{7,6},{8,11},{9,8},{10,9... | collective-permute-start | bytes 1327112 | tf_op jit(solution)/shard_map/ppermute | solution.py:217
  109.4 6.2 %shard_map.95 = bf16[4,2,288,512]{3,2,1,0:T(8,128)(2,1)} custom-call(s32[2]{0:T(128)S(1)} %pad_add_fusion.where_ref, bf16[4,576,384]{2,1,0:T(8,128)(2,1)S(1)} %all-to-all-done.near0.near1.refs_4_.refs_5_, bf16[4,576,384]{2,1,0:T(8,128)(2,1)S(1)} %all-to-all-done.near0.near1.refs_4_.refs_5_, ...), custom_call_target="tpu_custom_call" | custom-call | flops 1811939328 | bytes 8388608 | tf_op jit(solution)/shard_map/pallas_call | solution.py:89
  115.7 6.5 %collective-permute-done.4 = bf16[576,384]{1,0:T(8,128)(2,1)S(1)} collective-permute-done((bf16[576,384]{1,0:T(8,128)(2,1)S(1)}, bf16[576,384]{1,0:T(8,128)(2,1)S(1)}, u32[]{:S(2)}, u32[]{:S(2)}) %collective-permute-start.4) | collective-permute-done | bytes 442400 | tf_op jit(solution)/shard_map/ppermute | solution.py:217
  125.1 3.1 %collective-permute-start.8 = (bf16[4,576,384]{2,1,0:T(8,128)(2,1)}, bf16[4,576,384]{2,1,0:T(8,128)(2,1)}, u32[]{:S(2)}, u32[]{:S(2)}) collective-permute-start(bf16[4,576,384]{2,1,0:T(8,128)(2,1)} %pad_maximum_fusion.near0.near1.refs_4_.refs_5_), channel_id=1, source_target_pairs={{0,128},{128,0},{1,129},{129,1},{2,130},{130,2},{3,131},{131,3},{4... | collective-permute-start | bytes 5308424 | tf_op jit(solution)/shard_map/ppermute | solution.py:277
  128.3 4.5 %all-to-all-start.1 = ((bf16[4,576,512]{2,1,0:T(8,128)(2,1)}), bf16[4,576,512]{2,1,0:T(8,128)(2,1)}, u32[]{:S(2)}, u32[]{:S(2)}) async-start(bf16[4,576,512]{2,1,0:T(8,128)(2,1)} %bitcast.88), calls=%async_computation.1 | async-start | bytes 4718592 | tf_op jit(solution)/shard_map/all_to_all | solution.py:223
  134.0 6.6 %shard_map.96 = bf16[4,2,288,512]{3,2,1,0:T(8,128)(2,1)} custom-call(s32[2]{0:T(128)S(1)} %pad_add_fusion.where_ref, bf16[4,576,384]{2,1,0:T(8,128)(2,1)} %pad_maximum_fusion.near0.near1.refs_4_.refs_5_, bf16[4,576,384]{2,1,0:T(8,128)(2,1)} %pad_maximum_fusion.near0.near1.refs_4_.refs_5_, ...), custom_call_target="tpu_custom_call" | custom-call | flops 1811939328 | bytes 8388608 | tf_op jit(solution)/shard_map/pallas_call | solution.py:89
  140.6 21.6 %all-to-all-done.1 = bf16[4,576,512]{2,1,0:T(8,128)(2,1)} async-done(((bf16[4,576,512]{2,1,0:T(8,128)(2,1)}), bf16[4,576,512]{2,1,0:T(8,128)(2,1)}, u32[]{:S(2)}, u32[]{:S(2)}) %all-to-all-start.1) | async-done | bytes 2359328 | tf_op jit(solution)/shard_map/all_to_all | solution.py:223
  162.2 4.5 %all-to-all-start.2 = ((bf16[4,576,512]{2,1,0:T(8,128)(2,1)}), bf16[4,576,512]{2,1,0:T(8,128)(2,1)}, u32[]{:S(2)}, u32[]{:S(2)}) async-start(bf16[4,576,512]{2,1,0:T(8,128)(2,1)} %bitcast.87), calls=%async_computation.2 | async-start | bytes 4718592 | tf_op jit(solution)/shard_map/all_to_all | solution.py:223
  170.5 6.3 %shard_map.97.refs_0_ = bf16[2,8,2,64,1024]{4,3,2,1,0:T(8,128)(2,1)} custom-call(s32[1]{0:T(128)} %bitcast.4.zh_ref, bf16[4,2,2,144,512]{4,3,2,1,0:T(8,128)(2,1)} %bitcast.16.back_ref, f32[8,2,576]{2,1,0:T(2,128)S(1)} %maximum_bitcast_fusion.1.table_ref), custom_call_target="tpu_custom_call" | custom-call | flops 2415919104 | bytes 8388608 | tf_op jit(solution)/shard_map/pallas_call | solution.py:116
  176.7 18.4 %all-to-all-done.2 = bf16[4,576,512]{2,1,0:T(8,128)(2,1)} async-done(((bf16[4,576,512]{2,1,0:T(8,128)(2,1)}), bf16[4,576,512]{2,1,0:T(8,128)(2,1)}, u32[]{:S(2)}, u32[]{:S(2)}) %all-to-all-start.2) | async-done | bytes 2359328 | tf_op jit(solution)/shard_map/all_to_all | solution.py:223
  195.1 6.3 %shard_map.98 = bf16[2,8,2,64,1024]{4,3,2,1,0:T(8,128)(2,1)} custom-call(s32[1]{0:T(128)} %bitcast.4.zh_ref, bf16[4,2,2,144,512]{4,3,2,1,0:T(8,128)(2,1)} %bitcast.18.back_ref, f32[8,2,576]{2,1,0:T(2,128)S(1)} %maximum_bitcast_fusion.1.table_ref, bf16[2,8,2,64,1024]{4,3,2,1,0:T(8,128)(2,1)} %shard_map.97.refs_0_), custom_call_target="tpu_custom_call", output_to_operand_aliasing={{}: (3, {})} | custom-call | flops 2415919104 | bytes 8388608 | tf_op jit(solution)/shard_map/pallas_call | solution.py:116
  205.5 4.6 %shard_map.100 = (bf16[2,2,144,512]{3,2,1,0:T(8,128)(2,1)S(1)}, bf16[2,2,144,512]{3,2,1,0:T(8,128)(2,1)S(1)}, bf16[2,2,144,512]{3,2,1,0:T(8,128)(2,1)}, bf16[2,2,144,512]{3,2,1,0:T(8,128)(2,1)}) custom-call(s32[1]{0:T(128)} %bitcast.4.zh_ref, bf16[16,2,64,1152]{3,2,1,0:T(8,128)(2,1)} %bitcast.84, f32[8,576,2]{2,1,0:T(8,128)S(1)} %bitcast.78), custom_call_target="tpu_custom_call" | custom-call | flops 1207959552 | bytes 8388608 | tf_op jit(solution)/shard_map/pallas_call | solution.py:50
  212.3 3.7 %collective-permute-start.14 = (bf16[2,2,144,512]{3,2,1,0:T(8,128)(2,1)}, bf16[2,2,144,512]{3,2,1,0:T(8,128)(2,1)}, u32[]{:S(2)}, u32[]{:S(2)}) collective-permute-start(bf16[2,2,144,512]{3,2,1,0:T(8,128)(2,1)} %get-tuple-element.44), channel_id=1, source_target_pairs={{0,8},{4,12},{8,0},{12,4},{1,9},{5,13},{9,1},{13,5},{2,10},{6,14},... | collective-permute-start | bytes 1769480 | tf_op jit(solution)/shard_map/ppermute | solution.py:228
  218.5 4.6 %shard_map.99 = (bf16[2,2,144,512]{3,2,1,0:T(8,128)(2,1)S(1)}, bf16[2,2,144,512]{3,2,1,0:T(8,128)(2,1)}, bf16[2,2,144,512]{3,2,1,0:T(8,128)(2,1)}, bf16[2,2,144,512]{3,2,1,0:T(8,128)(2,1)}) custom-call(s32[1]{0:T(128)} %bitcast.4.zh_ref, bf16[16,2,64,1152]{3,2,1,0:T(8,128)(2,1)} %bitcast.85, f32[8,576,2]{2,1,0:T(8,128)S(1)} %bitcast.79), custom_call_target="tpu_custom_call" | custom-call | flops 1207959552 | bytes 8388608 | tf_op jit(solution)/shard_map/pallas_call | solution.py:50
  225.8 3.4 %collective-permute-start.11 = (bf16[2,2,144,512]{3,2,1,0:T(8,128)(2,1)}, bf16[2,2,144,512]{3,2,1,0:T(8,128)(2,1)}, u32[]{:S(2)}, u32[]{:S(2)}) collective-permute-start(bf16[2,2,144,512]{3,2,1,0:T(8,128)(2,1)} %get-tuple-element.40), channel_id=1, source_target_pairs={{0,8},{4,12},{8,0},{12,4},{1,9},{5,13},{9,1},{13,5},{2,10},{6,14},... | collective-permute-start | bytes 1769480 | tf_op jit(solution)/shard_map/ppermute | solution.py:228
  230.1 4.1 %collective-permute-start.12 = (bf16[2,2,144,512]{3,2,1,0:T(8,128)(2,1)}, bf16[2,2,144,512]{3,2,1,0:T(8,128)(2,1)}, u32[]{:S(2)}, u32[]{:S(2)}) collective-permute-start(bf16[2,2,144,512]{3,2,1,0:T(8,128)(2,1)} %get-tuple-element.41), channel_id=1, source_target_pairs={{0,12},{4,0},{8,4},{12,8},{1,13},{5,1},{9,5},{13,9},{2,14},{6,2},{... | collective-permute-start | bytes 1769480 | tf_op jit(solution)/shard_map/ppermute | solution.py:228
  239.4 4.2 %all-to-all-start.3 = ((bf16[4,128,1024]{2,1,0:T(8,128)(2,1)}), bf16[4,128,1024]{2,1,0:T(8,128)(2,1)}, u32[]{:S(2)}, u32[]{:S(2)}) async-start(bf16[4,128,1024]{2,1,0:T(8,128)(2,1)} %copy.89), calls=%async_computation.3 | async-start | bytes 2097152 | tf_op jit(solution)/shard_map/all_to_all | solution.py:321
  246.8 6.9 %shard_map.101.refs_8_ = f32[2,512,384]{2,1,0:T(8,128)S(1)} custom-call(s32[2]{0:T(128)S(1)} %pad_add_fusion.where_ref, bf16[2,288,512]{2,1,0:T(8,128)(2,1)S(1)} %bitcast.81, bf16[2,288,512]{2,1,0:T(8,128)(2,1)S(1)} %bitcast.82, bf16[2,288,512]{2,1,0:T(8,128)(2,1)} %bitcast.36.refs_2_, bf16[2,288,512]{2,1,0:T(8,128)(2,1)} %bitcast.37.refs_3_, ...), custom_call_target="tpu_custom_call" | custom-call | flops 1811939328 | bytes 8388608 | tf_op jit(solution)/shard_map/pallas_call | solution.py:160
  254.6 9.2 %collective-permute-done.11 = bf16[2,2,144,512]{3,2,1,0:T(8,128)(2,1)} collective-permute-done((bf16[2,2,144,512]{3,2,1,0:T(8,128)(2,1)}, bf16[2,2,144,512]{3,2,1,0:T(8,128)(2,1)}, u32[]{:S(2)}, u32[]{:S(2)}) %collective-permute-start.11) | collective-permute-done | bytes 589856 | tf_op jit(solution)/shard_map/ppermute | solution.py:228
  263.8 4.2 %collective-permute-done.12 = bf16[2,2,144,512]{3,2,1,0:T(8,128)(2,1)} collective-permute-done((bf16[2,2,144,512]{3,2,1,0:T(8,128)(2,1)}, bf16[2,2,144,512]{3,2,1,0:T(8,128)(2,1)}, u32[]{:S(2)}, u32[]{:S(2)}) %collective-permute-start.12) | collective-permute-done | bytes 589856 | tf_op jit(solution)/shard_map/ppermute | solution.py:228
  268.0 7.5 %shard_map.102 = bf16[2,512,384]{2,1,0:T(8,128)(2,1)S(1)} custom-call(s32[2]{0:T(128)S(1)} %pad_add_fusion.where_ref, bf16[2,288,512]{2,1,0:T(8,128)(2,1)S(1)} %bitcast.80, bf16[2,288,512]{2,1,0:T(8,128)(2,1)} %bitcast.31.refs_1_, bf16[2,288,512]{2,1,0:T(8,128)(2,1)} %bitcast.32.refs_2_, bf16[2,288,512]{2,1,0:T(8,128)(2,1)} %bitcast.33.refs_3_, ...), custom_call_target="tpu_custom_call" | custom-call | flops 1811939328 | bytes 8388608 | tf_op jit(solution)/shard_map/pallas_call | solution.py:160
  275.5 3.6 %collective-permute-start.16 = (bf16[512,384]{1,0:T(8,128)(2,1)S(1)}, bf16[512,384]{1,0:T(8,128)(2,1)S(1)}, u32[]{:S(2)}, u32[]{:S(2)}) collective-permute-start(bf16[512,384]{1,0:T(8,128)(2,1)S(1)} %select_bitcast_fusion), channel_id=1, source_target_pairs={{0,128},{128,0},{1,129},{129,1},{2,130},{130,2},{3,131},{131,3},{4... | collective-permute-start | bytes 1179656 | tf_op jit(solution)/shard_map/ppermute | solution.py:318
  281.7 7.4 %collective-permute-start.9 = (bf16[128,512]{1,0:T(8,128)(2,1)S(1)}, bf16[128,512]{1,0:T(8,128)(2,1)S(1)}, u32[]{:S(2)}, u32[]{:S(2)}) collective-permute-start(bf16[128,512]{1,0:T(8,128)(2,1)S(1)} %slice.89), channel_id=1, source_target_pairs={{0,128},{128,0},{1,129},{129,1},{2,130},{130,2},{3,131},{131,3},{4... | collective-permute-start | bytes 393224 | tf_op jit(solution)/shard_map/ppermute | solution.py:325
  (105 shorter events, 48.0 us)
Async XLA Ops:
  7.2 9.8 %copy-start = (bf16[2,64,4096]{2,1,0:T(8,128)(2,1)S(1)}, bf16[2,64,4096]{2,1,0:T(8,128)(2,1)}, u32[]{:S(2)}) copy-start(bf16[2,64,4096]{2,1,0:T(8,128)(2,1)} %param.8) | copy-start | bytes 3145732
  7.2 159.8 %all-gather.2.cloned.1.call-start = ((), (), s32[]{:S(2)}) async-start(), calls=%async_computation.5 | async-start | bytes 5013504 | tf_op jit(solution)/shard_map/all_gather | solution.py:269
  7.3 8.5 %copy-start.8 = (s32[2,64,8]{1,2,0:T(8,128)S(1)}, s32[2,64,8]{1,2,0:T(8,128)}, u32[]{:S(2)}) copy-start(s32[2,64,8]{1,2,0:T(8,128)} %param.10) | copy-start | bytes 12292
  7.3 8.5 %copy-start.9 = (s32[2,64,8]{1,2,0:T(8,128)S(1)}, s32[2,64,8]{1,2,0:T(8,128)}, u32[]{:S(2)}) copy-start(s32[2,64,8]{1,2,0:T(8,128)} %param.9) | copy-start | bytes 12292
  7.3 8.6 %copy-start.10 = (f32[2,64,8]{1,2,0:T(8,128)S(1)}, f32[2,64,8]{1,2,0:T(8,128)}, u32[]{:S(2)}) copy-start(f32[2,64,8]{1,2,0:T(8,128)} %param.11) | copy-start | bytes 12292
  10.3 15.6 %collective-permute-start.1 = (bf16[576,384]{1,0:T(8,128)(2,1)S(1)}, bf16[576,384]{1,0:T(8,128)(2,1)S(1)}, u32[]{:S(2)}, u32[]{:S(2)}) collective-permute-start(bf16[576,384]{1,0:T(8,128)(2,1)S(1)} %broadcast_select_fusion.5), channel_id=1, source_target_pairs={{0,2},{1,3},{2,0},{3,1},{4,6},{5,7},{6,4},{7,5},{8,10},{9,11},{10,... | collective-permute-start | bytes 1327112 | tf_op jit(solution)/shard_map/ppermute | solution.py:243
  18.6 6.4 %collective-permute-start = (bf16[128,576]{1,0:T(8,128)(2,1)}, bf16[128,576]{1,0:T(8,128)(2,1)S(1)}, u32[]{:S(2)}, u32[]{:S(2)}) collective-permute-start(bf16[128,576]{1,0:T(8,128)(2,1)} %pad_maximum_fusion.2), channel_id=1, source_target_pairs={{0,128},{128,0},{1,129},{129,1},{2,130},{130,2},{3,131},{131,3},{4... | collective-permute-start | bytes 442376 | tf_op jit(solution)/shard_map/ppermute | solution.py:266
  28.2 49.9 %all-to-all-start = ((bf16[4,576,384]{2,1,0:T(8,128)(2,1)}), bf16[4,576,384]{2,1,0:T(8,128)(2,1)S(1)}, u32[]{:S(2)}, u32[]{:S(2)}) async-start(bf16[4,576,384]{2,1,0:T(8,128)(2,1)} %broadcast_in_dim.50), calls=%async_computation | async-start | bytes 3538944 | tf_op jit(solution)/shard_map/all_to_all | solution.py:211
  32.7 45.4 %collective-permute-start.2 = (bf16[576,384]{1,0:T(8,128)(2,1)}, bf16[576,384]{1,0:T(8,128)(2,1)S(1)}, u32[]{:S(2)}, u32[]{:S(2)}) collective-permute-start(bf16[576,384]{1,0:T(8,128)(2,1)} %get-tuple-element.48), channel_id=1, source_target_pairs={{0,256},{256,0},{1,257},{257,1},{2,258},{258,2},{3,259},{259,3},{4... | collective-permute-start | bytes 1327112 | tf_op jit(solution)/shard_map/ppermute | solution.py:245
  78.1 31.3 %collective-permute-start.6 = (bf16[4,576,384]{2,1,0:T(8,128)(2,1)S(1)}, bf16[4,576,384]{2,1,0:T(8,128)(2,1)}, u32[]{:S(2)}, u32[]{:S(2)}) collective-permute-start(bf16[4,576,384]{2,1,0:T(8,128)(2,1)S(1)} %all-to-all-done.near0.near1.refs_4_.refs_5_), channel_id=1, source_target_pairs={{0,128},{128,0},{1,129},{129,1},{2,130},{130,2},{3,131},{131,3},{4... | collective-permute-start | bytes 5308424 | tf_op jit(solution)/shard_map/ppermute | solution.py:272
  94.6 13.4 %collective-permute-start.7 = (bf16[512,384]{1,0:T(8,128)(2,1)}, bf16[512,384]{1,0:T(8,128)(2,1)}, u32[]{:S(2)}, u32[]{:S(2)}) collective-permute-start(bf16[512,384]{1,0:T(8,128)(2,1)} %select_bitcast_fusion.1), channel_id=1, source_target_pairs={{0,128},{128,0},{1,129},{129,1},{2,130},{130,2},{3,131},{131,3},{4... | collective-permute-start | bytes 1179656 | tf_op jit(solution)/shard_map/ppermute | solution.py:250
  96.6 19.1 %collective-permute-start.3 = (bf16[576,384]{1,0:T(8,128)(2,1)S(1)}, bf16[576,384]{1,0:T(8,128)(2,1)S(1)}, u32[]{:S(2)}, u32[]{:S(2)}) collective-permute-start(bf16[576,384]{1,0:T(8,128)(2,1)S(1)} %collective-permute-done.2), channel_id=1, source_target_pairs={{0,1},{1,2},{2,3},{3,0},{4,5},{5,6},{6,7},{7,4},{8,9},{9,10},{10,1... | collective-permute-start | bytes 1327112 | tf_op jit(solution)/shard_map/ppermute | solution.py:217
  100.5 21.7 %collective-permute-start.4 = (bf16[576,384]{1,0:T(8,128)(2,1)S(1)}, bf16[576,384]{1,0:T(8,128)(2,1)S(1)}, u32[]{:S(2)}, u32[]{:S(2)}) collective-permute-start(bf16[576,384]{1,0:T(8,128)(2,1)S(1)} %collective-permute-done.2), channel_id=1, source_target_pairs={{0,2},{1,3},{2,0},{3,1},{4,6},{5,7},{6,4},{7,5},{8,10},{9,11},{10,... | collective-permute-start | bytes 1327112 | tf_op jit(solution)/shard_map/ppermute | solution.py:217
  104.9 18.8 %collective-permute-start.5 = (bf16[576,384]{1,0:T(8,128)(2,1)S(1)}, bf16[576,384]{1,0:T(8,128)(2,1)S(1)}, u32[]{:S(2)}, u32[]{:S(2)}) collective-permute-start(bf16[576,384]{1,0:T(8,128)(2,1)S(1)} %collective-permute-done.2), channel_id=1, source_target_pairs={{0,3},{1,0},{2,1},{3,2},{4,7},{5,4},{6,5},{7,6},{8,11},{9,8},{10,9... | collective-permute-start | bytes 1327112 | tf_op jit(solution)/shard_map/ppermute | solution.py:217
  109.4 6.2 %copy-start.2 = (bf16[2,512,384]{2,1,0:T(8,128)(2,1)}, bf16[2,512,384]{2,1,0:T(8,128)(2,1)S(1)}, u32[]{:S(2)}) copy-start(bf16[2,512,384]{2,1,0:T(8,128)(2,1)S(1)} %pad_maximum_fusion.1.weight_ref) | copy-start | bytes 2359300
  125.1 7.7 %collective-permute-start.8 = (bf16[4,576,384]{2,1,0:T(8,128)(2,1)}, bf16[4,576,384]{2,1,0:T(8,128)(2,1)}, u32[]{:S(2)}, u32[]{:S(2)}) collective-permute-start(bf16[4,576,384]{2,1,0:T(8,128)(2,1)} %pad_maximum_fusion.near0.near1.refs_4_.refs_5_), channel_id=1, source_target_pairs={{0,128},{128,0},{1,129},{129,1},{2,130},{130,2},{3,131},{131,3},{4... | collective-permute-start | bytes 5308424 | tf_op jit(solution)/shard_map/ppermute | solution.py:277
  128.3 33.9 %all-to-all-start.1 = ((bf16[4,576,512]{2,1,0:T(8,128)(2,1)}), bf16[4,576,512]{2,1,0:T(8,128)(2,1)}, u32[]{:S(2)}, u32[]{:S(2)}) async-start(bf16[4,576,512]{2,1,0:T(8,128)(2,1)} %bitcast.88), calls=%async_computation.1 | async-start | bytes 4718592 | tf_op jit(solution)/shard_map/all_to_all | solution.py:223
  132.8 1.1 copy-start.3
  162.2 33.0 %all-to-all-start.2 = ((bf16[4,576,512]{2,1,0:T(8,128)(2,1)}), bf16[4,576,512]{2,1,0:T(8,128)(2,1)}, u32[]{:S(2)}, u32[]{:S(2)}) async-start(bf16[4,576,512]{2,1,0:T(8,128)(2,1)} %bitcast.87), calls=%async_computation.2 | async-start | bytes 4718592 | tf_op jit(solution)/shard_map/all_to_all | solution.py:223
  166.7 114.1 %reduce-scatter.2.cloned.1.call-start = ((), (), s32[]{:S(2)}) async-start(), calls=%async_computation.6 | async-start | bytes 4456448 | tf_op jit(solution)/shard_map/reduce_scatter | solution.py:301
  203.8 1.7 copy-start.1
  210.1 13.0 %copy-start.4 = (bf16[2,2,144,512]{3,2,1,0:T(8,128)(2,1)}, bf16[2,2,144,512]{3,2,1,0:T(8,128)(2,1)S(1)}, u32[]{:S(2)}) copy-start(bf16[2,2,144,512]{3,2,1,0:T(8,128)(2,1)S(1)} %get-tuple-element.42) | copy-start | bytes 1769476
  210.1 19.2 %collective-permute-start.13 = (bf16[2,2,144,512]{3,2,1,0:T(8,128)(2,1)S(1)}, bf16[2,2,144,512]{3,2,1,0:T(8,128)(2,1)S(1)}, u32[]{:S(2)}, u32[]{:S(2)}) collective-permute-start(bf16[2,2,144,512]{3,2,1,0:T(8,128)(2,1)S(1)} %get-tuple-element.43), channel_id=1, source_target_pairs={{0,4},{4,8},{8,12},{12,0},{1,5},{5,9},{9,13},{13,1},{2,6},{6,10},{... | collective-permute-start | bytes 1769480 | tf_op jit(solution)/shard_map/ppermute | solution.py:228
  212.3 31.4 %collective-permute-start.14 = (bf16[2,2,144,512]{3,2,1,0:T(8,128)(2,1)}, bf16[2,2,144,512]{3,2,1,0:T(8,128)(2,1)}, u32[]{:S(2)}, u32[]{:S(2)}) collective-permute-start(bf16[2,2,144,512]{3,2,1,0:T(8,128)(2,1)} %get-tuple-element.44), channel_id=1, source_target_pairs={{0,8},{4,12},{8,0},{12,4},{1,9},{5,13},{9,1},{13,5},{2,10},{6,14},... | collective-permute-start | bytes 1769480 | tf_op jit(solution)/shard_map/ppermute | solution.py:228
  215.9 28.8 %collective-permute-start.15 = (bf16[2,2,144,512]{3,2,1,0:T(8,128)(2,1)}, bf16[2,2,144,512]{3,2,1,0:T(8,128)(2,1)}, u32[]{:S(2)}, u32[]{:S(2)}) collective-permute-start(bf16[2,2,144,512]{3,2,1,0:T(8,128)(2,1)} %get-tuple-element.45), channel_id=1, source_target_pairs={{0,12},{4,0},{8,4},{12,8},{1,13},{5,1},{9,5},{13,9},{2,14},{6,2},{... | collective-permute-start | bytes 1769480 | tf_op jit(solution)/shard_map/ppermute | solution.py:228
  223.1 31.5 %collective-permute-start.10 = (bf16[2,2,144,512]{3,2,1,0:T(8,128)(2,1)}, bf16[2,2,144,512]{3,2,1,0:T(8,128)(2,1)}, u32[]{:S(2)}, u32[]{:S(2)}) collective-permute-start(bf16[2,2,144,512]{3,2,1,0:T(8,128)(2,1)} %get-tuple-element.39), channel_id=1, source_target_pairs={{0,4},{4,8},{8,12},{12,0},{1,5},{5,9},{9,13},{13,1},{2,6},{6,10},{... | collective-permute-start | bytes 1769480 | tf_op jit(solution)/shard_map/ppermute | solution.py:228
  225.8 38.0 %collective-permute-start.11 = (bf16[2,2,144,512]{3,2,1,0:T(8,128)(2,1)}, bf16[2,2,144,512]{3,2,1,0:T(8,128)(2,1)}, u32[]{:S(2)}, u32[]{:S(2)}) collective-permute-start(bf16[2,2,144,512]{3,2,1,0:T(8,128)(2,1)} %get-tuple-element.40), channel_id=1, source_target_pairs={{0,8},{4,12},{8,0},{12,4},{1,9},{5,13},{9,1},{13,5},{2,10},{6,14},... | collective-permute-start | bytes 1769480 | tf_op jit(solution)/shard_map/ppermute | solution.py:228
  230.1 37.9 %collective-permute-start.12 = (bf16[2,2,144,512]{3,2,1,0:T(8,128)(2,1)}, bf16[2,2,144,512]{3,2,1,0:T(8,128)(2,1)}, u32[]{:S(2)}, u32[]{:S(2)}) collective-permute-start(bf16[2,2,144,512]{3,2,1,0:T(8,128)(2,1)} %get-tuple-element.41), channel_id=1, source_target_pairs={{0,12},{4,0},{8,4},{12,8},{1,13},{5,1},{9,5},{13,9},{2,14},{6,2},{... | collective-permute-start | bytes 1769480 | tf_op jit(solution)/shard_map/ppermute | solution.py:228
  239.4 39.7 %all-to-all-start.3 = ((bf16[4,128,1024]{2,1,0:T(8,128)(2,1)}), bf16[4,128,1024]{2,1,0:T(8,128)(2,1)}, u32[]{:S(2)}, u32[]{:S(2)}) async-start(bf16[4,128,1024]{2,1,0:T(8,128)(2,1)} %copy.89), calls=%async_computation.3 | async-start | bytes 2097152 | tf_op jit(solution)/shard_map/all_to_all | solution.py:321
  245.8 1.1 copy-start.7
  275.5 5.1 %collective-permute-start.16 = (bf16[512,384]{1,0:T(8,128)(2,1)S(1)}, bf16[512,384]{1,0:T(8,128)(2,1)S(1)}, u32[]{:S(2)}, u32[]{:S(2)}) collective-permute-start(bf16[512,384]{1,0:T(8,128)(2,1)S(1)} %select_bitcast_fusion), channel_id=1, source_target_pairs={{0,128},{128,0},{1,129},{129,1},{2,130},{130,2},{3,131},{131,3},{4... | collective-permute-start | bytes 1179656 | tf_op jit(solution)/shard_map/ppermute | solution.py:318
  281.7 8.4 %collective-permute-start.9 = (bf16[128,512]{1,0:T(8,128)(2,1)S(1)}, bf16[128,512]{1,0:T(8,128)(2,1)S(1)}, u32[]{:S(2)}, u32[]{:S(2)}) collective-permute-start(bf16[128,512]{1,0:T(8,128)(2,1)S(1)} %slice.89), channel_id=1, source_target_pairs={{0,128},{128,0},{1,129},{129,1},{2,130},{130,2},{3,131},{131,3},{4... | collective-permute-start | bytes 393224 | tf_op jit(solution)/shard_map/ppermute | solution.py:325
  (2 other events, 1.9 us)
Sparse Core Ops, SparseCore 0:
  26.9 109.8 all-gather.1
  201.5 75.3 reduce-scatter.1

commit v10 on v9

--- a/solution.py
+++ b/solution.py
@@ -97,6 +97,33 @@
     )(where, near, near, other, other, weight)
 
 
+def rows_away(near, other, weight, where):
+    _, rows, ff = near.shape
+    width = weight.shape[1]
+    part = rows // 2
+
+    def body(where_ref, near0, near1, other0, other1, weight_ref, *out_refs):
+        for d, out_ref in enumerate(out_refs):
+
+            @pl.when(pl.program_id(0) == d)
+            def _():
+                for k, (first, second) in enumerate(((near0, near1), (other0, other1))):
+                    total = dot(first[0], weight_ref[0], (1, 1))
+                    total += dot(second[0], weight_ref[1], (1, 1))
+                    out_ref[k] = total.astype(BF16)
+
+    pieces = quarters_of(part, ff, lambda d, where: (where[0] + d) & 3, True)
+    return call(
+        body,
+        (4,),
+        pieces + pieces + [pl.BlockSpec(weight.shape, lambda d, where: (0, 0, 0))],
+        [pl.BlockSpec((2, part, width), lambda d, where: (0, 0, 0))] * 4,
+        [jax.ShapeDtypeStruct((2, part, width), BF16)] * 4,
+        1,
+        32 * part * ff * width,
+    )(where, near, near, other, other, weight)
+
+
 def combine(half, returned, table, far, tok, so_far):
     _, _, batches, part, width = returned.shape
     rows = 4 * part
@@ -127,6 +154,37 @@
         16 * rows * 8 * tok * width,
         aliases={3: 0} if extra else {},
     )(far, returned, table, *extra)
+
+
+def combine_parts(half, returned, table, far, tok, so_far):
+    returned = [returned[d] for d in (0, 3, 2, 1)]
+    _, batches, part, width = returned[0].shape
+    rows = 4 * part
+
+    def body(zh_ref, *refs):
+        out_ref, table_ref = refs[-1], refs[4]
+        seat = table_ref[0, 0:1, :].astype(I32)
+        hit = seat == lax.broadcasted_iota(I32, (8 * tok, rows), 0)
+        gate = jnp.where(hit, table_ref[0, 1:2, :], 0.0)
+        high = gate.astype(BF16)
+        low = (gate - high.astype(F32)).astype(BF16)
+        source = jnp.concatenate([ref[0, 0] for ref in refs[:4]], axis=0)
+        total = dot(high, source, (1, 0)) + dot(low, source, (1, 0))
+        out_ref[...] = total.astype(BF16).reshape(out_ref.shape)
+
+    extra = () if so_far is None else (so_far,)
+    return call(
+        body,
+        (2, batches),
+        [pl.BlockSpec((1, 1, part, width), lambda k, m, zh: (k, m, 0, 0))] * 4
+        + [pl.BlockSpec((1, 2, rows), lambda k, m, zh: (half * 4 + k * 2 + m, 0, 0))]
+        + [pl.BlockSpec(memory_space=pl.ANY)] * len(extra),
+        pl.BlockSpec((1, 8, 1, tok, width), lambda k, m, zh: (zh[0] ^ half, 0, m, 0, k)),
+        jax.ShapeDtypeStruct((2, 8, batches, tok, 2 * width), BF16),
+        1,
+        16 * rows * 8 * tok * width,
+        aliases={6: 0} if extra else {},
+    )(far, *returned, table, *extra)
 
 
 def weight_sum(inbound, near, other, where, relative, so_far, scale, kind):
@@ -275,9 +333,8 @@
     back = swap_y(back)
     wide = jnp.stack(wide)
     wide_other = lax.ppermute(wide, "co", SWAP)
-    wide_back = rows_back(wide, wide_other, weight, here, True)
-    wide_back, back = lax.optimization_barrier((wide_back, back))
-    wide_back = swap_y(wide_back)
+    split = (2, batches, nzl * capacity, eighth)
+    wide_back = along_y(rows_away(wide, wide_other, weight, here), split)
 
     column = lax.dynamic_slice(
         line.reshape(2 * nzl, batches * tok, -1),
@@ -294,10 +351,11 @@
     column = jnp.stack([seats, column[1] + (column[2] + column[3])])
     lying = column.reshape(2, 4 * batches, buffer_rows).transpose(1, 0, 2)
     column = lax.dynamic_slice_in_dim(jnp.concatenate([column, column], axis=2), y, ny, 2)
-    standing = column.reshape(2, 4 * batches, buffer_rows).transpose(1, 2, 0)
+    column = column.reshape(2, 4 * batches, buffer_rows)
+    turned, standing = column.transpose(1, 0, 2), column.transpose(1, 2, 0)
 
     spread = combine(0, back, lying, far, tok, None)
-    spread = combine(1, wide_back, lying, far, tok, spread)
+    spread = combine_parts(1, wide_back, turned, far, tok, spread)
     expert_part = lax.psum_scatter(
         spread.reshape(2 * nzl * batches * tok, quarter),
         ("zh", "zl"),

time: 302 us -> 293 us (0.970)
  waiting for transfers between devices: 95.4 us -> 72.4 us
  local copies, waits for them, and re-layouts: 19.8 us -> 27 us
  starting transfers between devices: 104 us -> 109 us
    all_to_all x2 -> x1, waiting for transfers between devices: 40 us -> 0.01 us  [swap_y(): v = lax.all_to_all(v, 'y', split_axis=0, concat_axis=0, tiled=True)]
    ppermute x6 -> x9, waiting for transfers between devices: 15.3 us -> 32.9 us  [along_y(): lax.ppermute(v, 'y', [(i, (i + d) % ny) for i in range(ny)])]
    pallas_call x0 -> x2, Pallas kernels: none -> 13.1 us  [the longest x1 6.85 us: rows_away(): call(body, (4,), pieces + pieces + [pl.BlockSpec(weight.shape, lambda d,...]
    ppermute x6 -> x9, starting transfers between devices: 18.7 us -> 28.2 us  [along_y(): lax.ppermute(v, 'y', [(i, (i + d) % ny) for i in range(ny)])]
    pallas_call x2 -> x1, Pallas kernels: 12.8 us -> 6.25 us  [rows_back(): call(body, (4,), pieces + pieces + [pl.BlockSpec(weight.shape, lambda d,...]
    pallas_call x2 -> x1, Pallas kernels: 12.5 us -> 6.21 us  [combine(): call(body, (2, batches), [pl.BlockSpec((4, 1, 1, part, width), lambda k,...]
    all_to_all x2 -> x1, starting transfers between devices: 9.01 us -> 4.5 us  [swap_y(): v = lax.all_to_all(v, 'y', split_axis=0, concat_axis=0, tiled=True)]
    unnamed x25 -> x29, local copies, waits for them, and re-layouts: 5.89 us -> 6.51 us
  transfers between devices with their start and end apart: 23 -> 25, of which waited for: 10 -> 9; matrix products, arithmetic and copies ran while one was open for 8% -> 11% of each run, Pallas kernels for 14% -> 15%
where the time goes in v10:
time: 293 us; the launch traced here: 291 us
  starting transfers between devices  109 us (37%)
  waiting for transfers between devices  72.4 us (25%)
  Pallas kernels  48.9 us (17%)
  local copies, waits for them, and re-layouts  27 us (9%)
  other arithmetic  15.4 us (5%)
  between operations  14.8 us (5%)
    ppermute x9, waiting for transfers between devices, along_y(): lax.ppermute(v, 'y', [(i, (i + d) % ny) for i in range(ny)])  32.9 us
    ppermute x1, waiting for transfers between devices, on_device(): crossed = lax.ppermute(leave, 'zh', SWAP)  30.3 us
    ppermute x9, starting transfers between devices, along_y(): lax.ppermute(v, 'y', [(i, (i + d) % ny) for i in range(ny)])  28.2 us
    ppermute x1, starting transfers between devices, on_device(): near_other = lax.ppermute(near, 'co', SWAP)  15.2 us
    ppermute x1, starting transfers between devices, on_device(): crossed = lax.ppermute(leave, 'zh', SWAP)  14.6 us
    pallas_call x2, Pallas kernels, weight_sum(): call(body, (4,), [pl.BlockSpec((2, part, width), lambda d, where: (0, 0,...  14.3 us
    ppermute x3, starting transfers between devices, gather_back(): lax.ppermute(v, 'x', [(i, (i + d) % nx) for i in range(nx)])  11.4 us
    pallas_call x2, Pallas kernels, pick_rows(): call(body, (2, batches), [pl.BlockSpec((8, 1, tok, width), lambda k, m, z...  9.12 us
  transfers between devices with their start and end apart: 25, of which 9 were waited for; matrix products, arithmetic and copies ran while one was open for 11% of the time, Pallas kernels for 15%

profile of v10, /device:TPU:1, one launch (start us, length us, event | category | flops | bytes accessed | tf_op | source)
XLA Modules:
  0.0 290.5 jit_solution(5470758863082401894)
XLA Ops:
  7.3 2.9 fusion.1
  10.3 5.5 %collective-permute-start.1 = (bf16[576,384]{1,0:T(8,128)(2,1)S(1)}, bf16[576,384]{1,0:T(8,128)(2,1)S(1)}, u32[]{:S(2)}, u32[]{:S(2)}) collective-permute-start(bf16[576,384]{1,0:T(8,128)(2,1)S(1)} %broadcast_select_fusion.5), channel_id=1, source_target_pairs={{0,2},{1,3},{2,0},{3,1},{4,6},{5,7},{6,4},{7,5},{8,10},{9,11},{10,... | collective-permute-start | bytes 1327112 | tf_op jit(solution)/shard_map/ppermute | solution.py:301
  18.6 5.2 %collective-permute-start = (bf16[128,576]{1,0:T(8,128)(2,1)}, bf16[128,576]{1,0:T(8,128)(2,1)S(1)}, u32[]{:S(2)}, u32[]{:S(2)}) collective-permute-start(bf16[128,576]{1,0:T(8,128)(2,1)} %pad_maximum_fusion.2), channel_id=1, source_target_pairs={{0,128},{128,0},{1,129},{129,1},{2,130},{130,2},{3,131},{131,3},{4... | collective-permute-start | bytes 442376 | tf_op jit(solution)/shard_map/ppermute | solution.py:324
  28.1 4.5 %all-to-all-start = ((bf16[4,576,384]{2,1,0:T(8,128)(2,1)}), bf16[4,576,384]{2,1,0:T(8,128)(2,1)S(1)}, u32[]{:S(2)}, u32[]{:S(2)}) async-start(bf16[4,576,384]{2,1,0:T(8,128)(2,1)} %broadcast_in_dim.50), calls=%async_computation | async-start | bytes 3538944 | tf_op jit(solution)/shard_map/all_to_all | solution.py:269
  32.6 14.6 %collective-permute-start.2 = (bf16[576,384]{1,0:T(8,128)(2,1)}, bf16[576,384]{1,0:T(8,128)(2,1)S(1)}, u32[]{:S(2)}, u32[]{:S(2)}) collective-permute-start(bf16[576,384]{1,0:T(8,128)(2,1)} %get-tuple-element.52), channel_id=1, source_target_pairs={{0,256},{256,0},{1,257},{257,1},{2,258},{258,2},{3,259},{259,3},{4... | collective-permute-start | bytes 1327112 | tf_op jit(solution)/shard_map/ppermute | solution.py:303
  47.2 30.3 %collective-permute-done.2 = bf16[576,384]{1,0:T(8,128)(2,1)S(1)} collective-permute-done((bf16[576,384]{1,0:T(8,128)(2,1)}, bf16[576,384]{1,0:T(8,128)(2,1)S(1)}, u32[]{:S(2)}, u32[]{:S(2)}) %collective-permute-start.2) | collective-permute-done | bytes 442400 | tf_op jit(solution)/shard_map/ppermute | solution.py:303
  77.5 15.2 %collective-permute-start.6 = (bf16[4,576,384]{2,1,0:T(8,128)(2,1)S(1)}, bf16[4,576,384]{2,1,0:T(8,128)(2,1)}, u32[]{:S(2)}, u32[]{:S(2)}) collective-permute-start(bf16[4,576,384]{2,1,0:T(8,128)(2,1)S(1)} %all-to-all-done.near0.near1.refs_4_.refs_5_), channel_id=1, source_target_pairs={{0,128},{128,0},{1,129},{129,1},{2,130},{130,2},{3,131},{131,3},{4... | collective-permute-start | bytes 5308424 | tf_op jit(solution)/shard_map/ppermute | solution.py:330
  96.6 4.0 %collective-permute-start.3 = (bf16[576,384]{1,0:T(8,128)(2,1)S(1)}, bf16[576,384]{1,0:T(8,128)(2,1)S(1)}, u32[]{:S(2)}, u32[]{:S(2)}) collective-permute-start(bf16[576,384]{1,0:T(8,128)(2,1)S(1)} %collective-permute-done.2), channel_id=1, source_target_pairs={{0,1},{1,2},{2,3},{3,0},{4,5},{5,6},{6,7},{7,4},{8,9},{9,10},{10,1... | collective-permute-start | bytes 1327112 | tf_op jit(solution)/shard_map/ppermute | solution.py:275
  100.5 4.3 %collective-permute-start.4 = (bf16[576,384]{1,0:T(8,128)(2,1)S(1)}, bf16[576,384]{1,0:T(8,128)(2,1)S(1)}, u32[]{:S(2)}, u32[]{:S(2)}) collective-permute-start(bf16[576,384]{1,0:T(8,128)(2,1)S(1)} %collective-permute-done.2), channel_id=1, source_target_pairs={{0,2},{1,3},{2,0},{3,1},{4,6},{5,7},{6,4},{7,5},{8,10},{9,11},{10,... | collective-permute-start | bytes 1327112 | tf_op jit(solution)/shard_map/ppermute | solution.py:275
  104.8 3.1 %collective-permute-start.5 = (bf16[576,384]{1,0:T(8,128)(2,1)S(1)}, bf16[576,384]{1,0:T(8,128)(2,1)S(1)}, u32[]{:S(2)}, u32[]{:S(2)}) collective-permute-start(bf16[576,384]{1,0:T(8,128)(2,1)S(1)} %collective-permute-done.2), channel_id=1, source_target_pairs={{0,3},{1,0},{2,1},{3,2},{4,7},{5,4},{6,5},{7,6},{8,11},{9,8},{10,9... | collective-permute-start | bytes 1327112 | tf_op jit(solution)/shard_map/ppermute | solution.py:275
  109.4 6.2 %shard_map.95 = bf16[4,2,288,512]{3,2,1,0:T(8,128)(2,1)} custom-call(s32[2]{0:T(128)S(1)} %pad_add_fusion.where_ref, bf16[4,576,384]{2,1,0:T(8,128)(2,1)S(1)} %all-to-all-done.near0.near1.refs_4_.refs_5_, bf16[4,576,384]{2,1,0:T(8,128)(2,1)S(1)} %all-to-all-done.near0.near1.refs_4_.refs_5_, ...), custom_call_target="tpu_custom_call" | custom-call | flops 1811939328 | bytes 8388608 | tf_op jit(solution)/shard_map/pallas_call | solution.py:89
  115.7 6.5 %collective-permute-done.4 = bf16[576,384]{1,0:T(8,128)(2,1)S(1)} collective-permute-done((bf16[576,384]{1,0:T(8,128)(2,1)S(1)}, bf16[576,384]{1,0:T(8,128)(2,1)S(1)}, u32[]{:S(2)}, u32[]{:S(2)}) %collective-permute-start.4) | collective-permute-done | bytes 442400 | tf_op jit(solution)/shard_map/ppermute | solution.py:275
  125.2 3.1 %collective-permute-start.8 = (bf16[4,576,384]{2,1,0:T(8,128)(2,1)}, bf16[4,576,384]{2,1,0:T(8,128)(2,1)}, u32[]{:S(2)}, u32[]{:S(2)}) collective-permute-start(bf16[4,576,384]{2,1,0:T(8,128)(2,1)} %pad_maximum_fusion.near0.near1.refs_4_.refs_5_), channel_id=1, source_target_pairs={{0,128},{128,0},{1,129},{129,1},{2,130},{130,2},{3,131},{131,3},{4... | collective-permute-start | bytes 5308424 | tf_op jit(solution)/shard_map/ppermute | solution.py:335
  128.3 4.5 %all-to-all-start.1 = ((bf16[4,576,512]{2,1,0:T(8,128)(2,1)}), bf16[4,576,512]{2,1,0:T(8,128)(2,1)}, u32[]{:S(2)}, u32[]{:S(2)}) async-start(bf16[4,576,512]{2,1,0:T(8,128)(2,1)} %bitcast.94), calls=%async_computation.1 | async-start | bytes 4718592 | tf_op jit(solution)/shard_map/all_to_all | solution.py:281
  134.2 6.9 %shard_map.96 = (bf16[2,288,512]{2,1,0:T(8,128)(2,1)S(1)}, bf16[2,288,512]{2,1,0:T(8,128)(2,1)}, bf16[2,288,512]{2,1,0:T(8,128)(2,1)}, bf16[2,288,512]{2,1,0:T(8,128)(2,1)}) custom-call(s32[2]{0:T(128)S(1)} %pad_add_fusion.where_ref, bf16[4,576,384]{2,1,0:T(8,128)(2,1)} %pad_maximum_fusion.near0.near1.refs_4_.refs_5_, ...), custom_call_target="tpu_custom_call" | custom-call | flops 1811939328 | bytes 8388608 | tf_op jit(solution)/shard_map/pallas_call | solution.py:116
  141.1 4.6 %collective-permute-start.9 = (bf16[2,288,512]{2,1,0:T(8,128)(2,1)}, bf16[2,288,512]{2,1,0:T(8,128)(2,1)}, u32[]{:S(2)}, u32[]{:S(2)}) collective-permute-start(bf16[2,288,512]{2,1,0:T(8,128)(2,1)} %get-tuple-element.37), channel_id=1, source_target_pairs={{0,12},{4,0},{8,4},{12,8},{1,13},{5,1},{9,5},{13,9},{2,14},{6,2},{... | collective-permute-start | bytes 1769480 | tf_op jit(solution)/shard_map/ppermute | solution.py:286
  163.8 6.2 %shard_map.97.refs_5_ = bf16[2,8,2,64,1024]{4,3,2,1,0:T(8,128)(2,1)} custom-call(s32[1]{0:T(128)} %bitcast.4.zh_ref, bf16[4,2,2,144,512]{4,3,2,1,0:T(8,128)(2,1)} %bitcast.25.back_ref, f32[8,2,576]{2,1,0:T(2,128)S(1)} %maximum_bitcast_fusion.1.table_ref), custom_call_target="tpu_custom_call" | custom-call | flops 2415919104 | bytes 8388608 | tf_op jit(solution)/shard_map/pallas_call | solution.py:143
  170.0 3.4 %collective-permute-done.9 = bf16[2,288,512]{2,1,0:T(8,128)(2,1)} collective-permute-done((bf16[2,288,512]{2,1,0:T(8,128)(2,1)}, bf16[2,288,512]{2,1,0:T(8,128)(2,1)}, u32[]{:S(2)}, u32[]{:S(2)}) %collective-permute-start.9) | collective-permute-done | bytes 589856 | tf_op jit(solution)/shard_map/ppermute | solution.py:286
  174.9 12.9 %collective-permute-done.11 = bf16[2,288,512]{2,1,0:T(8,128)(2,1)} collective-permute-done((bf16[2,288,512]{2,1,0:T(8,128)(2,1)}, bf16[2,288,512]{2,1,0:T(8,128)(2,1)}, u32[]{:S(2)}, u32[]{:S(2)}) %collective-permute-start.11) | collective-permute-done | bytes 589856 | tf_op jit(solution)/shard_map/ppermute | solution.py:286
  187.7 6.2 %shard_map.98 = bf16[2,8,2,64,1024]{4,3,2,1,0:T(8,128)(2,1)} custom-call(s32[1]{0:T(128)} %bitcast.4.zh_ref, bf16[2,2,144,512]{3,2,1,0:T(8,128)(2,1)S(1)} %bitcast.85, bf16[2,2,144,512]{3,2,1,0:T(8,128)(2,1)} %bitcast.16.refs_1_, bf16[2,2,144,512]{3,2,1,0:T(8,128)(2,1)} %bitcast.17.refs_2_, ...), custom_call_target="tpu_custom_call", output_to_operand_aliasing={{}: (6, {})} | custom-call | flops 2415919104 | bytes 8388608 | tf_op jit(solution)/shard_map/pallas_call | solution.py:176
  197.7 4.5 %shard_map.100 = (bf16[2,2,144,512]{3,2,1,0:T(8,128)(2,1)S(1)}, bf16[2,2,144,512]{3,2,1,0:T(8,128)(2,1)S(1)}, bf16[2,2,144,512]{3,2,1,0:T(8,128)(2,1)}, bf16[2,2,144,512]{3,2,1,0:T(8,128)(2,1)}) custom-call(s32[1]{0:T(128)} %bitcast.4.zh_ref, bf16[16,2,64,1152]{3,2,1,0:T(8,128)(2,1)} %bitcast.91, f32[8,576,2]{2,1,0:T(8,128)S(1)} %bitcast.83), custom_call_target="tpu_custom_call" | custom-call | flops 1207959552 | bytes 8388608 | tf_op jit(solution)/shard_map/pallas_call | solution.py:50
  204.3 3.6 %collective-permute-start.17 = (bf16[2,2,144,512]{3,2,1,0:T(8,128)(2,1)}, bf16[2,2,144,512]{3,2,1,0:T(8,128)(2,1)}, u32[]{:S(2)}, u32[]{:S(2)}) collective-permute-start(bf16[2,2,144,512]{3,2,1,0:T(8,128)(2,1)} %get-tuple-element.48), channel_id=1, source_target_pairs={{0,8},{4,12},{8,0},{12,4},{1,9},{5,13},{9,1},{13,5},{2,10},{6,14},... | collective-permute-start | bytes 1769480 | tf_op jit(solution)/shard_map/ppermute | solution.py:286
  207.9 2.8 collective-permute-start.18
  210.7 4.6 %shard_map.99 = (bf16[2,2,144,512]{3,2,1,0:T(8,128)(2,1)S(1)}, bf16[2,2,144,512]{3,2,1,0:T(8,128)(2,1)}, bf16[2,2,144,512]{3,2,1,0:T(8,128)(2,1)}, bf16[2,2,144,512]{3,2,1,0:T(8,128)(2,1)}) custom-call(s32[1]{0:T(128)} %bitcast.4.zh_ref, bf16[16,2,64,1152]{3,2,1,0:T(8,128)(2,1)} %bitcast.92, f32[8,576,2]{2,1,0:T(8,128)S(1)} %bitcast.84), custom_call_target="tpu_custom_call" | custom-call | flops 1207959552 | bytes 8388608 | tf_op jit(solution)/shard_map/pallas_call | solution.py:50
  217.8 3.7 %collective-permute-start.14 = (bf16[2,2,144,512]{3,2,1,0:T(8,128)(2,1)}, bf16[2,2,144,512]{3,2,1,0:T(8,128)(2,1)}, u32[]{:S(2)}, u32[]{:S(2)}) collective-permute-start(bf16[2,2,144,512]{3,2,1,0:T(8,128)(2,1)} %get-tuple-element.44), channel_id=1, source_target_pairs={{0,8},{4,12},{8,0},{12,4},{1,9},{5,13},{9,1},{13,5},{2,10},{6,14},... | collective-permute-start | bytes 1769480 | tf_op jit(solution)/shard_map/ppermute | solution.py:286
  222.3 4.0 %collective-permute-start.15 = (bf16[2,2,144,512]{3,2,1,0:T(8,128)(2,1)}, bf16[2,2,144,512]{3,2,1,0:T(8,128)(2,1)}, u32[]{:S(2)}, u32[]{:S(2)}) collective-permute-start(bf16[2,2,144,512]{3,2,1,0:T(8,128)(2,1)} %get-tuple-element.45), channel_id=1, source_target_pairs={{0,12},{4,0},{8,4},{12,8},{1,13},{5,1},{9,5},{13,9},{2,14},{6,2},{... | collective-permute-start | bytes 1769480 | tf_op jit(solution)/shard_map/ppermute | solution.py:286
  231.5 4.5 %all-to-all-start.2 = ((bf16[4,128,1024]{2,1,0:T(8,128)(2,1)}), bf16[4,128,1024]{2,1,0:T(8,128)(2,1)}, u32[]{:S(2)}, u32[]{:S(2)}) async-start(bf16[4,128,1024]{2,1,0:T(8,128)(2,1)} %copy.98), calls=%async_computation.2 | async-start | bytes 2097152 | tf_op jit(solution)/shard_map/all_to_all | solution.py:379
  238.2 6.9 %shard_map.101.refs_8_ = f32[2,512,384]{2,1,0:T(8,128)S(1)} custom-call(s32[2]{0:T(128)S(1)} %pad_add_fusion.where_ref, bf16[2,288,512]{2,1,0:T(8,128)(2,1)S(1)} %bitcast.87, bf16[2,288,512]{2,1,0:T(8,128)(2,1)S(1)} %bitcast.88, bf16[2,288,512]{2,1,0:T(8,128)(2,1)} %bitcast.39.refs_2_, bf16[2,288,512]{2,1,0:T(8,128)(2,1)} %bitcast.40.refs_3_, ...), custom_call_target="tpu_custom_call" | custom-call | flops 1811939328 | bytes 8388608 | tf_op jit(solution)/shard_map/pallas_call | solution.py:218
  245.1 13.0 %collective-permute-done.13 = bf16[2,2,144,512]{3,2,1,0:T(8,128)(2,1)} collective-permute-done((bf16[2,2,144,512]{3,2,1,0:T(8,128)(2,1)}, bf16[2,2,144,512]{3,2,1,0:T(8,128)(2,1)}, u32[]{:S(2)}, u32[]{:S(2)}) %collective-permute-start.13) | collective-permute-done | bytes 589856 | tf_op jit(solution)/shard_map/ppermute | solution.py:286
  260.3 7.4 %shard_map.102 = bf16[2,512,384]{2,1,0:T(8,128)(2,1)S(1)} custom-call(s32[2]{0:T(128)S(1)} %pad_add_fusion.where_ref, bf16[2,288,512]{2,1,0:T(8,128)(2,1)S(1)} %bitcast.86, bf16[2,288,512]{2,1,0:T(8,128)(2,1)} %bitcast.34.refs_1_, bf16[2,288,512]{2,1,0:T(8,128)(2,1)} %bitcast.35.refs_2_, bf16[2,288,512]{2,1,0:T(8,128)(2,1)} %bitcast.36.refs_3_, ...), custom_call_target="tpu_custom_call" | custom-call | flops 1811939328 | bytes 8388608 | tf_op jit(solution)/shard_map/pallas_call | solution.py:218
  267.8 3.6 %collective-permute-start.19 = (bf16[512,384]{1,0:T(8,128)(2,1)S(1)}, bf16[512,384]{1,0:T(8,128)(2,1)S(1)}, u32[]{:S(2)}, u32[]{:S(2)}) collective-permute-start(bf16[512,384]{1,0:T(8,128)(2,1)S(1)} %select_bitcast_fusion), channel_id=1, source_target_pairs={{0,128},{128,0},{1,129},{129,1},{2,130},{130,2},{3,131},{131,3},{4... | collective-permute-start | bytes 1179656 | tf_op jit(solution)/shard_map/ppermute | solution.py:376
  274.0 7.0 %collective-permute-start.12 = (bf16[128,512]{1,0:T(8,128)(2,1)S(1)}, bf16[128,512]{1,0:T(8,128)(2,1)S(1)}, u32[]{:S(2)}, u32[]{:S(2)}) collective-permute-start(bf16[128,512]{1,0:T(8,128)(2,1)S(1)} %slice.89), channel_id=1, source_target_pairs={{0,128},{128,0},{1,129},{129,1},{2,130},{130,2},{3,131},{131,3},{4... | collective-permute-start | bytes 393224 | tf_op jit(solution)/shard_map/ppermute | solution.py:383
  (114 shorter events, 60.4 us)
Async XLA Ops:
  7.2 9.8 %copy-start = (bf16[2,64,4096]{2,1,0:T(8,128)(2,1)S(1)}, bf16[2,64,4096]{2,1,0:T(8,128)(2,1)}, u32[]{:S(2)}) copy-start(bf16[2,64,4096]{2,1,0:T(8,128)(2,1)} %param.8) | copy-start | bytes 3145732
  7.2 143.5 %all-gather.2.cloned.1.call-start = ((), (), s32[]{:S(2)}) async-start(), calls=%async_computation.4 | async-start | bytes 5013504 | tf_op jit(solution)/shard_map/all_gather | solution.py:327
  7.3 8.5 %copy-start.10 = (s32[2,64,8]{1,2,0:T(8,128)S(1)}, s32[2,64,8]{1,2,0:T(8,128)}, u32[]{:S(2)}) copy-start(s32[2,64,8]{1,2,0:T(8,128)} %param.10) | copy-start | bytes 12292
  7.3 8.5 %copy-start.11 = (s32[2,64,8]{1,2,0:T(8,128)S(1)}, s32[2,64,8]{1,2,0:T(8,128)}, u32[]{:S(2)}) copy-start(s32[2,64,8]{1,2,0:T(8,128)} %param.9) | copy-start | bytes 12292
  7.3 8.6 %copy-start.12 = (f32[2,64,8]{1,2,0:T(8,128)S(1)}, f32[2,64,8]{1,2,0:T(8,128)}, u32[]{:S(2)}) copy-start(f32[2,64,8]{1,2,0:T(8,128)} %param.11) | copy-start | bytes 12292
  10.3 15.6 %collective-permute-start.1 = (bf16[576,384]{1,0:T(8,128)(2,1)S(1)}, bf16[576,384]{1,0:T(8,128)(2,1)S(1)}, u32[]{:S(2)}, u32[]{:S(2)}) collective-permute-start(bf16[576,384]{1,0:T(8,128)(2,1)S(1)} %broadcast_select_fusion.5), channel_id=1, source_target_pairs={{0,2},{1,3},{2,0},{3,1},{4,6},{5,7},{6,4},{7,5},{8,10},{9,11},{10,... | collective-permute-start | bytes 1327112 | tf_op jit(solution)/shard_map/ppermute | solution.py:301
  18.6 6.4 %collective-permute-start = (bf16[128,576]{1,0:T(8,128)(2,1)}, bf16[128,576]{1,0:T(8,128)(2,1)S(1)}, u32[]{:S(2)}, u32[]{:S(2)}) collective-permute-start(bf16[128,576]{1,0:T(8,128)(2,1)} %pad_maximum_fusion.2), channel_id=1, source_target_pairs={{0,128},{128,0},{1,129},{129,1},{2,130},{130,2},{3,131},{131,3},{4... | collective-permute-start | bytes 442376 | tf_op jit(solution)/shard_map/ppermute | solution.py:324
  28.1 49.3 %all-to-all-start = ((bf16[4,576,384]{2,1,0:T(8,128)(2,1)}), bf16[4,576,384]{2,1,0:T(8,128)(2,1)S(1)}, u32[]{:S(2)}, u32[]{:S(2)}) async-start(bf16[4,576,384]{2,1,0:T(8,128)(2,1)} %broadcast_in_dim.50), calls=%async_computation | async-start | bytes 3538944 | tf_op jit(solution)/shard_map/all_to_all | solution.py:269
  32.6 44.8 %collective-permute-start.2 = (bf16[576,384]{1,0:T(8,128)(2,1)}, bf16[576,384]{1,0:T(8,128)(2,1)S(1)}, u32[]{:S(2)}, u32[]{:S(2)}) collective-permute-start(bf16[576,384]{1,0:T(8,128)(2,1)} %get-tuple-element.52), channel_id=1, source_target_pairs={{0,256},{256,0},{1,257},{257,1},{2,258},{258,2},{3,259},{259,3},{4... | collective-permute-start | bytes 1327112 | tf_op jit(solution)/shard_map/ppermute | solution.py:303
  77.5 31.9 %collective-permute-start.6 = (bf16[4,576,384]{2,1,0:T(8,128)(2,1)S(1)}, bf16[4,576,384]{2,1,0:T(8,128)(2,1)}, u32[]{:S(2)}, u32[]{:S(2)}) collective-permute-start(bf16[4,576,384]{2,1,0:T(8,128)(2,1)S(1)} %all-to-all-done.near0.near1.refs_4_.refs_5_), channel_id=1, source_target_pairs={{0,128},{128,0},{1,129},{129,1},{2,130},{130,2},{3,131},{131,3},{4... | collective-permute-start | bytes 5308424 | tf_op jit(solution)/shard_map/ppermute | solution.py:330
  94.6 13.4 %collective-permute-start.7 = (bf16[512,384]{1,0:T(8,128)(2,1)}, bf16[512,384]{1,0:T(8,128)(2,1)}, u32[]{:S(2)}, u32[]{:S(2)}) collective-permute-start(bf16[512,384]{1,0:T(8,128)(2,1)} %select_bitcast_fusion.1), channel_id=1, source_target_pairs={{0,128},{128,0},{1,129},{129,1},{2,130},{130,2},{3,131},{131,3},{4... | collective-permute-start | bytes 1179656 | tf_op jit(solution)/shard_map/ppermute | solution.py:308
  96.6 19.1 %collective-permute-start.3 = (bf16[576,384]{1,0:T(8,128)(2,1)S(1)}, bf16[576,384]{1,0:T(8,128)(2,1)S(1)}, u32[]{:S(2)}, u32[]{:S(2)}) collective-permute-start(bf16[576,384]{1,0:T(8,128)(2,1)S(1)} %collective-permute-done.2), channel_id=1, source_target_pairs={{0,1},{1,2},{2,3},{3,0},{4,5},{5,6},{6,7},{7,4},{8,9},{9,10},{10,1... | collective-permute-start | bytes 1327112 | tf_op jit(solution)/shard_map/ppermute | solution.py:275
  100.5 21.6 %collective-permute-start.4 = (bf16[576,384]{1,0:T(8,128)(2,1)S(1)}, bf16[576,384]{1,0:T(8,128)(2,1)S(1)}, u32[]{:S(2)}, u32[]{:S(2)}) collective-permute-start(bf16[576,384]{1,0:T(8,128)(2,1)S(1)} %collective-permute-done.2), channel_id=1, source_target_pairs={{0,2},{1,3},{2,0},{3,1},{4,6},{5,7},{6,4},{7,5},{8,10},{9,11},{10,... | collective-permute-start | bytes 1327112 | tf_op jit(solution)/shard_map/ppermute | solution.py:275
  104.8 18.8 %collective-permute-start.5 = (bf16[576,384]{1,0:T(8,128)(2,1)S(1)}, bf16[576,384]{1,0:T(8,128)(2,1)S(1)}, u32[]{:S(2)}, u32[]{:S(2)}) collective-permute-start(bf16[576,384]{1,0:T(8,128)(2,1)S(1)} %collective-permute-done.2), channel_id=1, source_target_pairs={{0,3},{1,0},{2,1},{3,2},{4,7},{5,4},{6,5},{7,6},{8,11},{9,8},{10,9... | collective-permute-start | bytes 1327112 | tf_op jit(solution)/shard_map/ppermute | solution.py:275
  109.4 6.3 %copy-start.2 = (bf16[2,512,384]{2,1,0:T(8,128)(2,1)}, bf16[2,512,384]{2,1,0:T(8,128)(2,1)S(1)}, u32[]{:S(2)}) copy-start(bf16[2,512,384]{2,1,0:T(8,128)(2,1)S(1)} %pad_maximum_fusion.1.weight_ref) | copy-start | bytes 2359300
  125.2 7.9 %collective-permute-start.8 = (bf16[4,576,384]{2,1,0:T(8,128)(2,1)}, bf16[4,576,384]{2,1,0:T(8,128)(2,1)}, u32[]{:S(2)}, u32[]{:S(2)}) collective-permute-start(bf16[4,576,384]{2,1,0:T(8,128)(2,1)} %pad_maximum_fusion.near0.near1.refs_4_.refs_5_), channel_id=1, source_target_pairs={{0,128},{128,0},{1,129},{129,1},{2,130},{130,2},{3,131},{131,3},{4... | collective-permute-start | bytes 5308424 | tf_op jit(solution)/shard_map/ppermute | solution.py:335
  128.3 35.5 %all-to-all-start.1 = ((bf16[4,576,512]{2,1,0:T(8,128)(2,1)}), bf16[4,576,512]{2,1,0:T(8,128)(2,1)}, u32[]{:S(2)}, u32[]{:S(2)}) async-start(bf16[4,576,512]{2,1,0:T(8,128)(2,1)} %bitcast.94), calls=%async_computation.1 | async-start | bytes 4718592 | tf_op jit(solution)/shard_map/all_to_all | solution.py:281
  132.8 140.2 %reduce-scatter.2.cloned.1.call-start = ((), (), s32[]{:S(2)}) async-start(), calls=%async_computation.5 | async-start | bytes 4456448 | tf_op jit(solution)/shard_map/reduce_scatter | solution.py:359
  141.1 32.3 %collective-permute-start.9 = (bf16[2,288,512]{2,1,0:T(8,128)(2,1)}, bf16[2,288,512]{2,1,0:T(8,128)(2,1)}, u32[]{:S(2)}, u32[]{:S(2)}) collective-permute-start(bf16[2,288,512]{2,1,0:T(8,128)(2,1)} %get-tuple-element.37), channel_id=1, source_target_pairs={{0,12},{4,0},{8,4},{12,8},{1,13},{5,1},{9,5},{13,9},{2,14},{6,2},{... | collective-permute-start | bytes 1769480 | tf_op jit(solution)/shard_map/ppermute | solution.py:286
  145.6 29.2 %collective-permute-start.10 = (bf16[2,288,512]{2,1,0:T(8,128)(2,1)}, bf16[2,288,512]{2,1,0:T(8,128)(2,1)}, u32[]{:S(2)}, u32[]{:S(2)}) collective-permute-start(bf16[2,288,512]{2,1,0:T(8,128)(2,1)} %get-tuple-element.38), channel_id=1, source_target_pairs={{0,8},{4,12},{8,0},{12,4},{1,9},{5,13},{9,1},{13,5},{2,10},{6,14},... | collective-permute-start | bytes 1769480 | tf_op jit(solution)/shard_map/ppermute | solution.py:286
  148.0 39.7 %collective-permute-start.11 = (bf16[2,288,512]{2,1,0:T(8,128)(2,1)}, bf16[2,288,512]{2,1,0:T(8,128)(2,1)}, u32[]{:S(2)}, u32[]{:S(2)}) collective-permute-start(bf16[2,288,512]{2,1,0:T(8,128)(2,1)} %get-tuple-element.39), channel_id=1, source_target_pairs={{0,4},{4,8},{8,12},{12,0},{1,5},{5,9},{9,13},{13,1},{2,6},{6,10},{... | collective-permute-start | bytes 1769480 | tf_op jit(solution)/shard_map/ppermute | solution.py:286
  202.3 13.0 %copy-start.4 = (bf16[2,2,144,512]{3,2,1,0:T(8,128)(2,1)}, bf16[2,2,144,512]{3,2,1,0:T(8,128)(2,1)S(1)}, u32[]{:S(2)}) copy-start(bf16[2,2,144,512]{3,2,1,0:T(8,128)(2,1)S(1)} %get-tuple-element.46) | copy-start | bytes 1769476
  202.3 19.2 %collective-permute-start.16 = (bf16[2,2,144,512]{3,2,1,0:T(8,128)(2,1)S(1)}, bf16[2,2,144,512]{3,2,1,0:T(8,128)(2,1)S(1)}, u32[]{:S(2)}, u32[]{:S(2)}) collective-permute-start(bf16[2,2,144,512]{3,2,1,0:T(8,128)(2,1)S(1)} %get-tuple-element.47), channel_id=1, source_target_pairs={{0,4},{4,8},{8,12},{12,0},{1,5},{5,9},{9,13},{13,1},{2,6},{6,10},{... | collective-permute-start | bytes 1769480 | tf_op jit(solution)/shard_map/ppermute | solution.py:286
  204.3 31.8 %collective-permute-start.17 = (bf16[2,2,144,512]{3,2,1,0:T(8,128)(2,1)}, bf16[2,2,144,512]{3,2,1,0:T(8,128)(2,1)}, u32[]{:S(2)}, u32[]{:S(2)}) collective-permute-start(bf16[2,2,144,512]{3,2,1,0:T(8,128)(2,1)} %get-tuple-element.48), channel_id=1, source_target_pairs={{0,8},{4,12},{8,0},{12,4},{1,9},{5,13},{9,1},{13,5},{2,10},{6,14},... | collective-permute-start | bytes 1769480 | tf_op jit(solution)/shard_map/ppermute | solution.py:286
  207.9 28.1 %collective-permute-start.18 = (bf16[2,2,144,512]{3,2,1,0:T(8,128)(2,1)}, bf16[2,2,144,512]{3,2,1,0:T(8,128)(2,1)}, u32[]{:S(2)}, u32[]{:S(2)}) collective-permute-start(bf16[2,2,144,512]{3,2,1,0:T(8,128)(2,1)} %get-tuple-element.49), channel_id=1, source_target_pairs={{0,12},{4,0},{8,4},{12,8},{1,13},{5,1},{9,5},{13,9},{2,14},{6,2},{... | collective-permute-start | bytes 1769480 | tf_op jit(solution)/shard_map/ppermute | solution.py:286
  215.3 42.8 %collective-permute-start.13 = (bf16[2,2,144,512]{3,2,1,0:T(8,128)(2,1)}, bf16[2,2,144,512]{3,2,1,0:T(8,128)(2,1)}, u32[]{:S(2)}, u32[]{:S(2)}) collective-permute-start(bf16[2,2,144,512]{3,2,1,0:T(8,128)(2,1)} %get-tuple-element.43), channel_id=1, source_target_pairs={{0,4},{4,8},{8,12},{12,0},{1,5},{5,9},{9,13},{13,1},{2,6},{6,10},{... | collective-permute-start | bytes 1769480 | tf_op jit(solution)/shard_map/ppermute | solution.py:286
  217.8 40.3 %collective-permute-start.14 = (bf16[2,2,144,512]{3,2,1,0:T(8,128)(2,1)}, bf16[2,2,144,512]{3,2,1,0:T(8,128)(2,1)}, u32[]{:S(2)}, u32[]{:S(2)}) collective-permute-start(bf16[2,2,144,512]{3,2,1,0:T(8,128)(2,1)} %get-tuple-element.44), channel_id=1, source_target_pairs={{0,8},{4,12},{8,0},{12,4},{1,9},{5,13},{9,1},{13,5},{2,10},{6,14},... | collective-permute-start | bytes 1769480 | tf_op jit(solution)/shard_map/ppermute | solution.py:286
  222.3 38.0 %collective-permute-start.15 = (bf16[2,2,144,512]{3,2,1,0:T(8,128)(2,1)}, bf16[2,2,144,512]{3,2,1,0:T(8,128)(2,1)}, u32[]{:S(2)}, u32[]{:S(2)}) collective-permute-start(bf16[2,2,144,512]{3,2,1,0:T(8,128)(2,1)} %get-tuple-element.45), channel_id=1, source_target_pairs={{0,12},{4,0},{8,4},{12,8},{1,13},{5,1},{9,5},{13,9},{2,14},{6,2},{... | collective-permute-start | bytes 1769480 | tf_op jit(solution)/shard_map/ppermute | solution.py:286
  231.5 39.8 %all-to-all-start.2 = ((bf16[4,128,1024]{2,1,0:T(8,128)(2,1)}), bf16[4,128,1024]{2,1,0:T(8,128)(2,1)}, u32[]{:S(2)}, u32[]{:S(2)}) async-start(bf16[4,128,1024]{2,1,0:T(8,128)(2,1)} %copy.98), calls=%async_computation.2 | async-start | bytes 2097152 | tf_op jit(solution)/shard_map/all_to_all | solution.py:379
  267.8 5.1 %collective-permute-start.19 = (bf16[512,384]{1,0:T(8,128)(2,1)S(1)}, bf16[512,384]{1,0:T(8,128)(2,1)S(1)}, u32[]{:S(2)}, u32[]{:S(2)}) collective-permute-start(bf16[512,384]{1,0:T(8,128)(2,1)S(1)} %select_bitcast_fusion), channel_id=1, source_target_pairs={{0,128},{128,0},{1,129},{129,1},{2,130},{130,2},{3,131},{131,3},{4... | collective-permute-start | bytes 1179656 | tf_op jit(solution)/shard_map/ppermute | solution.py:376
  273.0 8.9 %copy-start.9 = (bf16[128,1024]{1,0:T(8,128)(2,1)S(1)}, bf16[128,1024]{1,0:T(8,128)(2,1)}, u32[]{:S(2)}) copy-start(bf16[128,1024]{1,0:T(8,128)(2,1)} %reduce-scatter.2.cloned.1.call-done) | copy-start | bytes 786436
  274.0 8.0 %collective-permute-start.12 = (bf16[128,512]{1,0:T(8,128)(2,1)S(1)}, bf16[128,512]{1,0:T(8,128)(2,1)S(1)}, u32[]{:S(2)}, u32[]{:S(2)}) collective-permute-start(bf16[128,512]{1,0:T(8,128)(2,1)S(1)} %slice.89), channel_id=1, source_target_pairs={{0,128},{128,0},{1,129},{129,1},{2,130},{130,2},{3,131},{131,3},{4... | collective-permute-start | bytes 393224 | tf_op jit(solution)/shard_map/ppermute | solution.py:383
  (6 other events, 6.4 us)
Sparse Core Ops, SparseCore 0:
  26.9 109.6 all-gather.1
  194.1 74.3 reduce-scatter.1

commit v11 on v10

--- a/solution.py
+++ b/solution.py
@@ -326,7 +326,7 @@
     line, stay = lax.optimization_barrier((line, stay))
     line = lax.all_gather(line, ("zh", "zl"), axis=0, tiled=True)
 
-    near, crossed = lax.optimization_barrier((near, crossed))
+    near, crossed, weight = lax.optimization_barrier((near, crossed, weight))
     near_other = lax.ppermute(near, "co", SWAP)
     back = rows_back(near, near_other, weight, here, False)
     *wide, _ = lax.optimization_barrier((*gather_back(crossed), back))

time: 293 us -> 294 us (level)
  starting transfers between devices: 109 us -> 102 us
  waiting for transfers between devices: 72.4 us -> 79 us
    reduce_scatter x1, waiting for transfers between devices: 0.02 us -> 20 us  [on_device(): lax.psum_scatter(spread.reshape(2 * nzl * batches * tok, quarter), ('zh',...]
    ppermute x1, waiting for transfers between devices: 30.3 us -> 14.8 us  [on_device(): crossed = lax.ppermute(leave, 'zh', SWAP)]
    all_gather x1, waiting for transfers between devices: 0.02 us -> 12.9 us  [on_device(): line = lax.all_gather(line, ('zh', 'zl'), axis=0, tiled=True)]
    ppermute x1, starting transfers between devices: 15.2 us -> 2.95 us  [on_device(): near_other = lax.ppermute(near, 'co', SWAP)]
    ppermute x9, waiting for transfers between devices: 32.9 us -> 21.4 us  [along_y(): lax.ppermute(v, 'y', [(i, (i + d) % ny) for i in range(ny)])]
    ppermute x1, starting transfers between devices: 6.98 us -> 11.4 us  [on_device(): other = lax.ppermute(expert_part[:, eighth:], 'co', SWAP)]
  transfers between devices with their start and end apart: 25 -> 25, of which waited for: 9 -> 12; matrix products, arithmetic and copies ran while one was open for 11% -> 11% of each run, Pallas kernels for 15% -> 15%
where the time goes in v11:
time: 294 us; the launch traced here: 292 us
  starting transfers between devices  102 us (35%)
  waiting for transfers between devices  79 us (27%)
  Pallas kernels  48.9 us (17%)
  local copies, waits for them, and re-layouts  28 us (10%)
  other arithmetic  16.7 us (6%)
  between operations  14.7 us (5%)
    ppermute x9, starting transfers between devices, along_y(): lax.ppermute(v, 'y', [(i, (i + d) % ny) for i in range(ny)])  27.3 us
    ppermute x9, waiting for transfers between devices, along_y(): lax.ppermute(v, 'y', [(i, (i + d) % ny) for i in range(ny)])  21.4 us
    reduce_scatter x1, waiting for transfers between devices, on_device(): lax.psum_scatter(spread.reshape(2 * nzl * batches * tok, quarter), ('zh',...  20 us
    ppermute x1, waiting for transfers between devices, on_device(): crossed = lax.ppermute(leave, 'zh', SWAP)  14.8 us
    ppermute x1, starting transfers between devices, on_device(): crossed = lax.ppermute(leave, 'zh', SWAP)  14.4 us
    pallas_call x2, Pallas kernels, weight_sum(): call(body, (4,), [pl.BlockSpec((2, part, width), lambda d, where: (0, 0,...  14.3 us
    all_gather x1, waiting for transfers between devices, on_device(): line = lax.all_gather(line, ('zh', 'zl'), axis=0, tiled=True)  12.9 us
    ppermute x3, starting transfers between devices, gather_back(): lax.ppermute(v, 'x', [(i, (i + d) % nx) for i in range(nx)])  11.4 us
  transfers between devices with their start and end apart: 25, of which 12 were waited for; matrix products, arithmetic and copies ran while one was open for 11% of the time, Pallas kernels for 15%

profile of v11, /device:TPU:1, one launch (start us, length us, event | category | flops | bytes accessed | tf_op | source)
XLA Modules:
  0.0 292.3 jit_solution(12482927511268250913)
XLA Ops:
  7.3 2.9 fusion.1
  10.3 5.5 %collective-permute-start.1 = (bf16[576,384]{1,0:T(8,128)(2,1)S(1)}, bf16[576,384]{1,0:T(8,128)(2,1)S(1)}, u32[]{:S(2)}, u32[]{:S(2)}) collective-permute-start(bf16[576,384]{1,0:T(8,128)(2,1)S(1)} %broadcast_select_fusion.5), channel_id=1, source_target_pairs={{0,2},{1,3},{2,0},{3,1},{4,6},{5,7},{6,4},{7,5},{8,10},{9,11},{10,... | collective-permute-start | bytes 1327112 | tf_op jit(solution)/shard_map/ppermute | solution.py:301
  18.6 5.2 %collective-permute-start = (bf16[128,576]{1,0:T(8,128)(2,1)}, bf16[128,576]{1,0:T(8,128)(2,1)S(1)}, u32[]{:S(2)}, u32[]{:S(2)}) collective-permute-start(bf16[128,576]{1,0:T(8,128)(2,1)} %pad_maximum_fusion.2), channel_id=1, source_target_pairs={{0,128},{128,0},{1,129},{129,1},{2,130},{130,2},{3,131},{131,3},{4... | collective-permute-start | bytes 442376 | tf_op jit(solution)/shard_map/ppermute | solution.py:324
  28.1 4.5 %all-to-all-start = ((bf16[4,576,384]{2,1,0:T(8,128)(2,1)}), bf16[4,576,384]{2,1,0:T(8,128)(2,1)S(1)}, u32[]{:S(2)}, u32[]{:S(2)}) async-start(bf16[4,576,384]{2,1,0:T(8,128)(2,1)} %broadcast_in_dim.50), calls=%async_computation | async-start | bytes 3538944 | tf_op jit(solution)/shard_map/all_to_all | solution.py:269
  33.8 4.0 %collective-permute-start.3 = (bf16[512,384]{1,0:T(8,128)(2,1)S(1)}, bf16[512,384]{1,0:T(8,128)(2,1)S(1)}, u32[]{:S(2)}, u32[]{:S(2)}) collective-permute-start(bf16[512,384]{1,0:T(8,128)(2,1)S(1)} %select_bitcast_fusion.1), channel_id=1, source_target_pairs={{0,128},{128,0},{1,129},{129,1},{2,130},{130,2},{3,131},{131,3},{4... | collective-permute-start | bytes 1179656 | tf_op jit(solution)/shard_map/ppermute | solution.py:308
  37.8 14.4 %collective-permute-start.2 = (bf16[576,384]{1,0:T(8,128)(2,1)}, bf16[576,384]{1,0:T(8,128)(2,1)S(1)}, u32[]{:S(2)}, u32[]{:S(2)}) collective-permute-start(bf16[576,384]{1,0:T(8,128)(2,1)} %get-tuple-element.54), channel_id=1, source_target_pairs={{0,256},{256,0},{1,257},{257,1},{2,258},{258,2},{3,259},{259,3},{4... | collective-permute-start | bytes 1327112 | tf_op jit(solution)/shard_map/ppermute | solution.py:303
  54.3 14.8 %collective-permute-done.2 = bf16[576,384]{1,0:T(8,128)(2,1)S(1)} collective-permute-done((bf16[576,384]{1,0:T(8,128)(2,1)}, bf16[576,384]{1,0:T(8,128)(2,1)S(1)}, u32[]{:S(2)}, u32[]{:S(2)}) %collective-permute-start.2) | collective-permute-done | bytes 442400 | tf_op jit(solution)/shard_map/ppermute | solution.py:303
  69.2 2.9 %collective-permute-start.7 = (bf16[4,576,384]{2,1,0:T(8,128)(2,1)S(1)}, bf16[4,576,384]{2,1,0:T(8,128)(2,1)}, u32[]{:S(2)}, u32[]{:S(2)}) collective-permute-start(bf16[4,576,384]{2,1,0:T(8,128)(2,1)S(1)} %all-to-all-done.near0.near1.refs_4_.refs_5_), channel_id=1, source_target_pairs={{0,128},{128,0},{1,129},{129,1},{2,130},{130,2},{3,131},{131,3},{4... | collective-permute-start | bytes 5308424 | tf_op jit(solution)/shard_map/ppermute | solution.py:330
  72.1 4.0 %collective-permute-start.4 = (bf16[576,384]{1,0:T(8,128)(2,1)S(1)}, bf16[576,384]{1,0:T(8,128)(2,1)}, u32[]{:S(2)}, u32[]{:S(2)}) collective-permute-start(bf16[576,384]{1,0:T(8,128)(2,1)S(1)} %collective-permute-done.2), channel_id=1, source_target_pairs={{0,1},{1,2},{2,3},{3,0},{4,5},{5,6},{6,7},{7,4},{8,9},{9,10},{10,1... | collective-permute-start | bytes 1327112 | tf_op jit(solution)/shard_map/ppermute | solution.py:275
  76.2 4.3 %collective-permute-start.5 = (bf16[576,384]{1,0:T(8,128)(2,1)S(1)}, bf16[576,384]{1,0:T(8,128)(2,1)}, u32[]{:S(2)}, u32[]{:S(2)}) collective-permute-start(bf16[576,384]{1,0:T(8,128)(2,1)S(1)} %collective-permute-done.2), channel_id=1, source_target_pairs={{0,2},{1,3},{2,0},{3,1},{4,6},{5,7},{6,4},{7,5},{8,10},{9,11},{10,... | collective-permute-start | bytes 1327112 | tf_op jit(solution)/shard_map/ppermute | solution.py:275
  80.5 3.1 %collective-permute-start.6 = (bf16[576,384]{1,0:T(8,128)(2,1)S(1)}, bf16[576,384]{1,0:T(8,128)(2,1)}, u32[]{:S(2)}, u32[]{:S(2)}) collective-permute-start(bf16[576,384]{1,0:T(8,128)(2,1)S(1)} %collective-permute-done.2), channel_id=1, source_target_pairs={{0,3},{1,0},{2,1},{3,2},{4,7},{5,4},{6,5},{7,6},{8,11},{9,8},{10,9... | collective-permute-start | bytes 1327112 | tf_op jit(solution)/shard_map/ppermute | solution.py:275
  84.8 6.3 %shard_map.95 = bf16[4,2,288,512]{3,2,1,0:T(8,128)(2,1)} custom-call(s32[2]{0:T(128)S(1)} %pad_add_fusion.where_ref, bf16[4,576,384]{2,1,0:T(8,128)(2,1)S(1)} %all-to-all-done.near0.near1.refs_4_.refs_5_, bf16[4,576,384]{2,1,0:T(8,128)(2,1)S(1)} %all-to-all-done.near0.near1.refs_4_.refs_5_, ...), custom_call_target="tpu_custom_call" | custom-call | flops 1811939328 | bytes 8388608 | tf_op jit(solution)/shard_map/pallas_call | solution.py:89
  91.0 7.4 %collective-permute-done.5 = bf16[576,384]{1,0:T(8,128)(2,1)} collective-permute-done((bf16[576,384]{1,0:T(8,128)(2,1)S(1)}, bf16[576,384]{1,0:T(8,128)(2,1)}, u32[]{:S(2)}, u32[]{:S(2)}) %collective-permute-start.5) | collective-permute-done | bytes 442400 | tf_op jit(solution)/shard_map/ppermute | solution.py:275
  105.2 4.6 %all-to-all-start.1 = ((bf16[4,576,512]{2,1,0:T(8,128)(2,1)}), bf16[4,576,512]{2,1,0:T(8,128)(2,1)}, u32[]{:S(2)}, u32[]{:S(2)}) async-start(bf16[4,576,512]{2,1,0:T(8,128)(2,1)} %bitcast.94), calls=%async_computation.1 | async-start | bytes 4718592 | tf_op jit(solution)/shard_map/all_to_all | solution.py:281
  111.2 6.9 %shard_map.96 = (bf16[2,288,512]{2,1,0:T(8,128)(2,1)S(1)}, bf16[2,288,512]{2,1,0:T(8,128)(2,1)}, bf16[2,288,512]{2,1,0:T(8,128)(2,1)}, bf16[2,288,512]{2,1,0:T(8,128)(2,1)}) custom-call(s32[2]{0:T(128)S(1)} %pad_add_fusion.where_ref, bf16[4,576,384]{2,1,0:T(8,128)(2,1)} %pad_maximum_fusion.near0.near1.refs_4_.refs_5_, ...), custom_call_target="tpu_custom_call" | custom-call | flops 1811939328 | bytes 8388608 | tf_op jit(solution)/shard_map/pallas_call | solution.py:116
  118.1 5.2 %collective-permute-start.9 = (bf16[2,288,512]{2,1,0:T(8,128)(2,1)}, bf16[2,288,512]{2,1,0:T(8,128)(2,1)}, u32[]{:S(2)}, u32[]{:S(2)}) collective-permute-start(bf16[2,288,512]{2,1,0:T(8,128)(2,1)} %get-tuple-element.39), channel_id=1, source_target_pairs={{0,12},{4,0},{8,4},{12,8},{1,13},{5,1},{9,5},{13,9},{2,14},{6,2},{... | collective-permute-start | bytes 1769480 | tf_op jit(solution)/shard_map/ppermute | solution.py:286
  128.1 12.9 %all-gather.2.cloned.1.call-done = bf16[2048,1152]{1,0:T(8,128)(2,1)} async-done(((bf16[128,1152]{1,0:T(8,128)(2,1)}), bf16[2048,1152]{1,0:T(8,128)(2,1)}) %all-gather.2.cloned.1.call-update) | async-done | bytes 4718608 | tf_op jit(solution)/shard_map/all_gather | solution.py:327
  153.9 6.2 %shard_map.97.refs_5_ = bf16[2,8,2,64,1024]{4,3,2,1,0:T(8,128)(2,1)} custom-call(s32[1]{0:T(128)} %bitcast.4.zh_ref, bf16[4,2,2,144,512]{4,3,2,1,0:T(8,128)(2,1)} %bitcast.25.back_ref, f32[8,2,576]{2,1,0:T(2,128)S(1)} %maximum_bitcast_fusion.1.table_ref), custom_call_target="tpu_custom_call" | custom-call | flops 2415919104 | bytes 8388608 | tf_op jit(solution)/shard_map/pallas_call | solution.py:143
  160.2 5.0 %collective-permute-done.11 = bf16[2,288,512]{2,1,0:T(8,128)(2,1)} collective-permute-done((bf16[2,288,512]{2,1,0:T(8,128)(2,1)}, bf16[2,288,512]{2,1,0:T(8,128)(2,1)}, u32[]{:S(2)}, u32[]{:S(2)}) %collective-permute-start.11) | collective-permute-done | bytes 589856 | tf_op jit(solution)/shard_map/ppermute | solution.py:286
  165.1 6.2 %shard_map.98 = bf16[2,8,2,64,1024]{4,3,2,1,0:T(8,128)(2,1)} custom-call(s32[1]{0:T(128)} %bitcast.4.zh_ref, bf16[2,2,144,512]{3,2,1,0:T(8,128)(2,1)S(1)} %bitcast.85, bf16[2,2,144,512]{3,2,1,0:T(8,128)(2,1)} %bitcast.16.refs_1_, bf16[2,2,144,512]{3,2,1,0:T(8,128)(2,1)} %bitcast.17.refs_2_, ...), custom_call_target="tpu_custom_call", output_to_operand_aliasing={{}: (6, {})} | custom-call | flops 2415919104 | bytes 8388608 | tf_op jit(solution)/shard_map/pallas_call | solution.py:176
  175.1 4.6 %shard_map.100 = (bf16[2,2,144,512]{3,2,1,0:T(8,128)(2,1)S(1)}, bf16[2,2,144,512]{3,2,1,0:T(8,128)(2,1)S(1)}, bf16[2,2,144,512]{3,2,1,0:T(8,128)(2,1)}, bf16[2,2,144,512]{3,2,1,0:T(8,128)(2,1)}) custom-call(s32[1]{0:T(128)} %bitcast.4.zh_ref, bf16[16,2,64,1152]{3,2,1,0:T(8,128)(2,1)} %bitcast.91, f32[8,576,2]{2,1,0:T(8,128)S(1)} %bitcast.83), custom_call_target="tpu_custom_call" | custom-call | flops 1207959552 | bytes 8388608 | tf_op jit(solution)/shard_map/pallas_call | solution.py:50
  184.7 3.6 %collective-permute-start.18 = (bf16[2,2,144,512]{3,2,1,0:T(8,128)(2,1)}, bf16[2,2,144,512]{3,2,1,0:T(8,128)(2,1)}, u32[]{:S(2)}, u32[]{:S(2)}) collective-permute-start(bf16[2,2,144,512]{3,2,1,0:T(8,128)(2,1)} %get-tuple-element.51), channel_id=1, source_target_pairs={{0,12},{4,0},{8,4},{12,8},{1,13},{5,1},{9,5},{13,9},{2,14},{6,2},{... | collective-permute-start | bytes 1769480 | tf_op jit(solution)/shard_map/ppermute | solution.py:286
  188.2 4.6 %shard_map.99 = (bf16[2,2,144,512]{3,2,1,0:T(8,128)(2,1)S(1)}, bf16[2,2,144,512]{3,2,1,0:T(8,128)(2,1)}, bf16[2,2,144,512]{3,2,1,0:T(8,128)(2,1)}, bf16[2,2,144,512]{3,2,1,0:T(8,128)(2,1)}) custom-call(s32[1]{0:T(128)} %bitcast.4.zh_ref, bf16[16,2,64,1152]{3,2,1,0:T(8,128)(2,1)} %bitcast.92, f32[8,576,2]{2,1,0:T(8,128)S(1)} %bitcast.84), custom_call_target="tpu_custom_call" | custom-call | flops 1207959552 | bytes 8388608 | tf_op jit(solution)/shard_map/pallas_call | solution.py:50
  195.2 3.7 %collective-permute-start.14 = (bf16[2,2,144,512]{3,2,1,0:T(8,128)(2,1)}, bf16[2,2,144,512]{3,2,1,0:T(8,128)(2,1)}, u32[]{:S(2)}, u32[]{:S(2)}) collective-permute-start(bf16[2,2,144,512]{3,2,1,0:T(8,128)(2,1)} %get-tuple-element.46), channel_id=1, source_target_pairs={{0,8},{4,12},{8,0},{12,4},{1,9},{5,13},{9,1},{13,5},{2,10},{6,14},... | collective-permute-start | bytes 1769480 | tf_op jit(solution)/shard_map/ppermute | solution.py:286
  208.9 4.5 %all-to-all-start.2 = ((bf16[4,128,1024]{2,1,0:T(8,128)(2,1)}), bf16[4,128,1024]{2,1,0:T(8,128)(2,1)}, u32[]{:S(2)}, u32[]{:S(2)}) async-start(bf16[4,128,1024]{2,1,0:T(8,128)(2,1)} %copy.98), calls=%async_computation.2 | async-start | bytes 2097152 | tf_op jit(solution)/shard_map/all_to_all | solution.py:379
  216.3 6.8 %shard_map.101.refs_8_ = f32[2,512,384]{2,1,0:T(8,128)S(1)} custom-call(s32[2]{0:T(128)S(1)} %pad_add_fusion.where_ref, bf16[2,288,512]{2,1,0:T(8,128)(2,1)S(1)} %bitcast.87, bf16[2,288,512]{2,1,0:T(8,128)(2,1)S(1)} %bitcast.88, bf16[2,288,512]{2,1,0:T(8,128)(2,1)} %bitcast.39.refs_2_, bf16[2,288,512]{2,1,0:T(8,128)(2,1)} %bitcast.40.refs_3_, ...), custom_call_target="tpu_custom_call" | custom-call | flops 1811939328 | bytes 8388608 | tf_op jit(solution)/shard_map/pallas_call | solution.py:218
  225.4 5.2 %collective-permute-done.14 = bf16[2,2,144,512]{3,2,1,0:T(8,128)(2,1)} collective-permute-done((bf16[2,2,144,512]{3,2,1,0:T(8,128)(2,1)}, bf16[2,2,144,512]{3,2,1,0:T(8,128)(2,1)}, u32[]{:S(2)}, u32[]{:S(2)}) %collective-permute-start.14) | collective-permute-done | bytes 589856 | tf_op jit(solution)/shard_map/ppermute | solution.py:286
  230.6 7.0 %collective-permute-done.15 = bf16[2,2,144,512]{3,2,1,0:T(8,128)(2,1)} collective-permute-done((bf16[2,2,144,512]{3,2,1,0:T(8,128)(2,1)}, bf16[2,2,144,512]{3,2,1,0:T(8,128)(2,1)}, u32[]{:S(2)}, u32[]{:S(2)}) %collective-permute-start.15) | collective-permute-done | bytes 589856 | tf_op jit(solution)/shard_map/ppermute | solution.py:286
  237.6 7.4 %shard_map.102 = bf16[2,512,384]{2,1,0:T(8,128)(2,1)S(1)} custom-call(s32[2]{0:T(128)S(1)} %pad_add_fusion.where_ref, bf16[2,288,512]{2,1,0:T(8,128)(2,1)S(1)} %bitcast.86, bf16[2,288,512]{2,1,0:T(8,128)(2,1)} %bitcast.34.refs_1_, bf16[2,288,512]{2,1,0:T(8,128)(2,1)} %bitcast.35.refs_2_, bf16[2,288,512]{2,1,0:T(8,128)(2,1)} %bitcast.36.refs_3_, ...), custom_call_target="tpu_custom_call" | custom-call | flops 1811939328 | bytes 8388608 | tf_op jit(solution)/shard_map/pallas_call | solution.py:218
  245.1 3.6 %collective-permute-start.19 = (bf16[512,384]{1,0:T(8,128)(2,1)S(1)}, bf16[512,384]{1,0:T(8,128)(2,1)S(1)}, u32[]{:S(2)}, u32[]{:S(2)}) collective-permute-start(bf16[512,384]{1,0:T(8,128)(2,1)S(1)} %select_bitcast_fusion), channel_id=1, source_target_pairs={{0,128},{128,0},{1,129},{129,1},{2,130},{130,2},{3,131},{131,3},{4... | collective-permute-start | bytes 1179656 | tf_op jit(solution)/shard_map/ppermute | solution.py:376
  250.4 20.0 %reduce-scatter.2.cloned.1.call-done = bf16[128,1024]{1,0:T(8,128)(2,1)} async-done(((bf16[2048,1024]{1,0:T(8,128)(2,1)}), bf16[128,1024]{1,0:T(8,128)(2,1)}) %reduce-scatter.2.cloned.1.call-update) | async-done | bytes 262160 | tf_op jit(solution)/shard_map/reduce_scatter | solution.py:359
  271.3 11.4 %collective-permute-start.12 = (bf16[128,512]{1,0:T(8,128)(2,1)S(1)}, bf16[128,512]{1,0:T(8,128)(2,1)S(1)}, u32[]{:S(2)}, u32[]{:S(2)}) collective-permute-start(bf16[128,512]{1,0:T(8,128)(2,1)S(1)} %slice.89), channel_id=1, source_target_pairs={{0,128},{128,0},{1,129},{129,1},{2,130},{130,2},{3,131},{131,3},{4... | collective-permute-start | bytes 393224 | tf_op jit(solution)/shard_map/ppermute | solution.py:383
  (114 shorter events, 69.1 us)
Async XLA Ops:
  7.2 9.8 %copy-start = (bf16[2,64,4096]{2,1,0:T(8,128)(2,1)S(1)}, bf16[2,64,4096]{2,1,0:T(8,128)(2,1)}, u32[]{:S(2)}) copy-start(bf16[2,64,4096]{2,1,0:T(8,128)(2,1)} %param.8) | copy-start | bytes 3145732
  7.2 133.8 %all-gather.2.cloned.1.call-start = ((), (), s32[]{:S(2)}) async-start(), calls=%async_computation.4 | async-start | bytes 5013504 | tf_op jit(solution)/shard_map/all_gather | solution.py:327
  7.3 8.5 %copy-start.10 = (s32[2,64,8]{1,2,0:T(8,128)S(1)}, s32[2,64,8]{1,2,0:T(8,128)}, u32[]{:S(2)}) copy-start(s32[2,64,8]{1,2,0:T(8,128)} %param.10) | copy-start | bytes 12292
  7.3 8.5 %copy-start.11 = (s32[2,64,8]{1,2,0:T(8,128)S(1)}, s32[2,64,8]{1,2,0:T(8,128)}, u32[]{:S(2)}) copy-start(s32[2,64,8]{1,2,0:T(8,128)} %param.9) | copy-start | bytes 12292
  7.3 8.6 %copy-start.12 = (f32[2,64,8]{1,2,0:T(8,128)S(1)}, f32[2,64,8]{1,2,0:T(8,128)}, u32[]{:S(2)}) copy-start(f32[2,64,8]{1,2,0:T(8,128)} %param.11) | copy-start | bytes 12292
  10.3 15.6 %collective-permute-start.1 = (bf16[576,384]{1,0:T(8,128)(2,1)S(1)}, bf16[576,384]{1,0:T(8,128)(2,1)S(1)}, u32[]{:S(2)}, u32[]{:S(2)}) collective-permute-start(bf16[576,384]{1,0:T(8,128)(2,1)S(1)} %broadcast_select_fusion.5), channel_id=1, source_target_pairs={{0,2},{1,3},{2,0},{3,1},{4,6},{5,7},{6,4},{7,5},{8,10},{9,11},{10,... | collective-permute-start | bytes 1327112 | tf_op jit(solution)/shard_map/ppermute | solution.py:301
  18.6 6.4 %collective-permute-start = (bf16[128,576]{1,0:T(8,128)(2,1)}, bf16[128,576]{1,0:T(8,128)(2,1)S(1)}, u32[]{:S(2)}, u32[]{:S(2)}) collective-permute-start(bf16[128,576]{1,0:T(8,128)(2,1)} %pad_maximum_fusion.2), channel_id=1, source_target_pairs={{0,128},{128,0},{1,129},{129,1},{2,130},{130,2},{3,131},{131,3},{4... | collective-permute-start | bytes 442376 | tf_op jit(solution)/shard_map/ppermute | solution.py:324
  28.1 41.1 %all-to-all-start = ((bf16[4,576,384]{2,1,0:T(8,128)(2,1)}), bf16[4,576,384]{2,1,0:T(8,128)(2,1)S(1)}, u32[]{:S(2)}, u32[]{:S(2)}) async-start(bf16[4,576,384]{2,1,0:T(8,128)(2,1)} %broadcast_in_dim.50), calls=%async_computation | async-start | bytes 3538944 | tf_op jit(solution)/shard_map/all_to_all | solution.py:269
  33.8 18.4 %collective-permute-start.3 = (bf16[512,384]{1,0:T(8,128)(2,1)S(1)}, bf16[512,384]{1,0:T(8,128)(2,1)S(1)}, u32[]{:S(2)}, u32[]{:S(2)}) collective-permute-start(bf16[512,384]{1,0:T(8,128)(2,1)S(1)} %select_bitcast_fusion.1), channel_id=1, source_target_pairs={{0,128},{128,0},{1,129},{129,1},{2,130},{130,2},{3,131},{131,3},{4... | collective-permute-start | bytes 1179656 | tf_op jit(solution)/shard_map/ppermute | solution.py:308
  37.8 31.4 %collective-permute-start.2 = (bf16[576,384]{1,0:T(8,128)(2,1)}, bf16[576,384]{1,0:T(8,128)(2,1)S(1)}, u32[]{:S(2)}, u32[]{:S(2)}) collective-permute-start(bf16[576,384]{1,0:T(8,128)(2,1)} %get-tuple-element.54), channel_id=1, source_target_pairs={{0,256},{256,0},{1,257},{257,1},{2,258},{258,2},{3,259},{259,3},{4... | collective-permute-start | bytes 1327112 | tf_op jit(solution)/shard_map/ppermute | solution.py:303
  69.2 14.5 %collective-permute-start.7 = (bf16[4,576,384]{2,1,0:T(8,128)(2,1)S(1)}, bf16[4,576,384]{2,1,0:T(8,128)(2,1)}, u32[]{:S(2)}, u32[]{:S(2)}) collective-permute-start(bf16[4,576,384]{2,1,0:T(8,128)(2,1)S(1)} %all-to-all-done.near0.near1.refs_4_.refs_5_), channel_id=1, source_target_pairs={{0,128},{128,0},{1,129},{129,1},{2,130},{130,2},{3,131},{131,3},{4... | collective-permute-start | bytes 5308424 | tf_op jit(solution)/shard_map/ppermute | solution.py:330
  72.1 18.9 %collective-permute-start.4 = (bf16[576,384]{1,0:T(8,128)(2,1)S(1)}, bf16[576,384]{1,0:T(8,128)(2,1)}, u32[]{:S(2)}, u32[]{:S(2)}) collective-permute-start(bf16[576,384]{1,0:T(8,128)(2,1)S(1)} %collective-permute-done.2), channel_id=1, source_target_pairs={{0,1},{1,2},{2,3},{3,0},{4,5},{5,6},{6,7},{7,4},{8,9},{9,10},{10,1... | collective-permute-start | bytes 1327112 | tf_op jit(solution)/shard_map/ppermute | solution.py:275
  76.2 22.3 %collective-permute-start.5 = (bf16[576,384]{1,0:T(8,128)(2,1)S(1)}, bf16[576,384]{1,0:T(8,128)(2,1)}, u32[]{:S(2)}, u32[]{:S(2)}) collective-permute-start(bf16[576,384]{1,0:T(8,128)(2,1)S(1)} %collective-permute-done.2), channel_id=1, source_target_pairs={{0,2},{1,3},{2,0},{3,1},{4,6},{5,7},{6,4},{7,5},{8,10},{9,11},{10,... | collective-permute-start | bytes 1327112 | tf_op jit(solution)/shard_map/ppermute | solution.py:275
  80.5 19.3 %collective-permute-start.6 = (bf16[576,384]{1,0:T(8,128)(2,1)S(1)}, bf16[576,384]{1,0:T(8,128)(2,1)}, u32[]{:S(2)}, u32[]{:S(2)}) collective-permute-start(bf16[576,384]{1,0:T(8,128)(2,1)S(1)} %collective-permute-done.2), channel_id=1, source_target_pairs={{0,3},{1,0},{2,1},{3,2},{4,7},{5,4},{6,5},{7,6},{8,11},{9,8},{10,9... | collective-permute-start | bytes 1327112 | tf_op jit(solution)/shard_map/ppermute | solution.py:275
  102.6 7.5 %collective-permute-start.8 = (bf16[4,576,384]{2,1,0:T(8,128)(2,1)}, bf16[4,576,384]{2,1,0:T(8,128)(2,1)}, u32[]{:S(2)}, u32[]{:S(2)}) collective-permute-start(bf16[4,576,384]{2,1,0:T(8,128)(2,1)} %pad_maximum_fusion.near0.near1.refs_4_.refs_5_), channel_id=1, source_target_pairs={{0,128},{128,0},{1,129},{129,1},{2,130},{130,2},{3,131},{131,3},{4... | collective-permute-start | bytes 5308424 | tf_op jit(solution)/shard_map/ppermute | solution.py:335
  105.2 48.7 %all-to-all-start.1 = ((bf16[4,576,512]{2,1,0:T(8,128)(2,1)}), bf16[4,576,512]{2,1,0:T(8,128)(2,1)}, u32[]{:S(2)}, u32[]{:S(2)}) async-start(bf16[4,576,512]{2,1,0:T(8,128)(2,1)} %bitcast.94), calls=%async_computation.1 | async-start | bytes 4718592 | tf_op jit(solution)/shard_map/all_to_all | solution.py:281
  109.9 160.5 %reduce-scatter.2.cloned.1.call-start = ((), (), s32[]{:S(2)}) async-start(), calls=%async_computation.5 | async-start | bytes 4456448 | tf_op jit(solution)/shard_map/reduce_scatter | solution.py:359
  118.1 42.1 %collective-permute-start.9 = (bf16[2,288,512]{2,1,0:T(8,128)(2,1)}, bf16[2,288,512]{2,1,0:T(8,128)(2,1)}, u32[]{:S(2)}, u32[]{:S(2)}) collective-permute-start(bf16[2,288,512]{2,1,0:T(8,128)(2,1)} %get-tuple-element.39), channel_id=1, source_target_pairs={{0,12},{4,0},{8,4},{12,8},{1,13},{5,1},{9,5},{13,9},{2,14},{6,2},{... | collective-permute-start | bytes 1769480 | tf_op jit(solution)/shard_map/ppermute | solution.py:286
  123.3 36.9 %collective-permute-start.10 = (bf16[2,288,512]{2,1,0:T(8,128)(2,1)}, bf16[2,288,512]{2,1,0:T(8,128)(2,1)}, u32[]{:S(2)}, u32[]{:S(2)}) collective-permute-start(bf16[2,288,512]{2,1,0:T(8,128)(2,1)} %get-tuple-element.40), channel_id=1, source_target_pairs={{0,8},{4,12},{8,0},{12,4},{1,9},{5,13},{9,1},{13,5},{2,10},{6,14},... | collective-permute-start | bytes 1769480 | tf_op jit(solution)/shard_map/ppermute | solution.py:286
  125.2 40.0 %collective-permute-start.11 = (bf16[2,288,512]{2,1,0:T(8,128)(2,1)}, bf16[2,288,512]{2,1,0:T(8,128)(2,1)}, u32[]{:S(2)}, u32[]{:S(2)}) collective-permute-start(bf16[2,288,512]{2,1,0:T(8,128)(2,1)} %get-tuple-element.41), channel_id=1, source_target_pairs={{0,4},{4,8},{8,12},{12,0},{1,5},{5,9},{9,13},{13,1},{2,6},{6,10},{... | collective-permute-start | bytes 1769480 | tf_op jit(solution)/shard_map/ppermute | solution.py:286
  173.5 1.7 copy-start.1
  179.7 13.2 %copy-start.4 = (bf16[2,2,144,512]{3,2,1,0:T(8,128)(2,1)}, bf16[2,2,144,512]{3,2,1,0:T(8,128)(2,1)S(1)}, u32[]{:S(2)}) copy-start(bf16[2,2,144,512]{3,2,1,0:T(8,128)(2,1)S(1)} %get-tuple-element.48) | copy-start | bytes 1769476
  179.7 20.4 %collective-permute-start.16 = (bf16[2,2,144,512]{3,2,1,0:T(8,128)(2,1)S(1)}, bf16[2,2,144,512]{3,2,1,0:T(8,128)(2,1)S(1)}, u32[]{:S(2)}, u32[]{:S(2)}) collective-permute-start(bf16[2,2,144,512]{3,2,1,0:T(8,128)(2,1)S(1)} %get-tuple-element.49), channel_id=1, source_target_pairs={{0,4},{4,8},{8,12},{12,0},{1,5},{5,9},{9,13},{13,1},{2,6},{6,10},{... | collective-permute-start | bytes 1769480 | tf_op jit(solution)/shard_map/ppermute | solution.py:286
  182.0 31.4 %collective-permute-start.17 = (bf16[2,2,144,512]{3,2,1,0:T(8,128)(2,1)}, bf16[2,2,144,512]{3,2,1,0:T(8,128)(2,1)}, u32[]{:S(2)}, u32[]{:S(2)}) collective-permute-start(bf16[2,2,144,512]{3,2,1,0:T(8,128)(2,1)} %get-tuple-element.50), channel_id=1, source_target_pairs={{0,8},{4,12},{8,0},{12,4},{1,9},{5,13},{9,1},{13,5},{2,10},{6,14},... | collective-permute-start | bytes 1769480 | tf_op jit(solution)/shard_map/ppermute | solution.py:286
  184.7 29.5 %collective-permute-start.18 = (bf16[2,2,144,512]{3,2,1,0:T(8,128)(2,1)}, bf16[2,2,144,512]{3,2,1,0:T(8,128)(2,1)}, u32[]{:S(2)}, u32[]{:S(2)}) collective-permute-start(bf16[2,2,144,512]{3,2,1,0:T(8,128)(2,1)} %get-tuple-element.51), channel_id=1, source_target_pairs={{0,12},{4,0},{8,4},{12,8},{1,13},{5,1},{9,5},{13,9},{2,14},{6,2},{... | collective-permute-start | bytes 1769480 | tf_op jit(solution)/shard_map/ppermute | solution.py:286
  192.8 32.6 %collective-permute-start.13 = (bf16[2,2,144,512]{3,2,1,0:T(8,128)(2,1)}, bf16[2,2,144,512]{3,2,1,0:T(8,128)(2,1)}, u32[]{:S(2)}, u32[]{:S(2)}) collective-permute-start(bf16[2,2,144,512]{3,2,1,0:T(8,128)(2,1)} %get-tuple-element.45), channel_id=1, source_target_pairs={{0,4},{4,8},{8,12},{12,0},{1,5},{5,9},{9,13},{13,1},{2,6},{6,10},{... | collective-permute-start | bytes 1769480 | tf_op jit(solution)/shard_map/ppermute | solution.py:286
  195.2 35.4 %collective-permute-start.14 = (bf16[2,2,144,512]{3,2,1,0:T(8,128)(2,1)}, bf16[2,2,144,512]{3,2,1,0:T(8,128)(2,1)}, u32[]{:S(2)}, u32[]{:S(2)}) collective-permute-start(bf16[2,2,144,512]{3,2,1,0:T(8,128)(2,1)} %get-tuple-element.46), channel_id=1, source_target_pairs={{0,8},{4,12},{8,0},{12,4},{1,9},{5,13},{9,1},{13,5},{2,10},{6,14},... | collective-permute-start | bytes 1769480 | tf_op jit(solution)/shard_map/ppermute | solution.py:286
  200.9 36.8 %collective-permute-start.15 = (bf16[2,2,144,512]{3,2,1,0:T(8,128)(2,1)}, bf16[2,2,144,512]{3,2,1,0:T(8,128)(2,1)}, u32[]{:S(2)}, u32[]{:S(2)}) collective-permute-start(bf16[2,2,144,512]{3,2,1,0:T(8,128)(2,1)} %get-tuple-element.47), channel_id=1, source_target_pairs={{0,12},{4,0},{8,4},{12,8},{1,13},{5,1},{9,5},{13,9},{2,14},{6,2},{... | collective-permute-start | bytes 1769480 | tf_op jit(solution)/shard_map/ppermute | solution.py:286
  208.9 39.9 %all-to-all-start.2 = ((bf16[4,128,1024]{2,1,0:T(8,128)(2,1)}), bf16[4,128,1024]{2,1,0:T(8,128)(2,1)}, u32[]{:S(2)}, u32[]{:S(2)}) async-start(bf16[4,128,1024]{2,1,0:T(8,128)(2,1)} %copy.98), calls=%async_computation.2 | async-start | bytes 2097152 | tf_op jit(solution)/shard_map/all_to_all | solution.py:379
  245.1 5.1 %collective-permute-start.19 = (bf16[512,384]{1,0:T(8,128)(2,1)S(1)}, bf16[512,384]{1,0:T(8,128)(2,1)S(1)}, u32[]{:S(2)}, u32[]{:S(2)}) collective-permute-start(bf16[512,384]{1,0:T(8,128)(2,1)S(1)} %select_bitcast_fusion), channel_id=1, source_target_pairs={{0,128},{128,0},{1,129},{129,1},{2,130},{130,2},{3,131},{131,3},{4... | collective-permute-start | bytes 1179656 | tf_op jit(solution)/shard_map/ppermute | solution.py:376
  270.3 13.4 %copy-start.9 = (bf16[128,1024]{1,0:T(8,128)(2,1)S(1)}, bf16[128,1024]{1,0:T(8,128)(2,1)}, u32[]{:S(2)}) copy-start(bf16[128,1024]{1,0:T(8,128)(2,1)} %reduce-scatter.2.cloned.1.call-done) | copy-start | bytes 786436
  271.3 12.4 %collective-permute-start.12 = (bf16[128,512]{1,0:T(8,128)(2,1)S(1)}, bf16[128,512]{1,0:T(8,128)(2,1)S(1)}, u32[]{:S(2)}, u32[]{:S(2)}) collective-permute-start(bf16[128,512]{1,0:T(8,128)(2,1)S(1)} %slice.89), channel_id=1, source_target_pairs={{0,128},{128,0},{1,129},{129,1},{2,130},{130,2},{3,131},{131,3},{4... | collective-permute-start | bytes 393224 | tf_op jit(solution)/shard_map/ppermute | solution.py:383
  (6 other events, 5.9 us)
Sparse Core Ops, SparseCore 0:
  26.9 114.0 all-gather.1
  171.5 98.7 reduce-scatter.1
